TPU v7x, 32 devices: a whole 2x2x4 slice. The times are simulated.
32 devices in a mesh: row: 8 (over z, y), col: 4 (over x, core).
Axes of the slice: x: 2, y: 2, z: 4, core: 2. Of those that a mesh axis runs over, the one named last changes fastest.
Arguments:
- fock_matrix: bfloat16 [1536, 1536], P('row', 'col'), as said below
- density: bfloat16 [1536, 1536], P('row', 'col'), as said below
- margin: bfloat16 [1536, 1536], P('row', 'col'), as said below
- fill_patterns: int32 [3, 48, 48], P(None, 'row', 'col'), may hold values from 0 to 1, as said below
- first_filters: int32 [3, 48, 48], P(None, 'row', 'col'), may hold values from 0 to 1, as said below
- owner_order: int32 [48], replicated, may hold values from 0 to 47, as said below
- second_filters: int32 [7, 48, 48], P(None, 'row', 'col'), may hold values from 0 to 1, as said below
Outputs:
- evolved: bfloat16 [1536, 1536], P('row', 'col')
Inputs may be any that keep to these rules, and one draw needn't show every extreme that they name: `fock_matrix`: Symmetric. `density`: Symmetric. `margin`: Symmetric, with unit diagonal. `fill_patterns`: each entry says whether a block is kept; each pattern is symmetric and keeps every diagonal block. `first_filters`: each entry says whether a block of the product is kept; each filter is symmetric and keeps every diagonal block. `second_filters`: each entry says whether a block of the product is kept, indexed in owner order; each filter is symmetric and keeps every diagonal block. `owner_order`: A permutation of the 48 block indices.
All inputs are finite; a program needn't handle non-finite values.
Results may differ from a plain program's by a relative error of at most 0.012.
Values may be sent and summed in bfloat16 or wider, within the bound.
No kernel may reach another device: no remote copies, remote signals or barrier semaphores. Data moves between devices by JAX's collectives and lax.ppermute only.
A program may use at most 64 MiB of HBM per device.

v0:
```python
import jax
import jax.numpy as jnp
from jax import lax
from jax.sharding import PartitionSpec as P

BLK = 32
TERMS = 6
SQUARINGS = 2


def expand(mask, values):
    row_blocks = mask.shape[0]
    column_blocks = mask.shape[1]
    shaped = values.reshape(row_blocks, BLK, column_blocks, BLK) * mask[:, None, :, None].astype(
        values.dtype
    )
    return shaped.reshape(values.shape)


def panel_rows(matrix):
    return lax.all_gather(matrix, "col", axis=1, tiled=True)


def panel_times(row_panel, matrix):
    return jnp.dot(
        row_panel,
        lax.all_gather(matrix, "row", axis=0, tiled=True),
        preferred_element_type=jnp.float32,
    )


def reorder(generator, owner_order):
    row_blocks = generator.shape[0] // BLK
    column_blocks = generator.shape[1] // BLK
    wanted_rows = lax.dynamic_slice_in_dim(
        owner_order, lax.axis_index("row") * row_blocks, row_blocks
    )
    wanted_columns = lax.dynamic_slice_in_dim(
        owner_order, lax.axis_index("col") * column_blocks, column_blocks
    )
    segment = lax.all_gather(generator, "row", axis=0, tiled=True)
    arriving = segment.shape[0] // BLK
    source = jnp.arange(arriving, dtype=jnp.int32)
    select = (wanted_rows[:, None] == source[None, :]).astype(jnp.bfloat16)
    flattened = segment.reshape(arriving, -1)
    by_rows = jnp.dot(select, flattened, preferred_element_type=jnp.float32)
    by_rows = by_rows.reshape(generator.shape).astype(jnp.bfloat16)
    segment = lax.all_gather(by_rows, "col", axis=1, tiled=True)
    arriving = segment.shape[1] // BLK
    source = jnp.arange(arriving, dtype=jnp.int32)
    select = (source[:, None] == wanted_columns[None, :]).astype(jnp.bfloat16)
    shaped = segment.reshape(segment.shape[0], arriving, BLK)
    placed = jnp.einsum("pjk,ji->pik", shaped, select, preferred_element_type=jnp.float32)
    return placed.reshape(generator.shape).astype(jnp.bfloat16)


def on_device(
    fock_matrix, density, margin, fill_patterns, first_filters, owner_order, second_filters
):
    masked_fock = expand(fill_patterns[0], fock_matrix)
    masked_density = expand(fill_patterns[1], density)
    masked_margin = expand(fill_patterns[2], margin)
    fock_density = expand(
        first_filters[0], panel_times(panel_rows(masked_fock), masked_density)
    ).astype(jnp.bfloat16)
    margin_density = expand(
        first_filters[1], panel_times(panel_rows(masked_margin), masked_density)
    ).astype(jnp.bfloat16)
    generator = panel_times(panel_rows(fock_density), masked_margin) - panel_times(
        panel_rows(margin_density), masked_fock
    )
    generator = expand(first_filters[2], generator).astype(jnp.bfloat16)
    reordered = reorder(generator, owner_order)
    scaled = (reordered.astype(jnp.float32) * 0.25).astype(jnp.bfloat16)
    rows_here, columns_here = scaled.shape
    row_ids = lax.axis_index("row") * rows_here + jnp.arange(rows_here, dtype=jnp.int32)
    column_ids = lax.axis_index("col") * columns_here + jnp.arange(columns_here, dtype=jnp.int32)
    identity = (row_ids[:, None] == column_ids[None, :]).astype(jnp.float32)
    scaled_rows = panel_rows(scaled)
    series = (identity + scaled.astype(jnp.float32) / 6.0).astype(jnp.bfloat16)
    for number in range(TERMS - 1):
        degree = TERMS - 1 - number
        series = (
            identity + expand(second_filters[number], panel_times(scaled_rows, series)) / degree
        ).astype(jnp.bfloat16)
    for number in range(SQUARINGS):
        series = expand(
            second_filters[TERMS - 1 + number], panel_times(panel_rows(series), series)
        ).astype(jnp.bfloat16)
    return series


def solution(mesh):
    return jax.shard_map(
        on_device,
        mesh=mesh,
        in_specs=(
            P("row", "col"),
            P("row", "col"),
            P("row", "col"),
            P(None, "row", "col"),
            P(None, "row", "col"),
            P(),
            P(None, "row", "col"),
        ),
        out_specs=P("row", "col"),
        check_vma=False,
    )
```

profile of v0, /device:TPU:1, one launch (start us, length us, event | category | flops | bytes accessed | tf_op | source)
XLA Modules:
  0.0 493.1 jit_solution(8701894759051707856)
XLA Ops:
  14.0 8.9 %all_gather.58 = bf16[192,1536]{1,0:T(8,128)(2,1)S(1)} all-gather(bf16[192,384]{1,0:T(8,128)(2,1)S(1)} %copy-done.3), channel_id=1, replica_groups=mesh['row'=8,'col'=4] {'col'}, dimensions={1}, use_global_device_ids=true | all-gather | bytes 737280 | tf_op jit(solution)/shard_map/all_gather | solution.py:21
  22.9 7.6 %all_gather.62 = bf16[192,1536]{1,0:T(8,128)(2,1)S(1)} all-gather(bf16[192,384]{1,0:T(8,128)(2,1)S(1)} %copy-done.2), channel_id=1, replica_groups=mesh['row'=8,'col'=4] {'col'}, dimensions={1}, use_global_device_ids=true | all-gather | bytes 737280 | tf_op jit(solution)/shard_map/all_gather | solution.py:21
  30.5 21.0 %all-gather.12.cloned.1.call-done = bf16[1536,384]{1,0:T(8,128)(2,1)} async-done(((bf16[192,384]{1,0:T(8,128)(2,1)}), bf16[1536,384]{1,0:T(8,128)(2,1)}) %all-gather.12.cloned.1.call-update) | async-done | bytes 1179664 | tf_op jit(solution)/shard_map/all_gather | solution.py:27
  53.3 9.3 %all_gather.60 = bf16[192,1536]{1,0:T(8,128)(2,1)S(1)} all-gather(bf16[192,384]{1,0:T(8,128)(2,1)S(1)} %fusion.20), channel_id=1, replica_groups=mesh['row'=8,'col'=4] {'col'}, dimensions={1}, use_global_device_ids=true | all-gather | bytes 737280 | tf_op jit(solution)/shard_map/all_gather | solution.py:21
  63.1 7.6 %all_gather.63 = bf16[192,1536]{1,0:T(8,128)(2,1)S(1)} all-gather(bf16[192,384]{1,0:T(8,128)(2,1)S(1)} %fusion.21), channel_id=1, replica_groups=mesh['row'=8,'col'=4] {'col'}, dimensions={1}, use_global_device_ids=true | all-gather | bytes 737280 | tf_op jit(solution)/shard_map/all_gather | solution.py:21
  70.7 22.8 %all-gather.14.cloned.1.call-done = bf16[1536,384]{1,0:T(8,128)(2,1)} async-done(((bf16[192,384]{1,0:T(8,128)(2,1)}), bf16[1536,384]{1,0:T(8,128)(2,1)}) %all-gather.14.cloned.1.call-update) | async-done | bytes 1179664 | tf_op jit(solution)/shard_map/all_gather | solution.py:27
  95.2 40.3 %all-gather.16.cloned.1.call-done = bf16[1536,384]{1,0:T(8,128)(2,1)} async-done(((bf16[192,384]{1,0:T(8,128)(2,1)}), bf16[1536,384]{1,0:T(8,128)(2,1)}) %all-gather.16.cloned.1.call-update) | async-done | bytes 1179664 | tf_op jit(solution)/shard_map/all_gather | solution.py:27
  138.2 39.8 %all-gather.18.cloned.1.call-done = bf16[1536,384]{1,0:T(8,128)(2,1)} async-done(((bf16[192,384]{1,0:T(8,128)(2,1)}), bf16[1536,384]{1,0:T(8,128)(2,1)}) %all-gather.18.cloned.1.call-update) | async-done | bytes 1179664 | tf_op jit(solution)/shard_map/all_gather | solution.py:41
  180.3 10.3 %all_gather.66 = bf16[192,1536]{0,1:T(8,128)(2,1)S(1)} all-gather(bf16[192,384]{0,1:T(8,128)(2,1)S(1)} %copy.15), channel_id=1, replica_groups=mesh['row'=8,'col'=4] {'col'}, dimensions={1}, use_global_device_ids=true | all-gather | bytes 737280 | tf_op jit(solution)/shard_map/all_gather | solution.py:48
  192.9 8.7 %all_gather.67 = bf16[192,1536]{0,1:T(8,128)(2,1)S(1)} all-gather(bf16[192,384]{0,1:T(8,128)(2,1)S(1)} %bitcast.58), channel_id=1, replica_groups=mesh['row'=8,'col'=4] {'col'}, dimensions={1}, use_global_device_ids=true | all-gather | bytes 737280 | tf_op jit(solution)/shard_map/all_gather | solution.py:21
  201.6 27.9 %all-gather.20.cloned.1.call-done = bf16[1536,384]{1,0:T(8,128)(2,1)} async-done(((bf16[192,384]{1,0:T(8,128)(2,1)}), bf16[1536,384]{1,0:T(8,128)(2,1)}) %all-gather.20.cloned.1.call-update) | async-done | bytes 1179664 | tf_op jit(solution)/shard_map/all_gather | solution.py:27
  229.5 2.4 fusion.15
  232.7 39.3 %all-gather.22.cloned.1.call-done = bf16[1536,384]{1,0:T(8,128)(2,1)} async-done(((bf16[192,384]{1,0:T(8,128)(2,1)}), bf16[1536,384]{1,0:T(8,128)(2,1)}) %all-gather.22.cloned.1.call-update) | async-done | bytes 1179664 | tf_op jit(solution)/shard_map/all_gather | solution.py:27
  272.0 2.4 fusion.16
  275.3 39.1 %all-gather.24.cloned.1.call-done = bf16[1536,384]{1,0:T(8,128)(2,1)} async-done(((bf16[192,384]{1,0:T(8,128)(2,1)}), bf16[1536,384]{1,0:T(8,128)(2,1)}) %all-gather.24.cloned.1.call-update) | async-done | bytes 1179664 | tf_op jit(solution)/shard_map/all_gather | solution.py:27
  314.4 2.4 fusion.17
  317.6 39.3 %all-gather.26.cloned.1.call-done = bf16[1536,384]{1,0:T(8,128)(2,1)} async-done(((bf16[192,384]{1,0:T(8,128)(2,1)}), bf16[1536,384]{1,0:T(8,128)(2,1)}) %all-gather.26.cloned.1.call-update) | async-done | bytes 1179664 | tf_op jit(solution)/shard_map/all_gather | solution.py:27
  356.9 2.4 fusion.18
  360.0 39.3 %all-gather.28.cloned.1.call-done = bf16[1536,384]{1,0:T(8,128)(2,1)} async-done(((bf16[192,384]{1,0:T(8,128)(2,1)}), bf16[1536,384]{1,0:T(8,128)(2,1)}) %all-gather.28.cloned.1.call-update) | async-done | bytes 1179664 | tf_op jit(solution)/shard_map/all_gather | solution.py:27
  399.3 2.4 fusion.19
  402.9 9.3 %all_gather.73 = bf16[192,1536]{1,0:T(8,128)(2,1)S(1)} all-gather(bf16[192,384]{1,0:T(8,128)(2,1)S(1)} %copy-done.4), channel_id=1, replica_groups=mesh['row'=8,'col'=4] {'col'}, dimensions={1}, use_global_device_ids=true | all-gather | bytes 737280 | tf_op jit(solution)/shard_map/all_gather | solution.py:21
  412.2 29.6 %all-gather.30.cloned.1.call-done = bf16[1536,384]{1,0:T(8,128)(2,1)} async-done(((bf16[192,384]{1,0:T(8,128)(2,1)}), bf16[1536,384]{1,0:T(8,128)(2,1)}) %all-gather.30.cloned.1.call-update) | async-done | bytes 1179664 | tf_op jit(solution)/shard_map/all_gather | solution.py:27
  445.3 9.3 %all_gather.75 = bf16[192,1536]{1,0:T(8,128)(2,1)S(1)} all-gather(bf16[192,384]{1,0:T(8,128)(2,1)S(1)} %copy-done.1), channel_id=1, replica_groups=mesh['row'=8,'col'=4] {'col'}, dimensions={1}, use_global_device_ids=true | all-gather | bytes 737280 | tf_op jit(solution)/shard_map/all_gather | solution.py:21
  454.5 29.6 %all-gather.32.cloned.1.call-done = bf16[1536,384]{1,0:T(8,128)(2,1)} async-done(((bf16[192,384]{1,0:T(8,128)(2,1)}), bf16[1536,384]{1,0:T(8,128)(2,1)}) %all-gather.32.cloned.1.call-update) | async-done | bytes 1179664 | tf_op jit(solution)/shard_map/all_gather | solution.py:27
  (99 shorter events, 28.4 us)
Async XLA Ops:
  6.5 1.4 copy-start.5
  6.5 44.9 %all-gather.12.cloned.1.call-start = ((), (), s32[]{:S(2)}) async-start(), calls=%async_computation | async-start | bytes 1327104 | tf_op jit(solution)/shard_map/all_gather | solution.py:27
  8.0 1.4 copy-start.6
  8.7 84.8 %all-gather.14.cloned.1.call-start = ((), (), s32[]{:S(2)}) async-start(), calls=%async_computation.1 | async-start | bytes 1327104 | tf_op jit(solution)/shard_map/all_gather | solution.py:27
  9.4 1.5 copy-start.7
  10.1 1.5 copy-start.9
  10.2 125.4 %all-gather.16.cloned.1.call-start = ((), (), s32[]{:S(2)}) async-start(), calls=%async_computation.2 | async-start | bytes 1327104 | tf_op jit(solution)/shard_map/all_gather | solution.py:27
  11.6 166.3 %all-gather.18.cloned.1.call-start = ((), (), s32[]{:S(2)}) async-start(), calls=%async_computation.3 | async-start | bytes 1327104 | tf_op jit(solution)/shard_map/all_gather | solution.py:41
  13.1 0.9 copy-start.3
  13.1 9.8 %copy-start.2 = (bf16[192,384]{1,0:T(8,128)(2,1)S(1)}, bf16[192,384]{1,0:T(8,128)(2,1)}, u32[]{:S(2)}) copy-start(bf16[192,384]{1,0:T(8,128)(2,1)} %mul.182) | copy-start | bytes 442372
  51.5 11.1 %copy-start = (bf16[1536,384]{1,0:T(8,128)(2,1)S(1)}, bf16[1536,384]{1,0:T(8,128)(2,1)}, u32[]{:S(2)}) copy-start(bf16[1536,384]{1,0:T(8,128)(2,1)} %all-gather.12.cloned.1.call-done) | copy-start | bytes 3538948
  95.2 42.8 %copy-start.10 = (s32[48]{0:T(128)S(1)}, s32[48]{0:T(128)}, u32[]{:S(2)}) copy-start(s32[48]{0:T(128)} %param.12) | copy-start | bytes 580
  137.9 91.6 %all-gather.20.cloned.1.call-start = ((), (), s32[]{:S(2)}) async-start(), calls=%async_computation.4 | async-start | bytes 1327104 | tf_op jit(solution)/shard_map/all_gather | solution.py:27
  190.6 1.6 copy-start.8
  192.2 79.8 %all-gather.22.cloned.1.call-start = ((), (), s32[]{:S(2)}) async-start(), calls=%async_computation.5 | async-start | bytes 1327104 | tf_op jit(solution)/shard_map/all_gather | solution.py:27
  232.0 82.4 %all-gather.24.cloned.1.call-start = ((), (), s32[]{:S(2)}) async-start(), calls=%async_computation.6 | async-start | bytes 1327104 | tf_op jit(solution)/shard_map/all_gather | solution.py:27
  274.4 82.4 %all-gather.26.cloned.1.call-start = ((), (), s32[]{:S(2)}) async-start(), calls=%async_computation.7 | async-start | bytes 1327104 | tf_op jit(solution)/shard_map/all_gather | solution.py:27
  316.9 82.4 %all-gather.28.cloned.1.call-start = ((), (), s32[]{:S(2)}) async-start(), calls=%async_computation.8 | async-start | bytes 1327104 | tf_op jit(solution)/shard_map/all_gather | solution.py:27
  359.3 82.4 %all-gather.30.cloned.1.call-start = ((), (), s32[]{:S(2)}) async-start(), calls=%async_computation.9 | async-start | bytes 1327104 | tf_op jit(solution)/shard_map/all_gather | solution.py:27
  401.8 82.4 %all-gather.32.cloned.1.call-start = ((), (), s32[]{:S(2)}) async-start(), calls=%async_computation.10 | async-start | bytes 1327104 | tf_op jit(solution)/shard_map/all_gather | solution.py:27
  402.0 0.9 copy-start.4
  444.4 0.9 copy-start.1
Sparse Core Ops, SparseCore 0:
  9.5 41.8 all-gather.11
  53.6 39.7 all-gather.13
  95.7 39.8 all-gather.15
  138.1 39.8 all-gather.17
  192.3 37.1 all-gather.19
  232.1 39.8 all-gather.21
  274.6 39.8 all-gather.23
  317.0 39.8 all-gather.25
  359.5 39.8 all-gather.27
  401.9 39.8 all-gather.29
  444.3 39.8 all-gather.31
where the time goes:
time: 496 us; the launch traced here: 493 us
  waiting for transfers between devices  368 us (74%)
  blocking collectives  71 us (14%)
  matrix products  24.3 us (5%)
  between operations  13.6 us (3%)
  local copies, waits for them, and re-layouts  11.9 us (2%)
    all_gather x10, waiting for transfers between devices, panel_times(): lax.all_gather(matrix, 'row', axis=0, tiled=True)  328 us
    all_gather x7, blocking collectives, panel_rows(): return lax.all_gather(matrix, 'col', axis=1, tiled=True)  60.6 us
    all_gather x1, waiting for transfers between devices, reorder(): segment = lax.all_gather(generator, 'row', axis=0, tiled=True)  39.8 us
    dot_general x11, matrix products, panel_times(): jnp.dot(row_panel, lax.all_gather(matrix, 'row', axis=0, tiled=True), pre...  23.4 us
    all_gather x1, blocking collectives, reorder(): segment = lax.all_gather(by_rows, 'col', axis=1, tiled=True)  10.3 us
  transfers between devices with their start and end apart: 11, of which 11 were waited for; matrix products, arithmetic and copies ran while one was open for 3% of the time, Pallas kernels for 0%

commit v1 on v0

v1 whole, which is shorter than its diff:
```python
import functools

import jax
import jax.numpy as jnp
from jax import lax
from jax.experimental import pallas as pl
from jax.experimental.pallas import tpu as pltpu
from jax.sharding import PartitionSpec as P

BLK = 32
TERMS = 6
SQUARINGS = 2
FIRST = 3
AXES = ("row", "col")
F32 = jnp.float32
BF16 = jnp.bfloat16
TAIL = 16
VMEM_LIMIT = 60 * 1024 * 1024


def coordinates(r, c):
    return r // 2, r % 2, c // 2, c % 2


def permutation(rows, cols, source):
    pairs = []
    for r in range(rows):
        for c in range(cols):
            sr, sc = source(*coordinates(r, c))
            pairs.append((sr * cols + sc, r * cols + c))
    return pairs


class Moves:
    def __init__(self, rows, cols):
        self.rows, self.cols = rows, cols

    def move(self, value, source):
        return lax.ppermute(value, AXES, permutation(self.rows, self.cols, source))

    def relabel(self, value, k=0):
        return self.move(value, lambda z, y, x, e: (2 * (z ^ k) + e, 2 * x + y))

    def along_z(self, value, k):
        return self.move(value, lambda z, y, x, e: (2 * (z ^ k) + y, 2 * x + e))

    def in_plane(self, value, s):
        return self.move(value, lambda z, y, x, e: (2 * z + (y ^ (s & 1)), 2 * (x ^ (s >> 1)) + e))

    def core(self, value):
        return self.move(value, lambda z, y, x, e: (2 * z + y, 2 * x + 1 - e))


def place():
    r, c = lax.axis_index("row"), lax.axis_index("col")
    z, y, x, e = r // 2, r % 2, c // 2, c % 2
    return z, 2 * x + y, e


def iota(shape, axis):
    return lax.broadcasted_iota(jnp.int32, shape, axis)


def dot(a, b):
    return jnp.dot(a, b, preferred_element_type=F32)


def repeat_rows(rows, blocks):
    return (iota((rows, blocks), 0) // BLK == iota((rows, blocks), 1)).astype(BF16)


def repeat_columns(blocks, columns, first=0):
    return (iota((blocks, columns), 0) == iota((blocks, columns), 1) // BLK + first).astype(BF16)


def block_mask(tail, number, rows, columns):
    blocks = columns // BLK
    wide = dot(repeat_rows(rows, tail.shape[0]), tail).astype(BF16)
    return dot(wide, repeat_columns(tail.shape[1], columns, number * blocks))


def call(kernel, outs, ins, scratch, name):
    return pl.pallas_call(
        kernel,
        out_shape=outs,
        in_specs=ins,
        out_specs=jax.tree.map(lambda _: pl.BlockSpec(memory_space=pltpu.VMEM), outs),
        scratch_shapes=scratch,
        name=name,
        compiler_params=pltpu.CompilerParams(vmem_limit_bytes=VMEM_LIMIT),
    )


ANY = pl.BlockSpec(memory_space=pl.ANY)
INVMEM = pl.BlockSpec(memory_space=pltpu.VMEM)
INSMEM = pl.BlockSpec(memory_space=pltpu.SMEM)


def mask_kernel(fock, density, margin, fills, firsts, seconds, masked_density, pair):
    rows, columns = fock.shape
    row_blocks, column_blocks = rows // BLK, columns // BLK
    tall = repeat_rows(rows, row_blocks)
    wide = repeat_columns(column_blocks, columns)

    def masked(ref, number):
        mask = dot(dot(tall, fills[number].astype(BF16)).astype(BF16), wide)
        return (ref[...].astype(F32) * mask).astype(BF16)

    masked_density[...] = masked(density, 1)
    pair[0:rows, :] = masked(fock, 0)
    pair[rows : 2 * rows, :] = masked(margin, 2)
    top = (iota((TAIL, row_blocks), 0) == iota((TAIL, row_blocks), 1)).astype(BF16)
    tail = jnp.zeros((TAIL, columns), F32)
    for number in range(firsts.shape[0] + seconds.shape[0]):
        ref = firsts[number] if number < FIRST else seconds[number - FIRST]
        column = iota((column_blocks, columns), 1) - number * column_blocks
        spread = (iota((column_blocks, columns), 0) == column).astype(BF16)
        tail += dot(dot(top, ref.astype(BF16)).astype(BF16), spread)
    pair[2 * rows :, :] = tail.astype(BF16)


def copy_all(copies):
    for one in copies:
        one.start()
    for one in copies:
        one.wait()


def first_kernel(count, *refs):
    pairs, near, far = refs[:count], refs[count : 2 * count], refs[2 * count : 3 * count]
    out, left, right, tail, sems = refs[3 * count :]
    z, q, e = place()
    rows = near[0].shape[0]
    copies = [pltpu.make_async_copy(pairs[0].at[2 * rows :], tail, sems.at[0])]
    for s in range(count):
        copies.append(
            pltpu.make_async_copy(pairs[s].at[: 2 * rows], left.at[q ^ s], sems.at[len(copies)])
        )
        for ref, core in ((near[s], e), (far[s], 1 - e)):
            copies.append(
                pltpu.make_async_copy(
                    ref, right.at[z ^ s, pl.ds(core * rows, rows)], sems.at[len(copies)]
                )
            )
    copy_all(copies)
    total = dot(left[0], right[0])
    for k in range(1, count):
        total += dot(left[k], right[k])
    columns = total.shape[1]
    for number in range(2):
        part = pl.ds(number * rows, rows)
        mask = block_mask(tail[...], number, rows, columns)
        out[part, :] = (total[number * rows : (number + 1) * rows] * mask).astype(BF16)


def generator_kernel(count, *refs):
    lefts, near, far = refs[:count], refs[count : 2 * count], refs[2 * count : 3 * count]
    out, left, right, tail, sems = refs[3 * count :]
    z, q, e = place()
    rows = lefts[0].shape[0] // 2
    copies = [pltpu.make_async_copy(near[0].at[2 * rows :], tail, sems.at[0])]
    for s in range(count):
        copies.append(pltpu.make_async_copy(lefts[s], left.at[q ^ s], sems.at[len(copies)]))
        for ref, core in ((near[s], e), (far[s], 1 - e)):
            for half in range(2):
                copies.append(
                    pltpu.make_async_copy(
                        ref.at[pl.ds(half * rows, rows)],
                        right.at[1 - half, z ^ s, pl.ds(core * rows, rows)],
                        sems.at[len(copies)],
                    )
                )
    copy_all(copies)
    plus = dot(left[0, :rows], right[0, 0])
    minus = dot(left[0, rows:], right[1, 0])
    for k in range(1, count):
        plus += dot(left[k, :rows], right[0, k])
        minus += dot(left[k, rows:], right[1, k])
    mask = block_mask(tail[...], 2, rows, out.shape[1])
    generator = ((plus - minus) * mask).astype(BF16)
    out[...] = (generator.astype(F32) * 0.25).astype(BF16)


def series_kernel(layout, count, *refs):
    pieces = refs[: len(layout)]
    tails = refs[len(layout) : len(layout) + 2 * count]
    order = refs[len(layout) + 2 * count]
    panel, mine, whole, unit, current, wides, masks, sems = refs[len(layout) + 2 * count + 1 :]
    z, q, e = place()
    size, columns = panel.shape
    rows = mine.shape[0]
    copies = []
    for ref, (slots, plane, lane) in zip(pieces, layout):
        core = e if lane == 0 else 1 - e
        for index, k in enumerate(slots):
            copies.append(
                pltpu.make_async_copy(
                    ref.at[index],
                    whole.at[
                        pl.ds((2 * (z ^ k) + core) * rows, rows),
                        pl.ds(pl.multiple_of((q ^ plane) * columns, 128), columns),
                    ],
                    sems.at[len(copies)],
                )
            )
    for index, ref in enumerate(tails):
        core = e if index < count else 1 - e
        copies.append(
            pltpu.make_async_copy(
                ref.at[2 * rows :], wides.at[2 * (z ^ (index % count)) + core], sems.at[len(copies)]
            )
        )
    for one in copies:
        one.start()

    column_blocks = columns // BLK
    row_blocks = rows // BLK
    unit[...] = jnp.zeros_like(unit)
    inner = iota((BLK, columns), 1)
    for b in range(column_blocks):
        first = pl.multiple_of(order[q * column_blocks + b] * BLK, BLK)
        unit[pl.ds(first, BLK), :] = (inner == iota((BLK, columns), 0) + b * BLK).astype(BF16)

    for one in copies:
        one.wait()

    for p in range(wides.shape[0]):
        for a in range(row_blocks):
            first = pl.multiple_of(order[p * row_blocks + a] * BLK, BLK)
            row = wides[p][a : a + 1, :128]
            masks[pl.ds(first, BLK), :] = jnp.broadcast_to(row, (BLK, 128))

    tiles = size // rows

    def step(number, source, target):
        degree = TERMS - number
        if number > 0:
            spread = repeat_columns(128, columns, (FIRST + number - 1) * column_blocks)

        def body(t, carry):
            part = pl.ds(pl.multiple_of(t * rows, rows), rows)
            value = dot(whole[part, :], source[...])
            if number > 0:
                value = value * dot(masks[part, :], spread)
            target[part, :] = (unit[part, :].astype(F32) + value / degree).astype(BF16)
            return carry

        lax.fori_loop(0, tiles, body, 0)

    step(0, unit, current.at[0])
    for number in range(1, TERMS):
        step(number, current.at[(number - 1) % 2], current.at[number % 2])
    last = current.at[(TERMS - 1) % 2]
    for a in range(size // BLK):
        first = pl.multiple_of(order[a] * BLK, BLK)
        panel[a * BLK : (a + 1) * BLK, :] = last[pl.ds(first, BLK), :]
    start = (2 * z + e) * rows
    mine[...] = panel[pl.ds(pl.multiple_of(start, rows), rows), :]


def square_kernel(count, *refs):
    lefts = refs[:count]
    panel, pair, out, left, right, tail, sems = refs[count:]
    z, q, e = place()
    rows, columns = out.shape
    copies = [
        pltpu.make_async_copy(pair.at[2 * rows :], tail, sems.at[0]),
        pltpu.make_async_copy(panel, right, sems.at[1]),
    ]
    for s in range(count):
        copies.append(pltpu.make_async_copy(lefts[s], left.at[q ^ s], sems.at[len(copies)]))
    copy_all(copies)
    total = dot(left[0], right[0:columns])
    for k in range(1, count):
        total += dot(left[k], right[k * columns : (k + 1) * columns])
    mask = block_mask(tail[...], FIRST + TERMS - 1, rows, columns)
    out[...] = (total * mask).astype(BF16)


def evolve_kernel(count, *refs):
    lefts, near, far = refs[:count], refs[count : 2 * count], refs[2 * count : 3 * count]
    pair, out, left, right, tail, sems = refs[3 * count :]
    z, q, e = place()
    rows, columns = out.shape
    copies = [pltpu.make_async_copy(pair.at[2 * rows :], tail, sems.at[0])]
    for s in range(count):
        copies.append(pltpu.make_async_copy(lefts[s], left.at[q ^ s], sems.at[len(copies)]))
        for ref, core in ((near[s], e), (far[s], 1 - e)):
            copies.append(
                pltpu.make_async_copy(
                    ref, right.at[z ^ s, pl.ds(core * rows, rows)], sems.at[len(copies)]
                )
            )
    copy_all(copies)
    total = dot(left[0], right[0])
    for k in range(1, count):
        total += dot(left[k], right[k])
    mask = block_mask(tail[...], FIRST + TERMS, rows, columns)
    out[...] = (total * mask).astype(BF16)


def on_device(
    mesh_rows,
    mesh_cols,
    fock_matrix,
    density,
    margin,
    fill_patterns,
    first_filters,
    owner_order,
    second_filters,
):
    moves = Moves(mesh_rows, mesh_cols)
    count = mesh_cols
    slots = range(1, count)
    rows, columns = fock_matrix.shape
    size = rows * mesh_rows
    block = jax.ShapeDtypeStruct((rows, columns), BF16)

    masked_density, pair = call(
        mask_kernel,
        [block, jax.ShapeDtypeStruct((2 * rows + TAIL, columns), BF16)],
        [INVMEM] * 6,
        [],
        "mask",
    )(fock_matrix, density, margin, fill_patterns, first_filters, second_filters)

    density_near = [moves.relabel(masked_density, k) for k in range(count)]
    density_far = [moves.core(value) for value in density_near]
    pair = moves.relabel(pair)
    pair_rows = [pair] + [moves.in_plane(pair, s) for s in slots]
    pair_near = [pair] + [moves.along_z(pair, k) for k in slots]
    pair_far = [moves.core(value) for value in pair_near]

    products = call(
        functools.partial(first_kernel, count),
        jax.ShapeDtypeStruct((2 * rows, columns), BF16),
        [ANY] * (3 * count),
        [
            pltpu.VMEM((count, 2 * rows, columns), BF16),
            pltpu.VMEM((count, columns, columns), BF16),
            pltpu.VMEM((TAIL, columns), BF16),
            pltpu.SemaphoreType.DMA((1 + 3 * count,)),
        ],
        "first",
    )(*pair_rows, *density_near, *density_far)
    products = [products] + [moves.in_plane(products, s) for s in slots]

    generator = call(
        functools.partial(generator_kernel, count),
        block,
        [ANY] * (3 * count),
        [
            pltpu.VMEM((count, 2 * rows, columns), BF16),
            pltpu.VMEM((2, count, columns, columns), BF16),
            pltpu.VMEM((TAIL, columns), BF16),
            pltpu.SemaphoreType.DMA((1 + 5 * count,)),
        ],
        "generator",
    )(*products, *pair_near, *pair_far)

    lines = [generator] + [moves.along_z(generator, k) for k in slots]
    half = count // 2
    layout, pieces = [], []
    for first in (0, half):
        chosen = tuple(range(first, first + half))
        group = jnp.stack([lines[k] for k in chosen])
        planes = {0: [(chosen, group)]}
        for s in slots:
            if count == 4 and s == 3:
                continue
            planes[s] = [(chosen, moves.in_plane(group, s))]
        if count == 4:
            planes[3] = [
                (chosen[:1], moves.in_plane(planes[2][0][1][:1], 1)),
                (chosen[1:], moves.in_plane(planes[1][0][1][1:], 2)),
            ]
        for s, parts in planes.items():
            for held, value in parts:
                layout += [(held, s, 0), (held, s, 1)]
                pieces += [value, moves.core(value)]

    panel, mine = call(
        functools.partial(series_kernel, layout, count),
        [jax.ShapeDtypeStruct((size, columns), BF16), block],
        [ANY] * (len(layout) + 2 * count) + [INSMEM],
        [
            pltpu.VMEM((size, size), BF16),
            pltpu.VMEM((size, columns), BF16),
            pltpu.VMEM((2, size, columns), BF16),
            pltpu.VMEM((mesh_rows, TAIL, columns), BF16),
            pltpu.VMEM((size, 128), BF16),
            pltpu.SemaphoreType.DMA((mesh_rows * mesh_cols + 2 * count,)),
        ],
        "series",
    )(*pieces, *pair_near, *pair_far, owner_order)

    lefts = [mine] + [moves.in_plane(mine, s) for s in slots]
    square = call(
        functools.partial(square_kernel, count),
        block,
        [ANY] * (count + 2),
        [
            pltpu.VMEM((count, rows, columns), BF16),
            pltpu.VMEM((size, columns), BF16),
            pltpu.VMEM((TAIL, columns), BF16),
            pltpu.SemaphoreType.DMA((2 + count,)),
        ],
        "square",
    )(*lefts, panel, pair)

    near = [square] + [moves.along_z(square, k) for k in slots]
    lefts = [square] + [moves.in_plane(square, s) for s in slots]
    far = [moves.core(value) for value in near]
    evolved = call(
        functools.partial(evolve_kernel, count),
        block,
        [ANY] * (3 * count + 1),
        [
            pltpu.VMEM((count, rows, columns), BF16),
            pltpu.VMEM((count, columns, columns), BF16),
            pltpu.VMEM((TAIL, columns), BF16),
            pltpu.SemaphoreType.DMA((1 + 3 * count,)),
        ],
        "evolve",
    )(*lefts, *near, *far, pair)
    return moves.relabel(evolved)


def solution(mesh):
    return jax.shard_map(
        functools.partial(on_device, mesh.shape["row"], mesh.shape["col"]),
        mesh=mesh,
        in_specs=(
            P("row", "col"),
            P("row", "col"),
            P("row", "col"),
            P(None, "row", "col"),
            P(None, "row", "col"),
            P(),
            P(None, "row", "col"),
        ),
        out_specs=P("row", "col"),
        check_vma=False,
    )
```

time: 496 us -> 194 us (0.39)
  waiting for transfers between devices: 368 us -> 76.9 us
  blocking collectives: 71 us -> 0 us
  starting transfers between devices: 0.6 us -> 61.8 us
  Pallas kernels: 0 us -> 45.9 us
  matrix products: 24.3 us -> 0 us
  between operations: 13.6 us -> 0.58 us
    all_gather x11 -> x0, waiting for transfers between devices: 368 us -> none  [the longest x10 328 us: panel_times(): lax.all_gather(matrix, 'row', axis=0, tiled=True)]
    ppermute x0 -> x57, waiting for transfers between devices: none -> 76.9 us  [move(): return lax.ppermute(value, AXES, permutation(self.rows, self.cols, source))]
    all_gather x8 -> x0, blocking collectives: 71 us -> none  [the longest x7 60.6 us: panel_rows(): return lax.all_gather(matrix, 'col', axis=1, tiled=True)]
    ppermute x0 -> x57, starting transfers between devices: none -> 61.8 us  [move(): return lax.ppermute(value, AXES, permutation(self.rows, self.cols, source))]
    pallas_call x0 -> x6, Pallas kernels: none -> 45.9 us  [the longest x1 29 us: on_device(): call(functools.partial(series_kernel, layout, count), [jax.ShapeDtypeStru...]
    dot_general x13 -> x0, matrix products: 24.3 us -> none  [the longest x11 23.4 us: panel_times(): jnp.dot(row_panel, lax.all_gather(matrix, 'row', axis=0, tiled=True), pre...]
    mul x27 -> x0, local copies, waits for them, and re-layouts: 8.2 us -> none  [the longest x26 8.14 us: expand(): values.reshape(row_blocks, BLK, column_blocks, BLK)]
    unnamed x22 -> x110, local copies, waits for them, and re-layouts: 1.38 us -> 7.67 us
  transfers between devices with their start and end apart: 11 -> 57, of which waited for: 11 -> 25; matrix products, arithmetic and copies ran while one was open for 3% -> 0% of each run, Pallas kernels for 0% -> 2%
where the time goes in v1:
time: 194 us
  waiting for transfers between devices  76.9 us (40%)
  starting transfers between devices  61.8 us (32%)
  Pallas kernels  45.9 us (24%)
  local copies, waits for them, and re-layouts  7.73 us (4%)
    ppermute x57, waiting for transfers between devices, move(): return lax.ppermute(value, AXES, permutation(self.rows, self.cols, source))  76.9 us
    ppermute x57, starting transfers between devices, move(): return lax.ppermute(value, AXES, permutation(self.rows, self.cols, source))  61.8 us
    pallas_call x1, Pallas kernels, on_device(): call(functools.partial(series_kernel, layout, count), [jax.ShapeDtypeStru...  29 us
    unnamed x110, local copies, waits for them, and re-layouts  7.67 us
    pallas_call x1, Pallas kernels, on_device(): call(functools.partial(generator_kernel, count), block, [ANY] * (3 * coun...  3.9 us
  transfers between devices with their start and end apart: 57, of which 25 were waited for; matrix products, arithmetic and copies ran while one was open for 0% of the time, Pallas kernels for 2%

profile of v1, /device:TPU:1, one launch (start us, length us, event | category | flops | bytes accessed | tf_op | source)
XLA Modules:
  0.0 193.8 jit_solution(7665186983636403992)
XLA Ops:
  1.3 3.5 %mask.1 = (bf16[192,384]{1,0:T(8,128)(2,1)}, bf16[400,384]{1,0:T(8,128)(2,1)}) custom-call(bf16[192,384]{1,0:T(8,128)(2,1)} %fock.1, bf16[192,384]{1,0:T(8,128)(2,1)} %density.1, bf16[192,384]{1,0:T(8,128)(2,1)} %margin.1, s32[3,6,12]{2,1,0:T(8,128)} %fills.1, s32[3,6,12]{2,1,0:T(8,128)} %firsts.1, s32[7,6,12]{2,1,0:T(8,128)} %copy.8.seconds), custom_call_target="tpu_custom_call" | custom-call | tf_op jit(solution)/shard_map/mask/pallas_call | solution.py:320
  4.8 4.5 %collective-permute-start = (bf16[400,384]{1,0:T(8,128)(2,1)}, bf16[400,384]{1,0:T(8,128)(2,1)S(1)}, u32[]{:S(2)}, u32[]{:S(2)}) collective-permute-start(bf16[400,384]{1,0:T(8,128)(2,1)} %get-tuple-element.9), channel_id=1, source_target_pairs={{0,0},{4,1},{2,2},{6,3},{1,4},{5,5},{3,6},{7,7},{8,8},{12,9},{10,1... | collective-permute-start | bytes 921608 | tf_op jit(solution)/shard_map/ppermute | solution.py:39
  9.4 3.1 %collective-permute-start.7 = (bf16[192,384]{1,0:T(8,128)(2,1)}, bf16[192,384]{1,0:T(8,128)(2,1)S(1)}, u32[]{:S(2)}, u32[]{:S(2)}) collective-permute-start(bf16[192,384]{1,0:T(8,128)(2,1)} %get-tuple-element.10), channel_id=1, source_target_pairs={{24,0},{28,1},{26,2},{30,3},{25,4},{29,5},{27,6},{31,7},{16,8},{20... | collective-permute-start | bytes 442376 | tf_op jit(solution)/shard_map/ppermute | solution.py:39
  14.3 3.2 %collective-permute-start.4 = (bf16[192,384]{1,0:T(8,128)(2,1)}, bf16[192,384]{1,0:T(8,128)(2,1)S(1)}, u32[]{:S(2)}, u32[]{:S(2)}) collective-permute-start(bf16[192,384]{1,0:T(8,128)(2,1)} %get-tuple-element.10), channel_id=1, source_target_pairs={{0,0},{4,1},{2,2},{6,3},{1,4},{5,5},{3,6},{7,7},{8,8},{12,9},{10,1... | collective-permute-start | bytes 442376 | tf_op jit(solution)/shard_map/ppermute | solution.py:39
  19.4 6.6 %collective-permute-done.6.refs_6_ = bf16[192,384]{1,0:T(8,128)(2,1)S(1)} collective-permute-done((bf16[192,384]{1,0:T(8,128)(2,1)}, bf16[192,384]{1,0:T(8,128)(2,1)S(1)}, u32[]{:S(2)}, u32[]{:S(2)}) %collective-permute-start.6) | collective-permute-done | bytes 147488 | tf_op jit(solution)/shard_map/ppermute | solution.py:39
  32.0 3.4 %collective-permute-start.17 = (bf16[400,384]{1,0:T(8,128)(2,1)S(1)}, bf16[400,384]{1,0:T(8,128)(2,1)S(1)}, u32[]{:S(2)}, u32[]{:S(2)}) collective-permute-start(bf16[400,384]{1,0:T(8,128)(2,1)S(1)} %collective-permute-done.refs_0_.refs_4_.refs_20_.refs_5_.refs_12_), channel_id=1, source_target_pairs={{24,0},{25,1},{26,2},{27,3},{28,4},{29,5},{30,6},{31,7},{16,8},{17... | collective-permute-start | bytes 921608 | tf_op jit(solution)/shard_map/ppermute | solution.py:39
  39.5 3.7 %first.1.refs_0_ = bf16[384,384]{1,0:T(8,128)(2,1)} custom-call(bf16[400,384]{1,0:T(8,128)(2,1)} %copy-done, bf16[400,384]{1,0:T(8,128)(2,1)} %copy-done.16, bf16[400,384]{1,0:T(8,128)(2,1)} %copy-done.15, bf16[400,384]{1,0:T(8,128)(2,1)} %copy-done.14, bf16[192,384]{1,0:T(8,128)(2,1)} %copy-done.49, bf16[192,384]{1,0:T(8,128)(2,1)} %copy-done.48, ...), custom_call_target="tpu_custom_call" | custom-call | tf_op jit(solution)/shard_map/first/pallas_call | solution.py:335
  45.1 17.5 %collective-permute-done.16.refs_6_.refs_22_ = bf16[400,384]{1,0:T(8,128)(2,1)S(1)} collective-permute-done((bf16[400,384]{1,0:T(8,128)(2,1)S(1)}, bf16[400,384]{1,0:T(8,128)(2,1)S(1)}, u32[]{:S(2)}, u32[]{:S(2)}) %collective-permute-start.16) | collective-permute-done | bytes 307232 | tf_op jit(solution)/shard_map/ppermute | solution.py:39
  65.2 6.5 %collective-permute-done.13.refs_2_ = bf16[384,384]{1,0:T(8,128)(2,1)S(1)} collective-permute-done((bf16[384,384]{1,0:T(8,128)(2,1)}, bf16[384,384]{1,0:T(8,128)(2,1)S(1)}, u32[]{:S(2)}, u32[]{:S(2)}) %collective-permute-start.13) | collective-permute-done | bytes 294944 | tf_op jit(solution)/shard_map/ppermute | solution.py:39
  74.3 3.9 %generator.1 = bf16[192,384]{1,0:T(8,128)(2,1)} custom-call(bf16[384,384]{1,0:T(8,128)(2,1)} %first.1.refs_0_, bf16[384,384]{1,0:T(8,128)(2,1)} %copy-done.25, bf16[384,384]{1,0:T(8,128)(2,1)} %copy-done.24, bf16[384,384]{1,0:T(8,128)(2,1)} %copy-done.23, bf16[400,384]{1,0:T(8,128)(2,1)} %copy-done, bf16[400,384]{1,0:T(8,128)(2,1)} %copy-done.3, ...), custom_call_target="tpu_custom_call" | custom-call | tf_op jit(solution)/shard_map/generator/pallas_call | solution.py:349
  78.3 4.2 %collective-permute-done.22 = bf16[192,384]{1,0:T(8,128)(2,1)S(1)} collective-permute-done((bf16[192,384]{1,0:T(8,128)(2,1)}, bf16[192,384]{1,0:T(8,128)(2,1)S(1)}, u32[]{:S(2)}, u32[]{:S(2)}) %collective-permute-start.22) | collective-permute-done | bytes 147488 | tf_op jit(solution)/shard_map/ppermute | solution.py:39
  87.5 2.5 %collective-permute-done.33 = bf16[192,384]{1,0:T(8,128)(2,1)S(1)} collective-permute-done((bf16[192,384]{1,0:T(8,128)(2,1)}, bf16[192,384]{1,0:T(8,128)(2,1)S(1)}, u32[]{:S(2)}, u32[]{:S(2)}) %collective-permute-start.33) | collective-permute-done | bytes 147488 | tf_op jit(solution)/shard_map/ppermute | solution.py:39
  90.0 8.2 %collective-permute-done.32 = bf16[192,384]{1,0:T(8,128)(2,1)S(1)} collective-permute-done((bf16[192,384]{1,0:T(8,128)(2,1)}, bf16[192,384]{1,0:T(8,128)(2,1)S(1)}, u32[]{:S(2)}, u32[]{:S(2)}) %collective-permute-start.32) | collective-permute-done | bytes 147488 | tf_op jit(solution)/shard_map/ppermute | solution.py:39
  100.0 2.5 %collective-permute-start.23 = (bf16[2,192,384]{2,1,0:T(8,128)(2,1)S(1)}, bf16[2,192,384]{2,1,0:T(8,128)(2,1)S(1)}, u32[]{:S(2)}, u32[]{:S(2)}) collective-permute-start(bf16[2,192,384]{2,1,0:T(8,128)(2,1)S(1)} %pad_maximum_fusion.refs_0_), channel_id=1, source_target_pairs={{1,0},{0,1},{3,2},{2,3},{5,4},{4,5},{7,6},{6,7},{9,8},{8,9},{11,10... | collective-permute-start | bytes 884744 | tf_op jit(solution)/shard_map/ppermute | solution.py:39
  106.7 5.9 %collective-permute-start.27 = (bf16[2,192,384]{2,1,0:T(8,128)(2,1)S(1)}, bf16[2,192,384]{2,1,0:T(8,128)(2,1)S(1)}, u32[]{:S(2)}, u32[]{:S(2)}) collective-permute-start(bf16[2,192,384]{2,1,0:T(8,128)(2,1)S(1)} %collective-permute-done.26.refs_4_), channel_id=1, source_target_pairs={{1,0},{0,1},{3,2},{2,3},{5,4},{4,5},{7,6},{6,7},{9,8},{8,9},{11,10... | collective-permute-start | bytes 884744 | tf_op jit(solution)/shard_map/ppermute | solution.py:39
  113.6 3.1 %collective-permute-start.38 = (bf16[2,192,384]{2,1,0:T(8,128)(2,1)S(1)}, bf16[2,192,384]{2,1,0:T(8,128)(2,1)S(1)}, u32[]{:S(2)}, u32[]{:S(2)}) collective-permute-start(bf16[2,192,384]{2,1,0:T(8,128)(2,1)S(1)} %collective-permute-done.37.refs_14_), channel_id=1, source_target_pairs={{1,0},{0,1},{3,2},{2,3},{5,4},{4,5},{7,6},{6,7},{9,8},{8,9},{11,10... | collective-permute-start | bytes 884744 | tf_op jit(solution)/shard_map/ppermute | solution.py:39
  122.9 29.0 %series.1 = (bf16[1536,384]{1,0:T(8,128)(2,1)}, bf16[192,384]{1,0:T(8,128)(2,1)}) custom-call(bf16[2,192,384]{2,1,0:T(8,128)(2,1)} %copy-done.8, bf16[2,192,384]{2,1,0:T(8,128)(2,1)} %copy-done.17, bf16[2,192,384]{2,1,0:T(8,128)(2,1)} %copy-done.11, bf16[2,192,384]{2,1,0:T(8,128)(2,1)} %copy-done.20, bf16[2,192,384]{2,1,0:T(8,128)(2,1)} %copy-done.10, ...), custom_call_target="tpu_custom_call" | custom-call | tf_op jit(solution)/shard_map/series/pallas_call | solution.py:383
  154.6 3.6 %collective-permute-done.45.refs_3_ = bf16[192,384]{1,0:T(8,128)(2,1)S(1)} collective-permute-done((bf16[192,384]{1,0:T(8,128)(2,1)}, bf16[192,384]{1,0:T(8,128)(2,1)S(1)}, u32[]{:S(2)}, u32[]{:S(2)}) %collective-permute-start.45) | collective-permute-done | bytes 147488 | tf_op jit(solution)/shard_map/ppermute | solution.py:39
  158.3 2.7 %collective-permute-done.44.refs_2_ = bf16[192,384]{1,0:T(8,128)(2,1)S(1)} collective-permute-done((bf16[192,384]{1,0:T(8,128)(2,1)}, bf16[192,384]{1,0:T(8,128)(2,1)S(1)}, u32[]{:S(2)}, u32[]{:S(2)}) %collective-permute-start.44) | collective-permute-done | bytes 147488 | tf_op jit(solution)/shard_map/ppermute | solution.py:39
  162.7 2.8 %square.1.refs_0_.refs_4_ = bf16[192,384]{1,0:T(8,128)(2,1)} custom-call(bf16[192,384]{1,0:T(8,128)(2,1)} %get-tuple-element.11.refs_0_, bf16[192,384]{1,0:T(8,128)(2,1)} %copy-done.45, bf16[192,384]{1,0:T(8,128)(2,1)} %copy-done.44, bf16[192,384]{1,0:T(8,128)(2,1)} %copy-done.43, bf16[1536,384]{1,0:T(8,128)(2,1)} %get-tuple-element.12.refs_4_, ...), custom_call_target="tpu_custom_call" | custom-call | tf_op jit(solution)/shard_map/square/pallas_call | solution.py:399
  174.3 6.1 %collective-permute-done.50.refs_6_ = bf16[192,384]{1,0:T(8,128)(2,1)S(1)} collective-permute-done((bf16[192,384]{1,0:T(8,128)(2,1)}, bf16[192,384]{1,0:T(8,128)(2,1)S(1)}, u32[]{:S(2)}, u32[]{:S(2)}) %collective-permute-start.50) | collective-permute-done | bytes 147488 | tf_op jit(solution)/shard_map/ppermute | solution.py:39
  183.5 3.0 %evolve.1 = bf16[192,384]{1,0:T(8,128)(2,1)} custom-call(bf16[192,384]{1,0:T(8,128)(2,1)} %square.1.refs_0_.refs_4_, bf16[192,384]{1,0:T(8,128)(2,1)} %copy-done.39, bf16[192,384]{1,0:T(8,128)(2,1)} %copy-done.38, bf16[192,384]{1,0:T(8,128)(2,1)} %copy-done.37, bf16[192,384]{1,0:T(8,128)(2,1)} %square.1.refs_0_.refs_4_, bf16[192,384]{1,0:T(8,128)(2,1)} %copy-done.36, ...), custom_call_target="tpu_custom_call" | custom-call | tf_op jit(solution)/shard_map/evolve/pallas_call | solution.py:415
  186.5 3.0 %collective-permute-start.56 = (bf16[192,384]{1,0:T(8,128)(2,1)}, bf16[192,384]{1,0:T(8,128)(2,1)S(1)}, u32[]{:S(2)}, u32[]{:S(2)}) collective-permute-start(bf16[192,384]{1,0:T(8,128)(2,1)} %evolve.1), channel_id=1, source_target_pairs={{0,0},{4,1},{2,2},{6,3},{1,4},{5,5},{3,6},{7,7},{8,8},{12,9},{10,1... | collective-permute-start | bytes 442376 | tf_op jit(solution)/shard_map/ppermute | solution.py:39
  189.5 3.6 %collective-permute-done.56 = bf16[192,384]{1,0:T(8,128)(2,1)S(1)} collective-permute-done((bf16[192,384]{1,0:T(8,128)(2,1)}, bf16[192,384]{1,0:T(8,128)(2,1)S(1)}, u32[]{:S(2)}, u32[]{:S(2)}) %collective-permute-start.56) | collective-permute-done | bytes 147488 | tf_op jit(solution)/shard_map/ppermute | solution.py:39
  (212 shorter events, 57.1 us)
Async XLA Ops:
  4.8 12.7 %collective-permute-start = (bf16[400,384]{1,0:T(8,128)(2,1)}, bf16[400,384]{1,0:T(8,128)(2,1)S(1)}, u32[]{:S(2)}, u32[]{:S(2)}) collective-permute-start(bf16[400,384]{1,0:T(8,128)(2,1)} %get-tuple-element.9), channel_id=1, source_target_pairs={{0,0},{4,1},{2,2},{6,3},{1,4},{5,5},{3,6},{7,7},{8,8},{12,9},{10,1... | collective-permute-start | bytes 921608 | tf_op jit(solution)/shard_map/ppermute | solution.py:39
  12.5 13.4 %collective-permute-start.6 = (bf16[192,384]{1,0:T(8,128)(2,1)}, bf16[192,384]{1,0:T(8,128)(2,1)S(1)}, u32[]{:S(2)}, u32[]{:S(2)}) collective-permute-start(bf16[192,384]{1,0:T(8,128)(2,1)} %get-tuple-element.10), channel_id=1, source_target_pairs={{16,0},{20,1},{18,2},{22,3},{17,4},{21,5},{19,6},{23,7},{24,8},{28... | collective-permute-start | bytes 442376 | tf_op jit(solution)/shard_map/ppermute | solution.py:39
  13.1 14.0 %collective-permute-start.5 = (bf16[192,384]{1,0:T(8,128)(2,1)}, bf16[192,384]{1,0:T(8,128)(2,1)S(1)}, u32[]{:S(2)}, u32[]{:S(2)}) collective-permute-start(bf16[192,384]{1,0:T(8,128)(2,1)} %get-tuple-element.10), channel_id=1, source_target_pairs={{8,0},{12,1},{10,2},{14,3},{9,4},{13,5},{11,6},{15,7},{0,8},{4,9},... | collective-permute-start | bytes 442376 | tf_op jit(solution)/shard_map/ppermute | solution.py:39
  14.3 15.3 %collective-permute-start.4 = (bf16[192,384]{1,0:T(8,128)(2,1)}, bf16[192,384]{1,0:T(8,128)(2,1)S(1)}, u32[]{:S(2)}, u32[]{:S(2)}) collective-permute-start(bf16[192,384]{1,0:T(8,128)(2,1)} %get-tuple-element.10), channel_id=1, source_target_pairs={{0,0},{4,1},{2,2},{6,3},{1,4},{5,5},{3,6},{7,7},{8,8},{12,9},{10,1... | collective-permute-start | bytes 442376 | tf_op jit(solution)/shard_map/ppermute | solution.py:39
  17.6 18.0 %collective-permute-start.3 = (bf16[400,384]{1,0:T(8,128)(2,1)S(1)}, bf16[400,384]{1,0:T(8,128)(2,1)S(1)}, u32[]{:S(2)}, u32[]{:S(2)}) collective-permute-start(bf16[400,384]{1,0:T(8,128)(2,1)S(1)} %collective-permute-done.refs_0_.refs_4_.refs_20_.refs_5_.refs_12_), channel_id=1, source_target_pairs={{6,0},{7,1},{4,2},{5,3},{2,4},{3,5},{0,6},{1,7},{14,8},{15,9},{12,... | collective-permute-start | bytes 921608 | tf_op jit(solution)/shard_map/ppermute | solution.py:39
  18.6 11.0 %collective-permute-start.11 = (bf16[192,384]{1,0:T(8,128)(2,1)S(1)}, bf16[192,384]{1,0:T(8,128)(2,1)S(1)}, u32[]{:S(2)}, u32[]{:S(2)}) collective-permute-start(bf16[192,384]{1,0:T(8,128)(2,1)S(1)} %collective-permute-done.7.refs_7_), channel_id=1, source_target_pairs={{1,0},{0,1},{3,2},{2,3},{5,4},{4,5},{7,6},{6,7},{9,8},{8,9},{11,10... | collective-permute-start | bytes 442376 | tf_op jit(solution)/shard_map/ppermute | solution.py:39
  25.9 10.1 %collective-permute-start.2 = (bf16[400,384]{1,0:T(8,128)(2,1)S(1)}, bf16[400,384]{1,0:T(8,128)(2,1)S(1)}, u32[]{:S(2)}, u32[]{:S(2)}) collective-permute-start(bf16[400,384]{1,0:T(8,128)(2,1)S(1)} %collective-permute-done.refs_0_.refs_4_.refs_20_.refs_5_.refs_12_), channel_id=1, source_target_pairs={{2,0},{3,1},{0,2},{1,3},{6,4},{7,5},{4,6},{5,7},{10,8},{11,9},{8,1... | collective-permute-start | bytes 921608 | tf_op jit(solution)/shard_map/ppermute | solution.py:39
  32.0 11.6 %collective-permute-start.17 = (bf16[400,384]{1,0:T(8,128)(2,1)S(1)}, bf16[400,384]{1,0:T(8,128)(2,1)S(1)}, u32[]{:S(2)}, u32[]{:S(2)}) collective-permute-start(bf16[400,384]{1,0:T(8,128)(2,1)S(1)} %collective-permute-done.refs_0_.refs_4_.refs_20_.refs_5_.refs_12_), channel_id=1, source_target_pairs={{24,0},{25,1},{26,2},{27,3},{28,4},{29,5},{30,6},{31,7},{16,8},{17... | collective-permute-start | bytes 921608 | tf_op jit(solution)/shard_map/ppermute | solution.py:39
  35.4 27.2 %collective-permute-start.16 = (bf16[400,384]{1,0:T(8,128)(2,1)S(1)}, bf16[400,384]{1,0:T(8,128)(2,1)S(1)}, u32[]{:S(2)}, u32[]{:S(2)}) collective-permute-start(bf16[400,384]{1,0:T(8,128)(2,1)S(1)} %collective-permute-done.refs_0_.refs_4_.refs_20_.refs_5_.refs_12_), channel_id=1, source_target_pairs={{16,0},{17,1},{18,2},{19,3},{20,4},{21,5},{22,6},{23,7},{24,8},{25... | collective-permute-start | bytes 921608 | tf_op jit(solution)/shard_map/ppermute | solution.py:39
  35.6 27.6 %collective-permute-start.15 = (bf16[400,384]{1,0:T(8,128)(2,1)S(1)}, bf16[400,384]{1,0:T(8,128)(2,1)S(1)}, u32[]{:S(2)}, u32[]{:S(2)}) collective-permute-start(bf16[400,384]{1,0:T(8,128)(2,1)S(1)} %collective-permute-done.refs_0_.refs_4_.refs_20_.refs_5_.refs_12_), channel_id=1, source_target_pairs={{8,0},{9,1},{10,2},{11,3},{12,4},{13,5},{14,6},{15,7},{0,8},{1,9},... | collective-permute-start | bytes 921608 | tf_op jit(solution)/shard_map/ppermute | solution.py:39
  36.1 27.3 %collective-permute-start.18 = (bf16[400,384]{1,0:T(8,128)(2,1)S(1)}, bf16[400,384]{1,0:T(8,128)(2,1)S(1)}, u32[]{:S(2)}, u32[]{:S(2)}) collective-permute-start(bf16[400,384]{1,0:T(8,128)(2,1)S(1)} %collective-permute-done.refs_0_.refs_4_.refs_20_.refs_5_.refs_12_), channel_id=1, source_target_pairs={{1,0},{0,1},{3,2},{2,3},{5,4},{4,5},{7,6},{6,7},{9,8},{8,9},{11,10... | collective-permute-start | bytes 921608 | tf_op jit(solution)/shard_map/ppermute | solution.py:39
  43.3 21.3 %collective-permute-start.14 = (bf16[384,384]{1,0:T(8,128)(2,1)}, bf16[384,384]{1,0:T(8,128)(2,1)S(1)}, u32[]{:S(2)}, u32[]{:S(2)}) collective-permute-start(bf16[384,384]{1,0:T(8,128)(2,1)} %first.1.refs_0_), channel_id=1, source_target_pairs={{6,0},{7,1},{4,2},{5,3},{2,4},{3,5},{0,6},{1,7},{14,8},{15,9},{12,... | collective-permute-start | bytes 884744 | tf_op jit(solution)/shard_map/ppermute | solution.py:39
  43.6 29.0 %collective-permute-start.21 = (bf16[400,384]{1,0:T(8,128)(2,1)S(1)}, bf16[400,384]{1,0:T(8,128)(2,1)S(1)}, u32[]{:S(2)}, u32[]{:S(2)}) collective-permute-start(bf16[400,384]{1,0:T(8,128)(2,1)S(1)} %collective-permute-done.17.refs_7_.refs_23_), channel_id=1, source_target_pairs={{1,0},{0,1},{3,2},{2,3},{5,4},{4,5},{7,6},{6,7},{9,8},{8,9},{11,10... | collective-permute-start | bytes 921608 | tf_op jit(solution)/shard_map/ppermute | solution.py:39
  62.6 10.1 %collective-permute-start.20 = (bf16[400,384]{1,0:T(8,128)(2,1)S(1)}, bf16[400,384]{1,0:T(8,128)(2,1)S(1)}, u32[]{:S(2)}, u32[]{:S(2)}) collective-permute-start(bf16[400,384]{1,0:T(8,128)(2,1)S(1)} %collective-permute-done.16.refs_6_.refs_22_), channel_id=1, source_target_pairs={{1,0},{0,1},{3,2},{2,3},{5,4},{4,5},{7,6},{6,7},{9,8},{8,9},{11,10... | collective-permute-start | bytes 921608 | tf_op jit(solution)/shard_map/ppermute | solution.py:39
  83.5 19.1 %collective-permute-start.26 = (bf16[2,192,384]{2,1,0:T(8,128)(2,1)S(1)}, bf16[2,192,384]{2,1,0:T(8,128)(2,1)S(1)}, u32[]{:S(2)}, u32[]{:S(2)}) collective-permute-start(bf16[2,192,384]{2,1,0:T(8,128)(2,1)S(1)} %pad_maximum_fusion.refs_0_), channel_id=1, source_target_pairs={{2,0},{3,1},{0,2},{1,3},{6,4},{7,5},{4,6},{5,7},{10,8},{11,9},{8,1... | collective-permute-start | bytes 884744 | tf_op jit(solution)/shard_map/ppermute | solution.py:39
  86.2 12.0 %collective-permute-start.32 = (bf16[192,384]{1,0:T(8,128)(2,1)}, bf16[192,384]{1,0:T(8,128)(2,1)S(1)}, u32[]{:S(2)}, u32[]{:S(2)}) collective-permute-start(bf16[192,384]{1,0:T(8,128)(2,1)} %generator.1), channel_id=1, source_target_pairs={{16,0},{17,1},{18,2},{19,3},{20,4},{21,5},{22,6},{23,7},{24,8},{25... | collective-permute-start | bytes 442376 | tf_op jit(solution)/shard_map/ppermute | solution.py:39
  86.2 16.5 %collective-permute-start.24 = (bf16[2,192,384]{2,1,0:T(8,128)(2,1)S(1)}, bf16[2,192,384]{2,1,0:T(8,128)(2,1)S(1)}, u32[]{:S(2)}, u32[]{:S(2)}) collective-permute-start(bf16[2,192,384]{2,1,0:T(8,128)(2,1)S(1)} %pad_maximum_fusion.refs_0_), channel_id=1, source_target_pairs={{4,0},{5,1},{6,2},{7,3},{0,4},{1,5},{2,6},{3,7},{12,8},{13,9},{14,... | collective-permute-start | bytes 884744 | tf_op jit(solution)/shard_map/ppermute | solution.py:39
  102.5 10.0 %collective-permute-start.34 = (bf16[2,192,384]{2,1,0:T(8,128)(2,1)S(1)}, bf16[2,192,384]{2,1,0:T(8,128)(2,1)S(1)}, u32[]{:S(2)}, u32[]{:S(2)}) collective-permute-start(bf16[2,192,384]{2,1,0:T(8,128)(2,1)S(1)} %pad_maximum_fusion.1.refs_10_), channel_id=1, source_target_pairs={{1,0},{0,1},{3,2},{2,3},{5,4},{4,5},{7,6},{6,7},{9,8},{8,9},{11,10... | collective-permute-start | bytes 884744 | tf_op jit(solution)/shard_map/ppermute | solution.py:39
  102.7 10.4 %collective-permute-start.28 = (bf16[1,192,384]{2,1,0:T(8,128)(2,1)S(1)}, bf16[1,192,384]{2,1,0:T(8,128)(2,1)S(1)}, u32[]{:S(2)}, u32[]{:S(2)}) collective-permute-start(bf16[1,192,384]{2,1,0:T(8,128)(2,1)S(1)} %slice.16), channel_id=1, source_target_pairs={{4,0},{5,1},{6,2},{7,3},{0,4},{1,5},{2,6},{3,7},{12,8},{13,9},{14,... | collective-permute-start | bytes 442376 | tf_op jit(solution)/shard_map/ppermute | solution.py:39
  106.7 12.2 %collective-permute-start.27 = (bf16[2,192,384]{2,1,0:T(8,128)(2,1)S(1)}, bf16[2,192,384]{2,1,0:T(8,128)(2,1)S(1)}, u32[]{:S(2)}, u32[]{:S(2)}) collective-permute-start(bf16[2,192,384]{2,1,0:T(8,128)(2,1)S(1)} %collective-permute-done.26.refs_4_), channel_id=1, source_target_pairs={{1,0},{0,1},{3,2},{2,3},{5,4},{4,5},{7,6},{6,7},{9,8},{8,9},{11,10... | collective-permute-start | bytes 884744 | tf_op jit(solution)/shard_map/ppermute | solution.py:39
  167.8 12.6 %collective-permute-start.50 = (bf16[192,384]{1,0:T(8,128)(2,1)}, bf16[192,384]{1,0:T(8,128)(2,1)S(1)}, u32[]{:S(2)}, u32[]{:S(2)}) collective-permute-start(bf16[192,384]{1,0:T(8,128)(2,1)} %square.1.refs_0_.refs_4_), channel_id=1, source_target_pairs={{16,0},{17,1},{18,2},{19,3},{20,4},{21,5},{22,6},{23,7},{24,8},{25... | collective-permute-start | bytes 442376 | tf_op jit(solution)/shard_map/ppermute | solution.py:39
  167.8 13.0 %collective-permute-start.49 = (bf16[192,384]{1,0:T(8,128)(2,1)}, bf16[192,384]{1,0:T(8,128)(2,1)S(1)}, u32[]{:S(2)}, u32[]{:S(2)}) collective-permute-start(bf16[192,384]{1,0:T(8,128)(2,1)} %square.1.refs_0_.refs_4_), channel_id=1, source_target_pairs={{8,0},{9,1},{10,2},{11,3},{12,4},{13,5},{14,6},{15,7},{0,8},{1,9},... | collective-permute-start | bytes 442376 | tf_op jit(solution)/shard_map/ppermute | solution.py:39
  169.6 11.3 %collective-permute-start.48 = (bf16[192,384]{1,0:T(8,128)(2,1)}, bf16[192,384]{1,0:T(8,128)(2,1)S(1)}, u32[]{:S(2)}, u32[]{:S(2)}) collective-permute-start(bf16[192,384]{1,0:T(8,128)(2,1)} %square.1.refs_0_.refs_4_), channel_id=1, source_target_pairs={{6,0},{7,1},{4,2},{5,3},{2,4},{3,5},{0,6},{1,7},{14,8},{15,9},{12,... | collective-permute-start | bytes 442376 | tf_op jit(solution)/shard_map/ppermute | solution.py:39
  170.5 10.8 %collective-permute-start.47 = (bf16[192,384]{1,0:T(8,128)(2,1)}, bf16[192,384]{1,0:T(8,128)(2,1)S(1)}, u32[]{:S(2)}, u32[]{:S(2)}) collective-permute-start(bf16[192,384]{1,0:T(8,128)(2,1)} %square.1.refs_0_.refs_4_), channel_id=1, source_target_pairs={{2,0},{3,1},{0,2},{1,3},{6,4},{7,5},{4,6},{5,7},{10,8},{11,9},{8,1... | collective-permute-start | bytes 442376 | tf_op jit(solution)/shard_map/ppermute | solution.py:39
  (87 other events, 602.1 us)

commit v2 on v1

v2 whole, which is shorter than its diff:
```python
import functools

import jax
import jax.numpy as jnp
from jax import lax
from jax.experimental import pallas as pl
from jax.experimental.pallas import tpu as pltpu
from jax.sharding import PartitionSpec as P

BLK = 32
TERMS = 6
SQUARINGS = 2
FIRST = 3
AXES = ("row", "col")
F32 = jnp.float32
BF16 = jnp.bfloat16
TAIL = 16
VMEM_LIMIT = 60 * 1024 * 1024


def coordinates(r, c):
    return r // 2, r % 2, c // 2, c % 2


def permutation(rows, cols, source):
    pairs = []
    for r in range(rows):
        for c in range(cols):
            sr, sc = source(*coordinates(r, c))
            pairs.append((sr * cols + sc, r * cols + c))
    return pairs


class Moves:
    def __init__(self, rows, cols):
        self.rows, self.cols = rows, cols

    def move(self, value, source):
        return lax.ppermute(value, AXES, permutation(self.rows, self.cols, source))

    def relabel(self, value, k=0):
        return self.move(value, lambda z, y, x, e: (2 * (z ^ k) + e, 2 * x + y))

    def along_z(self, value, k):
        return self.move(value, lambda z, y, x, e: (2 * (z ^ k) + y, 2 * x + e))

    def in_plane(self, value, s):
        return self.move(value, lambda z, y, x, e: (2 * z + (y ^ (s & 1)), 2 * (x ^ (s >> 1)) + e))

    def core(self, value):
        return self.move(value, lambda z, y, x, e: (2 * z + y, 2 * x + 1 - e))


def place():
    r, c = lax.axis_index("row"), lax.axis_index("col")
    z, y, x, e = r // 2, r % 2, c // 2, c % 2
    return z, 2 * x + y, e


def iota(shape, axis):
    return lax.broadcasted_iota(jnp.int32, shape, axis)


def dot(a, b):
    return jnp.dot(a, b, preferred_element_type=F32)


def repeat_rows(rows, blocks):
    return (iota((rows, blocks), 0) // BLK == iota((rows, blocks), 1)).astype(BF16)


def repeat_columns(blocks, columns, first=0):
    return (iota((blocks, columns), 0) == iota((blocks, columns), 1) // BLK + first).astype(BF16)


def block_mask(tail, number, rows, columns):
    blocks = columns // BLK
    wide = dot(repeat_rows(rows, tail.shape[0]), tail).astype(BF16)
    return dot(wide, repeat_columns(tail.shape[1], columns, number * blocks))


def call(kernel, outs, ins, scratch, name, flops=1000):
    return pl.pallas_call(
        kernel,
        out_shape=outs,
        in_specs=ins,
        out_specs=jax.tree.map(lambda _: pl.BlockSpec(memory_space=pltpu.VMEM), outs),
        scratch_shapes=scratch,
        name=name,
        compiler_params=pltpu.CompilerParams(vmem_limit_bytes=VMEM_LIMIT),
        cost_estimate=pl.CostEstimate(flops=flops, bytes_accessed=1000, transcendentals=0),
    )


ANY = pl.BlockSpec(memory_space=pl.ANY)
INVMEM = pl.BlockSpec(memory_space=pltpu.VMEM)
INSMEM = pl.BlockSpec(memory_space=pltpu.SMEM)


def mask_kernel(fock, density, margin, fills, firsts, seconds, masked_density, pair):
    rows, columns = fock.shape
    row_blocks, column_blocks = rows // BLK, columns // BLK
    tall = repeat_rows(rows, row_blocks)
    wide = repeat_columns(column_blocks, columns)

    def masked(ref, number):
        mask = dot(dot(tall, fills[number].astype(BF16)).astype(BF16), wide)
        return (ref[...].astype(F32) * mask).astype(BF16)

    masked_density[...] = masked(density, 1)
    pair[0:rows, :] = masked(fock, 0)
    pair[rows : 2 * rows, :] = masked(margin, 2)
    top = (iota((TAIL, row_blocks), 0) == iota((TAIL, row_blocks), 1)).astype(BF16)
    tail = jnp.zeros((TAIL, columns), F32)
    for number in range(firsts.shape[0] + seconds.shape[0]):
        ref = firsts[number] if number < FIRST else seconds[number - FIRST]
        column = iota((column_blocks, columns), 1) - number * column_blocks
        spread = (iota((column_blocks, columns), 0) == column).astype(BF16)
        tail += dot(dot(top, ref.astype(BF16)).astype(BF16), spread)
    pair[2 * rows :, :] = tail.astype(BF16)


def chunk(index, length):
    return pl.ds(pl.multiple_of(index * length, length), length)


def start_all(copies):
    for one in copies:
        one.start()


def wait_all(copies):
    for one in copies:
        one.wait()


def repeat(times, body, unrolled):
    if unrolled:
        for t in range(times):
            body(t)
    else:

        def step(t, carry):
            body(t)
            return carry

        lax.fori_loop(0, times, step, 0)


def tail_of(copy, tail):
    copy.wait()
    return tail[...]


def first_kernel(count, *refs):
    pairs, near, far = refs[:count], refs[count : 2 * count], refs[2 * count : 3 * count]
    out, left, right, tail, sems = refs[3 * count :]
    z, q, e = place()
    rows, columns = near[0].shape
    copies = [pltpu.make_async_copy(pairs[0].at[2 * rows :], tail, sems.at[0])]
    for s in range(count):
        copies.append(
            pltpu.make_async_copy(
                pairs[s].at[: 2 * rows], left.at[:, chunk(q ^ s, columns)], sems.at[len(copies)]
            )
        )
        for ref, core in ((near[s], e), (far[s], 1 - e)):
            copies.append(
                pltpu.make_async_copy(
                    ref, right.at[chunk(2 * (z ^ s) + core, rows)], sems.at[len(copies)]
                )
            )
    start_all(copies)
    filters = tail_of(copies[0], tail)
    masks = [block_mask(filters, n, rows, columns) for n in range(2)]
    wait_all(copies[1:])
    total = dot(left[...], right[...])
    for n in range(2):
        part = slice(n * rows, (n + 1) * rows)
        out[part, :] = (total[part] * masks[n]).astype(BF16)


def generator_kernel(count, *refs):
    lefts, near, far = refs[:count], refs[count : 2 * count], refs[2 * count : 3 * count]
    out, left, right, tail, sems = refs[3 * count :]
    z, q, e = place()
    rows, columns = out.shape
    copies = [pltpu.make_async_copy(near[0].at[2 * rows :], tail, sems.at[0])]
    for s in range(count):
        for half in range(2):
            part = pl.ds(half * rows, rows)
            copies.append(
                pltpu.make_async_copy(
                    lefts[s].at[part], left.at[half, :, chunk(q ^ s, columns)], sems.at[len(copies)]
                )
            )
            for ref, core in ((near[s], e), (far[s], 1 - e)):
                copies.append(
                    pltpu.make_async_copy(
                        ref.at[part],
                        right.at[1 - half, chunk(2 * (z ^ s) + core, rows)],
                        sems.at[len(copies)],
                    )
                )
    start_all(copies)
    mask = block_mask(tail_of(copies[0], tail), 2, rows, columns)
    wait_all(copies[1:])
    plus = dot(left[0], right[0])
    minus = dot(left[1], right[1])
    generator = ((plus - minus) * mask).astype(BF16)
    out[...] = (generator.astype(F32) * 0.25).astype(BF16)


def series_kernel(layout, count, *refs):
    pieces = refs[: len(layout)]
    tails = refs[len(layout) : len(layout) + 2 * count]
    order = refs[len(layout) + 2 * count]
    panel, mine, whole, turned, wides, spread, sems = refs[len(layout) + 2 * count + 1 :]
    z, q, e = place()
    rows, columns = mine.shape
    size = panel.shape[1]
    row_blocks, column_blocks, blocks = rows // BLK, columns // BLK, size // BLK
    copies, early = [], []
    for ref, (slots, plane, lane) in zip(pieces, layout):
        core = e if lane == 0 else 1 - e
        for index, k in enumerate(slots):
            copies.append(
                pltpu.make_async_copy(
                    ref.at[index],
                    whole.at[chunk(2 * (z ^ k) + core, rows), chunk(q ^ plane, columns)],
                    sems.at[len(copies)],
                )
            )
    for index, ref in enumerate(tails):
        core = e if index < count else 1 - e
        early.append(
            pltpu.make_async_copy(
                ref.at[2 * rows :],
                wides.at[2 * (z ^ (index % count)) + core],
                sems.at[len(copies) + len(early)],
            )
        )
    start_all(early)
    start_all(copies)
    wait_all(early)
    filters = jnp.zeros((128, size), F32)
    for p in range(2 * count):
        column = iota((TAIL, size), 1) // BLK
        row = iota((TAIL, size), 0)
        near = ((row < row_blocks) & (column == row + p * row_blocks)).astype(BF16)
        filters += lax.dot_general(
            wides[p][:, :128], near, (((0,), (0,)), ((), ())), preferred_element_type=F32
        )
    spread[...] = filters

    wait_all(copies)
    small = size <= 1536

    def turn(t):
        tile = jnp.concatenate(
            [whole[chunk(order[t * column_blocks + a], BLK), :] for a in range(column_blocks)],
            axis=0,
        )
        turned[:, chunk(t, columns)] = tile.T

    def place_rows(b):
        whole[chunk(b, BLK), :] = turned[chunk(order[b], BLK), :]

    repeat(count, turn, small)
    repeat(blocks, place_rows, small)

    first = (2 * q + e) * rows
    unit = (iota((rows, size), 1) == iota((rows, size), 0) + first).astype(F32)
    own = unit + whole[chunk(2 * q + e, rows), :].astype(F32) / TERMS
    panel[...] = own.astype(BF16)
    width = size if small else 512
    for number in range(1, TERMS):
        current = panel[...]
        base = (FIRST + number - 1) * column_blocks + e * row_blocks

        def advance(t):
            part = chunk(t, width)
            product = dot(current, whole[:, part])
            mask = jnp.concatenate(
                [
                    jnp.broadcast_to(spread[pl.ds(base + b, 1), part], (BLK, width))
                    for b in range(row_blocks)
                ],
                axis=0,
            )
            here = iota((rows, width), 1) + t * width == iota((rows, width), 0) + first
            panel[:, part] = (here.astype(F32) + product * mask / (TERMS - number)).astype(BF16)

        repeat(size // width, advance, small)
    mine[...] = panel[:, chunk(z, columns)]


def turned_mask(tails, number, e, rows, columns):
    row_blocks, column_blocks = rows // BLK, columns // BLK
    pick = iota((rows, 128), 0) // BLK + number * column_blocks + e * row_blocks
    pick = (pick == iota((rows, 128), 1)).astype(BF16)
    mask = jnp.zeros((rows, columns), F32)
    for core in range(2):
        row = iota((TAIL, columns), 0)
        near = (row < row_blocks) & (iota((TAIL, columns), 1) // BLK == row + core * row_blocks)
        chosen = lax.dot_general(
            pick, tails[core][:, :128], (((1,), (1,)), ((), ())), preferred_element_type=F32
        )
        mask += dot(chosen.astype(BF16), near.astype(BF16))
    return mask


def square_kernel(count, *refs):
    near, far = refs[:count], refs[count : 2 * count]
    panel, pair, other, out, right, tails, sems = refs[2 * count :]
    z, q, e = place()
    rows, columns = out.shape
    copies = [
        pltpu.make_async_copy(pair.at[2 * rows :], tails.at[e], sems.at[0]),
        pltpu.make_async_copy(other.at[2 * rows :], tails.at[1 - e], sems.at[1]),
    ]
    for s in range(count):
        for ref, core in ((near[s], e), (far[s], 1 - e)):
            copies.append(
                pltpu.make_async_copy(
                    ref, right.at[chunk(2 * (q ^ s) + core, rows)], sems.at[len(copies)]
                )
            )
    start_all(copies)
    wait_all(copies[:2])
    mask = turned_mask(tails, FIRST + TERMS - 1, e, rows, columns)
    wait_all(copies[2:])
    out[...] = (dot(panel[...], right[...]) * mask).astype(BF16)


def evolve_kernel(count, *refs):
    groups = [refs[n * count : (n + 1) * count] for n in range(4)]
    line_near, line_far, plane_near, plane_far = groups
    pair, other, out, left, right, tails, sems = refs[4 * count :]
    z, q, e = place()
    rows, columns = out.shape
    copies = [
        pltpu.make_async_copy(pair.at[2 * rows :], tails.at[e], sems.at[0]),
        pltpu.make_async_copy(other.at[2 * rows :], tails.at[1 - e], sems.at[1]),
    ]
    for s in range(count):
        for ref, core in ((line_near[s], e), (line_far[s], 1 - e)):
            copies.append(
                pltpu.make_async_copy(
                    ref, left.at[chunk(core, rows), chunk(z ^ s, columns)], sems.at[len(copies)]
                )
            )
        for ref, core in ((plane_near[s], e), (plane_far[s], 1 - e)):
            copies.append(
                pltpu.make_async_copy(
                    ref, right.at[chunk(2 * (q ^ s) + core, rows)], sems.at[len(copies)]
                )
            )
    start_all(copies)
    wait_all(copies[:2])
    mask = block_mask(tails[pl.ds(e, 1)][0], FIRST + TERMS, rows, columns)
    wait_all(copies[2:])
    total = dot(left[...], right[...]).T
    chosen = jnp.where(e == 0, total[:rows], total[rows:])
    out[...] = (chosen * mask).astype(BF16)


def on_device(
    mesh_rows,
    mesh_cols,
    fock_matrix,
    density,
    margin,
    fill_patterns,
    first_filters,
    owner_order,
    second_filters,
):
    moves = Moves(mesh_rows, mesh_cols)
    count = mesh_cols
    slots = range(1, count)
    rows, columns = fock_matrix.shape
    size = rows * mesh_rows
    block = jax.ShapeDtypeStruct((rows, columns), BF16)

    masked_density, pair = call(
        mask_kernel,
        [block, jax.ShapeDtypeStruct((2 * rows + TAIL, columns), BF16)],
        [INVMEM] * 6,
        [],
        "mask",
    )(fock_matrix, density, margin, fill_patterns, first_filters, second_filters)

    density_near = [moves.relabel(masked_density, k) for k in range(count)]
    density_far = [moves.core(value) for value in density_near]
    held = pair
    pair = moves.relabel(held)
    pair_near = [pair] + [moves.relabel(held, k) for k in slots]
    pair_rows = [pair] + [moves.in_plane(pair, s) for s in slots]
    pair_far = [moves.core(value) for value in pair_near]

    products = call(
        functools.partial(first_kernel, count),
        jax.ShapeDtypeStruct((2 * rows, columns), BF16),
        [ANY] * (3 * count),
        [
            pltpu.VMEM((2 * rows, size), BF16),
            pltpu.VMEM((size, columns), BF16),
            pltpu.VMEM((TAIL, columns), BF16),
            pltpu.SemaphoreType.DMA((1 + 3 * count,)),
        ],
        "first",
    )(*pair_rows, *density_near, *density_far)
    products = [products] + [moves.in_plane(products, s) for s in slots]

    generator = call(
        functools.partial(generator_kernel, count),
        block,
        [ANY] * (3 * count),
        [
            pltpu.VMEM((2, rows, size), BF16),
            pltpu.VMEM((2, size, columns), BF16),
            pltpu.VMEM((TAIL, columns), BF16),
            pltpu.SemaphoreType.DMA((1 + 6 * count,)),
        ],
        "generator",
    )(*products, *pair_near, *pair_far)

    lines = [generator] + [moves.along_z(generator, k) for k in slots]
    half = count // 2
    layout, pieces = [], []
    for first in (0, half):
        chosen = tuple(range(first, first + half))
        group = jnp.stack([lines[k] for k in chosen])
        planes = {0: [(chosen, group)]}
        for s in slots:
            if count == 4 and s == 3:
                continue
            planes[s] = [(chosen, moves.in_plane(group, s))]
        if count == 4:
            planes[3] = [
                (chosen[:1], moves.in_plane(planes[2][0][1][:1], 1)),
                (chosen[1:], moves.in_plane(planes[1][0][1][1:], 2)),
            ]
        for s, parts in planes.items():
            for held, value in parts:
                layout += [(held, s, 0), (held, s, 1)]
                pieces += [value, moves.core(value)]

    panel, mine = call(
        functools.partial(series_kernel, layout, count),
        [jax.ShapeDtypeStruct((rows, size), BF16), block],
        [ANY] * (len(layout) + 2 * count) + [INSMEM],
        [
            pltpu.VMEM((size, size), BF16),
            pltpu.VMEM((size, size), BF16),
            pltpu.VMEM((mesh_rows, TAIL, columns), BF16),
            pltpu.VMEM((128, size), F32),
            pltpu.SemaphoreType.DMA((mesh_rows * mesh_cols + 2 * count,)),
        ],
        "series",
    )(*pieces, *pair_near, *pair_far, owner_order)

    near = [mine] + [moves.in_plane(mine, s) for s in slots]
    far = [moves.core(value) for value in near]
    square = call(
        functools.partial(square_kernel, count),
        block,
        [ANY] * (2 * count) + [INVMEM, ANY, ANY],
        [
            pltpu.VMEM((size, columns), BF16),
            pltpu.VMEM((2, TAIL, columns), BF16),
            pltpu.SemaphoreType.DMA((2 + 2 * count,)),
        ],
        "square",
    )(*near, *far, panel, pair, pair_far[0])

    line_near = [square] + [moves.along_z(square, k) for k in slots]
    line_far = [moves.core(value) for value in line_near]
    plane_near = [square] + [moves.in_plane(square, s) for s in slots]
    plane_far = [line_far[0]] + [moves.core(value) for value in plane_near[1:]]
    evolved = call(
        functools.partial(evolve_kernel, count),
        block,
        [ANY] * (4 * count + 2),
        [
            pltpu.VMEM((columns, size), BF16),
            pltpu.VMEM((size, columns), BF16),
            pltpu.VMEM((2, TAIL, columns), BF16),
            pltpu.SemaphoreType.DMA((2 + 4 * count,)),
        ],
        "evolve",
    )(*line_near, *line_far, *plane_near, *plane_far, pair, pair_far[0])
    return moves.relabel(evolved)


def solution(mesh):
    return jax.shard_map(
        functools.partial(on_device, mesh.shape["row"], mesh.shape["col"]),
        mesh=mesh,
        in_specs=(
            P("row", "col"),
            P("row", "col"),
            P("row", "col"),
            P(None, "row", "col"),
            P(None, "row", "col"),
            P(),
            P(None, "row", "col"),
        ),
        out_specs=P("row", "col"),
        check_vma=False,
    )
```

time: 194 us -> 188 us (0.969)
  Pallas kernels: 45.9 us -> 28.3 us
  waiting for transfers between devices: 76.9 us -> 87.7 us
    pallas_call x1, Pallas kernels: 29 us -> 10.8 us  [on_device(): call(functools.partial(series_kernel, layout, count), [jax.ShapeDtypeStru...]
    ppermute x57 -> x64, waiting for transfers between devices: 76.9 us -> 87.7 us  [move(): return lax.ppermute(value, AXES, permutation(self.rows, self.cols, source))]
    ppermute x57 -> x64, starting transfers between devices: 61.8 us -> 63.5 us  [move(): return lax.ppermute(value, AXES, permutation(self.rows, self.cols, source))]
    unnamed x110 -> x126, local copies, waits for them, and re-layouts: 7.67 us -> 6.55 us
  transfers between devices with their start and end apart: 57 -> 64, of which waited for: 25 -> 30; matrix products, arithmetic and copies ran while one was open for 0% -> 0% of each run, Pallas kernels for 2% -> 2%
where the time goes in v2:
time: 188 us
  waiting for transfers between devices  87.7 us (47%)
  starting transfers between devices  63.5 us (34%)
  Pallas kernels  28.3 us (15%)
  local copies, waits for them, and re-layouts  6.61 us (4%)
    ppermute x64, waiting for transfers between devices, move(): return lax.ppermute(value, AXES, permutation(self.rows, self.cols, source))  87.7 us
    ppermute x64, starting transfers between devices, move(): return lax.ppermute(value, AXES, permutation(self.rows, self.cols, source))  63.5 us
    pallas_call x1, Pallas kernels, on_device(): call(functools.partial(series_kernel, layout, count), [jax.ShapeDtypeStru...  10.8 us
    unnamed x126, local copies, waits for them, and re-layouts  6.55 us
  transfers between devices with their start and end apart: 64, of which 30 were waited for; matrix products, arithmetic and copies ran while one was open for 0% of the time, Pallas kernels for 2%

profile of v2, /device:TPU:1, one launch (start us, length us, event | category | flops | bytes accessed | tf_op | source)
XLA Modules:
  0.0 187.9 jit_solution(6020277092739948505)
XLA Ops:
  1.3 3.5 %mask.1 = (bf16[192,384]{1,0:T(8,128)(2,1)}, bf16[400,384]{1,0:T(8,128)(2,1)}) custom-call(bf16[192,384]{1,0:T(8,128)(2,1)} %fock.1, bf16[192,384]{1,0:T(8,128)(2,1)} %density.1, bf16[192,384]{1,0:T(8,128)(2,1)} %margin.1, s32[3,6,12]{2,1,0:T(8,128)} %fills.1, s32[3,6,12]{2,1,0:T(8,128)} %firsts.1, s32[7,6,12]{2,1,0:T(8,128)} %copy.8.seconds), custom_call_target="tpu_custom_call" | custom-call | flops 1000 | bytes 1000 | tf_op jit(solution)/shard_map/mask/pallas_call | solution.py:386
  4.8 5.7 %collective-permute-start.7 = (bf16[192,384]{1,0:T(8,128)(2,1)}, bf16[192,384]{1,0:T(8,128)(2,1)S(1)}, u32[]{:S(2)}, u32[]{:S(2)}) collective-permute-start(bf16[192,384]{1,0:T(8,128)(2,1)} %get-tuple-element.10), channel_id=1, source_target_pairs={{24,0},{28,1},{26,2},{30,3},{25,4},{29,5},{27,6},{31,7},{16,8},{20... | collective-permute-start | bytes 442376 | tf_op jit(solution)/shard_map/ppermute | solution.py:39
  15.2 7.7 %collective-permute-done.6.refs_6_ = bf16[192,384]{1,0:T(8,128)(2,1)S(1)} collective-permute-done((bf16[192,384]{1,0:T(8,128)(2,1)}, bf16[192,384]{1,0:T(8,128)(2,1)S(1)}, u32[]{:S(2)}, u32[]{:S(2)}) %collective-permute-start.6) | collective-permute-done | bytes 147488 | tf_op jit(solution)/shard_map/ppermute | solution.py:39
  23.5 3.3 %collective-permute-start = (bf16[400,384]{1,0:T(8,128)(2,1)}, bf16[400,384]{1,0:T(8,128)(2,1)S(1)}, u32[]{:S(2)}, u32[]{:S(2)}) collective-permute-start(bf16[400,384]{1,0:T(8,128)(2,1)} %get-tuple-element.9), channel_id=1, source_target_pairs={{0,0},{4,1},{2,2},{6,3},{1,4},{5,5},{3,6},{7,7},{8,8},{12,9},{10,1... | collective-permute-start | bytes 921608 | tf_op jit(solution)/shard_map/ppermute | solution.py:39
  29.2 2.5 %collective-permute-start.15 = (bf16[400,384]{1,0:T(8,128)(2,1)}, bf16[400,384]{1,0:T(8,128)(2,1)S(1)}, u32[]{:S(2)}, u32[]{:S(2)}) collective-permute-start(bf16[400,384]{1,0:T(8,128)(2,1)} %get-tuple-element.9), channel_id=1, source_target_pairs={{8,0},{12,1},{10,2},{14,3},{9,4},{13,5},{11,6},{15,7},{0,8},{4,9},... | collective-permute-start | bytes 921608 | tf_op jit(solution)/shard_map/ppermute | solution.py:39
  34.5 6.1 %collective-permute-done.17.refs_7_.refs_23_ = bf16[400,384]{1,0:T(8,128)(2,1)S(1)} collective-permute-done((bf16[400,384]{1,0:T(8,128)(2,1)}, bf16[400,384]{1,0:T(8,128)(2,1)S(1)}, u32[]{:S(2)}, u32[]{:S(2)}) %collective-permute-start.17) | collective-permute-done | bytes 307232 | tf_op jit(solution)/shard_map/ppermute | solution.py:39
  40.5 14.1 %collective-permute-done.16.refs_6_.refs_22_ = bf16[400,384]{1,0:T(8,128)(2,1)S(1)} collective-permute-done((bf16[400,384]{1,0:T(8,128)(2,1)}, bf16[400,384]{1,0:T(8,128)(2,1)S(1)}, u32[]{:S(2)}, u32[]{:S(2)}) %collective-permute-start.16) | collective-permute-done | bytes 307232 | tf_op jit(solution)/shard_map/ppermute | solution.py:39
  58.2 3.2 %first.1.refs_0_ = bf16[384,384]{1,0:T(8,128)(2,1)} custom-call(bf16[400,384]{1,0:T(8,128)(2,1)} %copy-done, bf16[400,384]{1,0:T(8,128)(2,1)} %copy-done.18, bf16[400,384]{1,0:T(8,128)(2,1)} %copy-done.17, bf16[400,384]{1,0:T(8,128)(2,1)} %copy-done.16, bf16[192,384]{1,0:T(8,128)(2,1)} %copy-done.58, bf16[192,384]{1,0:T(8,128)(2,1)} %copy-done.57, ...), custom_call_target="tpu_custom_call" | custom-call | flops 1000 | bytes 1000 | tf_op jit(solution)/shard_map/first/pallas_call | solution.py:402
  64.3 6.7 %collective-permute-done.14.refs_3_ = bf16[384,384]{1,0:T(8,128)(2,1)S(1)} collective-permute-done((bf16[384,384]{1,0:T(8,128)(2,1)}, bf16[384,384]{1,0:T(8,128)(2,1)S(1)}, u32[]{:S(2)}, u32[]{:S(2)}) %collective-permute-start.14) | collective-permute-done | bytes 294944 | tf_op jit(solution)/shard_map/ppermute | solution.py:39
  70.9 6.0 %collective-permute-done.13.refs_2_ = bf16[384,384]{1,0:T(8,128)(2,1)S(1)} collective-permute-done((bf16[384,384]{1,0:T(8,128)(2,1)}, bf16[384,384]{1,0:T(8,128)(2,1)S(1)}, u32[]{:S(2)}, u32[]{:S(2)}) %collective-permute-start.13) | collective-permute-done | bytes 294944 | tf_op jit(solution)/shard_map/ppermute | solution.py:39
  78.7 3.7 %generator.1 = bf16[192,384]{1,0:T(8,128)(2,1)} custom-call(bf16[384,384]{1,0:T(8,128)(2,1)} %first.1.refs_0_, bf16[384,384]{1,0:T(8,128)(2,1)} %copy-done.27, bf16[384,384]{1,0:T(8,128)(2,1)} %copy-done.26, bf16[384,384]{1,0:T(8,128)(2,1)} %copy-done.25, bf16[400,384]{1,0:T(8,128)(2,1)} %copy-done, bf16[400,384]{1,0:T(8,128)(2,1)} %copy-done.4, ...), custom_call_target="tpu_custom_call" | custom-call | flops 1000 | bytes 1000 | tf_op jit(solution)/shard_map/generator/pallas_call | solution.py:416
  84.6 4.0 %collective-permute-done.22 = bf16[192,384]{1,0:T(8,128)(2,1)S(1)} collective-permute-done((bf16[192,384]{1,0:T(8,128)(2,1)}, bf16[192,384]{1,0:T(8,128)(2,1)S(1)}, u32[]{:S(2)}, u32[]{:S(2)}) %collective-permute-start.22) | collective-permute-done | bytes 147488 | tf_op jit(solution)/shard_map/ppermute | solution.py:39
  93.0 3.6 %collective-permute-done.33 = bf16[192,384]{1,0:T(8,128)(2,1)S(1)} collective-permute-done((bf16[192,384]{1,0:T(8,128)(2,1)S(1)}, bf16[192,384]{1,0:T(8,128)(2,1)S(1)}, u32[]{:S(2)}, u32[]{:S(2)}) %collective-permute-start.33) | collective-permute-done | bytes 147488 | tf_op jit(solution)/shard_map/ppermute | solution.py:39
  96.6 9.2 %collective-permute-done.32 = bf16[192,384]{1,0:T(8,128)(2,1)S(1)} collective-permute-done((bf16[192,384]{1,0:T(8,128)(2,1)S(1)}, bf16[192,384]{1,0:T(8,128)(2,1)S(1)}, u32[]{:S(2)}, u32[]{:S(2)}) %collective-permute-start.32) | collective-permute-done | bytes 147488 | tf_op jit(solution)/shard_map/ppermute | solution.py:39
  110.1 2.7 %collective-permute-done.37.refs_14_ = bf16[2,192,384]{2,1,0:T(8,128)(2,1)S(1)} collective-permute-done((bf16[2,192,384]{2,1,0:T(8,128)(2,1)S(1)}, bf16[2,192,384]{2,1,0:T(8,128)(2,1)S(1)}, u32[]{:S(2)}, u32[]{:S(2)}) %collective-permute-start.37) | collective-permute-done | bytes 294944 | tf_op jit(solution)/shard_map/ppermute | solution.py:39
  113.5 4.7 %collective-permute-start.27 = (bf16[2,192,384]{2,1,0:T(8,128)(2,1)S(1)}, bf16[2,192,384]{2,1,0:T(8,128)(2,1)S(1)}, u32[]{:S(2)}, u32[]{:S(2)}) collective-permute-start(bf16[2,192,384]{2,1,0:T(8,128)(2,1)S(1)} %collective-permute-done.26.refs_4_), channel_id=1, source_target_pairs={{1,0},{0,1},{3,2},{2,3},{5,4},{4,5},{7,6},{6,7},{9,8},{8,9},{11,10... | collective-permute-start | bytes 884744 | tf_op jit(solution)/shard_map/ppermute | solution.py:39
  120.6 2.6 %collective-permute-start.38 = (bf16[2,192,384]{2,1,0:T(8,128)(2,1)S(1)}, bf16[2,192,384]{2,1,0:T(8,128)(2,1)S(1)}, u32[]{:S(2)}, u32[]{:S(2)}) collective-permute-start(bf16[2,192,384]{2,1,0:T(8,128)(2,1)S(1)} %collective-permute-done.37.refs_14_), channel_id=1, source_target_pairs={{1,0},{0,1},{3,2},{2,3},{5,4},{4,5},{7,6},{6,7},{9,8},{8,9},{11,10... | collective-permute-start | bytes 884744 | tf_op jit(solution)/shard_map/ppermute | solution.py:39
  128.2 10.8 %series.1 = (bf16[192,1536]{1,0:T(8,128)(2,1)}, bf16[192,384]{1,0:T(8,128)(2,1)}) custom-call(bf16[2,192,384]{2,1,0:T(8,128)(2,1)} %copy-done.8, bf16[2,192,384]{2,1,0:T(8,128)(2,1)} %copy-done.19, bf16[2,192,384]{2,1,0:T(8,128)(2,1)} %copy-done.11, bf16[2,192,384]{2,1,0:T(8,128)(2,1)} %copy-done.22, bf16[2,192,384]{2,1,0:T(8,128)(2,1)} %copy-done.10, ...), custom_call_target="tpu_custom_call" | custom-call | flops 1000 | bytes 1000 | tf_op jit(solution)/shard_map/series/pallas_call | solution.py:450
  152.3 3.6 %square.1.refs_0_.refs_8_ = bf16[192,384]{1,0:T(8,128)(2,1)} custom-call(bf16[192,384]{1,0:T(8,128)(2,1)} %get-tuple-element.11.refs_0_, bf16[192,384]{1,0:T(8,128)(2,1)} %copy-done.47, bf16[192,384]{1,0:T(8,128)(2,1)} %copy-done.46, bf16[192,384]{1,0:T(8,128)(2,1)} %copy-done.44, bf16[192,384]{1,0:T(8,128)(2,1)} %copy-done.49, bf16[192,384]{1,0:T(8,128)(2,1)} %copy-done.54, ...), custom_call_target="tpu_custom_call" | custom-call | flops 1000 | bytes 1000 | tf_op jit(solution)/shard_map/square/pallas_call | solution.py:466
  162.3 2.6 %collective-permute-done.58.refs_10_ = bf16[192,384]{1,0:T(8,128)(2,1)S(1)} collective-permute-done((bf16[192,384]{1,0:T(8,128)(2,1)}, bf16[192,384]{1,0:T(8,128)(2,1)S(1)}, u32[]{:S(2)}, u32[]{:S(2)}) %collective-permute-start.58) | collective-permute-done | bytes 147488 | tf_op jit(solution)/shard_map/ppermute | solution.py:39
  168.4 5.4 %collective-permute-done.51.refs_2_ = bf16[192,384]{1,0:T(8,128)(2,1)S(1)} collective-permute-done((bf16[192,384]{1,0:T(8,128)(2,1)}, bf16[192,384]{1,0:T(8,128)(2,1)S(1)}, u32[]{:S(2)}, u32[]{:S(2)}) %collective-permute-start.51) | collective-permute-done | bytes 147488 | tf_op jit(solution)/shard_map/ppermute | solution.py:39
  177.1 3.5 %evolve.1 = bf16[192,384]{1,0:T(8,128)(2,1)} custom-call(bf16[192,384]{1,0:T(8,128)(2,1)} %square.1.refs_0_.refs_8_, bf16[192,384]{1,0:T(8,128)(2,1)} %copy-done.41, bf16[192,384]{1,0:T(8,128)(2,1)} %copy-done.40, bf16[192,384]{1,0:T(8,128)(2,1)} %copy-done.39, bf16[192,384]{1,0:T(8,128)(2,1)} %copy-done.14, bf16[192,384]{1,0:T(8,128)(2,1)} %copy-done.52, ...), custom_call_target="tpu_custom_call" | custom-call | flops 1000 | bytes 1000 | tf_op jit(solution)/shard_map/evolve/pallas_call | solution.py:482
  180.5 2.9 %collective-permute-start.63 = (bf16[192,384]{1,0:T(8,128)(2,1)}, bf16[192,384]{1,0:T(8,128)(2,1)S(1)}, u32[]{:S(2)}, u32[]{:S(2)}) collective-permute-start(bf16[192,384]{1,0:T(8,128)(2,1)} %evolve.1), channel_id=1, source_target_pairs={{0,0},{4,1},{2,2},{6,3},{1,4},{5,5},{3,6},{7,7},{8,8},{12,9},{10,1... | collective-permute-start | bytes 442376 | tf_op jit(solution)/shard_map/ppermute | solution.py:39
  183.5 3.7 %collective-permute-done.63 = bf16[192,384]{1,0:T(8,128)(2,1)S(1)} collective-permute-done((bf16[192,384]{1,0:T(8,128)(2,1)}, bf16[192,384]{1,0:T(8,128)(2,1)S(1)}, u32[]{:S(2)}, u32[]{:S(2)}) %collective-permute-start.63) | collective-permute-done | bytes 147488 | tf_op jit(solution)/shard_map/ppermute | solution.py:39
  (242 shorter events, 65.6 us)
Async XLA Ops:
  4.8 10.4 %collective-permute-start.7 = (bf16[192,384]{1,0:T(8,128)(2,1)}, bf16[192,384]{1,0:T(8,128)(2,1)S(1)}, u32[]{:S(2)}, u32[]{:S(2)}) collective-permute-start(bf16[192,384]{1,0:T(8,128)(2,1)} %get-tuple-element.10), channel_id=1, source_target_pairs={{24,0},{28,1},{26,2},{30,3},{25,4},{29,5},{27,6},{31,7},{16,8},{20... | collective-permute-start | bytes 442376 | tf_op jit(solution)/shard_map/ppermute | solution.py:39
  10.5 12.4 %collective-permute-start.6 = (bf16[192,384]{1,0:T(8,128)(2,1)}, bf16[192,384]{1,0:T(8,128)(2,1)S(1)}, u32[]{:S(2)}, u32[]{:S(2)}) collective-permute-start(bf16[192,384]{1,0:T(8,128)(2,1)} %get-tuple-element.10), channel_id=1, source_target_pairs={{16,0},{20,1},{18,2},{22,3},{17,4},{21,5},{19,6},{23,7},{24,8},{28... | collective-permute-start | bytes 442376 | tf_op jit(solution)/shard_map/ppermute | solution.py:39
  10.5 16.2 %collective-permute-start.5 = (bf16[192,384]{1,0:T(8,128)(2,1)}, bf16[192,384]{1,0:T(8,128)(2,1)S(1)}, u32[]{:S(2)}, u32[]{:S(2)}) collective-permute-start(bf16[192,384]{1,0:T(8,128)(2,1)} %get-tuple-element.10), channel_id=1, source_target_pairs={{8,0},{12,1},{10,2},{14,3},{9,4},{13,5},{11,6},{15,7},{0,8},{4,9},... | collective-permute-start | bytes 442376 | tf_op jit(solution)/shard_map/ppermute | solution.py:39
  11.9 17.2 %collective-permute-start.4 = (bf16[192,384]{1,0:T(8,128)(2,1)}, bf16[192,384]{1,0:T(8,128)(2,1)S(1)}, u32[]{:S(2)}, u32[]{:S(2)}) collective-permute-start(bf16[192,384]{1,0:T(8,128)(2,1)} %get-tuple-element.10), channel_id=1, source_target_pairs={{0,0},{4,1},{2,2},{6,3},{1,4},{5,5},{3,6},{7,7},{8,8},{12,9},{10,1... | collective-permute-start | bytes 442376 | tf_op jit(solution)/shard_map/ppermute | solution.py:39
  15.2 13.9 %collective-permute-start.11 = (bf16[192,384]{1,0:T(8,128)(2,1)S(1)}, bf16[192,384]{1,0:T(8,128)(2,1)S(1)}, u32[]{:S(2)}, u32[]{:S(2)}) collective-permute-start(bf16[192,384]{1,0:T(8,128)(2,1)S(1)} %collective-permute-done.7.refs_7_), channel_id=1, source_target_pairs={{1,0},{0,1},{3,2},{2,3},{5,4},{4,5},{7,6},{6,7},{9,8},{8,9},{11,10... | collective-permute-start | bytes 442376 | tf_op jit(solution)/shard_map/ppermute | solution.py:39
  26.8 13.7 %collective-permute-start.17 = (bf16[400,384]{1,0:T(8,128)(2,1)}, bf16[400,384]{1,0:T(8,128)(2,1)S(1)}, u32[]{:S(2)}, u32[]{:S(2)}) collective-permute-start(bf16[400,384]{1,0:T(8,128)(2,1)} %get-tuple-element.9), channel_id=1, source_target_pairs={{24,0},{28,1},{26,2},{30,3},{25,4},{29,5},{27,6},{31,7},{16,8},{20... | collective-permute-start | bytes 921608 | tf_op jit(solution)/shard_map/ppermute | solution.py:39
  29.2 25.4 %collective-permute-start.16 = (bf16[400,384]{1,0:T(8,128)(2,1)}, bf16[400,384]{1,0:T(8,128)(2,1)S(1)}, u32[]{:S(2)}, u32[]{:S(2)}) collective-permute-start(bf16[400,384]{1,0:T(8,128)(2,1)} %get-tuple-element.9), channel_id=1, source_target_pairs={{16,0},{20,1},{18,2},{22,3},{17,4},{21,5},{19,6},{23,7},{24,8},{28... | collective-permute-start | bytes 921608 | tf_op jit(solution)/shard_map/ppermute | solution.py:39
  29.2 25.4 %collective-permute-start.15 = (bf16[400,384]{1,0:T(8,128)(2,1)}, bf16[400,384]{1,0:T(8,128)(2,1)S(1)}, u32[]{:S(2)}, u32[]{:S(2)}) collective-permute-start(bf16[400,384]{1,0:T(8,128)(2,1)} %get-tuple-element.9), channel_id=1, source_target_pairs={{8,0},{12,1},{10,2},{14,3},{9,4},{13,5},{11,6},{15,7},{0,8},{4,9},... | collective-permute-start | bytes 921608 | tf_op jit(solution)/shard_map/ppermute | solution.py:39
  32.1 23.0 %collective-permute-start.3 = (bf16[400,384]{1,0:T(8,128)(2,1)S(1)}, bf16[400,384]{1,0:T(8,128)(2,1)S(1)}, u32[]{:S(2)}, u32[]{:S(2)}) collective-permute-start(bf16[400,384]{1,0:T(8,128)(2,1)S(1)} %collective-permute-done.refs_0_.refs_4_.refs_20_.refs_9_.refs_16_), channel_id=1, source_target_pairs={{6,0},{7,1},{4,2},{5,3},{2,4},{3,5},{0,6},{1,7},{14,8},{15,9},{12,... | collective-permute-start | bytes 921608 | tf_op jit(solution)/shard_map/ppermute | solution.py:39
  34.2 21.0 %collective-permute-start.2 = (bf16[400,384]{1,0:T(8,128)(2,1)S(1)}, bf16[400,384]{1,0:T(8,128)(2,1)S(1)}, u32[]{:S(2)}, u32[]{:S(2)}) collective-permute-start(bf16[400,384]{1,0:T(8,128)(2,1)S(1)} %collective-permute-done.refs_0_.refs_4_.refs_20_.refs_9_.refs_16_), channel_id=1, source_target_pairs={{2,0},{3,1},{0,2},{1,3},{6,4},{7,5},{4,6},{5,7},{10,8},{11,9},{8,1... | collective-permute-start | bytes 921608 | tf_op jit(solution)/shard_map/ppermute | solution.py:39
  40.5 16.9 %collective-permute-start.1 = (bf16[400,384]{1,0:T(8,128)(2,1)S(1)}, bf16[400,384]{1,0:T(8,128)(2,1)S(1)}, u32[]{:S(2)}, u32[]{:S(2)}) collective-permute-start(bf16[400,384]{1,0:T(8,128)(2,1)S(1)} %collective-permute-done.refs_0_.refs_4_.refs_20_.refs_9_.refs_16_), channel_id=1, source_target_pairs={{4,0},{5,1},{6,2},{7,3},{0,4},{1,5},{2,6},{3,7},{12,8},{13,9},{14,... | collective-permute-start | bytes 921608 | tf_op jit(solution)/shard_map/ppermute | solution.py:39
  55.1 9.1 %collective-permute-start.19 = (bf16[400,384]{1,0:T(8,128)(2,1)S(1)}, bf16[400,384]{1,0:T(8,128)(2,1)S(1)}, u32[]{:S(2)}, u32[]{:S(2)}) collective-permute-start(bf16[400,384]{1,0:T(8,128)(2,1)S(1)} %collective-permute-done.15.refs_5_.refs_21_), channel_id=1, source_target_pairs={{1,0},{0,1},{3,2},{2,3},{5,4},{4,5},{7,6},{6,7},{9,8},{8,9},{11,10... | collective-permute-start | bytes 921608 | tf_op jit(solution)/shard_map/ppermute | solution.py:39
  55.2 9.0 %collective-permute-start.18 = (bf16[400,384]{1,0:T(8,128)(2,1)S(1)}, bf16[400,384]{1,0:T(8,128)(2,1)S(1)}, u32[]{:S(2)}, u32[]{:S(2)}) collective-permute-start(bf16[400,384]{1,0:T(8,128)(2,1)S(1)} %collective-permute-done.refs_0_.refs_4_.refs_20_.refs_9_.refs_16_), channel_id=1, source_target_pairs={{1,0},{0,1},{3,2},{2,3},{5,4},{4,5},{7,6},{6,7},{9,8},{8,9},{11,10... | collective-permute-start | bytes 921608 | tf_op jit(solution)/shard_map/ppermute | solution.py:39
  61.5 9.4 %collective-permute-start.14 = (bf16[384,384]{1,0:T(8,128)(2,1)}, bf16[384,384]{1,0:T(8,128)(2,1)S(1)}, u32[]{:S(2)}, u32[]{:S(2)}) collective-permute-start(bf16[384,384]{1,0:T(8,128)(2,1)} %first.1.refs_0_), channel_id=1, source_target_pairs={{6,0},{7,1},{4,2},{5,3},{2,4},{3,5},{0,6},{1,7},{14,8},{15,9},{12,... | collective-permute-start | bytes 884744 | tf_op jit(solution)/shard_map/ppermute | solution.py:39
  63.0 13.9 %collective-permute-start.13 = (bf16[384,384]{1,0:T(8,128)(2,1)}, bf16[384,384]{1,0:T(8,128)(2,1)S(1)}, u32[]{:S(2)}, u32[]{:S(2)}) collective-permute-start(bf16[384,384]{1,0:T(8,128)(2,1)} %first.1.refs_0_), channel_id=1, source_target_pairs={{2,0},{3,1},{0,2},{1,3},{6,4},{7,5},{4,6},{5,7},{10,8},{11,9},{8,1... | collective-permute-start | bytes 884744 | tf_op jit(solution)/shard_map/ppermute | solution.py:39
  63.4 14.5 %collective-permute-start.12 = (bf16[384,384]{1,0:T(8,128)(2,1)}, bf16[384,384]{1,0:T(8,128)(2,1)S(1)}, u32[]{:S(2)}, u32[]{:S(2)}) collective-permute-start(bf16[384,384]{1,0:T(8,128)(2,1)} %first.1.refs_0_), channel_id=1, source_target_pairs={{4,0},{5,1},{6,2},{7,3},{0,4},{1,5},{2,6},{3,7},{12,8},{13,9},{14,... | collective-permute-start | bytes 884744 | tf_op jit(solution)/shard_map/ppermute | solution.py:39
  89.6 18.5 %collective-permute-start.26 = (bf16[2,192,384]{2,1,0:T(8,128)(2,1)S(1)}, bf16[2,192,384]{2,1,0:T(8,128)(2,1)S(1)}, u32[]{:S(2)}, u32[]{:S(2)}) collective-permute-start(bf16[2,192,384]{2,1,0:T(8,128)(2,1)S(1)} %pad_maximum_fusion.refs_0_), channel_id=1, source_target_pairs={{2,0},{3,1},{0,2},{1,3},{6,4},{7,5},{4,6},{5,7},{10,8},{11,9},{8,1... | collective-permute-start | bytes 884744 | tf_op jit(solution)/shard_map/ppermute | solution.py:39
  92.2 13.6 %collective-permute-start.32 = (bf16[192,384]{1,0:T(8,128)(2,1)S(1)}, bf16[192,384]{1,0:T(8,128)(2,1)S(1)}, u32[]{:S(2)}, u32[]{:S(2)}) collective-permute-start(bf16[192,384]{1,0:T(8,128)(2,1)S(1)} %copy-done.15), channel_id=1, source_target_pairs={{16,0},{17,1},{18,2},{19,3},{20,4},{21,5},{22,6},{23,7},{24,8},{25... | collective-permute-start | bytes 442376 | tf_op jit(solution)/shard_map/ppermute | solution.py:39
  93.0 15.3 %collective-permute-start.24 = (bf16[2,192,384]{2,1,0:T(8,128)(2,1)S(1)}, bf16[2,192,384]{2,1,0:T(8,128)(2,1)S(1)}, u32[]{:S(2)}, u32[]{:S(2)}) collective-permute-start(bf16[2,192,384]{2,1,0:T(8,128)(2,1)S(1)} %pad_maximum_fusion.refs_0_), channel_id=1, source_target_pairs={{4,0},{5,1},{6,2},{7,3},{0,4},{1,5},{2,6},{3,7},{12,8},{13,9},{14,... | collective-permute-start | bytes 884744 | tf_op jit(solution)/shard_map/ppermute | solution.py:39
  108.2 10.1 %collective-permute-start.34 = (bf16[2,192,384]{2,1,0:T(8,128)(2,1)S(1)}, bf16[2,192,384]{2,1,0:T(8,128)(2,1)S(1)}, u32[]{:S(2)}, u32[]{:S(2)}) collective-permute-start(bf16[2,192,384]{2,1,0:T(8,128)(2,1)S(1)} %pad_maximum_fusion.1.refs_10_), channel_id=1, source_target_pairs={{1,0},{0,1},{3,2},{2,3},{5,4},{4,5},{7,6},{6,7},{9,8},{8,9},{11,10... | collective-permute-start | bytes 884744 | tf_op jit(solution)/shard_map/ppermute | solution.py:39
  108.3 11.2 %collective-permute-start.28 = (bf16[1,192,384]{2,1,0:T(8,128)(2,1)S(1)}, bf16[1,192,384]{2,1,0:T(8,128)(2,1)S(1)}, u32[]{:S(2)}, u32[]{:S(2)}) collective-permute-start(bf16[1,192,384]{2,1,0:T(8,128)(2,1)S(1)} %slice.16), channel_id=1, source_target_pairs={{4,0},{5,1},{6,2},{7,3},{0,4},{1,5},{2,6},{3,7},{12,8},{13,9},{14,... | collective-permute-start | bytes 442376 | tf_op jit(solution)/shard_map/ppermute | solution.py:39
  113.5 11.0 %collective-permute-start.27 = (bf16[2,192,384]{2,1,0:T(8,128)(2,1)S(1)}, bf16[2,192,384]{2,1,0:T(8,128)(2,1)S(1)}, u32[]{:S(2)}, u32[]{:S(2)}) collective-permute-start(bf16[2,192,384]{2,1,0:T(8,128)(2,1)S(1)} %collective-permute-done.26.refs_4_), channel_id=1, source_target_pairs={{1,0},{0,1},{3,2},{2,3},{5,4},{4,5},{7,6},{6,7},{9,8},{8,9},{11,10... | collective-permute-start | bytes 884744 | tf_op jit(solution)/shard_map/ppermute | solution.py:39
  162.3 11.5 %collective-permute-start.51 = (bf16[192,384]{1,0:T(8,128)(2,1)}, bf16[192,384]{1,0:T(8,128)(2,1)S(1)}, u32[]{:S(2)}, u32[]{:S(2)}) collective-permute-start(bf16[192,384]{1,0:T(8,128)(2,1)} %square.1.refs_0_.refs_8_), channel_id=1, source_target_pairs={{16,0},{17,1},{18,2},{19,3},{20,4},{21,5},{22,6},{23,7},{24,8},{25... | collective-permute-start | bytes 442376 | tf_op jit(solution)/shard_map/ppermute | solution.py:39
  164.9 9.5 %collective-permute-start.50 = (bf16[192,384]{1,0:T(8,128)(2,1)}, bf16[192,384]{1,0:T(8,128)(2,1)S(1)}, u32[]{:S(2)}, u32[]{:S(2)}) collective-permute-start(bf16[192,384]{1,0:T(8,128)(2,1)} %square.1.refs_0_.refs_8_), channel_id=1, source_target_pairs={{8,0},{9,1},{10,2},{11,3},{12,4},{13,5},{14,6},{15,7},{0,8},{1,9},... | collective-permute-start | bytes 442376 | tf_op jit(solution)/shard_map/ppermute | solution.py:39
  (102 other events, 730.8 us)

commit v3 on v2

--- a/solution.py
+++ b/solution.py
@@ -108,8 +108,8 @@
         return (ref[...].astype(F32) * mask).astype(BF16)
 
     masked_density[...] = masked(density, 1)
-    pair[0:rows, :] = masked(fock, 0)
-    pair[rows : 2 * rows, :] = masked(margin, 2)
+    pair[TAIL : TAIL + rows, :] = masked(fock, 0)
+    pair[TAIL + rows :, :] = masked(margin, 2)
     top = (iota((TAIL, row_blocks), 0) == iota((TAIL, row_blocks), 1)).astype(BF16)
     tail = jnp.zeros((TAIL, columns), F32)
     for number in range(firsts.shape[0] + seconds.shape[0]):
@@ -117,7 +117,7 @@
         column = iota((column_blocks, columns), 1) - number * column_blocks
         spread = (iota((column_blocks, columns), 0) == column).astype(BF16)
         tail += dot(dot(top, ref.astype(BF16)).astype(BF16), spread)
-    pair[2 * rows :, :] = tail.astype(BF16)
+    pair[:TAIL, :] = tail.astype(BF16)
 
 
 def chunk(index, length):
@@ -152,24 +152,25 @@
     return tail[...]
 
 
-def first_kernel(count, *refs):
-    pairs, near, far = refs[:count], refs[count : 2 * count], refs[2 * count : 3 * count]
-    out, left, right, tail, sems = refs[3 * count :]
+def first_kernel(count, starts, *refs):
+    pair, parts = refs[0], refs[1 : 1 + 2 * count]
+    near, far = refs[1 + 2 * count : 1 + 3 * count], refs[1 + 3 * count : 1 + 4 * count]
+    out, left, right, tail, sems = refs[1 + 4 * count :]
     z, q, e = place()
     rows, columns = near[0].shape
-    copies = [pltpu.make_async_copy(pairs[0].at[2 * rows :], tail, sems.at[0])]
+    copies = [pltpu.make_async_copy(pair.at[:TAIL], tail, sems.at[0])]
+
+    def bring(source, target):
+        copies.append(pltpu.make_async_copy(source, target, sems.at[len(copies)]))
+
     for s in range(count):
-        copies.append(
-            pltpu.make_async_copy(
-                pairs[s].at[: 2 * rows], left.at[:, chunk(q ^ s, columns)], sems.at[len(copies)]
-            )
-        )
-        for ref, core in ((near[s], e), (far[s], 1 - e)):
-            copies.append(
-                pltpu.make_async_copy(
-                    ref, right.at[chunk(2 * (z ^ s) + core, rows)], sems.at[len(copies)]
-                )
-            )
+        for half in range(2):
+            bring(
+                parts[2 * s + half].at[pl.ds(starts[s][half], rows)],
+                left.at[pl.ds(half * rows, rows), chunk(q ^ s, columns)],
+            )
+        bring(near[s], right.at[chunk(2 * (z ^ s) + e, rows)])
+        bring(far[s], right.at[chunk(2 * (z ^ s) + 1 - e, rows)])
     start_all(copies)
     filters = tail_of(copies[0], tail)
     masks = [block_mask(filters, n, rows, columns) for n in range(2)]
@@ -180,28 +181,34 @@
         out[part, :] = (total[part] * masks[n]).astype(BF16)
 
 
-def generator_kernel(count, *refs):
-    lefts, near, far = refs[:count], refs[count : 2 * count], refs[2 * count : 3 * count]
-    out, left, right, tail, sems = refs[3 * count :]
+def generator_kernel(count, starts, *refs):
+    parts, own, other = refs[: 2 * count], refs[2 * count], refs[2 * count + 1]
+    rest = refs[2 * count + 2 :]
+    fock_near, fock_far, margin_near, margin_far = [
+        rest[n * (count - 1) : (n + 1) * (count - 1)] for n in range(4)
+    ]
+    out, left, right, tail, sems = rest[4 * (count - 1) :]
     z, q, e = place()
     rows, columns = out.shape
-    copies = [pltpu.make_async_copy(near[0].at[2 * rows :], tail, sems.at[0])]
-    for s in range(count):
-        for half in range(2):
-            part = pl.ds(half * rows, rows)
-            copies.append(
-                pltpu.make_async_copy(
-                    lefts[s].at[part], left.at[half, :, chunk(q ^ s, columns)], sems.at[len(copies)]
-                )
-            )
-            for ref, core in ((near[s], e), (far[s], 1 - e)):
-                copies.append(
-                    pltpu.make_async_copy(
-                        ref.at[part],
-                        right.at[1 - half, chunk(2 * (z ^ s) + core, rows)],
-                        sems.at[len(copies)],
-                    )
-                )
+    copies = [pltpu.make_async_copy(own.at[:TAIL], tail, sems.at[0])]
+
+    def bring(source, target):
+        copies.append(pltpu.make_async_copy(source, target, sems.at[len(copies)]))
+
+    for half in range(2):
+        for s in range(count):
+            bring(
+                parts[2 * s + half].at[pl.ds(starts[s][half], rows)],
+                left.at[half, :, chunk(q ^ s, columns)],
+            )
+        part = pl.ds(TAIL + half * rows, rows)
+        bring(own.at[part], right.at[1 - half, chunk(2 * z + e, rows)])
+        bring(other.at[part], right.at[1 - half, chunk(2 * z + 1 - e, rows)])
+    for k in range(1, count):
+        for refs_of, core in ((fock_near, e), (fock_far, 1 - e)):
+            bring(refs_of[k - 1].at[TAIL:], right.at[1, chunk(2 * (z ^ k) + core, rows)])
+        for refs_of, core in ((margin_near, e), (margin_far, 1 - e)):
+            bring(refs_of[k - 1], right.at[0, chunk(2 * (z ^ k) + core, rows)])
     start_all(copies)
     mask = block_mask(tail_of(copies[0], tail), 2, rows, columns)
     wait_all(copies[1:])
@@ -235,7 +242,7 @@
         core = e if index < count else 1 - e
         early.append(
             pltpu.make_async_copy(
-                ref.at[2 * rows :],
+                ref.at[:TAIL],
                 wides.at[2 * (z ^ (index % count)) + core],
                 sems.at[len(copies) + len(early)],
             )
@@ -316,8 +323,8 @@
     z, q, e = place()
     rows, columns = out.shape
     copies = [
-        pltpu.make_async_copy(pair.at[2 * rows :], tails.at[e], sems.at[0]),
-        pltpu.make_async_copy(other.at[2 * rows :], tails.at[1 - e], sems.at[1]),
+        pltpu.make_async_copy(pair.at[:TAIL], tails.at[e], sems.at[0]),
+        pltpu.make_async_copy(other.at[:TAIL], tails.at[1 - e], sems.at[1]),
     ]
     for s in range(count):
         for ref, core in ((near[s], e), (far[s], 1 - e)):
@@ -340,8 +347,8 @@
     z, q, e = place()
     rows, columns = out.shape
     copies = [
-        pltpu.make_async_copy(pair.at[2 * rows :], tails.at[e], sems.at[0]),
-        pltpu.make_async_copy(other.at[2 * rows :], tails.at[1 - e], sems.at[1]),
+        pltpu.make_async_copy(pair.at[:TAIL], tails.at[e], sems.at[0]),
+        pltpu.make_async_copy(other.at[:TAIL], tails.at[1 - e], sems.at[1]),
     ]
     for s in range(count):
         for ref, core in ((line_near[s], e), (line_far[s], 1 - e)):
@@ -385,38 +392,59 @@
 
     masked_density, pair = call(
         mask_kernel,
-        [block, jax.ShapeDtypeStruct((2 * rows + TAIL, columns), BF16)],
+        [block, jax.ShapeDtypeStruct((TAIL + 2 * rows, columns), BF16)],
         [INVMEM] * 6,
         [],
         "mask",
     )(fock_matrix, density, margin, fill_patterns, first_filters, second_filters)
 
+    def plane_parts(value, first):
+        parts = [value, value]
+        starts = [(first, first + rows)]
+        planes = {}
+        for s in slots:
+            if count == 4 and s == 3:
+                top, bottom = planes[2][:rows], planes[1][rows:]
+                parts += [moves.in_plane(top, 1), moves.in_plane(bottom, 2)]
+                starts.append((0, 0))
+            else:
+                planes[s] = moves.in_plane(value[first : first + 2 * rows], s)
+                parts += [planes[s], planes[s]]
+                starts.append((0, rows))
+        return parts, starts
+
     density_near = [moves.relabel(masked_density, k) for k in range(count)]
+    pair = moves.relabel(pair)
+    soon, *density_near = lax.optimization_barrier((pair, *density_near))
+    parts, starts = plane_parts(soon, TAIL)
+    fock_near = [moves.along_z(pair[: TAIL + rows], k) for k in slots]
+    lone, *density_near = lax.optimization_barrier((pair[TAIL + rows :], *density_near))
+    margin_near = [moves.along_z(lone, k) for k in slots]
     density_far = [moves.core(value) for value in density_near]
-    held = pair
-    pair = moves.relabel(held)
-    pair_near = [pair] + [moves.relabel(held, k) for k in slots]
-    pair_rows = [pair] + [moves.in_plane(pair, s) for s in slots]
-    pair_far = [moves.core(value) for value in pair_near]
+    pair_far = moves.core(pair)
+    parts, fock_near, pair_far = lax.optimization_barrier((parts, fock_near, pair_far))
 
     products = call(
-        functools.partial(first_kernel, count),
+        functools.partial(first_kernel, count, starts),
         jax.ShapeDtypeStruct((2 * rows, columns), BF16),
-        [ANY] * (3 * count),
+        [ANY] * (1 + 4 * count),
         [
             pltpu.VMEM((2 * rows, size), BF16),
             pltpu.VMEM((size, columns), BF16),
             pltpu.VMEM((TAIL, columns), BF16),
-            pltpu.SemaphoreType.DMA((1 + 3 * count,)),
+            pltpu.SemaphoreType.DMA((1 + 4 * count,)),
         ],
         "first",
-    )(*pair_rows, *density_near, *density_far)
-    products = [products] + [moves.in_plane(products, s) for s in slots]
+    )(pair, *parts, *density_near, *density_far)
+    parts, starts = plane_parts(products, 0)
+    parts, margin_near = lax.optimization_barrier((parts, margin_near))
+    fock_far = [moves.core(value) for value in fock_near]
+    margin_far = [moves.core(value) for value in margin_near]
 
     generator = call(
-        functools.partial(generator_kernel, count),
+        functools.partial(generator_kernel, count, starts),
         block,
-        [ANY] * (3 * count),
+        [ANY] * (2 * count + 2 + 4 * (count - 1)),
         [
             pltpu.VMEM((2, rows, size), BF16),
             pltpu.VMEM((2, size, columns), BF16),
@@ -424,28 +452,33 @@
             pltpu.SemaphoreType.DMA((1 + 6 * count,)),
         ],
         "generator",
-    )(*products, *pair_near, *pair_far)
-
-    lines = [generator] + [moves.along_z(generator, k) for k in slots]
-    half = count // 2
+    )(*parts, pair, pair_far, *fock_near, *fock_far, *margin_near, *margin_far)
+    tails = [pair, *fock_near, pair_far, *fock_far]
+
+    first = jnp.stack([generator, moves.along_z(generator, 1)])
+    held, groups = (0, 1), [((0, 1), first)]
+    for k in range(2, count, 2):
+        groups.append(((k, k ^ 1), moves.along_z(first, k)))
     layout, pieces = [], []
-    for first in (0, half):
-        chosen = tuple(range(first, first + half))
-        group = jnp.stack([lines[k] for k in chosen])
-        planes = {0: [(chosen, group)]}
-        for s in slots:
-            if count == 4 and s == 3:
-                continue
-            planes[s] = [(chosen, moves.in_plane(group, s))]
+
+    def keep(held, s, value):
+        layout.extend([(held, s, 0), (held, s, 1)])
+        pieces.extend([value, moves.core(value)])
+
+    corners = []
+    for held, group in groups:
+        group, *corners = lax.optimization_barrier((group, *corners))
+        for s, value in enumerate(corners):
+            keep(before[s : s + 1], 3, value)
+        before = held
+        keep(held, 0, group)
+        planes = {s: moves.in_plane(group, s) for s in slots if not (count == 4 and s == 3)}
+        for s, value in planes.items():
+            keep(held, s, value)
         if count == 4:
-            planes[3] = [
-                (chosen[:1], moves.in_plane(planes[2][0][1][:1], 1)),
-                (chosen[1:], moves.in_plane(planes[1][0][1][1:], 2)),
-            ]
-        for s, parts in planes.items():
-            for held, value in parts:
-                layout += [(held, s, 0), (held, s, 1)]
-                pieces += [value, moves.core(value)]
+            corners = [moves.in_plane(planes[2][:1], 1), moves.in_plane(planes[1][1:], 2)]
+    for s, value in enumerate(corners):
+        keep(before[s : s + 1], 3, value)
 
     panel, mine = call(
         functools.partial(series_kernel, layout, count),
@@ -459,7 +492,7 @@
             pltpu.SemaphoreType.DMA((mesh_rows * mesh_cols + 2 * count,)),
         ],
         "series",
-    )(*pieces, *pair_near, *pair_far, owner_order)
+    )(*pieces, *tails, owner_order)
 
     near = [mine] + [moves.in_plane(mine, s) for s in slots]
     far = [moves.core(value) for value in near]
@@ -473,7 +506,7 @@
             pltpu.SemaphoreType.DMA((2 + 2 * count,)),
         ],
         "square",
-    )(*near, *far, panel, pair, pair_far[0])
+    )(*near, *far, panel, pair, pair_far)
 
     line_near = [square] + [moves.along_z(square, k) for k in slots]
     line_far = [moves.core(value) for value in line_near]
@@ -490,7 +523,7 @@
             pltpu.SemaphoreType.DMA((2 + 4 * count,)),
         ],
         "evolve",
-    )(*line_near, *line_far, *plane_near, *plane_far, pair, pair_far[0])
+    )(*line_near, *line_far, *plane_near, *plane_far, pair, pair_far)
     return moves.relabel(evolved)
 
 

time: 188 us -> 182 us (0.968)
  waiting for transfers between devices: 87.7 us -> 73.7 us
  starting transfers between devices: 63.5 us -> 70.1 us
    ppermute x64 -> x71, waiting for transfers between devices: 87.7 us -> 73.7 us  [move(): return lax.ppermute(value, AXES, permutation(self.rows, self.cols, source))]
    ppermute x64 -> x71, starting transfers between devices: 63.5 us -> 70.1 us  [move(): return lax.ppermute(value, AXES, permutation(self.rows, self.cols, source))]
    unnamed x126 -> x142, local copies, waits for them, and re-layouts: 6.55 us -> 7.55 us
  transfers between devices with their start and end apart: 64 -> 71, of which waited for: 30 -> 33; matrix products, arithmetic and copies ran while one was open for 0% -> 0% of each run, Pallas kernels for 2% -> 0%
where the time goes in v3:
time: 182 us
  waiting for transfers between devices  73.7 us (40%)
  starting transfers between devices  70.1 us (39%)
  Pallas kernels  28.6 us (16%)
  local copies, waits for them, and re-layouts  7.74 us (4%)
    ppermute x71, waiting for transfers between devices, move(): return lax.ppermute(value, AXES, permutation(self.rows, self.cols, source))  73.7 us
    ppermute x71, starting transfers between devices, move(): return lax.ppermute(value, AXES, permutation(self.rows, self.cols, source))  70.1 us
    pallas_call x1, Pallas kernels, on_device(): call(functools.partial(series_kernel, layout, count), [jax.ShapeDtypeStru...  11 us
    unnamed x142, local copies, waits for them, and re-layouts  7.55 us
    pallas_call x1, Pallas kernels, on_device(): call(functools.partial(generator_kernel, count, starts), block, [ANY] * (...  3.71 us
  transfers between devices with their start and end apart: 71, of which 33 were waited for; matrix products, arithmetic and copies ran while one was open for 0% of the time, Pallas kernels for 0%

profile of v3, /device:TPU:1, one launch (start us, length us, event | category | flops | bytes accessed | tf_op | source)
XLA Modules:
  0.0 181.8 jit_solution(4343049224131063049)
XLA Ops:
  1.3 3.5 %mask.1 = (bf16[192,384]{1,0:T(8,128)(2,1)}, bf16[400,384]{1,0:T(8,128)(2,1)}) custom-call(bf16[192,384]{1,0:T(8,128)(2,1)} %fock.1, bf16[192,384]{1,0:T(8,128)(2,1)} %density.1, bf16[192,384]{1,0:T(8,128)(2,1)} %margin.1, s32[3,6,12]{2,1,0:T(8,128)} %fills.1, s32[3,6,12]{2,1,0:T(8,128)} %firsts.1, s32[7,6,12]{2,1,0:T(8,128)} %copy.8.seconds), custom_call_target="tpu_custom_call" | custom-call | flops 1000 | bytes 1000 | tf_op jit(solution)/shard_map/mask/pallas_call | solution.py:393
  4.8 4.5 %collective-permute-start = (bf16[400,384]{1,0:T(8,128)(2,1)}, bf16[400,384]{1,0:T(8,128)(2,1)S(1)}, u32[]{:S(2)}, u32[]{:S(2)}) collective-permute-start(bf16[400,384]{1,0:T(8,128)(2,1)} %get-tuple-element.45), channel_id=1, source_target_pairs={{0,0},{4,1},{2,2},{6,3},{1,4},{5,5},{3,6},{7,7},{8,8},{12,9},{10,1... | collective-permute-start | bytes 921608 | tf_op jit(solution)/shard_map/ppermute | solution.py:39
  9.4 3.1 %collective-permute-start.4 = (bf16[192,384]{1,0:T(8,128)(2,1)}, bf16[192,384]{1,0:T(8,128)(2,1)S(1)}, u32[]{:S(2)}, u32[]{:S(2)}) collective-permute-start(bf16[192,384]{1,0:T(8,128)(2,1)} %get-tuple-element.46), channel_id=1, source_target_pairs={{24,0},{28,1},{26,2},{30,3},{25,4},{29,5},{27,6},{31,7},{16,8},{20... | collective-permute-start | bytes 442376 | tf_op jit(solution)/shard_map/ppermute | solution.py:39
  14.3 3.2 %collective-permute-start.1 = (bf16[192,384]{1,0:T(8,128)(2,1)}, bf16[192,384]{1,0:T(8,128)(2,1)S(1)}, u32[]{:S(2)}, u32[]{:S(2)}) collective-permute-start(bf16[192,384]{1,0:T(8,128)(2,1)} %get-tuple-element.46), channel_id=1, source_target_pairs={{0,0},{4,1},{2,2},{6,3},{1,4},{5,5},{3,6},{7,7},{8,8},{12,9},{10,1... | collective-permute-start | bytes 442376 | tf_op jit(solution)/shard_map/ppermute | solution.py:39
  18.6 6.0 %collective-permute-done.3.refs_11_ = bf16[192,384]{1,0:T(8,128)(2,1)S(1)} collective-permute-done((bf16[192,384]{1,0:T(8,128)(2,1)}, bf16[192,384]{1,0:T(8,128)(2,1)S(1)}, u32[]{:S(2)}, u32[]{:S(2)}) %collective-permute-start.3) | collective-permute-done | bytes 147488 | tf_op jit(solution)/shard_map/ppermute | solution.py:39
  25.9 2.6 %collective-permute-start.12 = (bf16[400,384]{1,0:T(8,128)(2,1)S(1)}, bf16[400,384]{1,0:T(8,128)(2,1)S(1)}, u32[]{:S(2)}, u32[]{:S(2)}) collective-permute-start(bf16[400,384]{1,0:T(8,128)(2,1)S(1)} %collective-permute-done.refs_0_.refs_1_.refs_2_.refs_8_.refs_20_.refs_9_.refs_16_), channel_id=1, source_target_pairs={{1,0},{0,1},{3,2},{2,3},{5,4},{4,5},{7,6},{6,7},{9,8},{8,9},{11,10... | collective-permute-start | bytes 921608 | tf_op jit(solution)/shard_map/ppermute | solution.py:39
  37.4 6.6 %collective-permute-done.10.refs_11_.refs_22_ = bf16[208,384]{1,0:T(8,128)(2,1)S(1)} collective-permute-done((bf16[208,384]{1,0:T(8,128)(2,1)S(1)}, bf16[208,384]{1,0:T(8,128)(2,1)S(1)}, u32[]{:S(2)}, u32[]{:S(2)}) %collective-permute-start.10) | collective-permute-done | bytes 159776 | tf_op jit(solution)/shard_map/ppermute | solution.py:39
  45.7 4.6 %collective-permute-done.8.refs_8_ = bf16[192,384]{1,0:T(8,128)(2,1)S(1)} collective-permute-done((bf16[192,384]{1,0:T(8,128)(2,1)S(1)}, bf16[192,384]{1,0:T(8,128)(2,1)S(1)}, u32[]{:S(2)}, u32[]{:S(2)}) %collective-permute-start.8) | collective-permute-done | bytes 147488 | tf_op jit(solution)/shard_map/ppermute | solution.py:39
  51.7 3.3 %first.1.refs_0_.refs_1_ = bf16[384,384]{1,0:T(8,128)(2,1)} custom-call(bf16[400,384]{1,0:T(8,128)(2,1)} %copy-done, bf16[400,384]{1,0:T(8,128)(2,1)} %copy-done, bf16[400,384]{1,0:T(8,128)(2,1)} %copy-done, bf16[384,384]{1,0:T(8,128)(2,1)} %copy-done.5, bf16[384,384]{1,0:T(8,128)(2,1)} %copy-done.5, bf16[384,384]{1,0:T(8,128)(2,1)} %copy-done.3, ...), custom_call_target="tpu_custom_call" | custom-call | flops 1000 | bytes 1000 | tf_op jit(solution)/shard_map/first/pallas_call | solution.py:427
  59.1 3.9 %collective-permute-done.18.refs_4_.refs_5_ = bf16[384,384]{1,0:T(8,128)(2,1)S(1)} collective-permute-done((bf16[384,384]{1,0:T(8,128)(2,1)}, bf16[384,384]{1,0:T(8,128)(2,1)S(1)}, u32[]{:S(2)}, u32[]{:S(2)}) %collective-permute-start.18) | collective-permute-done | bytes 294944 | tf_op jit(solution)/shard_map/ppermute | solution.py:39
  65.4 4.3 %collective-permute-done.22.refs_17_ = bf16[192,384]{1,0:T(8,128)(2,1)S(1)} collective-permute-done((bf16[192,384]{1,0:T(8,128)(2,1)S(1)}, bf16[192,384]{1,0:T(8,128)(2,1)S(1)}, u32[]{:S(2)}, u32[]{:S(2)}) %collective-permute-start.22) | collective-permute-done | bytes 147488 | tf_op jit(solution)/shard_map/ppermute | solution.py:39
  74.3 3.7 %generator.1 = bf16[192,384]{1,0:T(8,128)(2,1)} custom-call(bf16[384,384]{1,0:T(8,128)(2,1)} %first.1.refs_0_.refs_1_, bf16[384,384]{1,0:T(8,128)(2,1)} %first.1.refs_0_.refs_1_, bf16[384,384]{1,0:T(8,128)(2,1)} %copy-done.4, bf16[384,384]{1,0:T(8,128)(2,1)} %copy-done.4, bf16[384,384]{1,0:T(8,128)(2,1)} %copy-done.2, bf16[384,384]{1,0:T(8,128)(2,1)} %copy-done.2, ...), custom_call_target="tpu_custom_call" | custom-call | flops 1000 | bytes 1000 | tf_op jit(solution)/shard_map/generator/pallas_call | solution.py:444
  80.4 4.3 %collective-permute-done.30 = bf16[192,384]{1,0:T(8,128)(2,1)S(1)} collective-permute-done((bf16[192,384]{1,0:T(8,128)(2,1)}, bf16[192,384]{1,0:T(8,128)(2,1)S(1)}, u32[]{:S(2)}, u32[]{:S(2)}) %collective-permute-start.30) | collective-permute-done | bytes 147488 | tf_op jit(solution)/shard_map/ppermute | solution.py:39
  87.6 6.0 %collective-permute-done.34.refs_4_ = bf16[2,192,384]{2,1,0:T(8,128)(2,1)S(1)} collective-permute-done((bf16[2,192,384]{2,1,0:T(8,128)(2,1)S(1)}, bf16[2,192,384]{2,1,0:T(8,128)(2,1)S(1)}, u32[]{:S(2)}, u32[]{:S(2)}) %collective-permute-start.34) | collective-permute-done | bytes 294944 | tf_op jit(solution)/shard_map/ppermute | solution.py:39
  95.0 7.1 %collective-permute-done.36.refs_10_ = bf16[2,192,384]{2,1,0:T(8,128)(2,1)S(1)} collective-permute-done((bf16[2,192,384]{2,1,0:T(8,128)(2,1)S(1)}, bf16[2,192,384]{2,1,0:T(8,128)(2,1)S(1)}, u32[]{:S(2)}, u32[]{:S(2)}) %collective-permute-start.36) | collective-permute-done | bytes 294944 | tf_op jit(solution)/shard_map/ppermute | solution.py:39
  106.5 2.6 %collective-permute-done.44.refs_14_ = bf16[2,192,384]{2,1,0:T(8,128)(2,1)S(1)} collective-permute-done((bf16[2,192,384]{2,1,0:T(8,128)(2,1)S(1)}, bf16[2,192,384]{2,1,0:T(8,128)(2,1)S(1)}, u32[]{:S(2)}, u32[]{:S(2)}) %collective-permute-start.44) | collective-permute-done | bytes 294944 | tf_op jit(solution)/shard_map/ppermute | solution.py:39
  109.1 2.5 %collective-permute-start.39 = (bf16[1,192,384]{2,1,0:T(8,128)(2,1)S(1)}, bf16[1,192,384]{2,1,0:T(8,128)(2,1)S(1)}, u32[]{:S(2)}, u32[]{:S(2)}) collective-permute-start(bf16[1,192,384]{2,1,0:T(8,128)(2,1)S(1)} %collective-permute-done.37.refs_6_), channel_id=1, source_target_pairs={{1,0},{0,1},{3,2},{2,3},{5,4},{4,5},{7,6},{6,7},{9,8},{8,9},{11,10... | collective-permute-start | bytes 442376 | tf_op jit(solution)/shard_map/ppermute | solution.py:39
  122.6 11.0 %series.1 = (bf16[192,1536]{1,0:T(8,128)(2,1)}, bf16[192,384]{1,0:T(8,128)(2,1)}) custom-call(bf16[2,192,384]{2,1,0:T(8,128)(2,1)} %copy-done.6, bf16[2,192,384]{2,1,0:T(8,128)(2,1)} %copy-done.19, bf16[2,192,384]{2,1,0:T(8,128)(2,1)} %copy-done.8, bf16[2,192,384]{2,1,0:T(8,128)(2,1)} %copy-done.21, bf16[2,192,384]{2,1,0:T(8,128)(2,1)} %copy-done.7, ...), custom_call_target="tpu_custom_call" | custom-call | flops 1000 | bytes 1000 | tf_op jit(solution)/shard_map/series/pallas_call | solution.py:483
  145.9 3.6 %square.1.refs_0_.refs_8_ = bf16[192,384]{1,0:T(8,128)(2,1)} custom-call(bf16[192,384]{1,0:T(8,128)(2,1)} %get-tuple-element.83.refs_0_, bf16[192,384]{1,0:T(8,128)(2,1)} %copy-done.56, bf16[192,384]{1,0:T(8,128)(2,1)} %copy-done.54, bf16[192,384]{1,0:T(8,128)(2,1)} %copy-done.51, bf16[192,384]{1,0:T(8,128)(2,1)} %copy-done.59, bf16[192,384]{1,0:T(8,128)(2,1)} %copy-done.69, ...), custom_call_target="tpu_custom_call" | custom-call | flops 1000 | bytes 1000 | tf_op jit(solution)/shard_map/square/pallas_call | solution.py:499
  155.7 2.7 %collective-permute-done.65.refs_10_ = bf16[192,384]{1,0:T(8,128)(2,1)S(1)} collective-permute-done((bf16[192,384]{1,0:T(8,128)(2,1)}, bf16[192,384]{1,0:T(8,128)(2,1)S(1)}, u32[]{:S(2)}, u32[]{:S(2)}) %collective-permute-start.65) | collective-permute-done | bytes 147488 | tf_op jit(solution)/shard_map/ppermute | solution.py:39
  162.2 5.6 %collective-permute-done.58.refs_2_ = bf16[192,384]{1,0:T(8,128)(2,1)S(1)} collective-permute-done((bf16[192,384]{1,0:T(8,128)(2,1)}, bf16[192,384]{1,0:T(8,128)(2,1)S(1)}, u32[]{:S(2)}, u32[]{:S(2)}) %collective-permute-start.58) | collective-permute-done | bytes 147488 | tf_op jit(solution)/shard_map/ppermute | solution.py:39
  171.0 3.4 %evolve.1 = bf16[192,384]{1,0:T(8,128)(2,1)} custom-call(bf16[192,384]{1,0:T(8,128)(2,1)} %square.1.refs_0_.refs_8_, bf16[192,384]{1,0:T(8,128)(2,1)} %copy-done.43, bf16[192,384]{1,0:T(8,128)(2,1)} %copy-done.41, bf16[192,384]{1,0:T(8,128)(2,1)} %copy-done.39, bf16[192,384]{1,0:T(8,128)(2,1)} %copy-done.17, bf16[192,384]{1,0:T(8,128)(2,1)} %copy-done.65, ...), custom_call_target="tpu_custom_call" | custom-call | flops 1000 | bytes 1000 | tf_op jit(solution)/shard_map/evolve/pallas_call | solution.py:515
  174.5 2.9 %collective-permute-start.70 = (bf16[192,384]{1,0:T(8,128)(2,1)}, bf16[192,384]{1,0:T(8,128)(2,1)S(1)}, u32[]{:S(2)}, u32[]{:S(2)}) collective-permute-start(bf16[192,384]{1,0:T(8,128)(2,1)} %evolve.1), channel_id=1, source_target_pairs={{0,0},{4,1},{2,2},{6,3},{1,4},{5,5},{3,6},{7,7},{8,8},{12,9},{10,1... | collective-permute-start | bytes 442376 | tf_op jit(solution)/shard_map/ppermute | solution.py:39
  177.4 3.7 %collective-permute-done.70 = bf16[192,384]{1,0:T(8,128)(2,1)S(1)} collective-permute-done((bf16[192,384]{1,0:T(8,128)(2,1)}, bf16[192,384]{1,0:T(8,128)(2,1)S(1)}, u32[]{:S(2)}, u32[]{:S(2)}) %collective-permute-start.70) | collective-permute-done | bytes 147488 | tf_op jit(solution)/shard_map/ppermute | solution.py:39
  (278 shorter events, 76.1 us)
Async XLA Ops:
  4.8 19.7 %collective-permute-start = (bf16[400,384]{1,0:T(8,128)(2,1)}, bf16[400,384]{1,0:T(8,128)(2,1)S(1)}, u32[]{:S(2)}, u32[]{:S(2)}) collective-permute-start(bf16[400,384]{1,0:T(8,128)(2,1)} %get-tuple-element.45), channel_id=1, source_target_pairs={{0,0},{4,1},{2,2},{6,3},{1,4},{5,5},{3,6},{7,7},{8,8},{12,9},{10,1... | collective-permute-start | bytes 921608 | tf_op jit(solution)/shard_map/ppermute | solution.py:39
  9.4 9.2 %collective-permute-start.4 = (bf16[192,384]{1,0:T(8,128)(2,1)}, bf16[192,384]{1,0:T(8,128)(2,1)S(1)}, u32[]{:S(2)}, u32[]{:S(2)}) collective-permute-start(bf16[192,384]{1,0:T(8,128)(2,1)} %get-tuple-element.46), channel_id=1, source_target_pairs={{24,0},{28,1},{26,2},{30,3},{25,4},{29,5},{27,6},{31,7},{16,8},{20... | collective-permute-start | bytes 442376 | tf_op jit(solution)/shard_map/ppermute | solution.py:39
  12.5 12.0 %collective-permute-start.3 = (bf16[192,384]{1,0:T(8,128)(2,1)}, bf16[192,384]{1,0:T(8,128)(2,1)S(1)}, u32[]{:S(2)}, u32[]{:S(2)}) collective-permute-start(bf16[192,384]{1,0:T(8,128)(2,1)} %get-tuple-element.46), channel_id=1, source_target_pairs={{16,0},{20,1},{18,2},{22,3},{17,4},{21,5},{19,6},{23,7},{24,8},{28... | collective-permute-start | bytes 442376 | tf_op jit(solution)/shard_map/ppermute | solution.py:39
  13.1 11.4 %collective-permute-start.2 = (bf16[192,384]{1,0:T(8,128)(2,1)}, bf16[192,384]{1,0:T(8,128)(2,1)S(1)}, u32[]{:S(2)}, u32[]{:S(2)}) collective-permute-start(bf16[192,384]{1,0:T(8,128)(2,1)} %get-tuple-element.46), channel_id=1, source_target_pairs={{8,0},{12,1},{10,2},{14,3},{9,4},{13,5},{11,6},{15,7},{0,8},{4,9},... | collective-permute-start | bytes 442376 | tf_op jit(solution)/shard_map/ppermute | solution.py:39
  14.3 10.2 %collective-permute-start.1 = (bf16[192,384]{1,0:T(8,128)(2,1)}, bf16[192,384]{1,0:T(8,128)(2,1)S(1)}, u32[]{:S(2)}, u32[]{:S(2)}) collective-permute-start(bf16[192,384]{1,0:T(8,128)(2,1)} %get-tuple-element.46), channel_id=1, source_target_pairs={{0,0},{4,1},{2,2},{6,3},{1,4},{5,5},{3,6},{7,7},{8,8},{12,9},{10,1... | collective-permute-start | bytes 442376 | tf_op jit(solution)/shard_map/ppermute | solution.py:39
  24.6 8.5 %collective-permute-start.6 = (bf16[384,384]{1,0:T(8,128)(2,1)S(1)}, bf16[384,384]{1,0:T(8,128)(2,1)S(1)}, u32[]{:S(2)}, u32[]{:S(2)}) collective-permute-start(bf16[384,384]{1,0:T(8,128)(2,1)S(1)} %slice.36), channel_id=1, source_target_pairs={{2,0},{3,1},{0,2},{1,3},{6,4},{7,5},{4,6},{5,7},{10,8},{11,9},{8,1... | collective-permute-start | bytes 884744 | tf_op jit(solution)/shard_map/ppermute | solution.py:39
  25.9 19.1 %collective-permute-start.12 = (bf16[400,384]{1,0:T(8,128)(2,1)S(1)}, bf16[400,384]{1,0:T(8,128)(2,1)S(1)}, u32[]{:S(2)}, u32[]{:S(2)}) collective-permute-start(bf16[400,384]{1,0:T(8,128)(2,1)S(1)} %collective-permute-done.refs_0_.refs_1_.refs_2_.refs_8_.refs_20_.refs_9_.refs_16_), channel_id=1, source_target_pairs={{1,0},{0,1},{3,2},{2,3},{5,4},{4,5},{7,6},{6,7},{9,8},{8,9},{11,10... | collective-permute-start | bytes 921608 | tf_op jit(solution)/shard_map/ppermute | solution.py:39
  30.8 13.3 %collective-permute-start.10 = (bf16[208,384]{1,0:T(8,128)(2,1)S(1)}, bf16[208,384]{1,0:T(8,128)(2,1)S(1)}, u32[]{:S(2)}, u32[]{:S(2)}) collective-permute-start(bf16[208,384]{1,0:T(8,128)(2,1)S(1)} %slice.49), channel_id=1, source_target_pairs={{16,0},{17,1},{18,2},{19,3},{20,4},{21,5},{22,6},{23,7},{24,8},{25... | collective-permute-start | bytes 479240 | tf_op jit(solution)/shard_map/ppermute | solution.py:39
  33.1 11.7 %collective-permute-start.9 = (bf16[208,384]{1,0:T(8,128)(2,1)S(1)}, bf16[208,384]{1,0:T(8,128)(2,1)S(1)}, u32[]{:S(2)}, u32[]{:S(2)}) collective-permute-start(bf16[208,384]{1,0:T(8,128)(2,1)S(1)} %slice.49), channel_id=1, source_target_pairs={{8,0},{9,1},{10,2},{11,3},{12,4},{13,5},{14,6},{15,7},{0,8},{1,9},... | collective-permute-start | bytes 479240 | tf_op jit(solution)/shard_map/ppermute | solution.py:39
  33.9 11.6 %collective-permute-start.7 = (bf16[192,384]{1,0:T(8,128)(2,1)S(1)}, bf16[192,384]{1,0:T(8,128)(2,1)S(1)}, u32[]{:S(2)}, u32[]{:S(2)}) collective-permute-start(bf16[192,384]{1,0:T(8,128)(2,1)S(1)} %slice.47), channel_id=1, source_target_pairs={{4,0},{5,1},{6,2},{7,3},{0,4},{1,5},{2,6},{3,7},{12,8},{13,9},{14,... | collective-permute-start | bytes 442376 | tf_op jit(solution)/shard_map/ppermute | solution.py:39
  36.2 14.1 %collective-permute-start.13 = (bf16[192,384]{1,0:T(8,128)(2,1)S(1)}, bf16[192,384]{1,0:T(8,128)(2,1)S(1)}, u32[]{:S(2)}, u32[]{:S(2)}) collective-permute-start(bf16[192,384]{1,0:T(8,128)(2,1)S(1)} %collective-permute-done.1.refs_9_), channel_id=1, source_target_pairs={{1,0},{0,1},{3,2},{2,3},{5,4},{4,5},{7,6},{6,7},{9,8},{8,9},{11,10... | collective-permute-start | bytes 442376 | tf_op jit(solution)/shard_map/ppermute | solution.py:39
  55.3 9.5 %collective-permute-start.17 = (bf16[384,384]{1,0:T(8,128)(2,1)}, bf16[384,384]{1,0:T(8,128)(2,1)S(1)}, u32[]{:S(2)}, u32[]{:S(2)}) collective-permute-start(bf16[384,384]{1,0:T(8,128)(2,1)} %first.1.refs_0_.refs_1_), channel_id=1, source_target_pairs={{4,0},{5,1},{6,2},{7,3},{0,4},{1,5},{2,6},{3,7},{12,8},{13,9},{14,... | collective-permute-start | bytes 884744 | tf_op jit(solution)/shard_map/ppermute | solution.py:39
  55.6 9.5 %collective-permute-start.23 = (bf16[192,384]{1,0:T(8,128)(2,1)S(1)}, bf16[192,384]{1,0:T(8,128)(2,1)S(1)}, u32[]{:S(2)}, u32[]{:S(2)}) collective-permute-start(bf16[192,384]{1,0:T(8,128)(2,1)S(1)} %slice.50), channel_id=1, source_target_pairs={{24,0},{25,1},{26,2},{27,3},{28,4},{29,5},{30,6},{31,7},{16,8},{17... | collective-permute-start | bytes 442376 | tf_op jit(solution)/shard_map/ppermute | solution.py:39
  57.9 11.8 %collective-permute-start.22 = (bf16[192,384]{1,0:T(8,128)(2,1)S(1)}, bf16[192,384]{1,0:T(8,128)(2,1)S(1)}, u32[]{:S(2)}, u32[]{:S(2)}) collective-permute-start(bf16[192,384]{1,0:T(8,128)(2,1)S(1)} %slice.50), channel_id=1, source_target_pairs={{16,0},{17,1},{18,2},{19,3},{20,4},{21,5},{22,6},{23,7},{24,8},{25... | collective-permute-start | bytes 442376 | tf_op jit(solution)/shard_map/ppermute | solution.py:39
  58.0 12.9 %collective-permute-start.21 = (bf16[192,384]{1,0:T(8,128)(2,1)S(1)}, bf16[192,384]{1,0:T(8,128)(2,1)S(1)}, u32[]{:S(2)}, u32[]{:S(2)}) collective-permute-start(bf16[192,384]{1,0:T(8,128)(2,1)S(1)} %slice.50), channel_id=1, source_target_pairs={{8,0},{9,1},{10,2},{11,3},{12,4},{13,5},{14,6},{15,7},{0,8},{1,9},... | collective-permute-start | bytes 442376 | tf_op jit(solution)/shard_map/ppermute | solution.py:39
  63.0 8.6 %collective-permute-start.24 = (bf16[208,384]{1,0:T(8,128)(2,1)S(1)}, bf16[208,384]{1,0:T(8,128)(2,1)S(1)}, u32[]{:S(2)}, u32[]{:S(2)}) collective-permute-start(bf16[208,384]{1,0:T(8,128)(2,1)S(1)} %collective-permute-done.9.refs_10_.refs_21_), channel_id=1, source_target_pairs={{1,0},{0,1},{3,2},{2,3},{5,4},{4,5},{7,6},{6,7},{9,8},{8,9},{11,10... | collective-permute-start | bytes 479240 | tf_op jit(solution)/shard_map/ppermute | solution.py:39
  87.1 15.0 %collective-permute-start.36 = (bf16[2,192,384]{2,1,0:T(8,128)(2,1)S(1)}, bf16[2,192,384]{2,1,0:T(8,128)(2,1)S(1)}, u32[]{:S(2)}, u32[]{:S(2)}) collective-permute-start(bf16[2,192,384]{2,1,0:T(8,128)(2,1)S(1)} %pad_maximum_fusion.refs_0_), channel_id=1, source_target_pairs={{16,0},{17,1},{18,2},{19,3},{20,4},{21,5},{22,6},{23,7},{24,8},{25... | collective-permute-start | bytes 884744 | tf_op jit(solution)/shard_map/ppermute | solution.py:39
  93.6 8.5 %collective-permute-start.37 = (bf16[1,192,384]{2,1,0:T(8,128)(2,1)S(1)}, bf16[1,192,384]{2,1,0:T(8,128)(2,1)S(1)}, u32[]{:S(2)}, u32[]{:S(2)}) collective-permute-start(bf16[1,192,384]{2,1,0:T(8,128)(2,1)S(1)} %slice.53), channel_id=1, source_target_pairs={{4,0},{5,1},{6,2},{7,3},{0,4},{1,5},{2,6},{3,7},{12,8},{13,9},{14,... | collective-permute-start | bytes 442376 | tf_op jit(solution)/shard_map/ppermute | solution.py:39
  103.3 8.4 %collective-permute-start.42 = (bf16[2,192,384]{2,1,0:T(8,128)(2,1)S(1)}, bf16[2,192,384]{2,1,0:T(8,128)(2,1)S(1)}, u32[]{:S(2)}, u32[]{:S(2)}) collective-permute-start(bf16[2,192,384]{2,1,0:T(8,128)(2,1)S(1)} %collective-permute-done.36.refs_10_), channel_id=1, source_target_pairs={{4,0},{5,1},{6,2},{7,3},{0,4},{1,5},{2,6},{3,7},{12,8},{13,9},{14,... | collective-permute-start | bytes 884744 | tf_op jit(solution)/shard_map/ppermute | solution.py:39
  104.0 8.8 %collective-permute-start.31 = (bf16[2,192,384]{2,1,0:T(8,128)(2,1)S(1)}, bf16[2,192,384]{2,1,0:T(8,128)(2,1)S(1)}, u32[]{:S(2)}, u32[]{:S(2)}) collective-permute-start(bf16[2,192,384]{2,1,0:T(8,128)(2,1)S(1)} %pad_maximum_fusion.refs_0_), channel_id=1, source_target_pairs={{1,0},{0,1},{3,2},{2,3},{5,4},{4,5},{7,6},{6,7},{9,8},{8,9},{11,10... | collective-permute-start | bytes 884744 | tf_op jit(solution)/shard_map/ppermute | solution.py:39
  152.2 8.4 %collective-permute-start.60 = (bf16[192,384]{1,0:T(8,128)(2,1)}, bf16[192,384]{1,0:T(8,128)(2,1)S(1)}, u32[]{:S(2)}, u32[]{:S(2)}) collective-permute-start(bf16[192,384]{1,0:T(8,128)(2,1)} %square.1.refs_0_.refs_8_), channel_id=1, source_target_pairs={{1,0},{0,1},{3,2},{2,3},{5,4},{4,5},{7,6},{6,7},{9,8},{8,9},{11,10... | collective-permute-start | bytes 442376 | tf_op jit(solution)/shard_map/ppermute | solution.py:39
  155.7 12.0 %collective-permute-start.58 = (bf16[192,384]{1,0:T(8,128)(2,1)}, bf16[192,384]{1,0:T(8,128)(2,1)S(1)}, u32[]{:S(2)}, u32[]{:S(2)}) collective-permute-start(bf16[192,384]{1,0:T(8,128)(2,1)} %square.1.refs_0_.refs_8_), channel_id=1, source_target_pairs={{16,0},{17,1},{18,2},{19,3},{20,4},{21,5},{22,6},{23,7},{24,8},{25... | collective-permute-start | bytes 442376 | tf_op jit(solution)/shard_map/ppermute | solution.py:39
  158.5 9.9 %collective-permute-start.57 = (bf16[192,384]{1,0:T(8,128)(2,1)}, bf16[192,384]{1,0:T(8,128)(2,1)S(1)}, u32[]{:S(2)}, u32[]{:S(2)}) collective-permute-start(bf16[192,384]{1,0:T(8,128)(2,1)} %square.1.refs_0_.refs_8_), channel_id=1, source_target_pairs={{8,0},{9,1},{10,2},{11,3},{12,4},{13,5},{14,6},{15,7},{0,8},{1,9},... | collective-permute-start | bytes 442376 | tf_op jit(solution)/shard_map/ppermute | solution.py:39
  159.6 8.8 %collective-permute-start.69 = (bf16[192,384]{1,0:T(8,128)(2,1)S(1)}, bf16[192,384]{1,0:T(8,128)(2,1)S(1)}, u32[]{:S(2)}, u32[]{:S(2)}) collective-permute-start(bf16[192,384]{1,0:T(8,128)(2,1)S(1)} %collective-permute-done.66.refs_11_), channel_id=1, source_target_pairs={{1,0},{0,1},{3,2},{2,3},{5,4},{4,5},{7,6},{6,7},{9,8},{8,9},{11,10... | collective-permute-start | bytes 442376 | tf_op jit(solution)/shard_map/ppermute | solution.py:39
  (117 other events, 728.7 us)

commit v4 on v3

--- a/solution.py
+++ b/solution.py
@@ -43,6 +43,17 @@
 
     def along_z(self, value, k):
         return self.move(value, lambda z, y, x, e: (2 * (z ^ k) + y, 2 * x + e))
+
+    def line(self, value, relabel=False):
+        bits = [1 << b for b in range((self.rows // 2).bit_length() - 1)]
+        held = {0: value}
+        for bit in reversed(bits):
+            for k, part in list(held.items()):
+                if k == 0 and relabel:
+                    held[bit] = self.relabel(value, bit)
+                else:
+                    held[k | bit] = self.along_z(part, bit)
+        return [held[k] for k in range(1, self.rows // 2)]
 
     def in_plane(self, value, s):
         return self.move(value, lambda z, y, x, e: (2 * z + (y ^ (s & 1)), 2 * (x ^ (s >> 1)) + e))
@@ -386,6 +397,7 @@
     moves = Moves(mesh_rows, mesh_cols)
     count = mesh_cols
     slots = range(1, count)
+    half = count // 2
     rows, columns = fock_matrix.shape
     size = rows * mesh_rows
     block = jax.ShapeDtypeStruct((rows, columns), BF16)
@@ -413,16 +425,18 @@
                 starts.append((0, rows))
         return parts, starts
 
-    density_near = [moves.relabel(masked_density, k) for k in range(count)]
+    density_near = [moves.relabel(masked_density)] + moves.line(masked_density, True)
     pair = moves.relabel(pair)
-    soon, *density_near = lax.optimization_barrier((pair, *density_near))
+    soon, density_near[half] = lax.optimization_barrier((pair, density_near[half]))
     parts, starts = plane_parts(soon, TAIL)
-    fock_near = [moves.along_z(pair[: TAIL + rows], k) for k in slots]
+    fock_near = moves.line(pair[: TAIL + rows])
     lone, *density_near = lax.optimization_barrier((pair[TAIL + rows :], *density_near))
-    margin_near = [moves.along_z(lone, k) for k in slots]
+    margin_near = moves.line(lone)
     density_far = [moves.core(value) for value in density_near]
     pair_far = moves.core(pair)
-    parts, fock_near, pair_far = lax.optimization_barrier((parts, fock_near, pair_far))
+    parts, fock_near, pair_far, margin_near[half - 1] = lax.optimization_barrier(
+        (parts, fock_near, pair_far, margin_near[half - 1])
+    )
 
     products = call(
         functools.partial(first_kernel, count, starts),
@@ -435,6 +449,7 @@
             pltpu.SemaphoreType.DMA((1 + 4 * count,)),
         ],
         "first",
+        10**10,
     )(pair, *parts, *density_near, *density_far)
     parts, starts = plane_parts(products, 0)
     parts, margin_near = lax.optimization_barrier((parts, margin_near))
@@ -455,10 +470,12 @@
     )(*parts, pair, pair_far, *fock_near, *fock_far, *margin_near, *margin_far)
     tails = [pair, *fock_near, pair_far, *fock_far]
 
-    first = jnp.stack([generator, moves.along_z(generator, 1)])
-    held, groups = (0, 1), [((0, 1), first)]
-    for k in range(2, count, 2):
-        groups.append(((k, k ^ 1), moves.along_z(first, k)))
+    lines = [generator] + moves.line(generator)
+    lines[1 : half + 1] = lax.optimization_barrier(lines[1 : half + 1])
+    groups = []
+    for first in (0, half):
+        held = tuple(range(first, first + half))
+        groups.append((held, jnp.stack([lines[k] for k in held])))
     layout, pieces = [], []
 
     def keep(held, s, value):
@@ -508,7 +525,7 @@
         "square",
     )(*near, *far, panel, pair, pair_far)
 
-    line_near = [square] + [moves.along_z(square, k) for k in slots]
+    line_near = [square] + moves.line(square)
     line_far = [moves.core(value) for value in line_near]
     plane_near = [square] + [moves.in_plane(square, s) for s in slots]
     plane_far = [line_far[0]] + [moves.core(value) for value in plane_near[1:]]

time: 182 us -> 177 us (0.973)
  waiting for transfers between devices: 73.7 us -> 46.7 us
  starting transfers between devices: 70.1 us -> 92.7 us
    ppermute x71 -> x72, waiting for transfers between devices: 73.7 us -> 46.7 us  [move(): return lax.ppermute(value, AXES, permutation(self.rows, self.cols, source))]
    ppermute x71 -> x72, starting transfers between devices: 70.1 us -> 92.7 us  [move(): return lax.ppermute(value, AXES, permutation(self.rows, self.cols, source))]
  transfers between devices with their start and end apart: 71 -> 72, of which waited for: 33 -> 27; matrix products, arithmetic and copies ran while one was open for 0% -> 0% of each run, Pallas kernels for 0% -> 0%
where the time goes in v4:
time: 177 us
  starting transfers between devices  92.7 us (52%)
  waiting for transfers between devices  46.7 us (26%)
  Pallas kernels  28.6 us (16%)
  local copies, waits for them, and re-layouts  6.83 us (4%)
    ppermute x72, starting transfers between devices, move(): return lax.ppermute(value, AXES, permutation(self.rows, self.cols, source))  92.7 us
    ppermute x72, waiting for transfers between devices, move(): return lax.ppermute(value, AXES, permutation(self.rows, self.cols, source))  46.7 us
    pallas_call x1, Pallas kernels, on_device(): call(functools.partial(series_kernel, layout, count), [jax.ShapeDtypeStru...  11 us
    unnamed x142, local copies, waits for them, and re-layouts  6.63 us
    pallas_call x1, Pallas kernels, on_device(): call(functools.partial(generator_kernel, count, starts), block, [ANY] * (...  3.73 us
    pallas_call x1, Pallas kernels, on_device(): call(functools.partial(square_kernel, count), block, [ANY] * (2 * count)...  3.63 us
  transfers between devices with their start and end apart: 72, of which 27 were waited for; matrix products, arithmetic and copies ran while one was open for 0% of the time, Pallas kernels for 0%

profile of v4, /device:TPU:1, one launch (start us, length us, event | category | flops | bytes accessed | tf_op | source)
XLA Modules:
  0.0 176.6 jit_solution(16197260493317625096)
XLA Ops:
  1.3 3.5 %mask.1 = (bf16[192,384]{1,0:T(8,128)(2,1)}, bf16[400,384]{1,0:T(8,128)(2,1)}) custom-call(bf16[192,384]{1,0:T(8,128)(2,1)} %fock.1, bf16[192,384]{1,0:T(8,128)(2,1)} %density.1, bf16[192,384]{1,0:T(8,128)(2,1)} %margin.1, s32[3,6,12]{2,1,0:T(8,128)} %fills.1, s32[3,6,12]{2,1,0:T(8,128)} %firsts.1, s32[7,6,12]{2,1,0:T(8,128)} %copy.8.seconds), custom_call_target="tpu_custom_call" | custom-call | flops 1000 | bytes 1000 | tf_op jit(solution)/shard_map/mask/pallas_call | solution.py:405
  4.8 4.5 %collective-permute-start = (bf16[400,384]{1,0:T(8,128)(2,1)}, bf16[400,384]{1,0:T(8,128)(2,1)S(1)}, u32[]{:S(2)}, u32[]{:S(2)}) collective-permute-start(bf16[400,384]{1,0:T(8,128)(2,1)} %get-tuple-element.45), channel_id=1, source_target_pairs={{0,0},{4,1},{2,2},{6,3},{1,4},{5,5},{3,6},{7,7},{8,8},{12,9},{10,1... | collective-permute-start | bytes 921608 | tf_op jit(solution)/shard_map/ppermute | solution.py:39
  11.5 2.7 %collective-permute-start.11 = (bf16[192,384]{1,0:T(8,128)(2,1)}, bf16[192,384]{1,0:T(8,128)(2,1)S(1)}, u32[]{:S(2)}, u32[]{:S(2)}) collective-permute-start(bf16[192,384]{1,0:T(8,128)(2,1)} %get-tuple-element.46), channel_id=1, source_target_pairs={{8,0},{12,1},{10,2},{14,3},{9,4},{13,5},{11,6},{15,7},{0,8},{4,9},... | collective-permute-start | bytes 442376 | tf_op jit(solution)/shard_map/ppermute | solution.py:39
  23.1 3.1 %collective-permute-start.9 = (bf16[400,384]{1,0:T(8,128)(2,1)S(1)}, bf16[400,384]{1,0:T(8,128)(2,1)S(1)}, u32[]{:S(2)}, u32[]{:S(2)}) collective-permute-start(bf16[400,384]{1,0:T(8,128)(2,1)S(1)} %collective-permute-done.refs_0_.refs_1_.refs_2_.refs_8_.refs_20_.refs_9_.refs_16_), channel_id=1, source_target_pairs={{1,0},{0,1},{3,2},{2,3},{5,4},{4,5},{7,6},{6,7},{9,8},{8,9},{11,10... | collective-permute-start | bytes 921608 | tf_op jit(solution)/shard_map/ppermute | solution.py:39
  29.2 3.0 %collective-permute-start.13 = (bf16[192,384]{1,0:T(8,128)(2,1)S(1)}, bf16[192,384]{1,0:T(8,128)(2,1)S(1)}, u32[]{:S(2)}, u32[]{:S(2)}) collective-permute-start(bf16[192,384]{1,0:T(8,128)(2,1)S(1)} %slice.48), channel_id=1, source_target_pairs={{16,0},{17,1},{18,2},{19,3},{20,4},{21,5},{22,6},{23,7},{24,8},{25... | collective-permute-start | bytes 442376 | tf_op jit(solution)/shard_map/ppermute | solution.py:39
  34.3 2.7 %collective-permute-done.13.refs_17_ = bf16[192,384]{1,0:T(8,128)(2,1)S(1)} collective-permute-done((bf16[192,384]{1,0:T(8,128)(2,1)S(1)}, bf16[192,384]{1,0:T(8,128)(2,1)S(1)}, u32[]{:S(2)}, u32[]{:S(2)}) %collective-permute-start.13) | collective-permute-done | bytes 147488 | tf_op jit(solution)/shard_map/ppermute | solution.py:39
  37.1 2.9 %collective-permute-start.14 = (bf16[192,384]{1,0:T(8,128)(2,1)S(1)}, bf16[192,384]{1,0:T(8,128)(2,1)S(1)}, u32[]{:S(2)}, u32[]{:S(2)}) collective-permute-start(bf16[192,384]{1,0:T(8,128)(2,1)S(1)} %collective-permute-done.10.refs_9_), channel_id=1, source_target_pairs={{1,0},{0,1},{3,2},{2,3},{5,4},{4,5},{7,6},{6,7},{9,8},{8,9},{11,10... | collective-permute-start | bytes 442376 | tf_op jit(solution)/shard_map/ppermute | solution.py:39
  41.3 3.9 %collective-permute-done.5.refs_8_ = bf16[192,384]{1,0:T(8,128)(2,1)S(1)} collective-permute-done((bf16[192,384]{1,0:T(8,128)(2,1)S(1)}, bf16[192,384]{1,0:T(8,128)(2,1)S(1)}, u32[]{:S(2)}, u32[]{:S(2)}) %collective-permute-start.5) | collective-permute-done | bytes 147488 | tf_op jit(solution)/shard_map/ppermute | solution.py:39
  46.7 3.3 %first.1.refs_0_.refs_1_ = bf16[384,384]{1,0:T(8,128)(2,1)} custom-call(bf16[400,384]{1,0:T(8,128)(2,1)} %copy-done, bf16[400,384]{1,0:T(8,128)(2,1)} %copy-done, bf16[400,384]{1,0:T(8,128)(2,1)} %copy-done, bf16[384,384]{1,0:T(8,128)(2,1)} %copy-done.59, bf16[384,384]{1,0:T(8,128)(2,1)} %copy-done.59, bf16[384,384]{1,0:T(8,128)(2,1)} %copy-done.58, ...), custom_call_target="tpu_custom_call" | custom-call | flops 10000000000 | bytes 1000 | tf_op jit(solution)/shard_map/first/pallas_call | solution.py:441
  60.3 2.8 %collective-permute-start.25 = (bf16[208,384]{1,0:T(8,128)(2,1)S(1)}, bf16[208,384]{1,0:T(8,128)(2,1)S(1)}, u32[]{:S(2)}, u32[]{:S(2)}) collective-permute-start(bf16[208,384]{1,0:T(8,128)(2,1)S(1)} %collective-permute-done.7.refs_11_.refs_22_), channel_id=1, source_target_pairs={{1,0},{0,1},{3,2},{2,3},{5,4},{4,5},{7,6},{6,7},{9,8},{8,9},{11,10... | collective-permute-start | bytes 479240 | tf_op jit(solution)/shard_map/ppermute | solution.py:39
  64.3 3.3 %collective-permute-start.27 = (bf16[192,384]{1,0:T(8,128)(2,1)S(1)}, bf16[192,384]{1,0:T(8,128)(2,1)S(1)}, u32[]{:S(2)}, u32[]{:S(2)}) collective-permute-start(bf16[192,384]{1,0:T(8,128)(2,1)S(1)} %collective-permute-done.22.refs_16_), channel_id=1, source_target_pairs={{1,0},{0,1},{3,2},{2,3},{5,4},{4,5},{7,6},{6,7},{9,8},{8,9},{11,10... | collective-permute-start | bytes 442376 | tf_op jit(solution)/shard_map/ppermute | solution.py:39
  70.3 3.7 %generator.1 = bf16[192,384]{1,0:T(8,128)(2,1)} custom-call(bf16[384,384]{1,0:T(8,128)(2,1)} %first.1.refs_0_.refs_1_, bf16[384,384]{1,0:T(8,128)(2,1)} %first.1.refs_0_.refs_1_, bf16[384,384]{1,0:T(8,128)(2,1)} %copy-done.3, bf16[384,384]{1,0:T(8,128)(2,1)} %copy-done.3, bf16[384,384]{1,0:T(8,128)(2,1)} %copy-done.2, bf16[384,384]{1,0:T(8,128)(2,1)} %copy-done.2, ...), custom_call_target="tpu_custom_call" | custom-call | flops 1000 | bytes 1000 | tf_op jit(solution)/shard_map/generator/pallas_call | solution.py:459
  74.0 3.2 %collective-permute-start.31 = (bf16[192,384]{1,0:T(8,128)(2,1)}, bf16[192,384]{1,0:T(8,128)(2,1)S(1)}, u32[]{:S(2)}, u32[]{:S(2)}) collective-permute-start(bf16[192,384]{1,0:T(8,128)(2,1)} %generator.1), channel_id=1, source_target_pairs={{16,0},{17,1},{18,2},{19,3},{20,4},{21,5},{22,6},{23,7},{24,8},{25... | collective-permute-start | bytes 442376 | tf_op jit(solution)/shard_map/ppermute | solution.py:39
  77.2 7.5 %collective-permute-done.31 = bf16[192,384]{1,0:T(8,128)(2,1)S(1)} collective-permute-done((bf16[192,384]{1,0:T(8,128)(2,1)}, bf16[192,384]{1,0:T(8,128)(2,1)S(1)}, u32[]{:S(2)}, u32[]{:S(2)}) %collective-permute-start.31) | collective-permute-done | bytes 147488 | tf_op jit(solution)/shard_map/ppermute | solution.py:39
  88.1 4.9 %collective-permute-done.35.refs_4_ = bf16[2,192,384]{2,1,0:T(8,128)(2,1)S(1)} collective-permute-done((bf16[2,192,384]{2,1,0:T(8,128)(2,1)S(1)}, bf16[2,192,384]{2,1,0:T(8,128)(2,1)S(1)}, u32[]{:S(2)}, u32[]{:S(2)}) %collective-permute-start.35) | collective-permute-done | bytes 294944 | tf_op jit(solution)/shard_map/ppermute | solution.py:39
  94.5 2.6 %collective-permute-done.38.refs_6_ = bf16[1,192,384]{2,1,0:T(8,128)(2,1)S(1)} collective-permute-done((bf16[1,192,384]{2,1,0:T(8,128)(2,1)S(1)}, bf16[1,192,384]{2,1,0:T(8,128)(2,1)S(1)}, u32[]{:S(2)}, u32[]{:S(2)}) %collective-permute-start.38) | collective-permute-done | bytes 147488 | tf_op jit(solution)/shard_map/ppermute | solution.py:39
  99.0 4.5 %collective-permute-start.32 = (bf16[2,192,384]{2,1,0:T(8,128)(2,1)S(1)}, bf16[2,192,384]{2,1,0:T(8,128)(2,1)S(1)}, u32[]{:S(2)}, u32[]{:S(2)}) collective-permute-start(bf16[2,192,384]{2,1,0:T(8,128)(2,1)S(1)} %pad_maximum_fusion.refs_0_), channel_id=1, source_target_pairs={{1,0},{0,1},{3,2},{2,3},{5,4},{4,5},{7,6},{6,7},{9,8},{8,9},{11,10... | collective-permute-start | bytes 884744 | tf_op jit(solution)/shard_map/ppermute | solution.py:39
  104.0 3.7 %collective-permute-start.40 = (bf16[1,192,384]{2,1,0:T(8,128)(2,1)S(1)}, bf16[1,192,384]{2,1,0:T(8,128)(2,1)S(1)}, u32[]{:S(2)}, u32[]{:S(2)}) collective-permute-start(bf16[1,192,384]{2,1,0:T(8,128)(2,1)S(1)} %collective-permute-done.38.refs_6_), channel_id=1, source_target_pairs={{1,0},{0,1},{3,2},{2,3},{5,4},{4,5},{7,6},{6,7},{9,8},{8,9},{11,10... | collective-permute-start | bytes 442376 | tf_op jit(solution)/shard_map/ppermute | solution.py:39
  111.8 2.5 %collective-permute-done.47.refs_16_ = bf16[1,192,384]{2,1,0:T(8,128)(2,1)S(1)} collective-permute-done((bf16[1,192,384]{2,1,0:T(8,128)(2,1)S(1)}, bf16[1,192,384]{2,1,0:T(8,128)(2,1)S(1)}, u32[]{:S(2)}, u32[]{:S(2)}) %collective-permute-start.47) | collective-permute-done | bytes 147488 | tf_op jit(solution)/shard_map/ppermute | solution.py:39
  119.0 11.0 %series.1 = (bf16[192,1536]{1,0:T(8,128)(2,1)}, bf16[192,384]{1,0:T(8,128)(2,1)}) custom-call(bf16[2,192,384]{2,1,0:T(8,128)(2,1)} %copy-done.4, bf16[2,192,384]{2,1,0:T(8,128)(2,1)} %copy-done.17, bf16[2,192,384]{2,1,0:T(8,128)(2,1)} %copy-done.7, bf16[2,192,384]{2,1,0:T(8,128)(2,1)} %copy-done.19, bf16[2,192,384]{2,1,0:T(8,128)(2,1)} %copy-done.6, ...), custom_call_target="tpu_custom_call" | custom-call | flops 1000 | bytes 1000 | tf_op jit(solution)/shard_map/series/pallas_call | solution.py:500
  142.2 3.6 %square.1.refs_0_.refs_8_ = bf16[192,384]{1,0:T(8,128)(2,1)} custom-call(bf16[192,384]{1,0:T(8,128)(2,1)} %get-tuple-element.83.refs_0_, bf16[192,384]{1,0:T(8,128)(2,1)} %copy-done.47, bf16[192,384]{1,0:T(8,128)(2,1)} %copy-done.45, bf16[192,384]{1,0:T(8,128)(2,1)} %copy-done.43, bf16[192,384]{1,0:T(8,128)(2,1)} %copy-done.49, bf16[192,384]{1,0:T(8,128)(2,1)} %copy-done.57, ...), custom_call_target="tpu_custom_call" | custom-call | flops 1000 | bytes 1000 | tf_op jit(solution)/shard_map/square/pallas_call | solution.py:516
  165.8 3.5 %evolve.1 = bf16[192,384]{1,0:T(8,128)(2,1)} custom-call(bf16[192,384]{1,0:T(8,128)(2,1)} %square.1.refs_0_.refs_8_, bf16[192,384]{1,0:T(8,128)(2,1)} %copy-done.35, bf16[192,384]{1,0:T(8,128)(2,1)} %copy-done.30, bf16[192,384]{1,0:T(8,128)(2,1)} %copy-done.39, bf16[192,384]{1,0:T(8,128)(2,1)} %copy-done.16, bf16[192,384]{1,0:T(8,128)(2,1)} %copy-done.50, ...), custom_call_target="tpu_custom_call" | custom-call | flops 1000 | bytes 1000 | tf_op jit(solution)/shard_map/evolve/pallas_call | solution.py:532
  169.3 2.9 %collective-permute-start.71 = (bf16[192,384]{1,0:T(8,128)(2,1)}, bf16[192,384]{1,0:T(8,128)(2,1)S(1)}, u32[]{:S(2)}, u32[]{:S(2)}) collective-permute-start(bf16[192,384]{1,0:T(8,128)(2,1)} %evolve.1), channel_id=1, source_target_pairs={{0,0},{4,1},{2,2},{6,3},{1,4},{5,5},{3,6},{7,7},{8,8},{12,9},{10,1... | collective-permute-start | bytes 442376 | tf_op jit(solution)/shard_map/ppermute | solution.py:39
  172.2 3.7 %collective-permute-done.71 = bf16[192,384]{1,0:T(8,128)(2,1)S(1)} collective-permute-done((bf16[192,384]{1,0:T(8,128)(2,1)}, bf16[192,384]{1,0:T(8,128)(2,1)S(1)}, u32[]{:S(2)}, u32[]{:S(2)}) %collective-permute-start.71) | collective-permute-done | bytes 147488 | tf_op jit(solution)/shard_map/ppermute | solution.py:39
  (281 shorter events, 82.6 us)
Async XLA Ops:
  4.8 13.4 %collective-permute-start = (bf16[400,384]{1,0:T(8,128)(2,1)}, bf16[400,384]{1,0:T(8,128)(2,1)S(1)}, u32[]{:S(2)}, u32[]{:S(2)}) collective-permute-start(bf16[400,384]{1,0:T(8,128)(2,1)} %get-tuple-element.45), channel_id=1, source_target_pairs={{0,0},{4,1},{2,2},{6,3},{1,4},{5,5},{3,6},{7,7},{8,8},{12,9},{10,1... | collective-permute-start | bytes 921608 | tf_op jit(solution)/shard_map/ppermute | solution.py:39
  9.4 8.8 %collective-permute-start.1 = (bf16[192,384]{1,0:T(8,128)(2,1)}, bf16[192,384]{1,0:T(8,128)(2,1)S(1)}, u32[]{:S(2)}, u32[]{:S(2)}) collective-permute-start(bf16[192,384]{1,0:T(8,128)(2,1)} %get-tuple-element.46), channel_id=1, source_target_pairs={{16,0},{20,1},{18,2},{22,3},{17,4},{21,5},{19,6},{23,7},{24,8},{28... | collective-permute-start | bytes 442376 | tf_op jit(solution)/shard_map/ppermute | solution.py:39
  11.5 9.9 %collective-permute-start.11 = (bf16[192,384]{1,0:T(8,128)(2,1)}, bf16[192,384]{1,0:T(8,128)(2,1)S(1)}, u32[]{:S(2)}, u32[]{:S(2)}) collective-permute-start(bf16[192,384]{1,0:T(8,128)(2,1)} %get-tuple-element.46), channel_id=1, source_target_pairs={{8,0},{12,1},{10,2},{14,3},{9,4},{13,5},{11,6},{15,7},{0,8},{4,9},... | collective-permute-start | bytes 442376 | tf_op jit(solution)/shard_map/ppermute | solution.py:39
  14.2 8.8 %collective-permute-start.10 = (bf16[192,384]{1,0:T(8,128)(2,1)}, bf16[192,384]{1,0:T(8,128)(2,1)S(1)}, u32[]{:S(2)}, u32[]{:S(2)}) collective-permute-start(bf16[192,384]{1,0:T(8,128)(2,1)} %get-tuple-element.46), channel_id=1, source_target_pairs={{0,0},{4,1},{2,2},{6,3},{1,4},{5,5},{3,6},{7,7},{8,8},{12,9},{10,1... | collective-permute-start | bytes 442376 | tf_op jit(solution)/shard_map/ppermute | solution.py:39
  18.3 10.9 %collective-permute-start.3 = (bf16[384,384]{1,0:T(8,128)(2,1)S(1)}, bf16[384,384]{1,0:T(8,128)(2,1)S(1)}, u32[]{:S(2)}, u32[]{:S(2)}) collective-permute-start(bf16[384,384]{1,0:T(8,128)(2,1)S(1)} %slice.34), channel_id=1, source_target_pairs={{2,0},{3,1},{0,2},{1,3},{6,4},{7,5},{4,6},{5,7},{10,8},{11,9},{8,1... | collective-permute-start | bytes 884744 | tf_op jit(solution)/shard_map/ppermute | solution.py:39
  19.6 12.7 %collective-permute-start.2 = (bf16[384,384]{1,0:T(8,128)(2,1)S(1)}, bf16[384,384]{1,0:T(8,128)(2,1)S(1)}, u32[]{:S(2)}, u32[]{:S(2)}) collective-permute-start(bf16[384,384]{1,0:T(8,128)(2,1)S(1)} %slice.34), channel_id=1, source_target_pairs={{4,0},{5,1},{6,2},{7,3},{0,4},{1,5},{2,6},{3,7},{12,8},{13,9},{14,... | collective-permute-start | bytes 884744 | tf_op jit(solution)/shard_map/ppermute | solution.py:39
  19.6 9.5 %collective-permute-start.7 = (bf16[208,384]{1,0:T(8,128)(2,1)S(1)}, bf16[208,384]{1,0:T(8,128)(2,1)S(1)}, u32[]{:S(2)}, u32[]{:S(2)}) collective-permute-start(bf16[208,384]{1,0:T(8,128)(2,1)S(1)} %slice.47), channel_id=1, source_target_pairs={{16,0},{17,1},{18,2},{19,3},{20,4},{21,5},{22,6},{23,7},{24,8},{25... | collective-permute-start | bytes 479240 | tf_op jit(solution)/shard_map/ppermute | solution.py:39
  23.1 17.1 %collective-permute-start.9 = (bf16[400,384]{1,0:T(8,128)(2,1)S(1)}, bf16[400,384]{1,0:T(8,128)(2,1)S(1)}, u32[]{:S(2)}, u32[]{:S(2)}) collective-permute-start(bf16[400,384]{1,0:T(8,128)(2,1)S(1)} %collective-permute-done.refs_0_.refs_1_.refs_2_.refs_8_.refs_20_.refs_9_.refs_16_), channel_id=1, source_target_pairs={{1,0},{0,1},{3,2},{2,3},{5,4},{4,5},{7,6},{6,7},{9,8},{8,9},{11,10... | collective-permute-start | bytes 921608 | tf_op jit(solution)/shard_map/ppermute | solution.py:39
  26.9 13.1 %collective-permute-start.6 = (bf16[208,384]{1,0:T(8,128)(2,1)S(1)}, bf16[208,384]{1,0:T(8,128)(2,1)S(1)}, u32[]{:S(2)}, u32[]{:S(2)}) collective-permute-start(bf16[208,384]{1,0:T(8,128)(2,1)S(1)} %slice.47), channel_id=1, source_target_pairs={{8,0},{9,1},{10,2},{11,3},{12,4},{13,5},{14,6},{15,7},{0,8},{1,9},... | collective-permute-start | bytes 479240 | tf_op jit(solution)/shard_map/ppermute | solution.py:39
  29.1 11.4 %collective-permute-start.8 = (bf16[208,384]{1,0:T(8,128)(2,1)S(1)}, bf16[208,384]{1,0:T(8,128)(2,1)S(1)}, u32[]{:S(2)}, u32[]{:S(2)}) collective-permute-start(bf16[208,384]{1,0:T(8,128)(2,1)S(1)} %collective-permute-done.7.refs_11_.refs_22_), channel_id=1, source_target_pairs={{8,0},{9,1},{10,2},{11,3},{12,4},{13,5},{14,6},{15,7},{0,8},{1,9},... | collective-permute-start | bytes 479240 | tf_op jit(solution)/shard_map/ppermute | solution.py:39
  32.2 9.0 %collective-permute-start.4 = (bf16[192,384]{1,0:T(8,128)(2,1)S(1)}, bf16[192,384]{1,0:T(8,128)(2,1)S(1)}, u32[]{:S(2)}, u32[]{:S(2)}) collective-permute-start(bf16[192,384]{1,0:T(8,128)(2,1)S(1)} %slice.45), channel_id=1, source_target_pairs={{4,0},{5,1},{6,2},{7,3},{0,4},{1,5},{2,6},{3,7},{12,8},{13,9},{14,... | collective-permute-start | bytes 442376 | tf_op jit(solution)/shard_map/ppermute | solution.py:39
  37.1 8.1 %collective-permute-start.14 = (bf16[192,384]{1,0:T(8,128)(2,1)S(1)}, bf16[192,384]{1,0:T(8,128)(2,1)S(1)}, u32[]{:S(2)}, u32[]{:S(2)}) collective-permute-start(bf16[192,384]{1,0:T(8,128)(2,1)S(1)} %collective-permute-done.10.refs_9_), channel_id=1, source_target_pairs={{1,0},{0,1},{3,2},{2,3},{5,4},{4,5},{7,6},{6,7},{9,8},{8,9},{11,10... | collective-permute-start | bytes 442376 | tf_op jit(solution)/shard_map/ppermute | solution.py:39
  50.4 9.5 %collective-permute-start.18 = (bf16[384,384]{1,0:T(8,128)(2,1)}, bf16[384,384]{1,0:T(8,128)(2,1)S(1)}, u32[]{:S(2)}, u32[]{:S(2)}) collective-permute-start(bf16[384,384]{1,0:T(8,128)(2,1)} %first.1.refs_0_.refs_1_), channel_id=1, source_target_pairs={{4,0},{5,1},{6,2},{7,3},{0,4},{1,5},{2,6},{3,7},{12,8},{13,9},{14,... | collective-permute-start | bytes 884744 | tf_op jit(solution)/shard_map/ppermute | solution.py:39
  54.4 8.6 %collective-permute-start.23 = (bf16[192,384]{1,0:T(8,128)(2,1)S(1)}, bf16[192,384]{1,0:T(8,128)(2,1)S(1)}, u32[]{:S(2)}, u32[]{:S(2)}) collective-permute-start(bf16[192,384]{1,0:T(8,128)(2,1)S(1)} %collective-permute-done.13.refs_17_), channel_id=1, source_target_pairs={{8,0},{9,1},{10,2},{11,3},{12,4},{13,5},{14,6},{15,7},{0,8},{1,9},... | collective-permute-start | bytes 442376 | tf_op jit(solution)/shard_map/ppermute | solution.py:39
  54.5 13.2 %collective-permute-start.24 = (bf16[208,384]{1,0:T(8,128)(2,1)S(1)}, bf16[208,384]{1,0:T(8,128)(2,1)S(1)}, u32[]{:S(2)}, u32[]{:S(2)}) collective-permute-start(bf16[208,384]{1,0:T(8,128)(2,1)S(1)} %collective-permute-done.6.refs_10_.refs_21_), channel_id=1, source_target_pairs={{1,0},{0,1},{3,2},{2,3},{5,4},{4,5},{7,6},{6,7},{9,8},{8,9},{11,10... | collective-permute-start | bytes 479240 | tf_op jit(solution)/shard_map/ppermute | solution.py:39
  74.0 10.7 %collective-permute-start.31 = (bf16[192,384]{1,0:T(8,128)(2,1)}, bf16[192,384]{1,0:T(8,128)(2,1)S(1)}, u32[]{:S(2)}, u32[]{:S(2)}) collective-permute-start(bf16[192,384]{1,0:T(8,128)(2,1)} %generator.1), channel_id=1, source_target_pairs={{16,0},{17,1},{18,2},{19,3},{20,4},{21,5},{22,6},{23,7},{24,8},{25... | collective-permute-start | bytes 442376 | tf_op jit(solution)/shard_map/ppermute | solution.py:39
  98.7 8.9 %collective-permute-start.43 = (bf16[2,192,384]{2,1,0:T(8,128)(2,1)S(1)}, bf16[2,192,384]{2,1,0:T(8,128)(2,1)S(1)}, u32[]{:S(2)}, u32[]{:S(2)}) collective-permute-start(bf16[2,192,384]{2,1,0:T(8,128)(2,1)S(1)} %pad_maximum_fusion.1.refs_10_), channel_id=1, source_target_pairs={{4,0},{5,1},{6,2},{7,3},{0,4},{1,5},{2,6},{3,7},{12,8},{13,9},{14,... | collective-permute-start | bytes 884744 | tf_op jit(solution)/shard_map/ppermute | solution.py:39
  99.0 10.2 %collective-permute-start.32 = (bf16[2,192,384]{2,1,0:T(8,128)(2,1)S(1)}, bf16[2,192,384]{2,1,0:T(8,128)(2,1)S(1)}, u32[]{:S(2)}, u32[]{:S(2)}) collective-permute-start(bf16[2,192,384]{2,1,0:T(8,128)(2,1)S(1)} %pad_maximum_fusion.refs_0_), channel_id=1, source_target_pairs={{1,0},{0,1},{3,2},{2,3},{5,4},{4,5},{7,6},{6,7},{9,8},{8,9},{11,10... | collective-permute-start | bytes 884744 | tf_op jit(solution)/shard_map/ppermute | solution.py:39
  109.2 8.0 %collective-permute-start.42 = (bf16[2,192,384]{2,1,0:T(8,128)(2,1)S(1)}, bf16[2,192,384]{2,1,0:T(8,128)(2,1)S(1)}, u32[]{:S(2)}, u32[]{:S(2)}) collective-permute-start(bf16[2,192,384]{2,1,0:T(8,128)(2,1)S(1)} %pad_maximum_fusion.1.refs_10_), channel_id=1, source_target_pairs={{1,0},{0,1},{3,2},{2,3},{5,4},{4,5},{7,6},{6,7},{9,8},{8,9},{11,10... | collective-permute-start | bytes 884744 | tf_op jit(solution)/shard_map/ppermute | solution.py:39
  130.7 8.1 %collective-permute-start.52 = (bf16[192,384]{1,0:T(8,128)(2,1)}, bf16[192,384]{1,0:T(8,128)(2,1)S(1)}, u32[]{:S(2)}, u32[]{:S(2)}) collective-permute-start(bf16[192,384]{1,0:T(8,128)(2,1)} %get-tuple-element.83.refs_0_), channel_id=1, source_target_pairs={{2,0},{3,1},{0,2},{1,3},{6,4},{7,5},{4,6},{5,7},{10,8},{11,9},{8,1... | collective-permute-start | bytes 442376 | tf_op jit(solution)/shard_map/ppermute | solution.py:39
  131.9 8.2 %collective-permute-start.51 = (bf16[192,384]{1,0:T(8,128)(2,1)}, bf16[192,384]{1,0:T(8,128)(2,1)S(1)}, u32[]{:S(2)}, u32[]{:S(2)}) collective-permute-start(bf16[192,384]{1,0:T(8,128)(2,1)} %get-tuple-element.83.refs_0_), channel_id=1, source_target_pairs={{4,0},{5,1},{6,2},{7,3},{0,4},{1,5},{2,6},{3,7},{12,8},{13,9},{14,... | collective-permute-start | bytes 442376 | tf_op jit(solution)/shard_map/ppermute | solution.py:39
  147.8 9.3 %collective-permute-start.59 = (bf16[192,384]{1,0:T(8,128)(2,1)}, bf16[192,384]{1,0:T(8,128)(2,1)S(1)}, u32[]{:S(2)}, u32[]{:S(2)}) collective-permute-start(bf16[192,384]{1,0:T(8,128)(2,1)} %square.1.refs_0_.refs_8_), channel_id=1, source_target_pairs={{16,0},{17,1},{18,2},{19,3},{20,4},{21,5},{22,6},{23,7},{24,8},{25... | collective-permute-start | bytes 442376 | tf_op jit(solution)/shard_map/ppermute | solution.py:39
  148.4 8.7 %collective-permute-start.65 = (bf16[192,384]{1,0:T(8,128)(2,1)}, bf16[192,384]{1,0:T(8,128)(2,1)S(1)}, u32[]{:S(2)}, u32[]{:S(2)}) collective-permute-start(bf16[192,384]{1,0:T(8,128)(2,1)} %square.1.refs_0_.refs_8_), channel_id=1, source_target_pairs={{4,0},{5,1},{6,2},{7,3},{0,4},{1,5},{2,6},{3,7},{12,8},{13,9},{14,... | collective-permute-start | bytes 442376 | tf_op jit(solution)/shard_map/ppermute | solution.py:39
  149.1 9.4 %collective-permute-start.61 = (bf16[192,384]{1,0:T(8,128)(2,1)}, bf16[192,384]{1,0:T(8,128)(2,1)S(1)}, u32[]{:S(2)}, u32[]{:S(2)}) collective-permute-start(bf16[192,384]{1,0:T(8,128)(2,1)} %square.1.refs_0_.refs_8_), channel_id=1, source_target_pairs={{1,0},{0,1},{3,2},{2,3},{5,4},{4,5},{7,6},{6,7},{9,8},{8,9},{11,10... | collective-permute-start | bytes 442376 | tf_op jit(solution)/shard_map/ppermute | solution.py:39
  (118 other events, 777.2 us)

commit v5 on v4

--- a/solution.py
+++ b/solution.py
@@ -15,7 +15,7 @@
 F32 = jnp.float32
 BF16 = jnp.bfloat16
 TAIL = 16
-VMEM_LIMIT = 60 * 1024 * 1024
+MEGABYTE = 1024 * 1024
 
 
 def coordinates(r, c):
@@ -90,7 +90,7 @@
     return dot(wide, repeat_columns(tail.shape[1], columns, number * blocks))
 
 
-def call(kernel, outs, ins, scratch, name, flops=1000):
+def call(kernel, outs, ins, scratch, name, flops=1000, room=16):
     return pl.pallas_call(
         kernel,
         out_shape=outs,
@@ -98,7 +98,7 @@
         out_specs=jax.tree.map(lambda _: pl.BlockSpec(memory_space=pltpu.VMEM), outs),
         scratch_shapes=scratch,
         name=name,
-        compiler_params=pltpu.CompilerParams(vmem_limit_bytes=VMEM_LIMIT),
+        compiler_params=pltpu.CompilerParams(vmem_limit_bytes=room * MEGABYTE),
         cost_estimate=pl.CostEstimate(flops=flops, bytes_accessed=1000, transcendentals=0),
     )
 
@@ -108,19 +108,23 @@
 INSMEM = pl.BlockSpec(memory_space=pltpu.SMEM)
 
 
-def mask_kernel(fock, density, margin, fills, firsts, seconds, masked_density, pair):
+def masked(ref, fill):
+    rows, columns = ref.shape
+    tall = repeat_rows(rows, fill.shape[0])
+    wide = repeat_columns(fill.shape[1], columns)
+    mask = dot(dot(tall, fill.astype(BF16)).astype(BF16), wide)
+    return (ref[...].astype(F32) * mask).astype(BF16)
+
+
+def density_kernel(density, fills, out):
+    out[...] = masked(density, fills[1])
+
+
+def pair_kernel(fock, margin, fills, firsts, seconds, pair):
     rows, columns = fock.shape
     row_blocks, column_blocks = rows // BLK, columns // BLK
-    tall = repeat_rows(rows, row_blocks)
-    wide = repeat_columns(column_blocks, columns)
-
-    def masked(ref, number):
-        mask = dot(dot(tall, fills[number].astype(BF16)).astype(BF16), wide)
-        return (ref[...].astype(F32) * mask).astype(BF16)
-
-    masked_density[...] = masked(density, 1)
-    pair[TAIL : TAIL + rows, :] = masked(fock, 0)
-    pair[TAIL + rows :, :] = masked(margin, 2)
+    pair[TAIL : TAIL + rows, :] = masked(fock, fills[0])
+    pair[TAIL + rows :, :] = masked(margin, fills[2])
     top = (iota((TAIL, row_blocks), 0) == iota((TAIL, row_blocks), 1)).astype(BF16)
     tail = jnp.zeros((TAIL, columns), F32)
     for number in range(firsts.shape[0] + seconds.shape[0]):
@@ -193,33 +197,25 @@
 
 
 def generator_kernel(count, starts, *refs):
-    parts, own, other = refs[: 2 * count], refs[2 * count], refs[2 * count + 1]
-    rest = refs[2 * count + 2 :]
-    fock_near, fock_far, margin_near, margin_far = [
-        rest[n * (count - 1) : (n + 1) * (count - 1)] for n in range(4)
-    ]
-    out, left, right, tail, sems = rest[4 * (count - 1) :]
+    parts = refs[: 2 * count]
+    near, far = refs[2 * count : 3 * count], refs[3 * count : 4 * count]
+    out, left, right, tail, sems = refs[4 * count :]
     z, q, e = place()
     rows, columns = out.shape
-    copies = [pltpu.make_async_copy(own.at[:TAIL], tail, sems.at[0])]
+    copies = [pltpu.make_async_copy(near[0].at[:TAIL], tail, sems.at[0])]
 
     def bring(source, target):
         copies.append(pltpu.make_async_copy(source, target, sems.at[len(copies)]))
 
     for half in range(2):
+        part = pl.ds(TAIL + half * rows, rows)
         for s in range(count):
             bring(
                 parts[2 * s + half].at[pl.ds(starts[s][half], rows)],
                 left.at[half, :, chunk(q ^ s, columns)],
             )
-        part = pl.ds(TAIL + half * rows, rows)
-        bring(own.at[part], right.at[1 - half, chunk(2 * z + e, rows)])
-        bring(other.at[part], right.at[1 - half, chunk(2 * z + 1 - e, rows)])
-    for k in range(1, count):
-        for refs_of, core in ((fock_near, e), (fock_far, 1 - e)):
-            bring(refs_of[k - 1].at[TAIL:], right.at[1, chunk(2 * (z ^ k) + core, rows)])
-        for refs_of, core in ((margin_near, e), (margin_far, 1 - e)):
-            bring(refs_of[k - 1], right.at[0, chunk(2 * (z ^ k) + core, rows)])
+            bring(near[s].at[part], right.at[1 - half, chunk(2 * (z ^ s) + e, rows)])
+            bring(far[s].at[part], right.at[1 - half, chunk(2 * (z ^ s) + 1 - e, rows)])
     start_all(copies)
     mask = block_mask(tail_of(copies[0], tail), 2, rows, columns)
     wait_all(copies[1:])
@@ -239,13 +235,14 @@
     size = panel.shape[1]
     row_blocks, column_blocks, blocks = rows // BLK, columns // BLK, size // BLK
     copies, early = [], []
-    for ref, (slots, plane, lane) in zip(pieces, layout):
+    for ref, (runs, plane, lane) in zip(pieces, layout):
         core = e if lane == 0 else 1 - e
-        for index, k in enumerate(slots):
+        for row, k, inner, length in runs:
+            target = pl.multiple_of((2 * (z ^ k) + core) * rows + inner, BLK)
             copies.append(
                 pltpu.make_async_copy(
-                    ref.at[index],
-                    whole.at[chunk(2 * (z ^ k) + core, rows), chunk(q ^ plane, columns)],
+                    ref.at[pl.ds(row, length)],
+                    whole.at[pl.ds(target, length), chunk(q ^ plane, columns)],
                     sems.at[len(copies)],
                 )
             )
@@ -330,12 +327,13 @@
 
 def square_kernel(count, *refs):
     near, far = refs[:count], refs[count : 2 * count]
-    panel, pair, other, out, right, tails, sems = refs[2 * count :]
+    panel, pair, other, out, left, right, tails, sems = refs[2 * count :]
     z, q, e = place()
     rows, columns = out.shape
     copies = [
         pltpu.make_async_copy(pair.at[:TAIL], tails.at[e], sems.at[0]),
         pltpu.make_async_copy(other.at[:TAIL], tails.at[1 - e], sems.at[1]),
+        pltpu.make_async_copy(panel, left, sems.at[2]),
     ]
     for s in range(count):
         for ref, core in ((near[s], e), (far[s], 1 - e)):
@@ -348,7 +346,7 @@
     wait_all(copies[:2])
     mask = turned_mask(tails, FIRST + TERMS - 1, e, rows, columns)
     wait_all(copies[2:])
-    out[...] = (dot(panel[...], right[...]) * mask).astype(BF16)
+    out[...] = (dot(left[...], right[...]) * mask).astype(BF16)
 
 
 def evolve_kernel(count, *refs):
@@ -402,13 +400,18 @@
     size = rows * mesh_rows
     block = jax.ShapeDtypeStruct((rows, columns), BF16)
 
-    masked_density, pair = call(
-        mask_kernel,
-        [block, jax.ShapeDtypeStruct((TAIL + 2 * rows, columns), BF16)],
-        [INVMEM] * 6,
+    masked_density = call(density_kernel, block, [INVMEM] * 2, [], "density")(
+        density, fill_patterns
+    )
+    masked_density, fock_matrix = lax.optimization_barrier((masked_density, fock_matrix))
+    pair = call(
+        pair_kernel,
+        jax.ShapeDtypeStruct((TAIL + 2 * rows, columns), BF16),
+        [INVMEM] * 5,
         [],
-        "mask",
-    )(fock_matrix, density, margin, fill_patterns, first_filters, second_filters)
+        "pair",
+        10**10,
+    )(fock_matrix, margin, fill_patterns, first_filters, second_filters)
 
     def plane_parts(value, first):
         parts = [value, value]
@@ -429,13 +432,11 @@
     pair = moves.relabel(pair)
     soon, density_near[half] = lax.optimization_barrier((pair, density_near[half]))
     parts, starts = plane_parts(soon, TAIL)
-    fock_near = moves.line(pair[: TAIL + rows])
-    lone, *density_near = lax.optimization_barrier((pair[TAIL + rows :], *density_near))
-    margin_near = moves.line(lone)
+    pair_near = moves.line(soon)
     density_far = [moves.core(value) for value in density_near]
-    pair_far = moves.core(pair)
-    parts, fock_near, pair_far, margin_near[half - 1] = lax.optimization_barrier(
-        (parts, fock_near, pair_far, margin_near[half - 1])
+    pair_far = [moves.core(pair)]
+    parts, pair_far[0], pair_near[:half] = lax.optimization_barrier(
+        (parts, pair_far[0], pair_near[:half])
     )
 
     products = call(
@@ -452,14 +453,14 @@
         10**10,
     )(pair, *parts, *density_near, *density_far)
     parts, starts = plane_parts(products, 0)
-    parts, margin_near = lax.optimization_barrier((parts, margin_near))
-    fock_far = [moves.core(value) for value in fock_near]
-    margin_far = [moves.core(value) for value in margin_near]
+    parts, pair_near = lax.optimization_barrier((parts, pair_near))
+    pair_near = [pair] + pair_near
+    pair_far += [moves.core(value) for value in pair_near[1:]]
 
     generator = call(
         functools.partial(generator_kernel, count, starts),
         block,
-        [ANY] * (2 * count + 2 + 4 * (count - 1)),
+        [ANY] * (4 * count),
         [
             pltpu.VMEM((2, rows, size), BF16),
             pltpu.VMEM((2, size, columns), BF16),
@@ -467,35 +468,42 @@
             pltpu.SemaphoreType.DMA((1 + 6 * count,)),
         ],
         "generator",
-    )(*parts, pair, pair_far, *fock_near, *fock_far, *margin_near, *margin_far)
-    tails = [pair, *fock_near, pair_far, *fock_far]
+    )(*parts, *pair_near, *pair_far)
 
     lines = [generator] + moves.line(generator)
-    lines[1 : half + 1] = lax.optimization_barrier(lines[1 : half + 1])
-    groups = []
-    for first in (0, half):
-        held = tuple(range(first, first + half))
-        groups.append((held, jnp.stack([lines[k] for k in held])))
+    groups = [((0,), generator), (tuple(slots), jnp.concatenate(lines[1:], axis=0))]
     layout, pieces = [], []
 
-    def keep(held, s, value):
-        layout.extend([(held, s, 0), (held, s, 1)])
+    def keep(held, s, value, first=0):
+        runs, row = [], 0
+        while row < value.shape[0]:
+            index, inner = divmod(first + row, rows)
+            length = min(rows - inner, value.shape[0] - row)
+            runs.append((row, held[index], inner, length))
+            row += length
+        layout.extend([(runs, s, 0), (runs, s, 1)])
         pieces.extend([value, moves.core(value)])
 
-    corners = []
+    def corner(held, planes):
+        cut = planes[1].shape[0] // 2
+        keep(held, 3, moves.in_plane(planes[2][:cut], 1))
+        keep(held, 3, moves.in_plane(planes[1][cut:], 2), cut)
+
+    planes = {}
     for held, group in groups:
-        group, *corners = lax.optimization_barrier((group, *corners))
-        for s, value in enumerate(corners):
-            keep(before[s : s + 1], 3, value)
+        group, planes = lax.optimization_barrier((group, planes))
+        for s, value in planes.items():
+            keep(before, s, value)
+        if planes and count == 4:
+            corner(before, planes)
         before = held
         keep(held, 0, group)
         planes = {s: moves.in_plane(group, s) for s in slots if not (count == 4 and s == 3)}
-        for s, value in planes.items():
-            keep(held, s, value)
-        if count == 4:
-            corners = [moves.in_plane(planes[2][:1], 1), moves.in_plane(planes[1][1:], 2)]
-    for s, value in enumerate(corners):
-        keep(before[s : s + 1], 3, value)
+    for s, value in planes.items():
+        keep(before, s, value)
+    if count == 4:
+        corner(before, planes)
+    runs = sum(len(part[0]) for part in layout)
 
     panel, mine = call(
         functools.partial(series_kernel, layout, count),
@@ -506,24 +514,26 @@
             pltpu.VMEM((size, size), BF16),
             pltpu.VMEM((mesh_rows, TAIL, columns), BF16),
             pltpu.VMEM((128, size), F32),
-            pltpu.SemaphoreType.DMA((mesh_rows * mesh_cols + 2 * count,)),
+            pltpu.SemaphoreType.DMA((runs + 2 * count,)),
         ],
         "series",
-    )(*pieces, *tails, owner_order)
+        room=16 + 4 * size * size // MEGABYTE,
+    )(*pieces, *pair_near, *pair_far, owner_order)
 
     near = [mine] + [moves.in_plane(mine, s) for s in slots]
     far = [moves.core(value) for value in near]
     square = call(
         functools.partial(square_kernel, count),
         block,
-        [ANY] * (2 * count) + [INVMEM, ANY, ANY],
+        [ANY] * (2 * count + 3),
         [
+            pltpu.VMEM((rows, size), BF16),
             pltpu.VMEM((size, columns), BF16),
             pltpu.VMEM((2, TAIL, columns), BF16),
-            pltpu.SemaphoreType.DMA((2 + 2 * count,)),
+            pltpu.SemaphoreType.DMA((3 + 2 * count,)),
         ],
         "square",
-    )(*near, *far, panel, pair, pair_far)
+    )(*near, *far, panel, pair, pair_far[0])
 
     line_near = [square] + moves.line(square)
     line_far = [moves.core(value) for value in line_near]
@@ -540,7 +550,7 @@
             pltpu.SemaphoreType.DMA((2 + 4 * count,)),
         ],
         "evolve",
-    )(*line_near, *line_far, *plane_near, *plane_far, pair, pair_far)
+    )(*line_near, *line_far, *plane_near, *plane_far, pair, pair_far[0])
     return moves.relabel(evolved)
 
 

time: 177 us -> 165 us (0.932)
  starting transfers between devices: 92.7 us -> 73.5 us
  waiting for transfers between devices: 46.7 us -> 62.2 us
  local copies, waits for them, and re-layouts: 6.83 us -> 3.17 us
  Pallas kernels: 28.6 us -> 25.3 us
    ppermute x72 -> x66, starting transfers between devices: 92.7 us -> 73.5 us  [move(): return lax.ppermute(value, AXES, permutation(self.rows, self.cols, source))]
    ppermute x72 -> x66, waiting for transfers between devices: 46.7 us -> 62.2 us  [move(): return lax.ppermute(value, AXES, permutation(self.rows, self.cols, source))]
    unnamed x142 -> x14, local copies, waits for them, and re-layouts: 6.63 us -> 3.01 us
    pallas_call x2 -> x3, Pallas kernels: 7.13 us -> 4.8 us  [the longest x1 2.99 us: on_device(): call(functools.partial(square_kernel, count), block, [ANY] * (2 * count +...]
    pallas_call x1, Pallas kernels: 11 us -> 8.97 us  [on_device(): call(functools.partial(series_kernel, layout, count), [jax.ShapeDtypeStru...]
  transfers between devices with their start and end apart: 72 -> 66, of which waited for: 27 -> 28; matrix products, arithmetic and copies ran while one was open for 0% -> 0% of each run, Pallas kernels for 0% -> 0%
where the time goes in v5:
time: 165 us; the launch traced here: 164 us
  starting transfers between devices  73.5 us (45%)
  waiting for transfers between devices  62.2 us (38%)
  Pallas kernels  25.3 us (15%)
  local copies, waits for them, and re-layouts  3.17 us (2%)
    ppermute x66, starting transfers between devices, move(): return lax.ppermute(value, AXES, permutation(self.rows, self.cols, source))  73.5 us
    ppermute x66, waiting for transfers between devices, move(): return lax.ppermute(value, AXES, permutation(self.rows, self.cols, source))  62.2 us
    pallas_call x1, Pallas kernels, on_device(): call(functools.partial(series_kernel, layout, count), [jax.ShapeDtypeStru...  8.97 us
    pallas_call x1, Pallas kernels, on_device(): call(functools.partial(generator_kernel, count, starts), block, [ANY] * (...  4.9 us
    pallas_call x1, Pallas kernels, on_device(): call(functools.partial(evolve_kernel, count), block, [ANY] * (4 * count +...  3.32 us
  transfers between devices with their start and end apart: 66, of which 28 were waited for; matrix products, arithmetic and copies ran while one was open for 0% of the time, Pallas kernels for 0%

profile of v5, /device:TPU:1, one launch (start us, length us, event | category | flops | bytes accessed | tf_op | source)
XLA Modules:
  0.0 164.5 jit_solution(13447087674114242751)
XLA Ops:
  4.2 4.6 %collective-permute-start = (bf16[400,384]{1,0:T(8,128)(2,1)S(1)}, bf16[400,384]{1,0:T(8,128)(2,1)S(1)}, u32[]{:S(2)}, u32[]{:S(2)}) collective-permute-start(bf16[400,384]{1,0:T(8,128)(2,1)S(1)} %pair.1), channel_id=1, source_target_pairs={{0,0},{4,1},{2,2},{6,3},{1,4},{5,5},{3,6},{7,7},{8,8},{12,9},{10,1... | collective-permute-start | bytes 921608 | tf_op jit(solution)/shard_map/ppermute | solution.py:39
  10.8 2.7 %collective-permute-start.10 = (bf16[192,384]{1,0:T(8,128)(2,1)S(1)}, bf16[192,384]{1,0:T(8,128)(2,1)S(1)}, u32[]{:S(2)}, u32[]{:S(2)}) collective-permute-start(bf16[192,384]{1,0:T(8,128)(2,1)S(1)} %density.2), channel_id=1, source_target_pairs={{8,0},{12,1},{10,2},{14,3},{9,4},{13,5},{11,6},{15,7},{0,8},{4,9},... | collective-permute-start | bytes 442376 | tf_op jit(solution)/shard_map/ppermute | solution.py:39
  21.6 2.8 %collective-permute-start.6 = (bf16[400,384]{1,0:T(8,128)(2,1)S(1)}, bf16[400,384]{1,0:T(8,128)(2,1)S(1)}, u32[]{:S(2)}, u32[]{:S(2)}) collective-permute-start(bf16[400,384]{1,0:T(8,128)(2,1)S(1)} %collective-permute-done.refs_0_.refs_1_.refs_2_.refs_8_.refs_20_.refs_9_.refs_16_), channel_id=1, source_target_pairs={{1,0},{0,1},{3,2},{2,3},{5,4},{4,5},{7,6},{6,7},{9,8},{8,9},{11,10... | collective-permute-start | bytes 921608 | tf_op jit(solution)/shard_map/ppermute | solution.py:39
  26.7 9.2 %collective-permute-done.11.refs_12_ = bf16[192,384]{1,0:T(8,128)(2,1)S(1)} collective-permute-done((bf16[192,384]{1,0:T(8,128)(2,1)S(1)}, bf16[192,384]{1,0:T(8,128)(2,1)S(1)}, u32[]{:S(2)}, u32[]{:S(2)}) %collective-permute-start.11) | collective-permute-done | bytes 147488 | tf_op jit(solution)/shard_map/ppermute | solution.py:39
  35.9 2.8 %collective-permute-start.13 = (bf16[192,384]{1,0:T(8,128)(2,1)S(1)}, bf16[192,384]{1,0:T(8,128)(2,1)S(1)}, u32[]{:S(2)}, u32[]{:S(2)}) collective-permute-start(bf16[192,384]{1,0:T(8,128)(2,1)S(1)} %collective-permute-done.10.refs_10_), channel_id=1, source_target_pairs={{1,0},{0,1},{3,2},{2,3},{5,4},{4,5},{7,6},{6,7},{9,8},{8,9},{11,10... | collective-permute-start | bytes 442376 | tf_op jit(solution)/shard_map/ppermute | solution.py:39
  39.8 4.4 %collective-permute-done.5.refs_8_ = bf16[192,384]{1,0:T(8,128)(2,1)S(1)} collective-permute-done((bf16[192,384]{1,0:T(8,128)(2,1)S(1)}, bf16[192,384]{1,0:T(8,128)(2,1)S(1)}, u32[]{:S(2)}, u32[]{:S(2)}) %collective-permute-start.5) | collective-permute-done | bytes 147488 | tf_op jit(solution)/shard_map/ppermute | solution.py:39
  44.2 3.3 %first.1.refs_0_.refs_1_ = bf16[384,384]{1,0:T(8,128)(2,1)S(1)} custom-call(bf16[400,384]{1,0:T(8,128)(2,1)S(1)} %collective-permute-done.refs_0_.refs_1_.refs_2_.refs_8_.refs_20_.refs_9_.refs_16_, bf16[400,384]{1,0:T(8,128)(2,1)S(1)} %collective-permute-done.refs_0_.refs_1_.refs_2_.refs_8_.refs_20_.refs_9_.refs_16_, ...), custom_call_target="tpu_custom_call" | custom-call | flops 10000000000 | bytes 1000 | tf_op jit(solution)/shard_map/first/pallas_call | solution.py:442
  49.9 5.4 %collective-permute-done.17.refs_4_.refs_5_ = bf16[384,384]{1,0:T(8,128)(2,1)S(1)} collective-permute-done((bf16[384,384]{1,0:T(8,128)(2,1)S(1)}, bf16[384,384]{1,0:T(8,128)(2,1)S(1)}, u32[]{:S(2)}, u32[]{:S(2)}) %collective-permute-start.17) | collective-permute-done | bytes 294944 | tf_op jit(solution)/shard_map/ppermute | solution.py:39
  57.2 2.2 %collective-permute-done.18.refs_6_ = bf16[192,384]{1,0:T(8,128)(2,1)S(1)} collective-permute-done((bf16[192,384]{1,0:T(8,128)(2,1)S(1)}, bf16[192,384]{1,0:T(8,128)(2,1)S(1)}, u32[]{:S(2)}, u32[]{:S(2)}) %collective-permute-start.18) | collective-permute-done | bytes 147488 | tf_op jit(solution)/shard_map/ppermute | solution.py:39
  61.3 2.8 %collective-permute-start.21 = (bf16[400,384]{1,0:T(8,128)(2,1)S(1)}, bf16[400,384]{1,0:T(8,128)(2,1)S(1)}, u32[]{:S(2)}, u32[]{:S(2)}) collective-permute-start(bf16[400,384]{1,0:T(8,128)(2,1)S(1)} %collective-permute-done.7.refs_9_.refs_21_), channel_id=1, source_target_pairs={{1,0},{0,1},{3,2},{2,3},{5,4},{4,5},{7,6},{6,7},{9,8},{8,9},{11,10... | collective-permute-start | bytes 921608 | tf_op jit(solution)/shard_map/ppermute | solution.py:39
  66.2 4.9 %generator.1.refs_0_ = bf16[192,384]{1,0:T(8,128)(2,1)S(1)} custom-call(bf16[384,384]{1,0:T(8,128)(2,1)S(1)} %first.1.refs_0_.refs_1_, bf16[384,384]{1,0:T(8,128)(2,1)S(1)} %first.1.refs_0_.refs_1_, bf16[384,384]{1,0:T(8,128)(2,1)S(1)} %collective-permute-done.16.refs_2_.refs_3_, bf16[384,384]{1,0:T(8,128)(2,1)S(1)} %collective-permute-done.16.refs_2_.refs_3_, ...), custom_call_target="tpu_custom_call" | custom-call | flops 1000 | bytes 1000 | tf_op jit(solution)/shard_map/generator/pallas_call | solution.py:460
  73.5 7.1 %collective-permute-done.26 = bf16[192,384]{1,0:T(8,128)(2,1)S(1)} collective-permute-done((bf16[192,384]{1,0:T(8,128)(2,1)S(1)}, bf16[192,384]{1,0:T(8,128)(2,1)S(1)}, u32[]{:S(2)}, u32[]{:S(2)}) %collective-permute-start.26) | collective-permute-done | bytes 147488 | tf_op jit(solution)/shard_map/ppermute | solution.py:39
  81.7 3.4 %collective-permute-done.27 = bf16[192,384]{1,0:T(8,128)(2,1)S(1)} collective-permute-done((bf16[192,384]{1,0:T(8,128)(2,1)S(1)}, bf16[192,384]{1,0:T(8,128)(2,1)S(1)}, u32[]{:S(2)}, u32[]{:S(2)}) %collective-permute-start.27) | collective-permute-done | bytes 147488 | tf_op jit(solution)/shard_map/ppermute | solution.py:39
  88.4 3.0 %collective-permute-start.24 = (bf16[192,384]{1,0:T(8,128)(2,1)S(1)}, bf16[192,384]{1,0:T(8,128)(2,1)S(1)}, u32[]{:S(2)}, u32[]{:S(2)}) collective-permute-start(bf16[192,384]{1,0:T(8,128)(2,1)S(1)} %generator.1.refs_0_), channel_id=1, source_target_pairs={{1,0},{0,1},{3,2},{2,3},{5,4},{4,5},{7,6},{6,7},{9,8},{8,9},{11,10... | collective-permute-start | bytes 442376 | tf_op jit(solution)/shard_map/ppermute | solution.py:39
  91.4 6.0 %collective-permute-done.32.refs_6_ = bf16[96,384]{1,0:T(8,128)(2,1)S(1)} collective-permute-done((bf16[96,384]{1,0:T(8,128)(2,1)S(1)}, bf16[96,384]{1,0:T(8,128)(2,1)S(1)}, u32[]{:S(2)}, u32[]{:S(2)}) %collective-permute-start.32) | collective-permute-done | bytes 73760 | tf_op jit(solution)/shard_map/ppermute | solution.py:39
  97.4 3.2 %collective-permute-start.30 = (bf16[192,384]{1,0:T(8,128)(2,1)S(1)}, bf16[192,384]{1,0:T(8,128)(2,1)S(1)}, u32[]{:S(2)}, u32[]{:S(2)}) collective-permute-start(bf16[192,384]{1,0:T(8,128)(2,1)S(1)} %collective-permute-done.28.refs_2_), channel_id=1, source_target_pairs={{1,0},{0,1},{3,2},{2,3},{5,4},{4,5},{7,6},{6,7},{9,8},{8,9},{11,10... | collective-permute-start | bytes 442376 | tf_op jit(solution)/shard_map/ppermute | solution.py:39
  104.1 4.7 %collective-permute-done.41.refs_16_ = bf16[288,384]{1,0:T(8,128)(2,1)S(1)} collective-permute-done((bf16[288,384]{1,0:T(8,128)(2,1)S(1)}, bf16[288,384]{1,0:T(8,128)(2,1)S(1)}, u32[]{:S(2)}, u32[]{:S(2)}) %collective-permute-start.41) | collective-permute-done | bytes 221216 | tf_op jit(solution)/shard_map/ppermute | solution.py:39
  111.4 9.0 %series.1 = (bf16[192,1536]{1,0:T(8,128)(2,1)S(1)}, bf16[192,384]{1,0:T(8,128)(2,1)S(1)}) custom-call(bf16[192,384]{1,0:T(8,128)(2,1)S(1)} %generator.1.refs_0_, bf16[192,384]{1,0:T(8,128)(2,1)S(1)} %collective-permute-done.24.refs_1_, bf16[192,384]{1,0:T(8,128)(2,1)S(1)} %collective-permute-done.28.refs_2_, ...), custom_call_target="tpu_custom_call" | custom-call | flops 1000 | bytes 1000 | tf_op jit(solution)/shard_map/series/pallas_call | solution.py:508
  124.2 2.2 %collective-permute-done.47.refs_3_ = bf16[192,384]{1,0:T(8,128)(2,1)S(1)} collective-permute-done((bf16[192,384]{1,0:T(8,128)(2,1)S(1)}, bf16[192,384]{1,0:T(8,128)(2,1)S(1)}, u32[]{:S(2)}, u32[]{:S(2)}) %collective-permute-start.47) | collective-permute-done | bytes 147488 | tf_op jit(solution)/shard_map/ppermute | solution.py:39
  132.0 3.0 %square.1.refs_0_.refs_8_ = bf16[192,384]{1,0:T(8,128)(2,1)S(1)} custom-call(bf16[192,384]{1,0:T(8,128)(2,1)S(1)} %get-tuple-element.65.refs_0_, bf16[192,384]{1,0:T(8,128)(2,1)S(1)} %collective-permute-done.45.refs_1_, bf16[192,384]{1,0:T(8,128)(2,1)S(1)} %collective-permute-done.46.refs_2_, bf16[192,384]{1,0:T(8,128)(2,1)S(1)} %collective-permute-done.47.refs_3_, ...), custom_call_target="tpu_custom_call" | custom-call | flops 1000 | bytes 1000 | tf_op jit(solution)/shard_map/square/pallas_call | solution.py:525
  137.1 2.5 %collective-permute-start.53 = (bf16[192,384]{1,0:T(8,128)(2,1)S(1)}, bf16[192,384]{1,0:T(8,128)(2,1)S(1)}, u32[]{:S(2)}, u32[]{:S(2)}) collective-permute-start(bf16[192,384]{1,0:T(8,128)(2,1)S(1)} %square.1.refs_0_.refs_8_), channel_id=1, source_target_pairs={{16,0},{17,1},{18,2},{19,3},{20,4},{21,5},{22,6},{23,7},{24,8},{25... | collective-permute-start | bytes 442376 | tf_op jit(solution)/shard_map/ppermute | solution.py:39
  154.0 3.3 %evolve.1 = bf16[192,384]{1,0:T(8,128)(2,1)S(1)} custom-call(bf16[192,384]{1,0:T(8,128)(2,1)S(1)} %square.1.refs_0_.refs_8_, bf16[192,384]{1,0:T(8,128)(2,1)S(1)} %collective-permute-done.52.refs_1_, bf16[192,384]{1,0:T(8,128)(2,1)S(1)} %collective-permute-done.53.refs_2_, bf16[192,384]{1,0:T(8,128)(2,1)S(1)} %collective-permute-done.54.refs_3_, ...), custom_call_target="tpu_custom_call" | custom-call | flops 1000 | bytes 1000 | tf_op jit(solution)/shard_map/evolve/pallas_call | solution.py:542
  157.3 3.1 %collective-permute-start.65 = (bf16[192,384]{1,0:T(8,128)(2,1)S(1)}, bf16[192,384]{1,0:T(8,128)(2,1)S(1)}, u32[]{:S(2)}, u32[]{:S(2)}) collective-permute-start(bf16[192,384]{1,0:T(8,128)(2,1)S(1)} %evolve.1), channel_id=1, source_target_pairs={{0,0},{4,1},{2,2},{6,3},{1,4},{5,5},{3,6},{7,7},{8,8},{12,9},{10,1... | collective-permute-start | bytes 442376 | tf_op jit(solution)/shard_map/ppermute | solution.py:39
  160.5 3.3 %collective-permute-done.65 = bf16[192,384]{1,0:T(8,128)(2,1)S(1)} collective-permute-done((bf16[192,384]{1,0:T(8,128)(2,1)S(1)}, bf16[192,384]{1,0:T(8,128)(2,1)S(1)}, u32[]{:S(2)}, u32[]{:S(2)}) %collective-permute-start.65) | collective-permute-done | bytes 147488 | tf_op jit(solution)/shard_map/ppermute | solution.py:39
  (139 shorter events, 65.3 us)
Async XLA Ops:
  4.2 12.7 %collective-permute-start = (bf16[400,384]{1,0:T(8,128)(2,1)S(1)}, bf16[400,384]{1,0:T(8,128)(2,1)S(1)}, u32[]{:S(2)}, u32[]{:S(2)}) collective-permute-start(bf16[400,384]{1,0:T(8,128)(2,1)S(1)} %pair.1), channel_id=1, source_target_pairs={{0,0},{4,1},{2,2},{6,3},{1,4},{5,5},{3,6},{7,7},{8,8},{12,9},{10,1... | collective-permute-start | bytes 921608 | tf_op jit(solution)/shard_map/ppermute | solution.py:39
  8.7 8.1 %collective-permute-start.1 = (bf16[192,384]{1,0:T(8,128)(2,1)S(1)}, bf16[192,384]{1,0:T(8,128)(2,1)S(1)}, u32[]{:S(2)}, u32[]{:S(2)}) collective-permute-start(bf16[192,384]{1,0:T(8,128)(2,1)S(1)} %density.2), channel_id=1, source_target_pairs={{16,0},{20,1},{18,2},{22,3},{17,4},{21,5},{19,6},{23,7},{24,8},{28... | collective-permute-start | bytes 442376 | tf_op jit(solution)/shard_map/ppermute | solution.py:39
  10.8 9.0 %collective-permute-start.10 = (bf16[192,384]{1,0:T(8,128)(2,1)S(1)}, bf16[192,384]{1,0:T(8,128)(2,1)S(1)}, u32[]{:S(2)}, u32[]{:S(2)}) collective-permute-start(bf16[192,384]{1,0:T(8,128)(2,1)S(1)} %density.2), channel_id=1, source_target_pairs={{8,0},{12,1},{10,2},{14,3},{9,4},{13,5},{11,6},{15,7},{0,8},{4,9},... | collective-permute-start | bytes 442376 | tf_op jit(solution)/shard_map/ppermute | solution.py:39
  13.6 8.0 %collective-permute-start.9 = (bf16[192,384]{1,0:T(8,128)(2,1)S(1)}, bf16[192,384]{1,0:T(8,128)(2,1)S(1)}, u32[]{:S(2)}, u32[]{:S(2)}) collective-permute-start(bf16[192,384]{1,0:T(8,128)(2,1)S(1)} %density.2), channel_id=1, source_target_pairs={{0,0},{4,1},{2,2},{6,3},{1,4},{5,5},{3,6},{7,7},{8,8},{12,9},{10,1... | collective-permute-start | bytes 442376 | tf_op jit(solution)/shard_map/ppermute | solution.py:39
  18.2 8.5 %collective-permute-start.2 = (bf16[384,384]{1,0:T(8,128)(2,1)S(1)}, bf16[384,384]{1,0:T(8,128)(2,1)S(1)}, u32[]{:S(2)}, u32[]{:S(2)}) collective-permute-start(bf16[384,384]{1,0:T(8,128)(2,1)S(1)} %slice.28), channel_id=1, source_target_pairs={{4,0},{5,1},{6,2},{7,3},{0,4},{1,5},{2,6},{3,7},{12,8},{13,9},{14,... | collective-permute-start | bytes 884744 | tf_op jit(solution)/shard_map/ppermute | solution.py:39
  18.2 20.5 %collective-permute-start.8 = (bf16[400,384]{1,0:T(8,128)(2,1)S(1)}, bf16[400,384]{1,0:T(8,128)(2,1)S(1)}, u32[]{:S(2)}, u32[]{:S(2)}) collective-permute-start(bf16[400,384]{1,0:T(8,128)(2,1)S(1)} %collective-permute-done.refs_0_.refs_1_.refs_2_.refs_8_.refs_20_.refs_9_.refs_16_), channel_id=1, source_target_pairs={{16,0},{17,1},{18,2},{19,3},{20,4},{21,5},{22,6},{23,7},{24,8},{25... | collective-permute-start | bytes 921608 | tf_op jit(solution)/shard_map/ppermute | solution.py:39
  19.9 19.1 %collective-permute-start.7 = (bf16[400,384]{1,0:T(8,128)(2,1)S(1)}, bf16[400,384]{1,0:T(8,128)(2,1)S(1)}, u32[]{:S(2)}, u32[]{:S(2)}) collective-permute-start(bf16[400,384]{1,0:T(8,128)(2,1)S(1)} %collective-permute-done.refs_0_.refs_1_.refs_2_.refs_8_.refs_20_.refs_9_.refs_16_), channel_id=1, source_target_pairs={{8,0},{9,1},{10,2},{11,3},{12,4},{13,5},{14,6},{15,7},{0,8},{1,9},... | collective-permute-start | bytes 921608 | tf_op jit(solution)/shard_map/ppermute | solution.py:39
  21.6 17.6 %collective-permute-start.6 = (bf16[400,384]{1,0:T(8,128)(2,1)S(1)}, bf16[400,384]{1,0:T(8,128)(2,1)S(1)}, u32[]{:S(2)}, u32[]{:S(2)}) collective-permute-start(bf16[400,384]{1,0:T(8,128)(2,1)S(1)} %collective-permute-done.refs_0_.refs_1_.refs_2_.refs_8_.refs_20_.refs_9_.refs_16_), channel_id=1, source_target_pairs={{1,0},{0,1},{3,2},{2,3},{5,4},{4,5},{7,6},{6,7},{9,8},{8,9},{11,10... | collective-permute-start | bytes 921608 | tf_op jit(solution)/shard_map/ppermute | solution.py:39
  24.5 11.4 %collective-permute-start.11 = (bf16[192,384]{1,0:T(8,128)(2,1)S(1)}, bf16[192,384]{1,0:T(8,128)(2,1)S(1)}, u32[]{:S(2)}, u32[]{:S(2)}) collective-permute-start(bf16[192,384]{1,0:T(8,128)(2,1)S(1)} %collective-permute-done.1.refs_11_), channel_id=1, source_target_pairs={{8,0},{9,1},{10,2},{11,3},{12,4},{13,5},{14,6},{15,7},{0,8},{1,9},... | collective-permute-start | bytes 442376 | tf_op jit(solution)/shard_map/ppermute | solution.py:39
  26.7 12.8 %collective-permute-start.4 = (bf16[192,384]{1,0:T(8,128)(2,1)S(1)}, bf16[192,384]{1,0:T(8,128)(2,1)S(1)}, u32[]{:S(2)}, u32[]{:S(2)}) collective-permute-start(bf16[192,384]{1,0:T(8,128)(2,1)S(1)} %slice.37), channel_id=1, source_target_pairs={{4,0},{5,1},{6,2},{7,3},{0,4},{1,5},{2,6},{3,7},{12,8},{13,9},{14,... | collective-permute-start | bytes 442376 | tf_op jit(solution)/shard_map/ppermute | solution.py:39
  35.9 8.3 %collective-permute-start.13 = (bf16[192,384]{1,0:T(8,128)(2,1)S(1)}, bf16[192,384]{1,0:T(8,128)(2,1)S(1)}, u32[]{:S(2)}, u32[]{:S(2)}) collective-permute-start(bf16[192,384]{1,0:T(8,128)(2,1)S(1)} %collective-permute-done.10.refs_10_), channel_id=1, source_target_pairs={{1,0},{0,1},{3,2},{2,3},{5,4},{4,5},{7,6},{6,7},{9,8},{8,9},{11,10... | collective-permute-start | bytes 442376 | tf_op jit(solution)/shard_map/ppermute | solution.py:39
  47.8 9.1 %collective-permute-start.16 = (bf16[384,384]{1,0:T(8,128)(2,1)S(1)}, bf16[384,384]{1,0:T(8,128)(2,1)S(1)}, u32[]{:S(2)}, u32[]{:S(2)}) collective-permute-start(bf16[384,384]{1,0:T(8,128)(2,1)S(1)} %first.1.refs_0_.refs_1_), channel_id=1, source_target_pairs={{4,0},{5,1},{6,2},{7,3},{0,4},{1,5},{2,6},{3,7},{12,8},{13,9},{14,... | collective-permute-start | bytes 884744 | tf_op jit(solution)/shard_map/ppermute | solution.py:39
  49.3 7.9 %collective-permute-start.20 = (bf16[400,384]{1,0:T(8,128)(2,1)S(1)}, bf16[400,384]{1,0:T(8,128)(2,1)S(1)}, u32[]{:S(2)}, u32[]{:S(2)}) collective-permute-start(bf16[400,384]{1,0:T(8,128)(2,1)S(1)} %collective-permute-done.8.refs_10_.refs_22_), channel_id=1, source_target_pairs={{8,0},{9,1},{10,2},{11,3},{12,4},{13,5},{14,6},{15,7},{0,8},{1,9},... | collective-permute-start | bytes 921608 | tf_op jit(solution)/shard_map/ppermute | solution.py:39
  71.1 9.6 %collective-permute-start.26 = (bf16[192,384]{1,0:T(8,128)(2,1)S(1)}, bf16[192,384]{1,0:T(8,128)(2,1)S(1)}, u32[]{:S(2)}, u32[]{:S(2)}) collective-permute-start(bf16[192,384]{1,0:T(8,128)(2,1)S(1)} %generator.1.refs_0_), channel_id=1, source_target_pairs={{16,0},{17,1},{18,2},{19,3},{20,4},{21,5},{22,6},{23,7},{24,8},{25... | collective-permute-start | bytes 442376 | tf_op jit(solution)/shard_map/ppermute | solution.py:39
  72.1 9.7 %collective-permute-start.25 = (bf16[192,384]{1,0:T(8,128)(2,1)S(1)}, bf16[192,384]{1,0:T(8,128)(2,1)S(1)}, u32[]{:S(2)}, u32[]{:S(2)}) collective-permute-start(bf16[192,384]{1,0:T(8,128)(2,1)S(1)} %generator.1.refs_0_), channel_id=1, source_target_pairs={{8,0},{9,1},{10,2},{11,3},{12,4},{13,5},{14,6},{15,7},{0,8},{1,9},... | collective-permute-start | bytes 442376 | tf_op jit(solution)/shard_map/ppermute | solution.py:39
  85.3 15.3 %collective-permute-start.39 = (bf16[576,384]{1,0:T(8,128)(2,1)S(1)}, bf16[576,384]{1,0:T(8,128)(2,1)S(1)}, u32[]{:S(2)}, u32[]{:S(2)}) collective-permute-start(bf16[576,384]{1,0:T(8,128)(2,1)S(1)} %pad_maximum_fusion.refs_10_), channel_id=1, source_target_pairs={{2,0},{3,1},{0,2},{1,3},{6,4},{7,5},{4,6},{5,7},{10,8},{11,9},{8,1... | collective-permute-start | bytes 1327112 | tf_op jit(solution)/shard_map/ppermute | solution.py:39
  86.4 14.7 %collective-permute-start.37 = (bf16[576,384]{1,0:T(8,128)(2,1)S(1)}, bf16[576,384]{1,0:T(8,128)(2,1)S(1)}, u32[]{:S(2)}, u32[]{:S(2)}) collective-permute-start(bf16[576,384]{1,0:T(8,128)(2,1)S(1)} %pad_maximum_fusion.refs_10_), channel_id=1, source_target_pairs={{4,0},{5,1},{6,2},{7,3},{0,4},{1,5},{2,6},{3,7},{12,8},{13,9},{14,... | collective-permute-start | bytes 1327112 | tf_op jit(solution)/shard_map/ppermute | solution.py:39
  86.4 10.9 %collective-permute-start.32 = (bf16[96,384]{1,0:T(8,128)(2,1)S(1)}, bf16[96,384]{1,0:T(8,128)(2,1)S(1)}, u32[]{:S(2)}, u32[]{:S(2)}) collective-permute-start(bf16[96,384]{1,0:T(8,128)(2,1)S(1)} %slice.33), channel_id=1, source_target_pairs={{4,0},{5,1},{6,2},{7,3},{0,4},{1,5},{2,6},{3,7},{12,8},{13,9},{14,... | collective-permute-start | bytes 221192 | tf_op jit(solution)/shard_map/ppermute | solution.py:39
  88.0 12.6 %collective-permute-start.34 = (bf16[96,384]{1,0:T(8,128)(2,1)S(1)}, bf16[96,384]{1,0:T(8,128)(2,1)S(1)}, u32[]{:S(2)}, u32[]{:S(2)}) collective-permute-start(bf16[96,384]{1,0:T(8,128)(2,1)S(1)} %slice.34), channel_id=1, source_target_pairs={{2,0},{3,1},{0,2},{1,3},{6,4},{7,5},{4,6},{5,7},{10,8},{11,9},{8,1... | collective-permute-start | bytes 221192 | tf_op jit(solution)/shard_map/ppermute | solution.py:39
  88.4 12.8 %collective-permute-start.24 = (bf16[192,384]{1,0:T(8,128)(2,1)S(1)}, bf16[192,384]{1,0:T(8,128)(2,1)S(1)}, u32[]{:S(2)}, u32[]{:S(2)}) collective-permute-start(bf16[192,384]{1,0:T(8,128)(2,1)S(1)} %generator.1.refs_0_), channel_id=1, source_target_pairs={{1,0},{0,1},{3,2},{2,3},{5,4},{4,5},{7,6},{6,7},{9,8},{8,9},{11,10... | collective-permute-start | bytes 442376 | tf_op jit(solution)/shard_map/ppermute | solution.py:39
  101.2 9.0 %collective-permute-start.36 = (bf16[576,384]{1,0:T(8,128)(2,1)S(1)}, bf16[576,384]{1,0:T(8,128)(2,1)S(1)}, u32[]{:S(2)}, u32[]{:S(2)}) collective-permute-start(bf16[576,384]{1,0:T(8,128)(2,1)S(1)} %pad_maximum_fusion.refs_10_), channel_id=1, source_target_pairs={{1,0},{0,1},{3,2},{2,3},{5,4},{4,5},{7,6},{6,7},{9,8},{8,9},{11,10... | collective-permute-start | bytes 1327112 | tf_op jit(solution)/shard_map/ppermute | solution.py:39
  122.7 8.0 %collective-permute-start.45 = (bf16[192,384]{1,0:T(8,128)(2,1)S(1)}, bf16[192,384]{1,0:T(8,128)(2,1)S(1)}, u32[]{:S(2)}, u32[]{:S(2)}) collective-permute-start(bf16[192,384]{1,0:T(8,128)(2,1)S(1)} %get-tuple-element.65.refs_0_), channel_id=1, source_target_pairs={{4,0},{5,1},{6,2},{7,3},{0,4},{1,5},{2,6},{3,7},{12,8},{13,9},{14,... | collective-permute-start | bytes 442376 | tf_op jit(solution)/shard_map/ppermute | solution.py:39
  136.0 7.9 %collective-permute-start.60 = (bf16[192,384]{1,0:T(8,128)(2,1)S(1)}, bf16[192,384]{1,0:T(8,128)(2,1)S(1)}, u32[]{:S(2)}, u32[]{:S(2)}) collective-permute-start(bf16[192,384]{1,0:T(8,128)(2,1)S(1)} %square.1.refs_0_.refs_8_), channel_id=1, source_target_pairs={{2,0},{3,1},{0,2},{1,3},{6,4},{7,5},{4,6},{5,7},{10,8},{11,9},{8,1... | collective-permute-start | bytes 442376 | tf_op jit(solution)/shard_map/ppermute | solution.py:39
  137.1 8.9 %collective-permute-start.53 = (bf16[192,384]{1,0:T(8,128)(2,1)S(1)}, bf16[192,384]{1,0:T(8,128)(2,1)S(1)}, u32[]{:S(2)}, u32[]{:S(2)}) collective-permute-start(bf16[192,384]{1,0:T(8,128)(2,1)S(1)} %square.1.refs_0_.refs_8_), channel_id=1, source_target_pairs={{16,0},{17,1},{18,2},{19,3},{20,4},{21,5},{22,6},{23,7},{24,8},{25... | collective-permute-start | bytes 442376 | tf_op jit(solution)/shard_map/ppermute | solution.py:39
  (48 other events, 222.7 us)

commit v6 on v5

--- a/solution.py
+++ b/solution.py
@@ -162,35 +162,28 @@
         lax.fori_loop(0, times, step, 0)
 
 
-def tail_of(copy, tail):
-    copy.wait()
-    return tail[...]
+def in_order(near, far, e):
+    low = jnp.where(e == 0, near, far)
+    high = jnp.where(e == 0, far, near)
+    return jnp.concatenate([low, high], axis=0)
 
 
 def first_kernel(count, starts, *refs):
     pair, parts = refs[0], refs[1 : 1 + 2 * count]
     near, far = refs[1 + 2 * count : 1 + 3 * count], refs[1 + 3 * count : 1 + 4 * count]
-    out, left, right, tail, sems = refs[1 + 4 * count :]
+    out, left = refs[1 + 4 * count :]
     z, q, e = place()
     rows, columns = near[0].shape
-    copies = [pltpu.make_async_copy(pair.at[:TAIL], tail, sems.at[0])]
-
-    def bring(source, target):
-        copies.append(pltpu.make_async_copy(source, target, sems.at[len(copies)]))
-
     for s in range(count):
         for half in range(2):
-            bring(
-                parts[2 * s + half].at[pl.ds(starts[s][half], rows)],
-                left.at[pl.ds(half * rows, rows), chunk(q ^ s, columns)],
-            )
-        bring(near[s], right.at[chunk(2 * (z ^ s) + e, rows)])
-        bring(far[s], right.at[chunk(2 * (z ^ s) + 1 - e, rows)])
-    start_all(copies)
-    filters = tail_of(copies[0], tail)
-    masks = [block_mask(filters, n, rows, columns) for n in range(2)]
-    wait_all(copies[1:])
-    total = dot(left[...], right[...])
+            first = starts[s][half]
+            left[q ^ s, half * rows : (half + 1) * rows, :] = parts[2 * s + half][
+                first : first + rows, :
+            ]
+    masks = [block_mask(pair[:TAIL, :], n, rows, columns) for n in range(2)]
+    total = jnp.zeros((2 * rows, columns), F32)
+    for s in range(count):
+        total += dot(left[z ^ s], in_order(near[s][...], far[s][...], e))
     for n in range(2):
         part = slice(n * rows, (n + 1) * rows)
         out[part, :] = (total[part] * masks[n]).astype(BF16)
@@ -199,29 +192,24 @@
 def generator_kernel(count, starts, *refs):
     parts = refs[: 2 * count]
     near, far = refs[2 * count : 3 * count], refs[3 * count : 4 * count]
-    out, left, right, tail, sems = refs[4 * count :]
+    out, left = refs[4 * count :]
     z, q, e = place()
     rows, columns = out.shape
-    copies = [pltpu.make_async_copy(near[0].at[:TAIL], tail, sems.at[0])]
-
-    def bring(source, target):
-        copies.append(pltpu.make_async_copy(source, target, sems.at[len(copies)]))
-
     for half in range(2):
-        part = pl.ds(TAIL + half * rows, rows)
         for s in range(count):
-            bring(
-                parts[2 * s + half].at[pl.ds(starts[s][half], rows)],
-                left.at[half, :, chunk(q ^ s, columns)],
+            first = starts[s][half]
+            left[half, q ^ s] = parts[2 * s + half][first : first + rows, :]
+    mask = block_mask(near[0][:TAIL, :], 2, rows, columns)
+    total = jnp.zeros((rows, columns), F32)
+    for half in range(2):
+        first = TAIL + (1 - half) * rows
+        for s in range(count):
+            right = in_order(
+                near[s][first : first + rows, :], far[s][first : first + rows, :], e
             )
-            bring(near[s].at[part], right.at[1 - half, chunk(2 * (z ^ s) + e, rows)])
-            bring(far[s].at[part], right.at[1 - half, chunk(2 * (z ^ s) + 1 - e, rows)])
-    start_all(copies)
-    mask = block_mask(tail_of(copies[0], tail), 2, rows, columns)
-    wait_all(copies[1:])
-    plus = dot(left[0], right[0])
-    minus = dot(left[1], right[1])
-    generator = ((plus - minus) * mask).astype(BF16)
+            product = dot(left[half, z ^ s], right)
+            total = total + product if half == 0 else total - product
+    generator = (total * mask).astype(BF16)
     out[...] = (generator.astype(F32) * 0.25).astype(BF16)
 
 
@@ -234,30 +222,23 @@
     rows, columns = mine.shape
     size = panel.shape[1]
     row_blocks, column_blocks, blocks = rows // BLK, columns // BLK, size // BLK
-    copies, early = [], []
+    small = size <= 1536
+    copies = []
     for ref, (runs, plane, lane) in zip(pieces, layout):
         core = e if lane == 0 else 1 - e
         for row, k, inner, length in runs:
-            target = pl.multiple_of((2 * (z ^ k) + core) * rows + inner, BLK)
+            into = pl.ds(pl.multiple_of((2 * (z ^ k) + core) * rows + inner, BLK), length)
             copies.append(
                 pltpu.make_async_copy(
                     ref.at[pl.ds(row, length)],
-                    whole.at[pl.ds(target, length), chunk(q ^ plane, columns)],
+                    whole.at[into, chunk(q ^ plane, columns)],
                     sems.at[len(copies)],
                 )
             )
+    start_all(copies)
     for index, ref in enumerate(tails):
         core = e if index < count else 1 - e
-        early.append(
-            pltpu.make_async_copy(
-                ref.at[:TAIL],
-                wides.at[2 * (z ^ (index % count)) + core],
-                sems.at[len(copies) + len(early)],
-            )
-        )
-    start_all(early)
-    start_all(copies)
-    wait_all(early)
+        wides[2 * (z ^ (index % count)) + core] = ref[:TAIL, :]
     filters = jnp.zeros((128, size), F32)
     for p in range(2 * count):
         column = iota((TAIL, size), 1) // BLK
@@ -269,7 +250,6 @@
     spread[...] = filters
 
     wait_all(copies)
-    small = size <= 1536
 
     def turn(t):
         tile = jnp.concatenate(
@@ -327,56 +307,31 @@
 
 def square_kernel(count, *refs):
     near, far = refs[:count], refs[count : 2 * count]
-    panel, pair, other, out, left, right, tails, sems = refs[2 * count :]
+    panel, pair, other, out = refs[2 * count :]
     z, q, e = place()
     rows, columns = out.shape
-    copies = [
-        pltpu.make_async_copy(pair.at[:TAIL], tails.at[e], sems.at[0]),
-        pltpu.make_async_copy(other.at[:TAIL], tails.at[1 - e], sems.at[1]),
-        pltpu.make_async_copy(panel, left, sems.at[2]),
-    ]
+    tails = in_order(pair[:TAIL, :], other[:TAIL, :], e)
+    tails = [tails[:TAIL], tails[TAIL:]]
+    mask = turned_mask(tails, FIRST + TERMS - 1, e, rows, columns)
+    total = jnp.zeros((rows, columns), F32)
     for s in range(count):
-        for ref, core in ((near[s], e), (far[s], 1 - e)):
-            copies.append(
-                pltpu.make_async_copy(
-                    ref, right.at[chunk(2 * (q ^ s) + core, rows)], sems.at[len(copies)]
-                )
-            )
-    start_all(copies)
-    wait_all(copies[:2])
-    mask = turned_mask(tails, FIRST + TERMS - 1, e, rows, columns)
-    wait_all(copies[2:])
-    out[...] = (dot(left[...], right[...]) * mask).astype(BF16)
+        total += dot(panel[:, chunk(q ^ s, columns)], in_order(near[s][...], far[s][...], e))
+    out[...] = (total * mask).astype(BF16)
 
 
 def evolve_kernel(count, *refs):
     groups = [refs[n * count : (n + 1) * count] for n in range(4)]
     line_near, line_far, plane_near, plane_far = groups
-    pair, other, out, left, right, tails, sems = refs[4 * count :]
+    pair, out, right = refs[4 * count :]
     z, q, e = place()
     rows, columns = out.shape
-    copies = [
-        pltpu.make_async_copy(pair.at[:TAIL], tails.at[e], sems.at[0]),
-        pltpu.make_async_copy(other.at[:TAIL], tails.at[1 - e], sems.at[1]),
-    ]
     for s in range(count):
-        for ref, core in ((line_near[s], e), (line_far[s], 1 - e)):
-            copies.append(
-                pltpu.make_async_copy(
-                    ref, left.at[chunk(core, rows), chunk(z ^ s, columns)], sems.at[len(copies)]
-                )
-            )
-        for ref, core in ((plane_near[s], e), (plane_far[s], 1 - e)):
-            copies.append(
-                pltpu.make_async_copy(
-                    ref, right.at[chunk(2 * (q ^ s) + core, rows)], sems.at[len(copies)]
-                )
-            )
-    start_all(copies)
-    wait_all(copies[:2])
-    mask = block_mask(tails[pl.ds(e, 1)][0], FIRST + TERMS, rows, columns)
-    wait_all(copies[2:])
-    total = dot(left[...], right[...]).T
+        right[q ^ s] = in_order(plane_near[s][...], plane_far[s][...], e)
+    mask = block_mask(pair[:TAIL, :], FIRST + TERMS, rows, columns)
+    total = jnp.zeros((columns, columns), F32)
+    for s in range(count):
+        total += dot(in_order(line_near[s][...], line_far[s][...], e), right[z ^ s])
+    total = total.T
     chosen = jnp.where(e == 0, total[:rows], total[rows:])
     out[...] = (chosen * mask).astype(BF16)
 
@@ -403,7 +358,9 @@
     masked_density = call(density_kernel, block, [INVMEM] * 2, [], "density")(
         density, fill_patterns
     )
-    masked_density, fock_matrix = lax.optimization_barrier((masked_density, fock_matrix))
+    masked_density, fock_matrix, second_filters = lax.optimization_barrier(
+        (masked_density, fock_matrix, second_filters)
+    )
     pair = call(
         pair_kernel,
         jax.ShapeDtypeStruct((TAIL + 2 * rows, columns), BF16),
@@ -432,7 +389,8 @@
     pair = moves.relabel(pair)
     soon, density_near[half] = lax.optimization_barrier((pair, density_near[half]))
     parts, starts = plane_parts(soon, TAIL)
-    pair_near = moves.line(soon)
+    pair, *density_near = lax.optimization_barrier((pair, *density_near))
+    pair_near = moves.line(pair)
     density_far = [moves.core(value) for value in density_near]
     pair_far = [moves.core(pair)]
     parts, pair_far[0], pair_near[:half] = lax.optimization_barrier(
@@ -442,13 +400,8 @@
     products = call(
         functools.partial(first_kernel, count, starts),
         jax.ShapeDtypeStruct((2 * rows, columns), BF16),
-        [ANY] * (1 + 4 * count),
-        [
-            pltpu.VMEM((2 * rows, size), BF16),
-            pltpu.VMEM((size, columns), BF16),
-            pltpu.VMEM((TAIL, columns), BF16),
-            pltpu.SemaphoreType.DMA((1 + 4 * count,)),
-        ],
+        [INVMEM] * (1 + 4 * count),
+        [pltpu.VMEM((count, 2 * rows, columns), BF16)],
         "first",
         10**10,
     )(pair, *parts, *density_near, *density_far)
@@ -460,18 +413,11 @@
     generator = call(
         functools.partial(generator_kernel, count, starts),
         block,
-        [ANY] * (4 * count),
-        [
-            pltpu.VMEM((2, rows, size), BF16),
-            pltpu.VMEM((2, size, columns), BF16),
-            pltpu.VMEM((TAIL, columns), BF16),
-            pltpu.SemaphoreType.DMA((1 + 6 * count,)),
-        ],
+        [INVMEM] * (4 * count),
+        [pltpu.VMEM((2, count, rows, columns), BF16)],
         "generator",
     )(*parts, *pair_near, *pair_far)
 
-    lines = [generator] + moves.line(generator)
-    groups = [((0,), generator), (tuple(slots), jnp.concatenate(lines[1:], axis=0))]
     layout, pieces = [], []
 
     def keep(held, s, value, first=0):
@@ -484,37 +430,53 @@
         layout.extend([(runs, s, 0), (runs, s, 1)])
         pieces.extend([value, moves.core(value)])
 
-    def corner(held, planes):
+    def planes_of(group):
+        return {s: moves.in_plane(group, s) for s in slots if not (count == 4 and s == 3)}
+
+    def corners_of(planes):
+        if count != 4:
+            return []
         cut = planes[1].shape[0] // 2
-        keep(held, 3, moves.in_plane(planes[2][:cut], 1))
-        keep(held, 3, moves.in_plane(planes[1][cut:], 2), cut)
-
-    planes = {}
-    for held, group in groups:
-        group, planes = lax.optimization_barrier((group, planes))
+        return [moves.in_plane(planes[2][:cut], 1), moves.in_plane(planes[1][cut:], 2)]
+
+    def keep_all(held, group, planes, corners):
+        keep(held, 0, group)
         for s, value in planes.items():
-            keep(before, s, value)
-        if planes and count == 4:
-            corner(before, planes)
-        before = held
-        keep(held, 0, group)
-        planes = {s: moves.in_plane(group, s) for s in slots if not (count == 4 and s == 3)}
-    for s, value in planes.items():
-        keep(before, s, value)
+            keep(held, s, value)
+        first = 0
+        for value in corners:
+            keep(held, 3, value, first)
+            first += value.shape[0]
+
+    planes = planes_of(generator)
     if count == 4:
-        corner(before, planes)
+        near, far = moves.along_z(generator, 1), moves.along_z(generator, 2)
+        far, planes = lax.optimization_barrier((far, planes))
+        corners = corners_of(planes)
+        last = moves.along_z(far, 1)
+        middle = jnp.concatenate([near, far], axis=0)
+        later = planes_of(middle)
+        last, corners, later = lax.optimization_barrier((last, corners, later))
+        keep_all((0,), generator, planes, corners)
+        final = planes_of(last)
+        keep_all((1, 2), middle, later, corners_of(later))
+        keep_all((3,), last, final, corners_of(final))
+    else:
+        keep_all((0,), generator, planes, [])
+        rest = jnp.concatenate(moves.line(generator), axis=0)
+        keep_all(tuple(slots), rest, planes_of(rest), [])
     runs = sum(len(part[0]) for part in layout)
 
     panel, mine = call(
         functools.partial(series_kernel, layout, count),
         [jax.ShapeDtypeStruct((rows, size), BF16), block],
-        [ANY] * (len(layout) + 2 * count) + [INSMEM],
+        [ANY] * len(layout) + [INVMEM] * (2 * count) + [INSMEM],
         [
             pltpu.VMEM((size, size), BF16),
             pltpu.VMEM((size, size), BF16),
             pltpu.VMEM((mesh_rows, TAIL, columns), BF16),
             pltpu.VMEM((128, size), F32),
-            pltpu.SemaphoreType.DMA((runs + 2 * count,)),
+            pltpu.SemaphoreType.DMA((runs,)),
         ],
         "series",
         room=16 + 4 * size * size // MEGABYTE,
@@ -525,32 +487,23 @@
     square = call(
         functools.partial(square_kernel, count),
         block,
-        [ANY] * (2 * count + 3),
-        [
-            pltpu.VMEM((rows, size), BF16),
-            pltpu.VMEM((size, columns), BF16),
-            pltpu.VMEM((2, TAIL, columns), BF16),
-            pltpu.SemaphoreType.DMA((3 + 2 * count,)),
-        ],
+        [INVMEM] * (2 * count + 3),
+        [],
         "square",
     )(*near, *far, panel, pair, pair_far[0])
 
     line_near = [square] + moves.line(square)
+    soon, line_near[1] = lax.optimization_barrier((square, line_near[1]))
+    plane_near = [square] + [moves.in_plane(soon, s) for s in slots]
     line_far = [moves.core(value) for value in line_near]
-    plane_near = [square] + [moves.in_plane(square, s) for s in slots]
     plane_far = [line_far[0]] + [moves.core(value) for value in plane_near[1:]]
     evolved = call(
         functools.partial(evolve_kernel, count),
         block,
-        [ANY] * (4 * count + 2),
-        [
-            pltpu.VMEM((columns, size), BF16),
-            pltpu.VMEM((size, columns), BF16),
-            pltpu.VMEM((2, TAIL, columns), BF16),
-            pltpu.SemaphoreType.DMA((2 + 4 * count,)),
-        ],
+        [INVMEM] * (4 * count + 1),
+        [pltpu.VMEM((count, columns, columns), BF16)],
         "evolve",
-    )(*line_near, *line_far, *plane_near, *plane_far, pair, pair_far[0])
+    )(*line_near, *line_far, *plane_near, *plane_far, pair)
     return moves.relabel(evolved)
 
 

time: 165 us -> 158 us (0.958)
  Pallas kernels: 25.3 us -> 15.3 us
  starting transfers between devices: 73.5 us -> 80.6 us
  waiting for transfers between devices: 62.2 us -> 58.1 us
    pallas_call x3, Pallas kernels: 11.2 us -> 3.3 us  [the longest x1 1.33 us: on_device(): call(functools.partial(evolve_kernel, count), block, [INVMEM] * (4 * coun...]
    ppermute x66 -> x75, starting transfers between devices: 73.5 us -> 80.6 us  [move(): return lax.ppermute(value, AXES, permutation(self.rows, self.cols, source))]
    ppermute x66 -> x75, waiting for transfers between devices: 62.2 us -> 58.1 us  [move(): return lax.ppermute(value, AXES, permutation(self.rows, self.cols, source))]
    pallas_call x1, Pallas kernels: 3.3 us -> 1.22 us  [on_device(): call(functools.partial(first_kernel, count, starts), jax.ShapeDtypeStruct...]
  transfers between devices with their start and end apart: 66 -> 75, of which waited for: 28 -> 32; matrix products, arithmetic and copies ran while one was open for 0% -> 0% of each run, Pallas kernels for 0% -> 0%
where the time goes in v6:
time: 158 us
  starting transfers between devices  80.6 us (51%)
  waiting for transfers between devices  58.1 us (37%)
  Pallas kernels  15.3 us (10%)
  local copies, waits for them, and re-layouts  3.26 us (2%)
    ppermute x75, starting transfers between devices, move(): return lax.ppermute(value, AXES, permutation(self.rows, self.cols, source))  80.6 us
    ppermute x75, waiting for transfers between devices, move(): return lax.ppermute(value, AXES, permutation(self.rows, self.cols, source))  58.1 us
    pallas_call x1, Pallas kernels, on_device(): call(functools.partial(series_kernel, layout, count), [jax.ShapeDtypeStru...  8.94 us
  transfers between devices with their start and end apart: 75, of which 32 were waited for; matrix products, arithmetic and copies ran while one was open for 0% of the time, Pallas kernels for 0%

profile of v6, /device:TPU:1, one launch (start us, length us, event | category | flops | bytes accessed | tf_op | source)
XLA Modules:
  0.0 157.6 jit_solution(5921642179586153884)
XLA Ops:
  4.2 4.6 %collective-permute-start = (bf16[400,384]{1,0:T(8,128)(2,1)S(1)}, bf16[400,384]{1,0:T(8,128)(2,1)S(1)}, u32[]{:S(2)}, u32[]{:S(2)}) collective-permute-start(bf16[400,384]{1,0:T(8,128)(2,1)S(1)} %pair.1), channel_id=1, source_target_pairs={{0,0},{4,1},{2,2},{6,3},{1,4},{5,5},{3,6},{7,7},{8,8},{12,9},{10,1... | collective-permute-start | bytes 921608 | tf_op jit(solution)/shard_map/ppermute | solution.py:39
  8.8 2.1 %collective-permute-start.3 = (bf16[192,384]{1,0:T(8,128)(2,1)S(1)}, bf16[192,384]{1,0:T(8,128)(2,1)S(1)}, u32[]{:S(2)}, u32[]{:S(2)}) collective-permute-start(bf16[192,384]{1,0:T(8,128)(2,1)S(1)} %density.2), channel_id=1, source_target_pairs={{16,0},{20,1},{18,2},{22,3},{17,4},{21,5},{19,6},{23,7},{24,8},{28... | collective-permute-start | bytes 442376 | tf_op jit(solution)/shard_map/ppermute | solution.py:39
  10.9 2.7 %collective-permute-start.2 = (bf16[192,384]{1,0:T(8,128)(2,1)S(1)}, bf16[192,384]{1,0:T(8,128)(2,1)S(1)}, u32[]{:S(2)}, u32[]{:S(2)}) collective-permute-start(bf16[192,384]{1,0:T(8,128)(2,1)S(1)} %density.2), channel_id=1, source_target_pairs={{8,0},{12,1},{10,2},{14,3},{9,4},{13,5},{11,6},{15,7},{0,8},{4,9},... | collective-permute-start | bytes 442376 | tf_op jit(solution)/shard_map/ppermute | solution.py:39
  13.7 1.9 %collective-permute-start.1 = (bf16[192,384]{1,0:T(8,128)(2,1)S(1)}, bf16[192,384]{1,0:T(8,128)(2,1)S(1)}, u32[]{:S(2)}, u32[]{:S(2)}) collective-permute-start(bf16[192,384]{1,0:T(8,128)(2,1)S(1)} %density.2), channel_id=1, source_target_pairs={{0,0},{4,1},{2,2},{6,3},{1,4},{5,5},{3,6},{7,7},{8,8},{12,9},{10,1... | collective-permute-start | bytes 442376 | tf_op jit(solution)/shard_map/ppermute | solution.py:39
  20.4 1.8 %collective-permute-done.4.refs_12_ = bf16[192,384]{1,0:T(8,128)(2,1)S(1)} collective-permute-done((bf16[192,384]{1,0:T(8,128)(2,1)S(1)}, bf16[192,384]{1,0:T(8,128)(2,1)S(1)}, u32[]{:S(2)}, u32[]{:S(2)}) %collective-permute-start.4) | collective-permute-done | bytes 147488 | tf_op jit(solution)/shard_map/ppermute | solution.py:39
  22.2 2.2 %collective-permute-start.11 = (bf16[400,384]{1,0:T(8,128)(2,1)S(1)}, bf16[400,384]{1,0:T(8,128)(2,1)S(1)}, u32[]{:S(2)}, u32[]{:S(2)}) collective-permute-start(bf16[400,384]{1,0:T(8,128)(2,1)S(1)} %collective-permute-done.refs_0_.refs_1_.refs_2_.refs_8_.refs_30_.refs_9_.refs_16_), channel_id=1, source_target_pairs={{16,0},{17,1},{18,2},{19,3},{20,4},{21,5},{22,6},{23,7},{24,8},{25... | collective-permute-start | bytes 921608 | tf_op jit(solution)/shard_map/ppermute | solution.py:39
  27.3 2.2 %collective-permute-start.5 = (bf16[384,384]{1,0:T(8,128)(2,1)S(1)}, bf16[384,384]{1,0:T(8,128)(2,1)S(1)}, u32[]{:S(2)}, u32[]{:S(2)}) collective-permute-start(bf16[384,384]{1,0:T(8,128)(2,1)S(1)} %slice.34), channel_id=1, source_target_pairs={{4,0},{5,1},{6,2},{7,3},{0,4},{1,5},{2,6},{3,7},{12,8},{13,9},{14,... | collective-permute-start | bytes 884744 | tf_op jit(solution)/shard_map/ppermute | solution.py:39
  29.6 7.3 %collective-permute-done.5.refs_3_.refs_4_ = bf16[384,384]{1,0:T(8,128)(2,1)S(1)} collective-permute-done((bf16[384,384]{1,0:T(8,128)(2,1)S(1)}, bf16[384,384]{1,0:T(8,128)(2,1)S(1)}, u32[]{:S(2)}, u32[]{:S(2)}) %collective-permute-start.5) | collective-permute-done | bytes 294944 | tf_op jit(solution)/shard_map/ppermute | solution.py:39
  41.4 3.1 %collective-permute-done.8.refs_8_ = bf16[192,384]{1,0:T(8,128)(2,1)S(1)} collective-permute-done((bf16[192,384]{1,0:T(8,128)(2,1)S(1)}, bf16[192,384]{1,0:T(8,128)(2,1)S(1)}, u32[]{:S(2)}, u32[]{:S(2)}) %collective-permute-start.8) | collective-permute-done | bytes 147488 | tf_op jit(solution)/shard_map/ppermute | solution.py:39
  47.0 6.0 %collective-permute-done.17.refs_4_.refs_5_ = bf16[384,384]{1,0:T(8,128)(2,1)S(1)} collective-permute-done((bf16[384,384]{1,0:T(8,128)(2,1)S(1)}, bf16[384,384]{1,0:T(8,128)(2,1)S(1)}, u32[]{:S(2)}, u32[]{:S(2)}) %collective-permute-start.17) | collective-permute-done | bytes 294944 | tf_op jit(solution)/shard_map/ppermute | solution.py:39
  54.5 2.8 %collective-permute-done.18.refs_6_ = bf16[192,384]{1,0:T(8,128)(2,1)S(1)} collective-permute-done((bf16[192,384]{1,0:T(8,128)(2,1)S(1)}, bf16[192,384]{1,0:T(8,128)(2,1)S(1)}, u32[]{:S(2)}, u32[]{:S(2)}) %collective-permute-start.18) | collective-permute-done | bytes 147488 | tf_op jit(solution)/shard_map/ppermute | solution.py:39
  58.1 3.7 %collective-permute-start.21 = (bf16[400,384]{1,0:T(8,128)(2,1)S(1)}, bf16[400,384]{1,0:T(8,128)(2,1)S(1)}, u32[]{:S(2)}, u32[]{:S(2)}) collective-permute-start(bf16[400,384]{1,0:T(8,128)(2,1)S(1)} %collective-permute-done.10.refs_9_.refs_31_), channel_id=1, source_target_pairs={{1,0},{0,1},{3,2},{2,3},{5,4},{4,5},{7,6},{6,7},{9,8},{8,9},{11,10... | collective-permute-start | bytes 921608 | tf_op jit(solution)/shard_map/ppermute | solution.py:39
  66.9 3.7 %collective-permute-start.33 = (bf16[192,384]{1,0:T(8,128)(2,1)S(1)}, bf16[192,384]{1,0:T(8,128)(2,1)S(1)}, u32[]{:S(2)}, u32[]{:S(2)}) collective-permute-start(bf16[192,384]{1,0:T(8,128)(2,1)S(1)} %generator.1.refs_0_), channel_id=1, source_target_pairs={{8,0},{9,1},{10,2},{11,3},{12,4},{13,5},{14,6},{15,7},{0,8},{1,9},... | collective-permute-start | bytes 442376 | tf_op jit(solution)/shard_map/ppermute | solution.py:39
  70.6 5.0 %collective-permute-done.25 = bf16[192,384]{1,0:T(8,128)(2,1)S(1)} collective-permute-done((bf16[192,384]{1,0:T(8,128)(2,1)S(1)}, bf16[192,384]{1,0:T(8,128)(2,1)S(1)}, u32[]{:S(2)}, u32[]{:S(2)}) %collective-permute-start.25) | collective-permute-done | bytes 147488 | tf_op jit(solution)/shard_map/ppermute | solution.py:39
  78.8 5.0 %collective-permute-done.31.refs_6_ = bf16[96,384]{1,0:T(8,128)(2,1)S(1)} collective-permute-done((bf16[96,384]{1,0:T(8,128)(2,1)S(1)}, bf16[96,384]{1,0:T(8,128)(2,1)S(1)}, u32[]{:S(2)}, u32[]{:S(2)}) %collective-permute-start.31) | collective-permute-done | bytes 73760 | tf_op jit(solution)/shard_map/ppermute | solution.py:39
  83.8 3.1 %collective-permute-start.38 = (bf16[384,384]{1,0:T(8,128)(2,1)S(1)}, bf16[384,384]{1,0:T(8,128)(2,1)S(1)}, u32[]{:S(2)}, u32[]{:S(2)}) collective-permute-start(bf16[384,384]{1,0:T(8,128)(2,1)S(1)} %constant_dynamic-update-slice_fusion.refs_10_), channel_id=1, source_target_pairs={{1,0},{0,1},{3,2},{2,3},{5,4},{4,5},{7,6},{6,7},{9,8},{8,9},{11,10... | collective-permute-start | bytes 884744 | tf_op jit(solution)/shard_map/ppermute | solution.py:39
  94.0 2.2 %collective-permute-start.37 = (bf16[96,384]{1,0:T(8,128)(2,1)S(1)}, bf16[96,384]{1,0:T(8,128)(2,1)S(1)}, u32[]{:S(2)}, u32[]{:S(2)}) collective-permute-start(bf16[96,384]{1,0:T(8,128)(2,1)S(1)} %collective-permute-done.32.refs_8_), channel_id=1, source_target_pairs={{1,0},{0,1},{3,2},{2,3},{5,4},{4,5},{7,6},{6,7},{9,8},{8,9},{11,10... | collective-permute-start | bytes 221192 | tf_op jit(solution)/shard_map/ppermute | solution.py:39
  100.7 1.8 %collective-permute-start.51 = (bf16[96,384]{1,0:T(8,128)(2,1)S(1)}, bf16[96,384]{1,0:T(8,128)(2,1)S(1)}, u32[]{:S(2)}, u32[]{:S(2)}) collective-permute-start(bf16[96,384]{1,0:T(8,128)(2,1)S(1)} %collective-permute-done.50.refs_26_), channel_id=1, source_target_pairs={{1,0},{0,1},{3,2},{2,3},{5,4},{4,5},{7,6},{6,7},{9,8},{8,9},{11,10... | collective-permute-start | bytes 221192 | tf_op jit(solution)/shard_map/ppermute | solution.py:39
  106.3 8.9 %series.1 = (bf16[192,1536]{1,0:T(8,128)(2,1)S(1)}, bf16[192,384]{1,0:T(8,128)(2,1)S(1)}) custom-call(bf16[192,384]{1,0:T(8,128)(2,1)S(1)} %generator.1.refs_0_, bf16[192,384]{1,0:T(8,128)(2,1)S(1)} %collective-permute-done.24.refs_1_, bf16[192,384]{1,0:T(8,128)(2,1)S(1)} %collective-permute-done.26.refs_2_, ...), custom_call_target="tpu_custom_call" | custom-call | flops 1000 | bytes 1000 | tf_op jit(solution)/shard_map/series/pallas_call | solution.py:470
  119.0 2.5 %collective-permute-done.56.refs_3_ = bf16[192,384]{1,0:T(8,128)(2,1)S(1)} collective-permute-done((bf16[192,384]{1,0:T(8,128)(2,1)S(1)}, bf16[192,384]{1,0:T(8,128)(2,1)S(1)}, u32[]{:S(2)}, u32[]{:S(2)}) %collective-permute-start.56) | collective-permute-done | bytes 147488 | tf_op jit(solution)/shard_map/ppermute | solution.py:39
  130.7 6.5 %collective-permute-done.62.refs_2_ = bf16[192,384]{1,0:T(8,128)(2,1)S(1)} collective-permute-done((bf16[192,384]{1,0:T(8,128)(2,1)S(1)}, bf16[192,384]{1,0:T(8,128)(2,1)S(1)}, u32[]{:S(2)}, u32[]{:S(2)}) %collective-permute-start.62) | collective-permute-done | bytes 147488 | tf_op jit(solution)/shard_map/ppermute | solution.py:39
  144.0 2.2 %collective-permute-start.73 = (bf16[192,384]{1,0:T(8,128)(2,1)S(1)}, bf16[192,384]{1,0:T(8,128)(2,1)S(1)}, u32[]{:S(2)}, u32[]{:S(2)}) collective-permute-start(bf16[192,384]{1,0:T(8,128)(2,1)S(1)} %collective-permute-done.70.refs_11_), channel_id=1, source_target_pairs={{1,0},{0,1},{3,2},{2,3},{5,4},{4,5},{7,6},{6,7},{9,8},{8,9},{11,10... | collective-permute-start | bytes 442376 | tf_op jit(solution)/shard_map/ppermute | solution.py:39
  150.4 2.9 %collective-permute-start.74 = (bf16[192,384]{1,0:T(8,128)(2,1)S(1)}, bf16[192,384]{1,0:T(8,128)(2,1)S(1)}, u32[]{:S(2)}, u32[]{:S(2)}) collective-permute-start(bf16[192,384]{1,0:T(8,128)(2,1)S(1)} %evolve.1), channel_id=1, source_target_pairs={{0,0},{4,1},{2,2},{6,3},{1,4},{5,5},{3,6},{7,7},{8,8},{12,9},{10,1... | collective-permute-start | bytes 442376 | tf_op jit(solution)/shard_map/ppermute | solution.py:39
  153.4 3.5 %collective-permute-done.74 = bf16[192,384]{1,0:T(8,128)(2,1)S(1)} collective-permute-done((bf16[192,384]{1,0:T(8,128)(2,1)S(1)}, bf16[192,384]{1,0:T(8,128)(2,1)S(1)}, u32[]{:S(2)}, u32[]{:S(2)}) %collective-permute-start.74) | collective-permute-done | bytes 147488 | tf_op jit(solution)/shard_map/ppermute | solution.py:39
  (162 shorter events, 69.4 us)
Async XLA Ops:
  4.2 13.2 %collective-permute-start = (bf16[400,384]{1,0:T(8,128)(2,1)S(1)}, bf16[400,384]{1,0:T(8,128)(2,1)S(1)}, u32[]{:S(2)}, u32[]{:S(2)}) collective-permute-start(bf16[400,384]{1,0:T(8,128)(2,1)S(1)} %pair.1), channel_id=1, source_target_pairs={{0,0},{4,1},{2,2},{6,3},{1,4},{5,5},{3,6},{7,7},{8,8},{12,9},{10,1... | collective-permute-start | bytes 921608 | tf_op jit(solution)/shard_map/ppermute | solution.py:39
  8.8 8.1 %collective-permute-start.3 = (bf16[192,384]{1,0:T(8,128)(2,1)S(1)}, bf16[192,384]{1,0:T(8,128)(2,1)S(1)}, u32[]{:S(2)}, u32[]{:S(2)}) collective-permute-start(bf16[192,384]{1,0:T(8,128)(2,1)S(1)} %density.2), channel_id=1, source_target_pairs={{16,0},{20,1},{18,2},{22,3},{17,4},{21,5},{19,6},{23,7},{24,8},{28... | collective-permute-start | bytes 442376 | tf_op jit(solution)/shard_map/ppermute | solution.py:39
  10.9 7.8 %collective-permute-start.2 = (bf16[192,384]{1,0:T(8,128)(2,1)S(1)}, bf16[192,384]{1,0:T(8,128)(2,1)S(1)}, u32[]{:S(2)}, u32[]{:S(2)}) collective-permute-start(bf16[192,384]{1,0:T(8,128)(2,1)S(1)} %density.2), channel_id=1, source_target_pairs={{8,0},{12,1},{10,2},{14,3},{9,4},{13,5},{11,6},{15,7},{0,8},{4,9},... | collective-permute-start | bytes 442376 | tf_op jit(solution)/shard_map/ppermute | solution.py:39
  17.5 12.0 %collective-permute-start.6 = (bf16[384,384]{1,0:T(8,128)(2,1)S(1)}, bf16[384,384]{1,0:T(8,128)(2,1)S(1)}, u32[]{:S(2)}, u32[]{:S(2)}) collective-permute-start(bf16[384,384]{1,0:T(8,128)(2,1)S(1)} %slice.34), channel_id=1, source_target_pairs={{2,0},{3,1},{0,2},{1,3},{6,4},{7,5},{4,6},{5,7},{10,8},{11,9},{8,1... | collective-permute-start | bytes 884744 | tf_op jit(solution)/shard_map/ppermute | solution.py:39
  22.2 16.1 %collective-permute-start.11 = (bf16[400,384]{1,0:T(8,128)(2,1)S(1)}, bf16[400,384]{1,0:T(8,128)(2,1)S(1)}, u32[]{:S(2)}, u32[]{:S(2)}) collective-permute-start(bf16[400,384]{1,0:T(8,128)(2,1)S(1)} %collective-permute-done.refs_0_.refs_1_.refs_2_.refs_8_.refs_30_.refs_9_.refs_16_), channel_id=1, source_target_pairs={{16,0},{17,1},{18,2},{19,3},{20,4},{21,5},{22,6},{23,7},{24,8},{25... | collective-permute-start | bytes 921608 | tf_op jit(solution)/shard_map/ppermute | solution.py:39
  24.4 15.1 %collective-permute-start.10 = (bf16[400,384]{1,0:T(8,128)(2,1)S(1)}, bf16[400,384]{1,0:T(8,128)(2,1)S(1)}, u32[]{:S(2)}, u32[]{:S(2)}) collective-permute-start(bf16[400,384]{1,0:T(8,128)(2,1)S(1)} %collective-permute-done.refs_0_.refs_1_.refs_2_.refs_8_.refs_30_.refs_9_.refs_16_), channel_id=1, source_target_pairs={{8,0},{9,1},{10,2},{11,3},{12,4},{13,5},{14,6},{15,7},{0,8},{1,9},... | collective-permute-start | bytes 921608 | tf_op jit(solution)/shard_map/ppermute | solution.py:39
  25.5 15.2 %collective-permute-start.9 = (bf16[400,384]{1,0:T(8,128)(2,1)S(1)}, bf16[400,384]{1,0:T(8,128)(2,1)S(1)}, u32[]{:S(2)}, u32[]{:S(2)}) collective-permute-start(bf16[400,384]{1,0:T(8,128)(2,1)S(1)} %collective-permute-done.refs_0_.refs_1_.refs_2_.refs_8_.refs_30_.refs_9_.refs_16_), channel_id=1, source_target_pairs={{1,0},{0,1},{3,2},{2,3},{5,4},{4,5},{7,6},{6,7},{9,8},{8,9},{11,10... | collective-permute-start | bytes 921608 | tf_op jit(solution)/shard_map/ppermute | solution.py:39
  27.3 9.6 %collective-permute-start.5 = (bf16[384,384]{1,0:T(8,128)(2,1)S(1)}, bf16[384,384]{1,0:T(8,128)(2,1)S(1)}, u32[]{:S(2)}, u32[]{:S(2)}) collective-permute-start(bf16[384,384]{1,0:T(8,128)(2,1)S(1)} %slice.34), channel_id=1, source_target_pairs={{4,0},{5,1},{6,2},{7,3},{0,4},{1,5},{2,6},{3,7},{12,8},{13,9},{14,... | collective-permute-start | bytes 884744 | tf_op jit(solution)/shard_map/ppermute | solution.py:39
  29.5 11.8 %collective-permute-start.7 = (bf16[192,384]{1,0:T(8,128)(2,1)S(1)}, bf16[192,384]{1,0:T(8,128)(2,1)S(1)}, u32[]{:S(2)}, u32[]{:S(2)}) collective-permute-start(bf16[192,384]{1,0:T(8,128)(2,1)S(1)} %slice.45), channel_id=1, source_target_pairs={{4,0},{5,1},{6,2},{7,3},{0,4},{1,5},{2,6},{3,7},{12,8},{13,9},{14,... | collective-permute-start | bytes 442376 | tf_op jit(solution)/shard_map/ppermute | solution.py:39
  66.9 8.6 %collective-permute-start.25 = (bf16[192,384]{1,0:T(8,128)(2,1)S(1)}, bf16[192,384]{1,0:T(8,128)(2,1)S(1)}, u32[]{:S(2)}, u32[]{:S(2)}) collective-permute-start(bf16[192,384]{1,0:T(8,128)(2,1)S(1)} %generator.1.refs_0_), channel_id=1, source_target_pairs={{16,0},{17,1},{18,2},{19,3},{20,4},{21,5},{22,6},{23,7},{24,8},{25... | collective-permute-start | bytes 442376 | tf_op jit(solution)/shard_map/ppermute | solution.py:39
  66.9 8.6 %collective-permute-start.33 = (bf16[192,384]{1,0:T(8,128)(2,1)S(1)}, bf16[192,384]{1,0:T(8,128)(2,1)S(1)}, u32[]{:S(2)}, u32[]{:S(2)}) collective-permute-start(bf16[192,384]{1,0:T(8,128)(2,1)S(1)} %generator.1.refs_0_), channel_id=1, source_target_pairs={{8,0},{9,1},{10,2},{11,3},{12,4},{13,5},{14,6},{15,7},{0,8},{1,9},... | collective-permute-start | bytes 442376 | tf_op jit(solution)/shard_map/ppermute | solution.py:39
  75.6 11.8 %collective-permute-start.35 = (bf16[384,384]{1,0:T(8,128)(2,1)S(1)}, bf16[384,384]{1,0:T(8,128)(2,1)S(1)}, u32[]{:S(2)}, u32[]{:S(2)}) collective-permute-start(bf16[384,384]{1,0:T(8,128)(2,1)S(1)} %constant_dynamic-update-slice_fusion.refs_10_), channel_id=1, source_target_pairs={{2,0},{3,1},{0,2},{1,3},{6,4},{7,5},{4,6},{5,7},{10,8},{11,9},{8,1... | collective-permute-start | bytes 884744 | tf_op jit(solution)/shard_map/ppermute | solution.py:39
  75.9 11.6 %collective-permute-start.34 = (bf16[384,384]{1,0:T(8,128)(2,1)S(1)}, bf16[384,384]{1,0:T(8,128)(2,1)S(1)}, u32[]{:S(2)}, u32[]{:S(2)}) collective-permute-start(bf16[384,384]{1,0:T(8,128)(2,1)S(1)} %constant_dynamic-update-slice_fusion.refs_10_), channel_id=1, source_target_pairs={{4,0},{5,1},{6,2},{7,3},{0,4},{1,5},{2,6},{3,7},{12,8},{13,9},{14,... | collective-permute-start | bytes 884744 | tf_op jit(solution)/shard_map/ppermute | solution.py:39
  77.5 9.5 %collective-permute-start.32 = (bf16[96,384]{1,0:T(8,128)(2,1)S(1)}, bf16[96,384]{1,0:T(8,128)(2,1)S(1)}, u32[]{:S(2)}, u32[]{:S(2)}) collective-permute-start(bf16[96,384]{1,0:T(8,128)(2,1)S(1)} %slice.40), channel_id=1, source_target_pairs={{2,0},{3,1},{0,2},{1,3},{6,4},{7,5},{4,6},{5,7},{10,8},{11,9},{8,1... | collective-permute-start | bytes 221192 | tf_op jit(solution)/shard_map/ppermute | solution.py:39
  78.8 8.1 %collective-permute-start.30 = (bf16[192,384]{1,0:T(8,128)(2,1)S(1)}, bf16[192,384]{1,0:T(8,128)(2,1)S(1)}, u32[]{:S(2)}, u32[]{:S(2)}) collective-permute-start(bf16[192,384]{1,0:T(8,128)(2,1)S(1)} %collective-permute-done.25), channel_id=1, source_target_pairs={{8,0},{9,1},{10,2},{11,3},{12,4},{13,5},{14,6},{15,7},{0,8},{1,9},... | collective-permute-start | bytes 442376 | tf_op jit(solution)/shard_map/ppermute | solution.py:39
  89.7 7.8 %collective-permute-start.41 = (bf16[192,384]{1,0:T(8,128)(2,1)S(1)}, bf16[192,384]{1,0:T(8,128)(2,1)S(1)}, u32[]{:S(2)}, u32[]{:S(2)}) collective-permute-start(bf16[192,384]{1,0:T(8,128)(2,1)S(1)} %slice.41), channel_id=1, source_target_pairs={{4,0},{5,1},{6,2},{7,3},{0,4},{1,5},{2,6},{3,7},{12,8},{13,9},{14,... | collective-permute-start | bytes 442376 | tf_op jit(solution)/shard_map/ppermute | solution.py:39
  91.2 13.8 %collective-permute-start.39 = (bf16[384,384]{1,0:T(8,128)(2,1)S(1)}, bf16[384,384]{1,0:T(8,128)(2,1)S(1)}, u32[]{:S(2)}, u32[]{:S(2)}) collective-permute-start(bf16[384,384]{1,0:T(8,128)(2,1)S(1)} %collective-permute-done.34.refs_12_), channel_id=1, source_target_pairs={{1,0},{0,1},{3,2},{2,3},{5,4},{4,5},{7,6},{6,7},{9,8},{8,9},{11,10... | collective-permute-start | bytes 884744 | tf_op jit(solution)/shard_map/ppermute | solution.py:39
  97.1 8.0 %collective-permute-start.40 = (bf16[384,384]{1,0:T(8,128)(2,1)S(1)}, bf16[384,384]{1,0:T(8,128)(2,1)S(1)}, u32[]{:S(2)}, u32[]{:S(2)}) collective-permute-start(bf16[384,384]{1,0:T(8,128)(2,1)S(1)} %collective-permute-done.35.refs_14_), channel_id=1, source_target_pairs={{1,0},{0,1},{3,2},{2,3},{5,4},{4,5},{7,6},{6,7},{9,8},{8,9},{11,10... | collective-permute-start | bytes 884744 | tf_op jit(solution)/shard_map/ppermute | solution.py:39
  117.1 8.0 %collective-permute-start.54 = (bf16[192,384]{1,0:T(8,128)(2,1)S(1)}, bf16[192,384]{1,0:T(8,128)(2,1)S(1)}, u32[]{:S(2)}, u32[]{:S(2)}) collective-permute-start(bf16[192,384]{1,0:T(8,128)(2,1)S(1)} %get-tuple-element.89.refs_0_), channel_id=1, source_target_pairs={{4,0},{5,1},{6,2},{7,3},{0,4},{1,5},{2,6},{3,7},{12,8},{13,9},{14,... | collective-permute-start | bytes 442376 | tf_op jit(solution)/shard_map/ppermute | solution.py:39
  118.0 7.7 %collective-permute-start.57 = (bf16[192,384]{1,0:T(8,128)(2,1)S(1)}, bf16[192,384]{1,0:T(8,128)(2,1)S(1)}, u32[]{:S(2)}, u32[]{:S(2)}) collective-permute-start(bf16[192,384]{1,0:T(8,128)(2,1)S(1)} %get-tuple-element.89.refs_0_), channel_id=1, source_target_pairs={{1,0},{0,1},{3,2},{2,3},{5,4},{4,5},{7,6},{6,7},{9,8},{8,9},{11,10... | collective-permute-start | bytes 442376 | tf_op jit(solution)/shard_map/ppermute | solution.py:39
  127.4 9.8 %collective-permute-start.62 = (bf16[192,384]{1,0:T(8,128)(2,1)S(1)}, bf16[192,384]{1,0:T(8,128)(2,1)S(1)}, u32[]{:S(2)}, u32[]{:S(2)}) collective-permute-start(bf16[192,384]{1,0:T(8,128)(2,1)S(1)} %square.1.refs_0_.refs_8_), channel_id=1, source_target_pairs={{16,0},{17,1},{18,2},{19,3},{20,4},{21,5},{22,6},{23,7},{24,8},{25... | collective-permute-start | bytes 442376 | tf_op jit(solution)/shard_map/ppermute | solution.py:39
  128.9 8.9 %collective-permute-start.61 = (bf16[192,384]{1,0:T(8,128)(2,1)S(1)}, bf16[192,384]{1,0:T(8,128)(2,1)S(1)}, u32[]{:S(2)}, u32[]{:S(2)}) collective-permute-start(bf16[192,384]{1,0:T(8,128)(2,1)S(1)} %square.1.refs_0_.refs_8_), channel_id=1, source_target_pairs={{8,0},{9,1},{10,2},{11,3},{12,4},{13,5},{14,6},{15,7},{0,8},{1,9},... | collective-permute-start | bytes 442376 | tf_op jit(solution)/shard_map/ppermute | solution.py:39
  130.0 9.8 %collective-permute-start.64 = (bf16[192,384]{1,0:T(8,128)(2,1)S(1)}, bf16[192,384]{1,0:T(8,128)(2,1)S(1)}, u32[]{:S(2)}, u32[]{:S(2)}) collective-permute-start(bf16[192,384]{1,0:T(8,128)(2,1)S(1)} %square.1.refs_0_.refs_8_), channel_id=1, source_target_pairs={{1,0},{0,1},{3,2},{2,3},{5,4},{4,5},{7,6},{6,7},{9,8},{8,9},{11,10... | collective-permute-start | bytes 442376 | tf_op jit(solution)/shard_map/ppermute | solution.py:39
  139.7 8.0 %collective-permute-start.68 = (bf16[192,384]{1,0:T(8,128)(2,1)S(1)}, bf16[192,384]{1,0:T(8,128)(2,1)S(1)}, u32[]{:S(2)}, u32[]{:S(2)}) collective-permute-start(bf16[192,384]{1,0:T(8,128)(2,1)S(1)} %square.1.refs_0_.refs_8_), channel_id=1, source_target_pairs={{4,0},{5,1},{6,2},{7,3},{0,4},{1,5},{2,6},{3,7},{12,8},{13,9},{14,... | collective-permute-start | bytes 442376 | tf_op jit(solution)/shard_map/ppermute | solution.py:39
  (58 other events, 246.4 us)

commit v7 on v6

v7 whole, which is shorter than its diff:
```python
import functools

import jax
import jax.numpy as jnp
from jax import lax
from jax.experimental import pallas as pl
from jax.experimental.pallas import tpu as pltpu
from jax.sharding import PartitionSpec as P

BLK = 32
TERMS = 6
SQUARINGS = 2
FIRST = 3
AXES = ("row", "col")
F32 = jnp.float32
BF16 = jnp.bfloat16
TAIL = 16
MEGABYTE = 1024 * 1024


def coordinates(r, c):
    return r // 2, r % 2, c // 2, c % 2


def permutation(rows, cols, source):
    pairs = []
    for r in range(rows):
        for c in range(cols):
            sr, sc = source(*coordinates(r, c))
            pairs.append((sr * cols + sc, r * cols + c))
    return pairs


class Moves:
    def __init__(self, rows, cols):
        self.rows, self.cols = rows, cols

    def move(self, value, source):
        return lax.ppermute(value, AXES, permutation(self.rows, self.cols, source))

    def relabel(self, value, k=0):
        return self.move(value, lambda z, y, x, e: (2 * (z ^ k) + e, 2 * x + y))

    def along_z(self, value, k):
        return self.move(value, lambda z, y, x, e: (2 * (z ^ k) + y, 2 * x + e))

    def line(self, value, relabel=False, gate=None):
        bits = [1 << b for b in range((self.rows // 2).bit_length() - 1)]
        held = {0: value}
        for bit in reversed(bits):
            for k, part in list(held.items()):
                if k == 0 and relabel:
                    held[bit] = self.relabel(value, bit)
                else:
                    if k and gate is not None:
                        part, _ = lax.optimization_barrier((part, gate))
                    held[k | bit] = self.along_z(part, bit)
        return [held[k] for k in range(1, self.rows // 2)]

    def in_plane(self, value, s):
        return self.move(value, lambda z, y, x, e: (2 * z + (y ^ (s & 1)), 2 * (x ^ (s >> 1)) + e))

    def plane(self, value, relabel=False):
        if relabel:
            return [
                self.move(value, lambda z, y, x, e: (2 * z + e, 2 * (x ^ (s >> 1)) + (y ^ (s & 1))))
                for s in range(1, self.cols)
            ]
        return [self.in_plane(value, s) for s in range(1, self.cols)]

    def core(self, value):
        return self.move(value, lambda z, y, x, e: (2 * z + y, 2 * x + 1 - e))

    def cores(self, values):
        length = values[0].shape[0]
        far = self.core(jnp.concatenate(values, axis=0) if len(values) > 1 else values[0])
        return [(far, n * length) for n in range(len(values))]


def place():
    r, c = lax.axis_index("row"), lax.axis_index("col")
    z, y, x, e = r // 2, r % 2, c // 2, c % 2
    return z, 2 * x + y, e


def iota(shape, axis):
    return lax.broadcasted_iota(jnp.int32, shape, axis)


def dot(a, b):
    return jnp.dot(a, b, preferred_element_type=F32)


def repeat_rows(rows, blocks):
    return (iota((rows, blocks), 0) // BLK == iota((rows, blocks), 1)).astype(BF16)


def repeat_columns(blocks, columns, first=0):
    return (iota((blocks, columns), 0) == iota((blocks, columns), 1) // BLK + first).astype(BF16)


def block_mask(tail, number, rows, columns):
    blocks = columns // BLK
    wide = dot(repeat_rows(rows, tail.shape[0]), tail).astype(BF16)
    return dot(wide, repeat_columns(tail.shape[1], columns, number * blocks))


def call(kernel, outs, ins, scratch, name, flops=1000, room=16):
    return pl.pallas_call(
        kernel,
        out_shape=outs,
        in_specs=ins,
        out_specs=jax.tree.map(lambda _: pl.BlockSpec(memory_space=pltpu.VMEM), outs),
        scratch_shapes=scratch,
        name=name,
        compiler_params=pltpu.CompilerParams(vmem_limit_bytes=room * MEGABYTE),
        cost_estimate=pl.CostEstimate(flops=flops, bytes_accessed=1000, transcendentals=0),
    )


def views_call(kernel, views, outs, scratch, name, flops=1000, extra=()):
    arrays, spec = [], {}
    for key, items in views.items():
        spec[key] = []
        for value, first in items:
            known = [n for n, other in enumerate(arrays) if other is value]
            if not known:
                arrays.append(value)
            spec[key].append((known[0] if known else len(arrays) - 1, first))

    def body(*refs):
        def take(key, n, length, shift=0):
            index, first = spec[key][n]
            return refs[index][first + shift : first + shift + length, :]

        kernel(take, *refs[len(arrays) :])

    operands = [*arrays, *extra]
    return call(body, outs, [INVMEM] * len(operands), scratch, name, flops)(*operands)


ANY = pl.BlockSpec(memory_space=pl.ANY)
INVMEM = pl.BlockSpec(memory_space=pltpu.VMEM)
INSMEM = pl.BlockSpec(memory_space=pltpu.SMEM)


def masked(ref, fill):
    rows, columns = ref.shape
    tall = repeat_rows(rows, fill.shape[0])
    wide = repeat_columns(fill.shape[1], columns)
    mask = dot(dot(tall, fill.astype(BF16)).astype(BF16), wide)
    return (ref[...].astype(F32) * mask).astype(BF16)


def density_kernel(density, fills, out):
    out[...] = masked(density, fills[1])


def pair_kernel(fock, margin, density, fills, firsts, seconds, duo, trio):
    rows, columns = fock.shape
    row_blocks, column_blocks = rows // BLK, columns // BLK
    for half, (ref, number) in enumerate(((fock, 0), (margin, 2))):
        value = masked(ref, fills[number])
        duo[half * rows : (half + 1) * rows, :] = value
        trio[TAIL + half * rows : TAIL + (half + 1) * rows, :] = value
    trio[TAIL + 2 * rows :, :] = density[...]
    top = (iota((TAIL, row_blocks), 0) == iota((TAIL, row_blocks), 1)).astype(BF16)
    tail = jnp.zeros((TAIL, columns), F32)
    for number in range(firsts.shape[0] + seconds.shape[0]):
        ref = firsts[number] if number < FIRST else seconds[number - FIRST]
        column = iota((column_blocks, columns), 1) - number * column_blocks
        spread = (iota((column_blocks, columns), 0) == column).astype(BF16)
        tail += dot(dot(top, ref.astype(BF16)).astype(BF16), spread)
    trio[:TAIL, :] = tail.astype(BF16)


def chunk(index, length):
    return pl.ds(pl.multiple_of(index * length, length), length)


def start_all(copies):
    for one in copies:
        one.start()


def wait_all(copies):
    for one in copies:
        one.wait()


def repeat(times, body, unrolled):
    if unrolled:
        for t in range(times):
            body(t)
    else:

        def step(t, carry):
            body(t)
            return carry

        lax.fori_loop(0, times, step, 0)


def in_order(near, far, e):
    low = jnp.where(e == 0, near, far)
    high = jnp.where(e == 0, far, near)
    return jnp.concatenate([low, high], axis=0)


def first_kernel(count, take, out, left):
    z, q, e = place()
    rows, columns = out.shape[0] // 2, out.shape[1]
    for s in range(count):
        left[q ^ s] = take("plane", s, 2 * rows)
    tail = take("tail", 0, TAIL)
    masks = [block_mask(tail, n, rows, columns) for n in range(2)]
    total = jnp.zeros((2 * rows, columns), F32)
    for s in range(count):
        total += dot(left[z ^ s], in_order(take("near", s, rows), take("far", s, rows), e))
    for n in range(2):
        part = slice(n * rows, (n + 1) * rows)
        out[part, :] = (total[part] * masks[n]).astype(BF16)


def generator_kernel(count, take, out, left):
    z, q, e = place()
    rows, columns = out.shape
    for s in range(count):
        for half in range(2):
            left[half, q ^ s] = take("plane", s, rows, half * rows)
    mask = block_mask(take("tail", 0, TAIL), 2, rows, columns)
    total = jnp.zeros((rows, columns), F32)
    for half in range(2):
        shift = (1 - half) * rows
        for s in range(count):
            right = in_order(take("near", s, rows, shift), take("far", s, rows, shift), e)
            product = dot(left[half, z ^ s], right)
            total = total + product if half == 0 else total - product
    generator = (total * mask).astype(BF16)
    out[...] = (generator.astype(F32) * 0.25).astype(BF16)


def series_kernel(layout, count, pieces, *refs):
    arrays, tails, order = refs[:pieces], refs[pieces : pieces + 2 * count], refs[pieces + 2 * count]
    panel, mine, whole, turned, wides, spread, sems = refs[pieces + 2 * count + 1 :]
    z, q, e = place()
    rows, columns = mine.shape
    size = panel.shape[1]
    row_blocks, column_blocks, blocks = rows // BLK, columns // BLK, size // BLK
    small = size <= 1536
    copies = []
    for index, first, k, plane, lane in layout:
        core = e if lane == 0 else 1 - e
        copies.append(
            pltpu.make_async_copy(
                arrays[index].at[pl.ds(first, rows)],
                whole.at[chunk(2 * (z ^ k) + core, rows), chunk(q ^ plane, columns)],
                sems.at[len(copies)],
            )
        )
    start_all(copies)
    for index, ref in enumerate(tails):
        core = e if index < count else 1 - e
        wides[2 * (z ^ (index % count)) + core] = ref[...]
    filters = jnp.zeros((128, size), F32)
    for p in range(2 * count):
        column = iota((TAIL, size), 1) // BLK
        row = iota((TAIL, size), 0)
        near = ((row < row_blocks) & (column == row + p * row_blocks)).astype(BF16)
        filters += lax.dot_general(
            wides[p][:, :128], near, (((0,), (0,)), ((), ())), preferred_element_type=F32
        )
    spread[...] = filters

    wait_all(copies)

    def turn(t):
        tile = jnp.concatenate(
            [whole[chunk(order[t * column_blocks + a], BLK), :] for a in range(column_blocks)],
            axis=0,
        )
        turned[:, chunk(t, columns)] = tile.T

    def place_rows(b):
        whole[chunk(b, BLK), :] = turned[chunk(order[b], BLK), :]

    repeat(count, turn, small)
    repeat(blocks, place_rows, small)

    first = (2 * q + e) * rows
    unit = (iota((rows, size), 1) == iota((rows, size), 0) + first).astype(F32)
    own = unit + whole[chunk(2 * q + e, rows), :].astype(F32) / TERMS
    panel[...] = own.astype(BF16)
    width = size if small else 512
    for number in range(1, TERMS):
        current = panel[...]
        base = (FIRST + number - 1) * column_blocks + e * row_blocks

        def advance(t):
            part = chunk(t, width)
            product = dot(current, whole[:, part])
            mask = jnp.concatenate(
                [
                    jnp.broadcast_to(spread[pl.ds(base + b, 1), part], (BLK, width))
                    for b in range(row_blocks)
                ],
                axis=0,
            )
            here = iota((rows, width), 1) + t * width == iota((rows, width), 0) + first
            panel[:, part] = (here.astype(F32) + product * mask / (TERMS - number)).astype(BF16)

        repeat(size // width, advance, small)
    mine[...] = panel[:, chunk(z, columns)]


def turned_mask(tails, number, e, rows, columns):
    row_blocks, column_blocks = rows // BLK, columns // BLK
    pick = iota((rows, 128), 0) // BLK + number * column_blocks + e * row_blocks
    pick = (pick == iota((rows, 128), 1)).astype(BF16)
    mask = jnp.zeros((rows, columns), F32)
    for core in range(2):
        row = iota((TAIL, columns), 0)
        near = (row < row_blocks) & (iota((TAIL, columns), 1) // BLK == row + core * row_blocks)
        chosen = lax.dot_general(
            pick, tails[core][:, :128], (((1,), (1,)), ((), ())), preferred_element_type=F32
        )
        mask += dot(chosen.astype(BF16), near.astype(BF16))
    return mask


def square_kernel(count, take, panel, out):
    z, q, e = place()
    rows, columns = out.shape
    tails = in_order(take("tail", 0, TAIL), take("tail", 1, TAIL), e)
    mask = turned_mask([tails[:TAIL], tails[TAIL:]], FIRST + TERMS - 1, e, rows, columns)
    total = jnp.zeros((rows, columns), F32)
    for s in range(count):
        right = in_order(take("near", s, rows), take("far", s, rows), e)
        total += dot(panel[:, chunk(q ^ s, columns)], right)
    out[...] = (total * mask).astype(BF16)


def evolve_kernel(count, take, out, right):
    z, q, e = place()
    rows, columns = out.shape
    for s in range(count):
        right[q ^ s] = in_order(take("plane_near", s, rows), take("plane_far", s, rows), e)
    mask = block_mask(take("tail", 0, TAIL), FIRST + TERMS, rows, columns)
    total = jnp.zeros((columns, columns), F32)
    for s in range(count):
        total += dot(
            in_order(take("line_near", s, rows), take("line_far", s, rows), e), right[z ^ s]
        )
    total = total.T
    chosen = jnp.where(e == 0, total[:rows], total[rows:])
    out[...] = (chosen * mask).astype(BF16)


def on_device(
    mesh_rows,
    mesh_cols,
    fock_matrix,
    density,
    margin,
    fill_patterns,
    first_filters,
    owner_order,
    second_filters,
):
    moves = Moves(mesh_rows, mesh_cols)
    count = mesh_cols
    half = count // 2
    rows, columns = fock_matrix.shape
    size = rows * mesh_rows
    block = jax.ShapeDtypeStruct((rows, columns), BF16)
    barrier = lax.optimization_barrier

    def whole(values):
        return [(value, 0) for value in values]

    masked_density = call(density_kernel, block, [INVMEM] * 2, [], "density")(
        density, fill_patterns
    )
    later, fock_matrix, second_filters = barrier((masked_density, fock_matrix, second_filters))
    duo, trio = call(
        pair_kernel,
        [
            jax.ShapeDtypeStruct((2 * rows, columns), BF16),
            jax.ShapeDtypeStruct((TAIL + 3 * rows, columns), BF16),
        ],
        [INVMEM] * 6,
        [],
        "pair",
        10**10,
    )(fock_matrix, margin, later, fill_patterns, first_filters, second_filters)

    trio = moves.relabel(trio)
    fock_rows = moves.plane(duo, True)
    density_line = moves.line(masked_density, True)
    density_near = [(trio, TAIL + 2 * rows)] + whole(density_line)
    density_line = list(barrier((*density_line, *fock_rows))[: count - 1])
    trio_far = moves.core(trio)
    density_far = [(trio_far, TAIL + 2 * rows)] + moves.cores(density_line)
    pair, *_ = barrier((trio[: TAIL + 2 * rows], *density_line, *fock_rows))

    products = views_call(
        functools.partial(first_kernel, count),
        {
            "plane": [(trio, TAIL)] + whole(fock_rows),
            "tail": [(trio, 0)],
            "near": density_near,
            "far": density_far,
        },
        jax.ShapeDtypeStruct((2 * rows, columns), BF16),
        [pltpu.VMEM((count, 2 * rows, columns), BF16)],
        "first",
        10**10,
    )
    product_rows = [products] + moves.plane(products)
    pair_line = moves.line(pair, gate=products)
    pair_line = list(barrier((*pair_line, *product_rows[1:]))[: count - 1])
    pair_far = [(trio_far, 0)] + moves.cores(pair_line[:half]) + moves.cores(pair_line[half:])
    pair_near = [(trio, 0)] + whole(pair_line)

    generator = views_call(
        functools.partial(generator_kernel, count),
        {
            "plane": whole(product_rows),
            "tail": [(trio, 0)],
            "near": [(value, first + TAIL) for value, first in pair_near],
            "far": [(value, first + TAIL) for value, first in pair_far],
        },
        block,
        [pltpu.VMEM((2, count, rows, columns), BF16)],
        "generator",
    )

    lines = [generator] + moves.line(generator)
    arrays, layout, planes = [], [], []
    for held in (range(1), range(1, half + 1), range(half + 1, count)):
        group = jnp.concatenate([lines[k] for k in held], axis=0) if len(held) > 1 else lines[held[0]]
        if len(held) > 1:
            group, *planes = barrier((group, *planes))
        planes = [group] + moves.plane(group)
        ready = planes
        if 1 < len(held) < count - 1:
            *ready, _ = barrier((*planes, *lines[half + 1 :]))[: count + 1]
        far = moves.cores(ready)
        for s, value in enumerate(planes):
            for lane, (array, start) in enumerate(((value, 0), far[s])):
                if not any(other is array for other in arrays):
                    arrays.append(array)
                index = [n for n, other in enumerate(arrays) if other is array][0]
                for n, k in enumerate(held):
                    layout.append((index, start + n * rows, k, s, lane))
    tails = [value[first : first + TAIL] for value, first in pair_near + pair_far]

    panel, mine = call(
        functools.partial(series_kernel, layout, count, len(arrays)),
        [jax.ShapeDtypeStruct((rows, size), BF16), block],
        [ANY] * len(arrays) + [INVMEM] * (2 * count) + [INSMEM],
        [
            pltpu.VMEM((size, size), BF16),
            pltpu.VMEM((size, size), BF16),
            pltpu.VMEM((mesh_rows, TAIL, columns), BF16),
            pltpu.VMEM((128, size), F32),
            pltpu.SemaphoreType.DMA((len(layout),)),
        ],
        "series",
        room=16 + 4 * size * size // MEGABYTE,
    )(*arrays, *tails, owner_order)

    near = [mine] + moves.plane(mine)
    square = views_call(
        functools.partial(square_kernel, count),
        {"near": whole(near), "far": moves.cores(near), "tail": [(trio, 0), (trio_far, 0)]},
        block,
        [],
        "square",
        extra=[panel],
    )

    line = moves.line(square)
    plane_near = [square] + moves.plane(square)
    plane_far = moves.cores(plane_near)
    evolved = views_call(
        functools.partial(evolve_kernel, count),
        {
            "plane_near": whole(plane_near),
            "plane_far": plane_far,
            "line_near": whole([square] + line),
            "line_far": plane_far[:1] + moves.cores(line),
            "tail": [(trio, 0)],
        },
        block,
        [pltpu.VMEM((count, columns, columns), BF16)],
        "evolve",
    )
    return moves.relabel(evolved)


def solution(mesh):
    return jax.shard_map(
        functools.partial(on_device, mesh.shape["row"], mesh.shape["col"]),
        mesh=mesh,
        in_specs=(
            P("row", "col"),
            P("row", "col"),
            P("row", "col"),
            P(None, "row", "col"),
            P(None, "row", "col"),
            P(),
            P(None, "row", "col"),
        ),
        out_specs=P("row", "col"),
        check_vma=False,
    )
```

time: 158 us -> 157 us (level)
  starting transfers between devices: 80.6 us -> 48.3 us
  waiting for transfers between devices: 58.1 us -> 87.2 us
  local copies, waits for them, and re-layouts: 3.26 us -> 5.61 us
    ppermute x75 -> x45, starting transfers between devices: 80.6 us -> 48.3 us  [move(): return lax.ppermute(value, AXES, permutation(self.rows, self.cols, source))]
    ppermute x75 -> x45, waiting for transfers between devices: 58.1 us -> 87.2 us  [move(): return lax.ppermute(value, AXES, permutation(self.rows, self.cols, source))]
    unnamed x16 -> x13, local copies, waits for them, and re-layouts: 2.32 us -> 4.81 us
  transfers between devices with their start and end apart: 75 -> 45, of which waited for: 32 -> 31; matrix products, arithmetic and copies ran while one was open for 0% -> 0% of each run, Pallas kernels for 0% -> 1%
where the time goes in v7:
time: 157 us
  waiting for transfers between devices  87.2 us (56%)
  starting transfers between devices  48.3 us (31%)
  Pallas kernels  15.2 us (10%)
  local copies, waits for them, and re-layouts  5.61 us (4%)
    ppermute x45, waiting for transfers between devices, move(): return lax.ppermute(value, AXES, permutation(self.rows, self.cols, source))  87.2 us
    ppermute x45, starting transfers between devices, move(): return lax.ppermute(value, AXES, permutation(self.rows, self.cols, source))  48.3 us
    pallas_call x1, Pallas kernels, on_device(): call(functools.partial(series_kernel, layout, count, len(arrays)), [jax.S...  8.85 us
    unnamed x13, local copies, waits for them, and re-layouts  4.81 us
    pallas_call x4, Pallas kernels, views_call(): call(body, outs, [INVMEM] * len(operands), scratch, name, flops)(*operands)  4.52 us
  transfers between devices with their start and end apart: 45, of which 31 were waited for; matrix products, arithmetic and copies ran while one was open for 0% of the time, Pallas kernels for 1%

profile of v7, /device:TPU:1, one launch (start us, length us, event | category | flops | bytes accessed | tf_op | source)
XLA Modules:
  0.0 157.1 jit_solution(1449614331465443197)
XLA Ops:
  6.7 4.6 %collective-permute-start = (bf16[592,384]{1,0:T(8,128)(2,1)S(1)}, bf16[592,384]{1,0:T(8,128)(2,1)S(1)}, u32[]{:S(2)}, u32[]{:S(2)}) collective-permute-start(bf16[592,384]{1,0:T(8,128)(2,1)S(1)} %get-tuple-element.28), channel_id=1, source_target_pairs={{0,0},{4,1},{2,2},{6,3},{1,4},{5,5},{3,6},{7,7},{8,8},{12,9},{10,1... | collective-permute-start | bytes 1363976 | tf_op jit(solution)/shard_map/ppermute | solution.py:39
  11.3 2.1 %collective-permute-start.5 = (bf16[192,384]{1,0:T(8,128)(2,1)S(1)}, bf16[192,384]{1,0:T(8,128)(2,1)S(1)}, u32[]{:S(2)}, u32[]{:S(2)}) collective-permute-start(bf16[192,384]{1,0:T(8,128)(2,1)S(1)} %density.2), channel_id=1, source_target_pairs={{16,0},{20,1},{18,2},{22,3},{17,4},{21,5},{19,6},{23,7},{24,8},{28... | collective-permute-start | bytes 442376 | tf_op jit(solution)/shard_map/ppermute | solution.py:39
  13.4 2.7 %collective-permute-start.4 = (bf16[192,384]{1,0:T(8,128)(2,1)S(1)}, bf16[192,384]{1,0:T(8,128)(2,1)S(1)}, u32[]{:S(2)}, u32[]{:S(2)}) collective-permute-start(bf16[192,384]{1,0:T(8,128)(2,1)S(1)} %density.2), channel_id=1, source_target_pairs={{8,0},{12,1},{10,2},{14,3},{9,4},{13,5},{11,6},{15,7},{0,8},{4,9},... | collective-permute-start | bytes 442376 | tf_op jit(solution)/shard_map/ppermute | solution.py:39
  17.1 2.3 %collective-permute-done.5.refs_5_ = bf16[192,384]{1,0:T(8,128)(2,1)S(1)} collective-permute-done((bf16[192,384]{1,0:T(8,128)(2,1)S(1)}, bf16[192,384]{1,0:T(8,128)(2,1)S(1)}, u32[]{:S(2)}, u32[]{:S(2)}) %collective-permute-start.5) | collective-permute-done | bytes 147488 | tf_op jit(solution)/shard_map/ppermute | solution.py:39
  21.3 3.4 %collective-permute-done.6.refs_6_ = bf16[192,384]{1,0:T(8,128)(2,1)S(1)} collective-permute-done((bf16[192,384]{1,0:T(8,128)(2,1)S(1)}, bf16[192,384]{1,0:T(8,128)(2,1)S(1)}, u32[]{:S(2)}, u32[]{:S(2)}) %collective-permute-start.6) | collective-permute-done | bytes 147488 | tf_op jit(solution)/shard_map/ppermute | solution.py:39
  25.8 4.0 %collective-permute-done.2.refs_2_ = bf16[384,384]{1,0:T(8,128)(2,1)S(1)} collective-permute-done((bf16[384,384]{1,0:T(8,128)(2,1)S(1)}, bf16[384,384]{1,0:T(8,128)(2,1)S(1)}, u32[]{:S(2)}, u32[]{:S(2)}) %collective-permute-start.2) | collective-permute-done | bytes 294944 | tf_op jit(solution)/shard_map/ppermute | solution.py:39
  35.6 13.0 %collective-permute-done.13.refs_6_ = bf16[400,384]{1,0:T(8,128)(2,1)S(1)} collective-permute-done((bf16[400,384]{1,0:T(8,128)(2,1)S(1)}, bf16[400,384]{1,0:T(8,128)(2,1)S(1)}, u32[]{:S(2)}, u32[]{:S(2)}) %collective-permute-start.13) | collective-permute-done | bytes 307232 | tf_op jit(solution)/shard_map/ppermute | solution.py:39
  51.2 6.3 %collective-permute-done.11.refs_3_ = bf16[384,384]{1,0:T(8,128)(2,1)S(1)} collective-permute-done((bf16[384,384]{1,0:T(8,128)(2,1)S(1)}, bf16[384,384]{1,0:T(8,128)(2,1)S(1)}, u32[]{:S(2)}, u32[]{:S(2)}) %collective-permute-start.11) | collective-permute-done | bytes 294944 | tf_op jit(solution)/shard_map/ppermute | solution.py:39
  57.5 5.5 %collective-permute-done.10.refs_2_ = bf16[384,384]{1,0:T(8,128)(2,1)S(1)} collective-permute-done((bf16[384,384]{1,0:T(8,128)(2,1)S(1)}, bf16[384,384]{1,0:T(8,128)(2,1)S(1)}, u32[]{:S(2)}, u32[]{:S(2)}) %collective-permute-start.10) | collective-permute-done | bytes 294944 | tf_op jit(solution)/shard_map/ppermute | solution.py:39
  68.7 2.7 %collective-permute-start.22 = (bf16[192,384]{1,0:T(8,128)(2,1)S(1)}, bf16[192,384]{1,0:T(8,128)(2,1)S(1)}, u32[]{:S(2)}, u32[]{:S(2)}) collective-permute-start(bf16[192,384]{1,0:T(8,128)(2,1)S(1)} %generator.1.refs_0_), channel_id=1, source_target_pairs={{16,0},{17,1},{18,2},{19,3},{20,4},{21,5},{22,6},{23,7},{24,8},{25... | collective-permute-start | bytes 442376 | tf_op jit(solution)/shard_map/ppermute | solution.py:39
  74.0 4.4 %collective-permute-done.22 = bf16[192,384]{1,0:T(8,128)(2,1)S(1)} collective-permute-done((bf16[192,384]{1,0:T(8,128)(2,1)S(1)}, bf16[192,384]{1,0:T(8,128)(2,1)S(1)}, u32[]{:S(2)}, u32[]{:S(2)}) %collective-permute-start.22) | collective-permute-done | bytes 147488 | tf_op jit(solution)/shard_map/ppermute | solution.py:39
  80.4 2.5 %collective-permute-start.25 = (bf16[384,384]{1,0:T(8,128)(2,1)S(1)}, bf16[384,384]{1,0:T(8,128)(2,1)S(1)}, u32[]{:S(2)}, u32[]{:S(2)}) collective-permute-start(bf16[384,384]{1,0:T(8,128)(2,1)S(1)} %pad_maximum_fusion.8.refs_5_), channel_id=1, source_target_pairs={{6,0},{7,1},{4,2},{5,3},{2,4},{3,5},{0,6},{1,7},{14,8},{15,9},{12,... | collective-permute-start | bytes 884744 | tf_op jit(solution)/shard_map/ppermute | solution.py:39
  84.6 2.8 %collective-permute-done.26.refs_10_ = bf16[192,384]{1,0:T(8,128)(2,1)S(1)} collective-permute-done((bf16[192,384]{1,0:T(8,128)(2,1)S(1)}, bf16[192,384]{1,0:T(8,128)(2,1)S(1)}, u32[]{:S(2)}, u32[]{:S(2)}) %collective-permute-start.26) | collective-permute-done | bytes 147488 | tf_op jit(solution)/shard_map/ppermute | solution.py:39
  88.7 6.9 %collective-permute-done.24.refs_8_ = bf16[384,384]{1,0:T(8,128)(2,1)S(1)} collective-permute-done((bf16[384,384]{1,0:T(8,128)(2,1)S(1)}, bf16[384,384]{1,0:T(8,128)(2,1)S(1)}, u32[]{:S(2)}, u32[]{:S(2)}) %collective-permute-start.24) | collective-permute-done | bytes 294944 | tf_op jit(solution)/shard_map/ppermute | solution.py:39
  101.3 2.6 %collective-permute-done.30.refs_14_ = bf16[192,384]{1,0:T(8,128)(2,1)S(1)} collective-permute-done((bf16[192,384]{1,0:T(8,128)(2,1)S(1)}, bf16[192,384]{1,0:T(8,128)(2,1)S(1)}, u32[]{:S(2)}, u32[]{:S(2)}) %collective-permute-start.30) | collective-permute-done | bytes 147488 | tf_op jit(solution)/shard_map/ppermute | solution.py:39
  103.9 3.2 %collective-permute-done.29.refs_13_ = bf16[192,384]{1,0:T(8,128)(2,1)S(1)} collective-permute-done((bf16[192,384]{1,0:T(8,128)(2,1)S(1)}, bf16[192,384]{1,0:T(8,128)(2,1)S(1)}, u32[]{:S(2)}, u32[]{:S(2)}) %collective-permute-start.29) | collective-permute-done | bytes 147488 | tf_op jit(solution)/shard_map/ppermute | solution.py:39
  109.7 8.8 %series.1 = (bf16[192,1536]{1,0:T(8,128)(2,1)S(1)}, bf16[192,384]{1,0:T(8,128)(2,1)S(1)}) custom-call(bf16[192,384]{1,0:T(8,128)(2,1)S(1)} %generator.1.refs_0_, bf16[768,384]{1,0:T(8,128)(2,1)S(1)} %collective-permute-done.20.refs_1_, bf16[192,384]{1,0:T(8,128)(2,1)S(1)} %collective-permute-done.17.refs_2_, ...), custom_call_target="tpu_custom_call" | custom-call | flops 1000 | bytes 1000 | tf_op jit(solution)/shard_map/series/pallas_call | solution.py:458
  118.6 2.1 %collective-permute-start.34 = (bf16[192,384]{1,0:T(8,128)(2,1)S(1)}, bf16[192,384]{1,0:T(8,128)(2,1)S(1)}, u32[]{:S(2)}, u32[]{:S(2)}) collective-permute-start(bf16[192,384]{1,0:T(8,128)(2,1)S(1)} %get-tuple-element.43.refs_0_), channel_id=1, source_target_pairs={{6,0},{7,1},{4,2},{5,3},{2,4},{3,5},{0,6},{1,7},{14,8},{15,9},{12,... | collective-permute-start | bytes 442376 | tf_op jit(solution)/shard_map/ppermute | solution.py:39
  121.3 3.3 %collective-permute-done.34.refs_3_ = bf16[192,384]{1,0:T(8,128)(2,1)S(1)} collective-permute-done((bf16[192,384]{1,0:T(8,128)(2,1)S(1)}, bf16[192,384]{1,0:T(8,128)(2,1)S(1)}, u32[]{:S(2)}, u32[]{:S(2)}) %collective-permute-start.34) | collective-permute-done | bytes 147488 | tf_op jit(solution)/shard_map/ppermute | solution.py:39
  124.6 3.1 %collective-permute-done.33.refs_2_ = bf16[192,384]{1,0:T(8,128)(2,1)S(1)} collective-permute-done((bf16[192,384]{1,0:T(8,128)(2,1)S(1)}, bf16[192,384]{1,0:T(8,128)(2,1)S(1)}, u32[]{:S(2)}, u32[]{:S(2)}) %collective-permute-start.33) | collective-permute-done | bytes 147488 | tf_op jit(solution)/shard_map/ppermute | solution.py:39
  136.1 4.6 %collective-permute-done.41.refs_6_ = bf16[192,384]{1,0:T(8,128)(2,1)S(1)} collective-permute-done((bf16[192,384]{1,0:T(8,128)(2,1)S(1)}, bf16[192,384]{1,0:T(8,128)(2,1)S(1)}, u32[]{:S(2)}, u32[]{:S(2)}) %collective-permute-start.41) | collective-permute-done | bytes 147488 | tf_op jit(solution)/shard_map/ppermute | solution.py:39
  144.7 2.5 %collective-permute-start.43 = (bf16[576,384]{1,0:T(8,128)(2,1)S(1)}, bf16[576,384]{1,0:T(8,128)(2,1)S(1)}, u32[]{:S(2)}, u32[]{:S(2)}) collective-permute-start(bf16[576,384]{1,0:T(8,128)(2,1)S(1)} %pad_maximum_fusion.7), channel_id=1, source_target_pairs={{1,0},{0,1},{3,2},{2,3},{5,4},{4,5},{7,6},{6,7},{9,8},{8,9},{11,10... | collective-permute-start | bytes 1327112 | tf_op jit(solution)/shard_map/ppermute | solution.py:39
  150.0 3.3 %collective-permute-start.44 = (bf16[192,384]{1,0:T(8,128)(2,1)S(1)}, bf16[192,384]{1,0:T(8,128)(2,1)S(1)}, u32[]{:S(2)}, u32[]{:S(2)}) collective-permute-start(bf16[192,384]{1,0:T(8,128)(2,1)S(1)} %evolve.1), channel_id=1, source_target_pairs={{0,0},{4,1},{2,2},{6,3},{1,4},{5,5},{3,6},{7,7},{8,8},{12,9},{10,1... | collective-permute-start | bytes 442376 | tf_op jit(solution)/shard_map/ppermute | solution.py:39
  153.3 3.2 %collective-permute-done.44 = bf16[192,384]{1,0:T(8,128)(2,1)S(1)} collective-permute-done((bf16[192,384]{1,0:T(8,128)(2,1)S(1)}, bf16[192,384]{1,0:T(8,128)(2,1)S(1)}, u32[]{:S(2)}, u32[]{:S(2)}) %collective-permute-start.44) | collective-permute-done | bytes 147488 | tf_op jit(solution)/shard_map/ppermute | solution.py:39
  (104 shorter events, 57.0 us)
Async XLA Ops:
  6.7 23.7 %collective-permute-start = (bf16[592,384]{1,0:T(8,128)(2,1)S(1)}, bf16[592,384]{1,0:T(8,128)(2,1)S(1)}, u32[]{:S(2)}, u32[]{:S(2)}) collective-permute-start(bf16[592,384]{1,0:T(8,128)(2,1)S(1)} %get-tuple-element.28), channel_id=1, source_target_pairs={{0,0},{4,1},{2,2},{6,3},{1,4},{5,5},{3,6},{7,7},{8,8},{12,9},{10,1... | collective-permute-start | bytes 1363976 | tf_op jit(solution)/shard_map/ppermute | solution.py:39
  11.3 8.2 %collective-permute-start.5 = (bf16[192,384]{1,0:T(8,128)(2,1)S(1)}, bf16[192,384]{1,0:T(8,128)(2,1)S(1)}, u32[]{:S(2)}, u32[]{:S(2)}) collective-permute-start(bf16[192,384]{1,0:T(8,128)(2,1)S(1)} %density.2), channel_id=1, source_target_pairs={{16,0},{20,1},{18,2},{22,3},{17,4},{21,5},{19,6},{23,7},{24,8},{28... | collective-permute-start | bytes 442376 | tf_op jit(solution)/shard_map/ppermute | solution.py:39
  16.1 9.7 %collective-permute-start.3 = (bf16[384,384]{1,0:T(8,128)(2,1)S(1)}, bf16[384,384]{1,0:T(8,128)(2,1)S(1)}, u32[]{:S(2)}, u32[]{:S(2)}) collective-permute-start(bf16[384,384]{1,0:T(8,128)(2,1)S(1)} %get-tuple-element.29), channel_id=1, source_target_pairs={{3,0},{7,1},{1,2},{5,3},{2,4},{6,5},{0,6},{4,7},{11,8},{15,9},{9,1... | collective-permute-start | bytes 884744 | tf_op jit(solution)/shard_map/ppermute | solution.py:39
  16.1 13.7 %collective-permute-start.2 = (bf16[384,384]{1,0:T(8,128)(2,1)S(1)}, bf16[384,384]{1,0:T(8,128)(2,1)S(1)}, u32[]{:S(2)}, u32[]{:S(2)}) collective-permute-start(bf16[384,384]{1,0:T(8,128)(2,1)S(1)} %get-tuple-element.29), channel_id=1, source_target_pairs={{2,0},{6,1},{0,2},{4,3},{3,4},{7,5},{1,6},{5,7},{10,8},{14,9},{8,1... | collective-permute-start | bytes 884744 | tf_op jit(solution)/shard_map/ppermute | solution.py:39
  19.4 11.0 %collective-permute-start.1 = (bf16[384,384]{1,0:T(8,128)(2,1)S(1)}, bf16[384,384]{1,0:T(8,128)(2,1)S(1)}, u32[]{:S(2)}, u32[]{:S(2)}) collective-permute-start(bf16[384,384]{1,0:T(8,128)(2,1)S(1)} %get-tuple-element.29), channel_id=1, source_target_pairs={{1,0},{5,1},{3,2},{7,3},{0,4},{4,5},{2,6},{6,7},{9,8},{13,9},{11,1... | collective-permute-start | bytes 884744 | tf_op jit(solution)/shard_map/ppermute | solution.py:39
  31.8 16.8 %collective-permute-start.13 = (bf16[400,384]{1,0:T(8,128)(2,1)S(1)}, bf16[400,384]{1,0:T(8,128)(2,1)S(1)}, u32[]{:S(2)}, u32[]{:S(2)}) collective-permute-start(bf16[400,384]{1,0:T(8,128)(2,1)S(1)} %slice.36), channel_id=1, source_target_pairs={{16,0},{17,1},{18,2},{19,3},{20,4},{21,5},{22,6},{23,7},{24,8},{25... | collective-permute-start | bytes 921608 | tf_op jit(solution)/shard_map/ppermute | solution.py:39
  33.1 18.2 %collective-permute-start.12 = (bf16[400,384]{1,0:T(8,128)(2,1)S(1)}, bf16[400,384]{1,0:T(8,128)(2,1)S(1)}, u32[]{:S(2)}, u32[]{:S(2)}) collective-permute-start(bf16[400,384]{1,0:T(8,128)(2,1)S(1)} %slice.36), channel_id=1, source_target_pairs={{8,0},{9,1},{10,2},{11,3},{12,4},{13,5},{14,6},{15,7},{0,8},{1,9},... | collective-permute-start | bytes 921608 | tf_op jit(solution)/shard_map/ppermute | solution.py:39
  48.6 16.2 %collective-permute-start.14 = (bf16[400,384]{1,0:T(8,128)(2,1)S(1)}, bf16[400,384]{1,0:T(8,128)(2,1)S(1)}, u32[]{:S(2)}, u32[]{:S(2)}) collective-permute-start(bf16[400,384]{1,0:T(8,128)(2,1)S(1)} %collective-permute-done.13.refs_6_), channel_id=1, source_target_pairs={{8,0},{9,1},{10,2},{11,3},{12,4},{13,5},{14,6},{15,7},{0,8},{1,9},... | collective-permute-start | bytes 921608 | tf_op jit(solution)/shard_map/ppermute | solution.py:39
  48.6 9.0 %collective-permute-start.11 = (bf16[384,384]{1,0:T(8,128)(2,1)S(1)}, bf16[384,384]{1,0:T(8,128)(2,1)S(1)}, u32[]{:S(2)}, u32[]{:S(2)}) collective-permute-start(bf16[384,384]{1,0:T(8,128)(2,1)S(1)} %first.1.refs_0_), channel_id=1, source_target_pairs={{6,0},{7,1},{4,2},{5,3},{2,4},{3,5},{0,6},{1,7},{14,8},{15,9},{12,... | collective-permute-start | bytes 884744 | tf_op jit(solution)/shard_map/ppermute | solution.py:39
  50.1 12.9 %collective-permute-start.10 = (bf16[384,384]{1,0:T(8,128)(2,1)S(1)}, bf16[384,384]{1,0:T(8,128)(2,1)S(1)}, u32[]{:S(2)}, u32[]{:S(2)}) collective-permute-start(bf16[384,384]{1,0:T(8,128)(2,1)S(1)} %first.1.refs_0_), channel_id=1, source_target_pairs={{2,0},{3,1},{0,2},{1,3},{6,4},{7,5},{4,6},{5,7},{10,8},{11,9},{8,1... | collective-permute-start | bytes 884744 | tf_op jit(solution)/shard_map/ppermute | solution.py:39
  50.4 14.3 %collective-permute-start.9 = (bf16[384,384]{1,0:T(8,128)(2,1)S(1)}, bf16[384,384]{1,0:T(8,128)(2,1)S(1)}, u32[]{:S(2)}, u32[]{:S(2)}) collective-permute-start(bf16[384,384]{1,0:T(8,128)(2,1)S(1)} %first.1.refs_0_), channel_id=1, source_target_pairs={{4,0},{5,1},{6,2},{7,3},{0,4},{1,5},{2,6},{3,7},{12,8},{13,9},{14,... | collective-permute-start | bytes 884744 | tf_op jit(solution)/shard_map/ppermute | solution.py:39
  68.7 9.7 %collective-permute-start.22 = (bf16[192,384]{1,0:T(8,128)(2,1)S(1)}, bf16[192,384]{1,0:T(8,128)(2,1)S(1)}, u32[]{:S(2)}, u32[]{:S(2)}) collective-permute-start(bf16[192,384]{1,0:T(8,128)(2,1)S(1)} %generator.1.refs_0_), channel_id=1, source_target_pairs={{16,0},{17,1},{18,2},{19,3},{20,4},{21,5},{22,6},{23,7},{24,8},{25... | collective-permute-start | bytes 442376 | tf_op jit(solution)/shard_map/ppermute | solution.py:39
  80.4 8.3 %collective-permute-start.25 = (bf16[384,384]{1,0:T(8,128)(2,1)S(1)}, bf16[384,384]{1,0:T(8,128)(2,1)S(1)}, u32[]{:S(2)}, u32[]{:S(2)}) collective-permute-start(bf16[384,384]{1,0:T(8,128)(2,1)S(1)} %pad_maximum_fusion.8.refs_5_), channel_id=1, source_target_pairs={{6,0},{7,1},{4,2},{5,3},{2,4},{3,5},{0,6},{1,7},{14,8},{15,9},{12,... | collective-permute-start | bytes 884744 | tf_op jit(solution)/shard_map/ppermute | solution.py:39
  82.8 12.8 %collective-permute-start.24 = (bf16[384,384]{1,0:T(8,128)(2,1)S(1)}, bf16[384,384]{1,0:T(8,128)(2,1)S(1)}, u32[]{:S(2)}, u32[]{:S(2)}) collective-permute-start(bf16[384,384]{1,0:T(8,128)(2,1)S(1)} %pad_maximum_fusion.8.refs_5_), channel_id=1, source_target_pairs={{2,0},{3,1},{0,2},{1,3},{6,4},{7,5},{4,6},{5,7},{10,8},{11,9},{8,1... | collective-permute-start | bytes 884744 | tf_op jit(solution)/shard_map/ppermute | solution.py:39
  83.1 13.5 %collective-permute-start.23 = (bf16[384,384]{1,0:T(8,128)(2,1)S(1)}, bf16[384,384]{1,0:T(8,128)(2,1)S(1)}, u32[]{:S(2)}, u32[]{:S(2)}) collective-permute-start(bf16[384,384]{1,0:T(8,128)(2,1)S(1)} %pad_maximum_fusion.8.refs_5_), channel_id=1, source_target_pairs={{4,0},{5,1},{6,2},{7,3},{0,4},{1,5},{2,6},{3,7},{12,8},{13,9},{14,... | collective-permute-start | bytes 884744 | tf_op jit(solution)/shard_map/ppermute | solution.py:39
  96.7 13.0 %collective-permute-start.27 = (bf16[1536,384]{1,0:T(8,128)(2,1)S(1)}, bf16[1536,384]{1,0:T(8,128)(2,1)S(1)}, u32[]{:S(2)}, u32[]{:S(2)}) collective-permute-start(bf16[1536,384]{1,0:T(8,128)(2,1)S(1)} %pad_maximum_fusion), channel_id=1, source_target_pairs={{1,0},{0,1},{3,2},{2,3},{5,4},{4,5},{7,6},{6,7},{9,8},{8,9},{11,10... | collective-permute-start | bytes 3538952 | tf_op jit(solution)/shard_map/ppermute | solution.py:39
  99.7 7.4 %collective-permute-start.29 = (bf16[192,384]{1,0:T(8,128)(2,1)S(1)}, bf16[192,384]{1,0:T(8,128)(2,1)S(1)}, u32[]{:S(2)}, u32[]{:S(2)}) collective-permute-start(bf16[192,384]{1,0:T(8,128)(2,1)S(1)} %collective-permute-done.26.refs_10_), channel_id=1, source_target_pairs={{2,0},{3,1},{0,2},{1,3},{6,4},{7,5},{4,6},{5,7},{10,8},{11,9},{8,1... | collective-permute-start | bytes 442376 | tf_op jit(solution)/shard_map/ppermute | solution.py:39
  99.9 7.5 %collective-permute-start.28 = (bf16[192,384]{1,0:T(8,128)(2,1)S(1)}, bf16[192,384]{1,0:T(8,128)(2,1)S(1)}, u32[]{:S(2)}, u32[]{:S(2)}) collective-permute-start(bf16[192,384]{1,0:T(8,128)(2,1)S(1)} %collective-permute-done.26.refs_10_), channel_id=1, source_target_pairs={{4,0},{5,1},{6,2},{7,3},{0,4},{1,5},{2,6},{3,7},{12,8},{13,9},{14,... | collective-permute-start | bytes 442376 | tf_op jit(solution)/shard_map/ppermute | solution.py:39
  100.3 7.8 %collective-permute-start.20 = (bf16[768,384]{1,0:T(8,128)(2,1)S(1)}, bf16[768,384]{1,0:T(8,128)(2,1)S(1)}, u32[]{:S(2)}, u32[]{:S(2)}) collective-permute-start(bf16[768,384]{1,0:T(8,128)(2,1)S(1)} %pad_maximum_fusion.2), channel_id=1, source_target_pairs={{1,0},{0,1},{3,2},{2,3},{5,4},{4,5},{7,6},{6,7},{9,8},{8,9},{11,10... | collective-permute-start | bytes 1769480 | tf_op jit(solution)/shard_map/ppermute | solution.py:39
  120.9 7.4 %collective-permute-start.32 = (bf16[192,384]{1,0:T(8,128)(2,1)S(1)}, bf16[192,384]{1,0:T(8,128)(2,1)S(1)}, u32[]{:S(2)}, u32[]{:S(2)}) collective-permute-start(bf16[192,384]{1,0:T(8,128)(2,1)S(1)} %get-tuple-element.43.refs_0_), channel_id=1, source_target_pairs={{4,0},{5,1},{6,2},{7,3},{0,4},{1,5},{2,6},{3,7},{12,8},{13,9},{14,... | collective-permute-start | bytes 442376 | tf_op jit(solution)/shard_map/ppermute | solution.py:39
  131.5 9.2 %collective-permute-start.41 = (bf16[192,384]{1,0:T(8,128)(2,1)S(1)}, bf16[192,384]{1,0:T(8,128)(2,1)S(1)}, u32[]{:S(2)}, u32[]{:S(2)}) collective-permute-start(bf16[192,384]{1,0:T(8,128)(2,1)S(1)} %square.1.refs_0_), channel_id=1, source_target_pairs={{16,0},{17,1},{18,2},{19,3},{20,4},{21,5},{22,6},{23,7},{24,8},{25... | collective-permute-start | bytes 442376 | tf_op jit(solution)/shard_map/ppermute | solution.py:39
  132.8 7.9 %collective-permute-start.38 = (bf16[192,384]{1,0:T(8,128)(2,1)S(1)}, bf16[192,384]{1,0:T(8,128)(2,1)S(1)}, u32[]{:S(2)}, u32[]{:S(2)}) collective-permute-start(bf16[192,384]{1,0:T(8,128)(2,1)S(1)} %square.1.refs_0_), channel_id=1, source_target_pairs={{6,0},{7,1},{4,2},{5,3},{2,4},{3,5},{0,6},{1,7},{14,8},{15,9},{12,... | collective-permute-start | bytes 442376 | tf_op jit(solution)/shard_map/ppermute | solution.py:39
  134.3 8.3 %collective-permute-start.36 = (bf16[192,384]{1,0:T(8,128)(2,1)S(1)}, bf16[192,384]{1,0:T(8,128)(2,1)S(1)}, u32[]{:S(2)}, u32[]{:S(2)}) collective-permute-start(bf16[192,384]{1,0:T(8,128)(2,1)S(1)} %square.1.refs_0_), channel_id=1, source_target_pairs={{4,0},{5,1},{6,2},{7,3},{0,4},{1,5},{2,6},{3,7},{12,8},{13,9},{14,... | collective-permute-start | bytes 442376 | tf_op jit(solution)/shard_map/ppermute | solution.py:39
  135.4 7.8 %collective-permute-start.40 = (bf16[192,384]{1,0:T(8,128)(2,1)S(1)}, bf16[192,384]{1,0:T(8,128)(2,1)S(1)}, u32[]{:S(2)}, u32[]{:S(2)}) collective-permute-start(bf16[192,384]{1,0:T(8,128)(2,1)S(1)} %square.1.refs_0_), channel_id=1, source_target_pairs={{8,0},{9,1},{10,2},{11,3},{12,4},{13,5},{14,6},{15,7},{0,8},{1,9},... | collective-permute-start | bytes 442376 | tf_op jit(solution)/shard_map/ppermute | solution.py:39
  (27 other events, 122.2 us)

commit v8 on v7

--- a/solution.py
+++ b/solution.py
@@ -44,7 +44,7 @@
     def along_z(self, value, k):
         return self.move(value, lambda z, y, x, e: (2 * (z ^ k) + y, 2 * x + e))
 
-    def line(self, value, relabel=False, gate=None):
+    def line(self, value, relabel=False, second=None, gate=None):
         bits = [1 << b for b in range((self.rows // 2).bit_length() - 1)]
         held = {0: value}
         for bit in reversed(bits):
@@ -55,6 +55,8 @@
                     if k and gate is not None:
                         part, _ = lax.optimization_barrier((part, gate))
                     held[k | bit] = self.along_z(part, bit)
+            if second is not None:
+                held[0] = second
         return [held[k] for k in range(1, self.rows // 2)]
 
     def in_plane(self, value, s):
@@ -381,7 +383,7 @@
     masked_density = call(density_kernel, block, [INVMEM] * 2, [], "density")(
         density, fill_patterns
     )
-    later, fock_matrix, second_filters = barrier((masked_density, fock_matrix, second_filters))
+    later, second_filters = barrier((masked_density, second_filters))
     duo, trio = call(
         pair_kernel,
         [
@@ -396,12 +398,17 @@
 
     trio = moves.relabel(trio)
     fock_rows = moves.plane(duo, True)
-    density_line = moves.line(masked_density, True)
+    density_line = moves.line(masked_density, True, gate=trio)
     density_near = [(trio, TAIL + 2 * rows)] + whole(density_line)
-    density_line = list(barrier((*density_line, *fock_rows))[: count - 1])
+    pair = trio[: TAIL + 2 * rows]
+    pair_second, *_ = barrier((pair, *density_line))
+    pair_line = moves.line(pair, second=pair_second)
+    early = (*density_line, *fock_rows, pair_line[half - 1])
+    *density_line, pair_line[half - 1] = [
+        value for n, value in enumerate(barrier(early)) if n < count - 1 or n == len(early) - 1
+    ]
     trio_far = moves.core(trio)
     density_far = [(trio_far, TAIL + 2 * rows)] + moves.cores(density_line)
-    pair, *_ = barrier((trio[: TAIL + 2 * rows], *density_line, *fock_rows))
 
     products = views_call(
         functools.partial(first_kernel, count),
@@ -417,7 +424,6 @@
         10**10,
     )
     product_rows = [products] + moves.plane(products)
-    pair_line = moves.line(pair, gate=products)
     pair_line = list(barrier((*pair_line, *product_rows[1:]))[: count - 1])
     pair_far = [(trio_far, 0)] + moves.cores(pair_line[:half]) + moves.cores(pair_line[half:])
     pair_near = [(trio, 0)] + whole(pair_line)
@@ -436,16 +442,18 @@
     )
 
     lines = [generator] + moves.line(generator)
-    arrays, layout, planes = [], [], []
+    arrays, layout, planes, done = [], [], [], []
     for held in (range(1), range(1, half + 1), range(half + 1, count)):
-        group = jnp.concatenate([lines[k] for k in held], axis=0) if len(held) > 1 else lines[held[0]]
+        group = lines[held[0]]
         if len(held) > 1:
+            group = jnp.concatenate([lines[k] for k in held], axis=0)
+        if held[0] == 1:
             group, *planes = barrier((group, *planes))
         planes = [group] + moves.plane(group)
-        ready = planes
-        if 1 < len(held) < count - 1:
-            *ready, _ = barrier((*planes, *lines[half + 1 :]))[: count + 1]
-        far = moves.cores(ready)
+        done.append((held, planes))
+    done[1] = (done[1][0], list(barrier((*done[1][1], *done[2][1][1:]))[:count]))
+    for held, planes in done:
+        far = moves.cores(planes)
         for s, value in enumerate(planes):
             for lane, (array, start) in enumerate(((value, 0), far[s])):
                 if not any(other is array for other in arrays):

time: 157 us -> 149 us (0.949)
  waiting for transfers between devices: 87.2 us -> 75.3 us
  starting transfers between devices: 48.3 us -> 51.6 us
    ppermute x45, waiting for transfers between devices: 87.2 us -> 75.3 us  [move(): return lax.ppermute(value, AXES, permutation(self.rows, self.cols, source))]
    ppermute x45, starting transfers between devices: 48.3 us -> 51.6 us  [move(): return lax.ppermute(value, AXES, permutation(self.rows, self.cols, source))]
  transfers between devices with their start and end apart: 45 -> 45, of which waited for: 31 -> 30; matrix products, arithmetic and copies ran while one was open for 0% -> 0% of each run, Pallas kernels for 1% -> 1%
where the time goes in v8:
time: 149 us; the launch traced here: 148 us
  waiting for transfers between devices  75.3 us (51%)
  starting transfers between devices  51.6 us (35%)
  Pallas kernels  15.2 us (10%)
  local copies, waits for them, and re-layouts  5.61 us (4%)
    ppermute x45, waiting for transfers between devices, move(): return lax.ppermute(value, AXES, permutation(self.rows, self.cols, source))  75.3 us
    ppermute x45, starting transfers between devices, move(): return lax.ppermute(value, AXES, permutation(self.rows, self.cols, source))  51.6 us
    pallas_call x1, Pallas kernels, on_device(): call(functools.partial(series_kernel, layout, count, len(arrays)), [jax.S...  8.84 us
    unnamed x13, local copies, waits for them, and re-layouts  4.81 us
    pallas_call x4, Pallas kernels, views_call(): call(body, outs, [INVMEM] * len(operands), scratch, name, flops)(*operands)  4.52 us
  transfers between devices with their start and end apart: 45, of which 30 were waited for; matrix products, arithmetic and copies ran while one was open for 0% of the time, Pallas kernels for 1%

profile of v8, /device:TPU:1, one launch (start us, length us, event | category | flops | bytes accessed | tf_op | source)
XLA Modules:
  0.0 148.4 jit_solution(8263113077344466875)
XLA Ops:
  6.7 4.6 %collective-permute-start = (bf16[592,384]{1,0:T(8,128)(2,1)S(1)}, bf16[592,384]{1,0:T(8,128)(2,1)S(1)}, u32[]{:S(2)}, u32[]{:S(2)}) collective-permute-start(bf16[592,384]{1,0:T(8,128)(2,1)S(1)} %get-tuple-element.27), channel_id=1, source_target_pairs={{0,0},{4,1},{2,2},{6,3},{1,4},{5,5},{3,6},{7,7},{8,8},{12,9},{10,1... | collective-permute-start | bytes 1363976 | tf_op jit(solution)/shard_map/ppermute | solution.py:39
  13.4 4.3 %collective-permute-done.refs_0_.refs_4_.refs_5_.refs_9_ = bf16[592,384]{1,0:T(8,128)(2,1)S(1)} collective-permute-done((bf16[592,384]{1,0:T(8,128)(2,1)S(1)}, bf16[592,384]{1,0:T(8,128)(2,1)S(1)}, u32[]{:S(2)}, u32[]{:S(2)}) %collective-permute-start) | collective-permute-done | bytes 454688 | tf_op jit(solution)/shard_map/ppermute | solution.py:39
  17.7 3.5 %collective-permute-start.8 = (bf16[400,384]{1,0:T(8,128)(2,1)S(1)}, bf16[400,384]{1,0:T(8,128)(2,1)S(1)}, u32[]{:S(2)}, u32[]{:S(2)}) collective-permute-start(bf16[400,384]{1,0:T(8,128)(2,1)S(1)} %slice.36), channel_id=1, source_target_pairs={{16,0},{17,1},{18,2},{19,3},{20,4},{21,5},{22,6},{23,7},{24,8},{25... | collective-permute-start | bytes 921608 | tf_op jit(solution)/shard_map/ppermute | solution.py:39
  25.3 2.4 %collective-permute-done.4.refs_4_ = bf16[192,384]{1,0:T(8,128)(2,1)S(1)} collective-permute-done((bf16[192,384]{1,0:T(8,128)(2,1)S(1)}, bf16[192,384]{1,0:T(8,128)(2,1)S(1)}, u32[]{:S(2)}, u32[]{:S(2)}) %collective-permute-start.4) | collective-permute-done | bytes 147488 | tf_op jit(solution)/shard_map/ppermute | solution.py:39
  27.7 4.9 %collective-permute-start.6 = (bf16[192,384]{1,0:T(8,128)(2,1)S(1)}, bf16[192,384]{1,0:T(8,128)(2,1)S(1)}, u32[]{:S(2)}, u32[]{:S(2)}) collective-permute-start(bf16[192,384]{1,0:T(8,128)(2,1)S(1)} %collective-permute-done.5.refs_5_), channel_id=1, source_target_pairs={{8,0},{9,1},{10,2},{11,3},{12,4},{13,5},{14,6},{15,7},{0,8},{1,9},... | collective-permute-start | bytes 442376 | tf_op jit(solution)/shard_map/ppermute | solution.py:39
  32.6 5.1 %collective-permute-done.2.refs_2_ = bf16[384,384]{1,0:T(8,128)(2,1)S(1)} collective-permute-done((bf16[384,384]{1,0:T(8,128)(2,1)S(1)}, bf16[384,384]{1,0:T(8,128)(2,1)S(1)}, u32[]{:S(2)}, u32[]{:S(2)}) %collective-permute-start.2) | collective-permute-done | bytes 294944 | tf_op jit(solution)/shard_map/ppermute | solution.py:39
  41.5 2.5 %collective-permute-start.12 = (bf16[384,384]{1,0:T(8,128)(2,1)S(1)}, bf16[384,384]{1,0:T(8,128)(2,1)S(1)}, u32[]{:S(2)}, u32[]{:S(2)}) collective-permute-start(bf16[384,384]{1,0:T(8,128)(2,1)S(1)} %first.1.refs_0_), channel_id=1, source_target_pairs={{6,0},{7,1},{4,2},{5,3},{2,4},{3,5},{0,6},{1,7},{14,8},{15,9},{12,... | collective-permute-start | bytes 884744 | tf_op jit(solution)/shard_map/ppermute | solution.py:39
  44.3 3.4 %collective-permute-done.13.refs_5_ = bf16[400,384]{1,0:T(8,128)(2,1)S(1)} collective-permute-done((bf16[400,384]{1,0:T(8,128)(2,1)S(1)}, bf16[400,384]{1,0:T(8,128)(2,1)S(1)}, u32[]{:S(2)}, u32[]{:S(2)}) %collective-permute-start.13) | collective-permute-done | bytes 307232 | tf_op jit(solution)/shard_map/ppermute | solution.py:39
  47.7 6.6 %collective-permute-done.14.refs_7_ = bf16[400,384]{1,0:T(8,128)(2,1)S(1)} collective-permute-done((bf16[400,384]{1,0:T(8,128)(2,1)S(1)}, bf16[400,384]{1,0:T(8,128)(2,1)S(1)}, u32[]{:S(2)}, u32[]{:S(2)}) %collective-permute-start.14) | collective-permute-done | bytes 307232 | tf_op jit(solution)/shard_map/ppermute | solution.py:39
  54.3 2.4 %collective-permute-done.11.refs_2_ = bf16[384,384]{1,0:T(8,128)(2,1)S(1)} collective-permute-done((bf16[384,384]{1,0:T(8,128)(2,1)S(1)}, bf16[384,384]{1,0:T(8,128)(2,1)S(1)}, u32[]{:S(2)}, u32[]{:S(2)}) %collective-permute-start.11) | collective-permute-done | bytes 294944 | tf_op jit(solution)/shard_map/ppermute | solution.py:39
  65.9 5.0 %collective-permute-done.22 = bf16[192,384]{1,0:T(8,128)(2,1)S(1)} collective-permute-done((bf16[192,384]{1,0:T(8,128)(2,1)S(1)}, bf16[192,384]{1,0:T(8,128)(2,1)S(1)}, u32[]{:S(2)}, u32[]{:S(2)}) %collective-permute-start.22) | collective-permute-done | bytes 147488 | tf_op jit(solution)/shard_map/ppermute | solution.py:39
  76.2 3.1 %collective-permute-done.26.refs_10_ = bf16[192,384]{1,0:T(8,128)(2,1)S(1)} collective-permute-done((bf16[192,384]{1,0:T(8,128)(2,1)S(1)}, bf16[192,384]{1,0:T(8,128)(2,1)S(1)}, u32[]{:S(2)}, u32[]{:S(2)}) %collective-permute-start.26) | collective-permute-done | bytes 147488 | tf_op jit(solution)/shard_map/ppermute | solution.py:39
  82.7 5.1 %collective-permute-done.24.refs_8_ = bf16[384,384]{1,0:T(8,128)(2,1)S(1)} collective-permute-done((bf16[384,384]{1,0:T(8,128)(2,1)S(1)}, bf16[384,384]{1,0:T(8,128)(2,1)S(1)}, u32[]{:S(2)}, u32[]{:S(2)}) %collective-permute-start.24) | collective-permute-done | bytes 294944 | tf_op jit(solution)/shard_map/ppermute | solution.py:39
  87.8 2.2 %collective-permute-done.23.refs_7_ = bf16[384,384]{1,0:T(8,128)(2,1)S(1)} collective-permute-done((bf16[384,384]{1,0:T(8,128)(2,1)S(1)}, bf16[384,384]{1,0:T(8,128)(2,1)S(1)}, u32[]{:S(2)}, u32[]{:S(2)}) %collective-permute-start.23) | collective-permute-done | bytes 294944 | tf_op jit(solution)/shard_map/ppermute | solution.py:39
  90.0 4.1 %collective-permute-done.28.refs_13_ = bf16[192,384]{1,0:T(8,128)(2,1)S(1)} collective-permute-done((bf16[192,384]{1,0:T(8,128)(2,1)S(1)}, bf16[192,384]{1,0:T(8,128)(2,1)S(1)}, u32[]{:S(2)}, u32[]{:S(2)}) %collective-permute-start.28) | collective-permute-done | bytes 147488 | tf_op jit(solution)/shard_map/ppermute | solution.py:39
  96.7 2.5 %collective-permute-done.20.refs_1_ = bf16[768,384]{1,0:T(8,128)(2,1)S(1)} collective-permute-done((bf16[768,384]{1,0:T(8,128)(2,1)S(1)}, bf16[768,384]{1,0:T(8,128)(2,1)S(1)}, u32[]{:S(2)}, u32[]{:S(2)}) %collective-permute-start.20) | collective-permute-done | bytes 589856 | tf_op jit(solution)/shard_map/ppermute | solution.py:39
  100.1 8.8 %series.1 = (bf16[192,1536]{1,0:T(8,128)(2,1)S(1)}, bf16[192,384]{1,0:T(8,128)(2,1)S(1)}) custom-call(bf16[192,384]{1,0:T(8,128)(2,1)S(1)} %generator.1.refs_0_, bf16[768,384]{1,0:T(8,128)(2,1)S(1)} %collective-permute-done.20.refs_1_, bf16[192,384]{1,0:T(8,128)(2,1)S(1)} %collective-permute-done.17.refs_2_, ...), custom_call_target="tpu_custom_call" | custom-call | flops 1000 | bytes 1000 | tf_op jit(solution)/shard_map/series/pallas_call | solution.py:466
  111.7 3.3 %collective-permute-done.34.refs_3_ = bf16[192,384]{1,0:T(8,128)(2,1)S(1)} collective-permute-done((bf16[192,384]{1,0:T(8,128)(2,1)S(1)}, bf16[192,384]{1,0:T(8,128)(2,1)S(1)}, u32[]{:S(2)}, u32[]{:S(2)}) %collective-permute-start.34) | collective-permute-done | bytes 147488 | tf_op jit(solution)/shard_map/ppermute | solution.py:39
  115.0 3.1 %collective-permute-done.33.refs_2_ = bf16[192,384]{1,0:T(8,128)(2,1)S(1)} collective-permute-done((bf16[192,384]{1,0:T(8,128)(2,1)S(1)}, bf16[192,384]{1,0:T(8,128)(2,1)S(1)}, u32[]{:S(2)}, u32[]{:S(2)}) %collective-permute-start.33) | collective-permute-done | bytes 147488 | tf_op jit(solution)/shard_map/ppermute | solution.py:39
  121.8 2.1 %collective-permute-start.41 = (bf16[192,384]{1,0:T(8,128)(2,1)S(1)}, bf16[192,384]{1,0:T(8,128)(2,1)S(1)}, u32[]{:S(2)}, u32[]{:S(2)}) collective-permute-start(bf16[192,384]{1,0:T(8,128)(2,1)S(1)} %square.1.refs_0_), channel_id=1, source_target_pairs={{16,0},{17,1},{18,2},{19,3},{20,4},{21,5},{22,6},{23,7},{24,8},{25... | collective-permute-start | bytes 442376 | tf_op jit(solution)/shard_map/ppermute | solution.py:39
  126.8 4.3 %collective-permute-done.41.refs_6_ = bf16[192,384]{1,0:T(8,128)(2,1)S(1)} collective-permute-done((bf16[192,384]{1,0:T(8,128)(2,1)S(1)}, bf16[192,384]{1,0:T(8,128)(2,1)S(1)}, u32[]{:S(2)}, u32[]{:S(2)}) %collective-permute-start.41) | collective-permute-done | bytes 147488 | tf_op jit(solution)/shard_map/ppermute | solution.py:39
  134.6 2.7 %collective-permute-done.42.refs_7_ = bf16[192,384]{1,0:T(8,128)(2,1)S(1)} collective-permute-done((bf16[192,384]{1,0:T(8,128)(2,1)S(1)}, bf16[192,384]{1,0:T(8,128)(2,1)S(1)}, u32[]{:S(2)}, u32[]{:S(2)}) %collective-permute-start.42) | collective-permute-done | bytes 147488 | tf_op jit(solution)/shard_map/ppermute | solution.py:39
  141.3 3.3 %collective-permute-start.44 = (bf16[192,384]{1,0:T(8,128)(2,1)S(1)}, bf16[192,384]{1,0:T(8,128)(2,1)S(1)}, u32[]{:S(2)}, u32[]{:S(2)}) collective-permute-start(bf16[192,384]{1,0:T(8,128)(2,1)S(1)} %evolve.1), channel_id=1, source_target_pairs={{0,0},{4,1},{2,2},{6,3},{1,4},{5,5},{3,6},{7,7},{8,8},{12,9},{10,1... | collective-permute-start | bytes 442376 | tf_op jit(solution)/shard_map/ppermute | solution.py:39
  144.6 3.2 %collective-permute-done.44 = bf16[192,384]{1,0:T(8,128)(2,1)S(1)} collective-permute-done((bf16[192,384]{1,0:T(8,128)(2,1)S(1)}, bf16[192,384]{1,0:T(8,128)(2,1)S(1)}, u32[]{:S(2)}, u32[]{:S(2)}) %collective-permute-start.44) | collective-permute-done | bytes 147488 | tf_op jit(solution)/shard_map/ppermute | solution.py:39
  (104 shorter events, 55.6 us)
Async XLA Ops:
  6.7 11.0 %collective-permute-start = (bf16[592,384]{1,0:T(8,128)(2,1)S(1)}, bf16[592,384]{1,0:T(8,128)(2,1)S(1)}, u32[]{:S(2)}, u32[]{:S(2)}) collective-permute-start(bf16[592,384]{1,0:T(8,128)(2,1)S(1)} %get-tuple-element.27), channel_id=1, source_target_pairs={{0,0},{4,1},{2,2},{6,3},{1,4},{5,5},{3,6},{7,7},{8,8},{12,9},{10,1... | collective-permute-start | bytes 1363976 | tf_op jit(solution)/shard_map/ppermute | solution.py:39
  11.3 13.1 %collective-permute-start.5 = (bf16[192,384]{1,0:T(8,128)(2,1)S(1)}, bf16[192,384]{1,0:T(8,128)(2,1)S(1)}, u32[]{:S(2)}, u32[]{:S(2)}) collective-permute-start(bf16[192,384]{1,0:T(8,128)(2,1)S(1)} %density.2), channel_id=1, source_target_pairs={{16,0},{20,1},{18,2},{22,3},{17,4},{21,5},{19,6},{23,7},{24,8},{28... | collective-permute-start | bytes 442376 | tf_op jit(solution)/shard_map/ppermute | solution.py:39
  17.7 20.0 %collective-permute-start.8 = (bf16[400,384]{1,0:T(8,128)(2,1)S(1)}, bf16[400,384]{1,0:T(8,128)(2,1)S(1)}, u32[]{:S(2)}, u32[]{:S(2)}) collective-permute-start(bf16[400,384]{1,0:T(8,128)(2,1)S(1)} %slice.36), channel_id=1, source_target_pairs={{16,0},{17,1},{18,2},{19,3},{20,4},{21,5},{22,6},{23,7},{24,8},{25... | collective-permute-start | bytes 921608 | tf_op jit(solution)/shard_map/ppermute | solution.py:39
  22.8 9.8 %collective-permute-start.3 = (bf16[384,384]{1,0:T(8,128)(2,1)S(1)}, bf16[384,384]{1,0:T(8,128)(2,1)S(1)}, u32[]{:S(2)}, u32[]{:S(2)}) collective-permute-start(bf16[384,384]{1,0:T(8,128)(2,1)S(1)} %get-tuple-element.28), channel_id=1, source_target_pairs={{3,0},{7,1},{1,2},{5,3},{2,4},{6,5},{0,6},{4,7},{11,8},{15,9},{9,1... | collective-permute-start | bytes 884744 | tf_op jit(solution)/shard_map/ppermute | solution.py:39
  22.8 14.9 %collective-permute-start.2 = (bf16[384,384]{1,0:T(8,128)(2,1)S(1)}, bf16[384,384]{1,0:T(8,128)(2,1)S(1)}, u32[]{:S(2)}, u32[]{:S(2)}) collective-permute-start(bf16[384,384]{1,0:T(8,128)(2,1)S(1)} %get-tuple-element.28), channel_id=1, source_target_pairs={{2,0},{6,1},{0,2},{4,3},{3,4},{7,5},{1,6},{5,7},{10,8},{14,9},{8,1... | collective-permute-start | bytes 884744 | tf_op jit(solution)/shard_map/ppermute | solution.py:39
  24.3 13.3 %collective-permute-start.1 = (bf16[384,384]{1,0:T(8,128)(2,1)S(1)}, bf16[384,384]{1,0:T(8,128)(2,1)S(1)}, u32[]{:S(2)}, u32[]{:S(2)}) collective-permute-start(bf16[384,384]{1,0:T(8,128)(2,1)S(1)} %get-tuple-element.28), channel_id=1, source_target_pairs={{1,0},{5,1},{3,2},{7,3},{0,4},{4,5},{2,6},{6,7},{9,8},{13,9},{11,1... | collective-permute-start | bytes 884744 | tf_op jit(solution)/shard_map/ppermute | solution.py:39
  27.7 10.0 %collective-permute-start.6 = (bf16[192,384]{1,0:T(8,128)(2,1)S(1)}, bf16[192,384]{1,0:T(8,128)(2,1)S(1)}, u32[]{:S(2)}, u32[]{:S(2)}) collective-permute-start(bf16[192,384]{1,0:T(8,128)(2,1)S(1)} %collective-permute-done.5.refs_5_), channel_id=1, source_target_pairs={{8,0},{9,1},{10,2},{11,3},{12,4},{13,5},{14,6},{15,7},{0,8},{1,9},... | collective-permute-start | bytes 442376 | tf_op jit(solution)/shard_map/ppermute | solution.py:39
  38.5 9.3 %collective-permute-start.13 = (bf16[400,384]{1,0:T(8,128)(2,1)S(1)}, bf16[400,384]{1,0:T(8,128)(2,1)S(1)}, u32[]{:S(2)}, u32[]{:S(2)}) collective-permute-start(bf16[400,384]{1,0:T(8,128)(2,1)S(1)} %slice.36), channel_id=1, source_target_pairs={{8,0},{9,1},{10,2},{11,3},{12,4},{13,5},{14,6},{15,7},{0,8},{1,9},... | collective-permute-start | bytes 921608 | tf_op jit(solution)/shard_map/ppermute | solution.py:39
  40.2 14.1 %collective-permute-start.14 = (bf16[400,384]{1,0:T(8,128)(2,1)S(1)}, bf16[400,384]{1,0:T(8,128)(2,1)S(1)}, u32[]{:S(2)}, u32[]{:S(2)}) collective-permute-start(bf16[400,384]{1,0:T(8,128)(2,1)S(1)} %collective-permute-done.8.refs_6_), channel_id=1, source_target_pairs={{8,0},{9,1},{10,2},{11,3},{12,4},{13,5},{14,6},{15,7},{0,8},{1,9},... | collective-permute-start | bytes 921608 | tf_op jit(solution)/shard_map/ppermute | solution.py:39
  41.5 12.9 %collective-permute-start.12 = (bf16[384,384]{1,0:T(8,128)(2,1)S(1)}, bf16[384,384]{1,0:T(8,128)(2,1)S(1)}, u32[]{:S(2)}, u32[]{:S(2)}) collective-permute-start(bf16[384,384]{1,0:T(8,128)(2,1)S(1)} %first.1.refs_0_), channel_id=1, source_target_pairs={{6,0},{7,1},{4,2},{5,3},{2,4},{3,5},{0,6},{1,7},{14,8},{15,9},{12,... | collective-permute-start | bytes 884744 | tf_op jit(solution)/shard_map/ppermute | solution.py:39
  43.9 12.8 %collective-permute-start.11 = (bf16[384,384]{1,0:T(8,128)(2,1)S(1)}, bf16[384,384]{1,0:T(8,128)(2,1)S(1)}, u32[]{:S(2)}, u32[]{:S(2)}) collective-permute-start(bf16[384,384]{1,0:T(8,128)(2,1)S(1)} %first.1.refs_0_), channel_id=1, source_target_pairs={{2,0},{3,1},{0,2},{1,3},{6,4},{7,5},{4,6},{5,7},{10,8},{11,9},{8,1... | collective-permute-start | bytes 884744 | tf_op jit(solution)/shard_map/ppermute | solution.py:39
  43.9 13.8 %collective-permute-start.10 = (bf16[384,384]{1,0:T(8,128)(2,1)S(1)}, bf16[384,384]{1,0:T(8,128)(2,1)S(1)}, u32[]{:S(2)}, u32[]{:S(2)}) collective-permute-start(bf16[384,384]{1,0:T(8,128)(2,1)S(1)} %first.1.refs_0_), channel_id=1, source_target_pairs={{4,0},{5,1},{6,2},{7,3},{0,4},{1,5},{2,6},{3,7},{12,8},{13,9},{14,... | collective-permute-start | bytes 884744 | tf_op jit(solution)/shard_map/ppermute | solution.py:39
  61.7 9.2 %collective-permute-start.22 = (bf16[192,384]{1,0:T(8,128)(2,1)S(1)}, bf16[192,384]{1,0:T(8,128)(2,1)S(1)}, u32[]{:S(2)}, u32[]{:S(2)}) collective-permute-start(bf16[192,384]{1,0:T(8,128)(2,1)S(1)} %generator.1.refs_0_), channel_id=1, source_target_pairs={{16,0},{17,1},{18,2},{19,3},{20,4},{21,5},{22,6},{23,7},{24,8},{25... | collective-permute-start | bytes 442376 | tf_op jit(solution)/shard_map/ppermute | solution.py:39
  63.0 7.9 %collective-permute-start.21 = (bf16[192,384]{1,0:T(8,128)(2,1)S(1)}, bf16[192,384]{1,0:T(8,128)(2,1)S(1)}, u32[]{:S(2)}, u32[]{:S(2)}) collective-permute-start(bf16[192,384]{1,0:T(8,128)(2,1)S(1)} %generator.1.refs_0_), channel_id=1, source_target_pairs={{8,0},{9,1},{10,2},{11,3},{12,4},{13,5},{14,6},{15,7},{0,8},{1,9},... | collective-permute-start | bytes 442376 | tf_op jit(solution)/shard_map/ppermute | solution.py:39
  63.2 7.7 %collective-permute-start.19 = (bf16[192,384]{1,0:T(8,128)(2,1)S(1)}, bf16[192,384]{1,0:T(8,128)(2,1)S(1)}, u32[]{:S(2)}, u32[]{:S(2)}) collective-permute-start(bf16[192,384]{1,0:T(8,128)(2,1)S(1)} %generator.1.refs_0_), channel_id=1, source_target_pairs={{6,0},{7,1},{4,2},{5,3},{2,4},{3,5},{0,6},{1,7},{14,8},{15,9},{12,... | collective-permute-start | bytes 442376 | tf_op jit(solution)/shard_map/ppermute | solution.py:39
  72.5 8.4 %collective-permute-start.25 = (bf16[384,384]{1,0:T(8,128)(2,1)S(1)}, bf16[384,384]{1,0:T(8,128)(2,1)S(1)}, u32[]{:S(2)}, u32[]{:S(2)}) collective-permute-start(bf16[384,384]{1,0:T(8,128)(2,1)S(1)} %pad_maximum_fusion.8.refs_5_), channel_id=1, source_target_pairs={{6,0},{7,1},{4,2},{5,3},{2,4},{3,5},{0,6},{1,7},{14,8},{15,9},{12,... | collective-permute-start | bytes 884744 | tf_op jit(solution)/shard_map/ppermute | solution.py:39
  73.9 13.9 %collective-permute-start.24 = (bf16[384,384]{1,0:T(8,128)(2,1)S(1)}, bf16[384,384]{1,0:T(8,128)(2,1)S(1)}, u32[]{:S(2)}, u32[]{:S(2)}) collective-permute-start(bf16[384,384]{1,0:T(8,128)(2,1)S(1)} %pad_maximum_fusion.8.refs_5_), channel_id=1, source_target_pairs={{2,0},{3,1},{0,2},{1,3},{6,4},{7,5},{4,6},{5,7},{10,8},{11,9},{8,1... | collective-permute-start | bytes 884744 | tf_op jit(solution)/shard_map/ppermute | solution.py:39
  76.1 13.9 %collective-permute-start.23 = (bf16[384,384]{1,0:T(8,128)(2,1)S(1)}, bf16[384,384]{1,0:T(8,128)(2,1)S(1)}, u32[]{:S(2)}, u32[]{:S(2)}) collective-permute-start(bf16[384,384]{1,0:T(8,128)(2,1)S(1)} %pad_maximum_fusion.8.refs_5_), channel_id=1, source_target_pairs={{4,0},{5,1},{6,2},{7,3},{0,4},{1,5},{2,6},{3,7},{12,8},{13,9},{14,... | collective-permute-start | bytes 884744 | tf_op jit(solution)/shard_map/ppermute | solution.py:39
  79.4 10.7 %collective-permute-start.29 = (bf16[192,384]{1,0:T(8,128)(2,1)S(1)}, bf16[192,384]{1,0:T(8,128)(2,1)S(1)}, u32[]{:S(2)}, u32[]{:S(2)}) collective-permute-start(bf16[192,384]{1,0:T(8,128)(2,1)S(1)} %collective-permute-done.26.refs_10_), channel_id=1, source_target_pairs={{6,0},{7,1},{4,2},{5,3},{2,4},{3,5},{0,6},{1,7},{14,8},{15,9},{12,... | collective-permute-start | bytes 442376 | tf_op jit(solution)/shard_map/ppermute | solution.py:39
  79.8 14.4 %collective-permute-start.28 = (bf16[192,384]{1,0:T(8,128)(2,1)S(1)}, bf16[192,384]{1,0:T(8,128)(2,1)S(1)}, u32[]{:S(2)}, u32[]{:S(2)}) collective-permute-start(bf16[192,384]{1,0:T(8,128)(2,1)S(1)} %collective-permute-done.26.refs_10_), channel_id=1, source_target_pairs={{2,0},{3,1},{0,2},{1,3},{6,4},{7,5},{4,6},{5,7},{10,8},{11,9},{8,1... | collective-permute-start | bytes 442376 | tf_op jit(solution)/shard_map/ppermute | solution.py:39
  80.8 14.1 %collective-permute-start.27 = (bf16[192,384]{1,0:T(8,128)(2,1)S(1)}, bf16[192,384]{1,0:T(8,128)(2,1)S(1)}, u32[]{:S(2)}, u32[]{:S(2)}) collective-permute-start(bf16[192,384]{1,0:T(8,128)(2,1)S(1)} %collective-permute-done.26.refs_10_), channel_id=1, source_target_pairs={{4,0},{5,1},{6,2},{7,3},{0,4},{1,5},{2,6},{3,7},{12,8},{13,9},{14,... | collective-permute-start | bytes 442376 | tf_op jit(solution)/shard_map/ppermute | solution.py:39
  110.2 7.9 %collective-permute-start.33 = (bf16[192,384]{1,0:T(8,128)(2,1)S(1)}, bf16[192,384]{1,0:T(8,128)(2,1)S(1)}, u32[]{:S(2)}, u32[]{:S(2)}) collective-permute-start(bf16[192,384]{1,0:T(8,128)(2,1)S(1)} %get-tuple-element.43.refs_0_), channel_id=1, source_target_pairs={{2,0},{3,1},{0,2},{1,3},{6,4},{7,5},{4,6},{5,7},{10,8},{11,9},{8,1... | collective-permute-start | bytes 442376 | tf_op jit(solution)/shard_map/ppermute | solution.py:39
  121.8 9.3 %collective-permute-start.41 = (bf16[192,384]{1,0:T(8,128)(2,1)S(1)}, bf16[192,384]{1,0:T(8,128)(2,1)S(1)}, u32[]{:S(2)}, u32[]{:S(2)}) collective-permute-start(bf16[192,384]{1,0:T(8,128)(2,1)S(1)} %square.1.refs_0_), channel_id=1, source_target_pairs={{16,0},{17,1},{18,2},{19,3},{20,4},{21,5},{22,6},{23,7},{24,8},{25... | collective-permute-start | bytes 442376 | tf_op jit(solution)/shard_map/ppermute | solution.py:39
  126.6 8.0 %collective-permute-start.40 = (bf16[192,384]{1,0:T(8,128)(2,1)S(1)}, bf16[192,384]{1,0:T(8,128)(2,1)S(1)}, u32[]{:S(2)}, u32[]{:S(2)}) collective-permute-start(bf16[192,384]{1,0:T(8,128)(2,1)S(1)} %square.1.refs_0_), channel_id=1, source_target_pairs={{8,0},{9,1},{10,2},{11,3},{12,4},{13,5},{14,6},{15,7},{0,8},{1,9},... | collective-permute-start | bytes 442376 | tf_op jit(solution)/shard_map/ppermute | solution.py:39
  (27 other events, 120.9 us)

commit v9 on v8

--- a/solution.py
+++ b/solution.py
@@ -146,34 +146,37 @@
 INSMEM = pl.BlockSpec(memory_space=pltpu.SMEM)
 
 
-def masked(ref, fill):
-    rows, columns = ref.shape
-    tall = repeat_rows(rows, fill.shape[0])
-    wide = repeat_columns(fill.shape[1], columns)
-    mask = dot(dot(tall, fill.astype(BF16)).astype(BF16), wide)
-    return (ref[...].astype(F32) * mask).astype(BF16)
-
-
-def density_kernel(density, fills, out):
-    out[...] = masked(density, fills[1])
-
-
-def pair_kernel(fock, margin, density, fills, firsts, seconds, duo, trio):
-    rows, columns = fock.shape
+def mask_kernel(inputs, *refs):
+    sources, (tailed, duo) = refs[:inputs], refs[inputs : inputs + 2]
+    held, sems = refs[inputs + 2 : -1], refs[-1]
+    copies = [
+        pltpu.make_async_copy(source, target, sems.at[n])
+        for n, (source, target) in enumerate(zip(sources, held))
+    ]
+    fills, density, fock, margin, firsts, seconds = held
+    rows, columns = density.shape
     row_blocks, column_blocks = rows // BLK, columns // BLK
-    for half, (ref, number) in enumerate(((fock, 0), (margin, 2))):
-        value = masked(ref, fills[number])
-        duo[half * rows : (half + 1) * rows, :] = value
-        trio[TAIL + half * rows : TAIL + (half + 1) * rows, :] = value
-    trio[TAIL + 2 * rows :, :] = density[...]
+    start_all(copies)
+    tall = repeat_rows(rows, row_blocks)
+    wide = repeat_columns(column_blocks, columns)
+
+    def masked(ref, number):
+        mask = dot(dot(tall, fills[number].astype(BF16)).astype(BF16), wide)
+        return (ref[...].astype(F32) * mask).astype(BF16)
+
+    wait_all(copies[:2])
+    tailed[TAIL:, :] = masked(density, 1)
+    wait_all(copies[2:])
+    duo[:rows, :] = masked(fock, 0)
+    duo[rows:, :] = masked(margin, 2)
     top = (iota((TAIL, row_blocks), 0) == iota((TAIL, row_blocks), 1)).astype(BF16)
     tail = jnp.zeros((TAIL, columns), F32)
-    for number in range(firsts.shape[0] + seconds.shape[0]):
-        ref = firsts[number] if number < FIRST else seconds[number - FIRST]
+    for number in range(FIRST + seconds.shape[1]):
+        block = firsts[number] if number < FIRST else seconds[:, number - FIRST, :]
         column = iota((column_blocks, columns), 1) - number * column_blocks
         spread = (iota((column_blocks, columns), 0) == column).astype(BF16)
-        tail += dot(dot(top, ref.astype(BF16)).astype(BF16), spread)
-    trio[:TAIL, :] = tail.astype(BF16)
+        tail += dot(dot(top, block.astype(BF16)).astype(BF16), spread)
+    tailed[:TAIL, :] = tail.astype(BF16)
 
 
 def chunk(index, length):
@@ -380,43 +383,43 @@
     def whole(values):
         return [(value, 0) for value in values]
 
-    masked_density = call(density_kernel, block, [INVMEM] * 2, [], "density")(
-        density, fill_patterns
-    )
-    later, second_filters = barrier((masked_density, second_filters))
-    duo, trio = call(
-        pair_kernel,
+    inputs = (
+        fill_patterns,
+        density,
+        fock_matrix,
+        margin,
+        first_filters,
+        second_filters.transpose(1, 0, 2),
+    )
+    tailed, duo = call(
+        functools.partial(mask_kernel, len(inputs)),
         [
+            jax.ShapeDtypeStruct((TAIL + rows, columns), BF16),
             jax.ShapeDtypeStruct((2 * rows, columns), BF16),
-            jax.ShapeDtypeStruct((TAIL + 3 * rows, columns), BF16),
         ],
-        [INVMEM] * 6,
-        [],
-        "pair",
-        10**10,
-    )(fock_matrix, margin, later, fill_patterns, first_filters, second_filters)
-
-    trio = moves.relabel(trio)
+        [pl.BlockSpec(memory_space=pltpu.HBM)] * len(inputs),
+        [pltpu.VMEM(value.shape, value.dtype) for value in inputs]
+        + [pltpu.SemaphoreType.DMA((len(inputs),))],
+        "mask",
+    )(*inputs)
+
+    pair = moves.relabel(duo)
     fock_rows = moves.plane(duo, True)
-    density_line = moves.line(masked_density, True, gate=trio)
-    density_near = [(trio, TAIL + 2 * rows)] + whole(density_line)
-    pair = trio[: TAIL + 2 * rows]
+    density_line = [moves.relabel(tailed)] + moves.line(tailed, True)
     pair_second, *_ = barrier((pair, *density_line))
     pair_line = moves.line(pair, second=pair_second)
-    early = (*density_line, *fock_rows, pair_line[half - 1])
-    *density_line, pair_line[half - 1] = [
-        value for n, value in enumerate(barrier(early)) if n < count - 1 or n == len(early) - 1
-    ]
-    trio_far = moves.core(trio)
-    density_far = [(trio_far, TAIL + 2 * rows)] + moves.cores(density_line)
+    ready = list(barrier((*density_line, *fock_rows, pair))[:count])
+    density_far = moves.cores(ready)
+    density_near = whole(density_line)
+    other = moves.core(pair)
 
     products = views_call(
         functools.partial(first_kernel, count),
         {
-            "plane": [(trio, TAIL)] + whole(fock_rows),
-            "tail": [(trio, 0)],
-            "near": density_near,
-            "far": density_far,
+            "plane": whole([pair] + fock_rows),
+            "tail": density_near,
+            "near": [(value, first + TAIL) for value, first in density_near],
+            "far": [(value, first + TAIL) for value, first in density_far],
         },
         jax.ShapeDtypeStruct((2 * rows, columns), BF16),
         [pltpu.VMEM((count, 2 * rows, columns), BF16)],
@@ -425,16 +428,16 @@
     )
     product_rows = [products] + moves.plane(products)
     pair_line = list(barrier((*pair_line, *product_rows[1:]))[: count - 1])
-    pair_far = [(trio_far, 0)] + moves.cores(pair_line[:half]) + moves.cores(pair_line[half:])
-    pair_near = [(trio, 0)] + whole(pair_line)
+    pair_far = [(other, 0)] + moves.cores(pair_line[:half]) + moves.cores(pair_line[half:])
+    pair_near = whole([pair] + pair_line)
 
     generator = views_call(
         functools.partial(generator_kernel, count),
         {
             "plane": whole(product_rows),
-            "tail": [(trio, 0)],
-            "near": [(value, first + TAIL) for value, first in pair_near],
-            "far": [(value, first + TAIL) for value, first in pair_far],
+            "tail": density_near,
+            "near": pair_near,
+            "far": pair_far,
         },
         block,
         [pltpu.VMEM((2, count, rows, columns), BF16)],
@@ -442,18 +445,22 @@
     )
 
     lines = [generator] + moves.line(generator)
-    arrays, layout, planes, done = [], [], [], []
+    arrays, layout, done, own_far = [], [], [], []
     for held in (range(1), range(1, half + 1), range(half + 1, count)):
         group = lines[held[0]]
         if len(held) > 1:
             group = jnp.concatenate([lines[k] for k in held], axis=0)
         if held[0] == 1:
-            group, *planes = barrier((group, *planes))
+            group, *_ = barrier((group, *done[0][1]))
+        if held[0] > 1:
+            group, _ = barrier((group, own_far[0][0]))
         planes = [group] + moves.plane(group)
+        if held[0] == 0:
+            own_far = moves.cores(planes)
         done.append((held, planes))
     done[1] = (done[1][0], list(barrier((*done[1][1], *done[2][1][1:]))[:count]))
     for held, planes in done:
-        far = moves.cores(planes)
+        far = own_far if held[0] == 0 else moves.cores(planes)
         for s, value in enumerate(planes):
             for lane, (array, start) in enumerate(((value, 0), far[s])):
                 if not any(other is array for other in arrays):
@@ -461,7 +468,7 @@
                 index = [n for n, other in enumerate(arrays) if other is array][0]
                 for n, k in enumerate(held):
                     layout.append((index, start + n * rows, k, s, lane))
-    tails = [value[first : first + TAIL] for value, first in pair_near + pair_far]
+    tails = [value[first : first + TAIL] for value, first in density_near + density_far]
 
     panel, mine = call(
         functools.partial(series_kernel, layout, count, len(arrays)),
@@ -481,7 +488,7 @@
     near = [mine] + moves.plane(mine)
     square = views_call(
         functools.partial(square_kernel, count),
-        {"near": whole(near), "far": moves.cores(near), "tail": [(trio, 0), (trio_far, 0)]},
+        {"near": whole(near), "far": moves.cores(near), "tail": [density_near[0], density_far[0]]},
         block,
         [],
         "square",
@@ -498,7 +505,7 @@
             "plane_far": plane_far,
             "line_near": whole([square] + line),
             "line_far": plane_far[:1] + moves.cores(line),
-            "tail": [(trio, 0)],
+            "tail": density_near,
         },
         block,
         [pltpu.VMEM((count, columns, columns), BF16)],

time: 149 us -> 170 us (1.14)
  waiting for transfers between devices: 75.3 us -> 95.3 us
    ppermute x45 -> x46, waiting for transfers between devices: 75.3 us -> 95.3 us  [move(): return lax.ppermute(value, AXES, permutation(self.rows, self.cols, source))]
    ppermute x45 -> x46, starting transfers between devices: 51.6 us -> 52.5 us  [move(): return lax.ppermute(value, AXES, permutation(self.rows, self.cols, source))]
    unnamed x13 -> x15, local copies, waits for them, and re-layouts: 4.81 us -> 5.55 us
  transfers between devices with their start and end apart: 45 -> 46, of which waited for: 30 -> 29; matrix products, arithmetic and copies ran while one was open for 0% -> 0% of each run, Pallas kernels for 1% -> 1%
where the time goes in v9:
time: 170 us
  waiting for transfers between devices  95.3 us (56%)
  starting transfers between devices  52.5 us (31%)
  Pallas kernels  15.7 us (9%)
  local copies, waits for them, and re-layouts  5.56 us (3%)
    ppermute x46, waiting for transfers between devices, move(): return lax.ppermute(value, AXES, permutation(self.rows, self.cols, source))  95.3 us
    ppermute x46, starting transfers between devices, move(): return lax.ppermute(value, AXES, permutation(self.rows, self.cols, source))  52.5 us
    pallas_call x1, Pallas kernels, on_device(): call(functools.partial(series_kernel, layout, count, len(arrays)), [jax.S...  8.84 us
    unnamed x15, local copies, waits for them, and re-layouts  5.55 us
    pallas_call x4, Pallas kernels, views_call(): call(body, outs, [INVMEM] * len(operands), scratch, name, flops)(*operands)  4.44 us
  transfers between devices with their start and end apart: 46, of which 29 were waited for; matrix products, arithmetic and copies ran while one was open for 0% of the time, Pallas kernels for 1%

profile of v9, /device:TPU:1, one launch (start us, length us, event | category | flops | bytes accessed | tf_op | source)
XLA Modules:
  0.0 169.9 jit_solution(17593279077960242139)
XLA Ops:
  4.9 2.5 %mask.1 = (bf16[208,384]{1,0:T(8,128)(2,1)S(1)}, bf16[384,384]{1,0:T(8,128)(2,1)S(1)}) custom-call(s32[3,6,12]{2,1,0:T(8,128)S(1)} %copy-done.4, bf16[192,384]{1,0:T(8,128)(2,1)S(1)} %copy-done, bf16[192,384]{1,0:T(8,128)(2,1)S(1)} %copy-done.1, bf16[192,384]{1,0:T(8,128)(2,1)S(1)} %copy-done.2, s32[3,6,12]{2,1,0:T(8,128)S(1)} %copy-done.5, ...), custom_call_target="tpu_custom_call" | custom-call | flops 1000 | bytes 1000 | tf_op jit(solution)/shard_map/mask/pallas_call | solution.py:394
  7.4 4.5 %collective-permute-start.4 = (bf16[208,384]{1,0:T(8,128)(2,1)S(1)}, bf16[208,384]{1,0:T(8,128)(2,1)S(1)}, u32[]{:S(2)}, u32[]{:S(2)}) collective-permute-start(bf16[208,384]{1,0:T(8,128)(2,1)S(1)} %get-tuple-element.24), channel_id=1, source_target_pairs={{0,0},{4,1},{2,2},{6,3},{1,4},{5,5},{3,6},{7,7},{8,8},{12,9},{10,1... | collective-permute-start | bytes 479240 | tf_op jit(solution)/shard_map/ppermute | solution.py:39
  13.0 3.8 %collective-permute-start.6 = (bf16[208,384]{1,0:T(8,128)(2,1)S(1)}, bf16[208,384]{1,0:T(8,128)(2,1)S(1)}, u32[]{:S(2)}, u32[]{:S(2)}) collective-permute-start(bf16[208,384]{1,0:T(8,128)(2,1)S(1)} %get-tuple-element.24), channel_id=1, source_target_pairs={{16,0},{20,1},{18,2},{22,3},{17,4},{21,5},{19,6},{23,7},{24,8},{28... | collective-permute-start | bytes 479240 | tf_op jit(solution)/shard_map/ppermute | solution.py:39
  18.7 2.7 %collective-permute-start.2 = (bf16[384,384]{1,0:T(8,128)(2,1)S(1)}, bf16[384,384]{1,0:T(8,128)(2,1)S(1)}, u32[]{:S(2)}, u32[]{:S(2)}) collective-permute-start(bf16[384,384]{1,0:T(8,128)(2,1)S(1)} %get-tuple-element.23), channel_id=1, source_target_pairs={{2,0},{6,1},{0,2},{4,3},{3,4},{7,5},{1,6},{5,7},{10,8},{14,9},{8,1... | collective-permute-start | bytes 884744 | tf_op jit(solution)/shard_map/ppermute | solution.py:39
  22.6 10.6 %collective-permute-done.refs_0_.refs_8_ = bf16[384,384]{1,0:T(8,128)(2,1)S(1)} collective-permute-done((bf16[384,384]{1,0:T(8,128)(2,1)S(1)}, bf16[384,384]{1,0:T(8,128)(2,1)S(1)}, u32[]{:S(2)}, u32[]{:S(2)}) %collective-permute-start) | collective-permute-done | bytes 294944 | tf_op jit(solution)/shard_map/ppermute | solution.py:39
  36.4 14.9 %collective-permute-done.13.refs_10_ = bf16[384,384]{1,0:T(8,128)(2,1)S(1)} collective-permute-done((bf16[384,384]{1,0:T(8,128)(2,1)S(1)}, bf16[384,384]{1,0:T(8,128)(2,1)S(1)}, u32[]{:S(2)}, u32[]{:S(2)}) %collective-permute-start.13) | collective-permute-done | bytes 294944 | tf_op jit(solution)/shard_map/ppermute | solution.py:39
  56.0 3.4 %collective-permute-done.14.refs_11_ = bf16[384,384]{1,0:T(8,128)(2,1)S(1)} collective-permute-done((bf16[384,384]{1,0:T(8,128)(2,1)S(1)}, bf16[384,384]{1,0:T(8,128)(2,1)S(1)}, u32[]{:S(2)}, u32[]{:S(2)}) %collective-permute-start.14) | collective-permute-done | bytes 294944 | tf_op jit(solution)/shard_map/ppermute | solution.py:39
  62.6 6.4 %collective-permute-done.11.refs_3_ = bf16[384,384]{1,0:T(8,128)(2,1)S(1)} collective-permute-done((bf16[384,384]{1,0:T(8,128)(2,1)S(1)}, bf16[384,384]{1,0:T(8,128)(2,1)S(1)}, u32[]{:S(2)}, u32[]{:S(2)}) %collective-permute-start.11) | collective-permute-done | bytes 294944 | tf_op jit(solution)/shard_map/ppermute | solution.py:39
  74.1 2.4 %collective-permute-start.20 = (bf16[192,384]{1,0:T(8,128)(2,1)S(1)}, bf16[192,384]{1,0:T(8,128)(2,1)S(1)}, u32[]{:S(2)}, u32[]{:S(2)}) collective-permute-start(bf16[192,384]{1,0:T(8,128)(2,1)S(1)} %generator.1.refs_0_), channel_id=1, source_target_pairs={{6,0},{7,1},{4,2},{5,3},{2,4},{3,5},{0,6},{1,7},{14,8},{15,9},{12,... | collective-permute-start | bytes 442376 | tf_op jit(solution)/shard_map/ppermute | solution.py:39
  76.8 3.3 %collective-permute-done.20.refs_4_ = bf16[192,384]{1,0:T(8,128)(2,1)S(1)} collective-permute-done((bf16[192,384]{1,0:T(8,128)(2,1)S(1)}, bf16[192,384]{1,0:T(8,128)(2,1)S(1)}, u32[]{:S(2)}, u32[]{:S(2)}) %collective-permute-start.20) | collective-permute-done | bytes 147488 | tf_op jit(solution)/shard_map/ppermute | solution.py:39
  80.1 3.4 %collective-permute-done.19.refs_3_ = bf16[192,384]{1,0:T(8,128)(2,1)S(1)} collective-permute-done((bf16[192,384]{1,0:T(8,128)(2,1)S(1)}, bf16[192,384]{1,0:T(8,128)(2,1)S(1)}, u32[]{:S(2)}, u32[]{:S(2)}) %collective-permute-start.19) | collective-permute-done | bytes 147488 | tf_op jit(solution)/shard_map/ppermute | solution.py:39
  86.3 8.1 %collective-permute-done.23 = bf16[192,384]{1,0:T(8,128)(2,1)S(1)} collective-permute-done((bf16[192,384]{1,0:T(8,128)(2,1)S(1)}, bf16[192,384]{1,0:T(8,128)(2,1)S(1)}, u32[]{:S(2)}, u32[]{:S(2)}) %collective-permute-start.23) | collective-permute-done | bytes 147488 | tf_op jit(solution)/shard_map/ppermute | solution.py:39
  97.1 2.8 %collective-permute-done.27.refs_10_ = bf16[192,384]{1,0:T(8,128)(2,1)S(1)} collective-permute-done((bf16[192,384]{1,0:T(8,128)(2,1)S(1)}, bf16[192,384]{1,0:T(8,128)(2,1)S(1)}, u32[]{:S(2)}, u32[]{:S(2)}) %collective-permute-start.27) | collective-permute-done | bytes 147488 | tf_op jit(solution)/shard_map/ppermute | solution.py:39
  104.2 5.2 %collective-permute-done.26.refs_9_ = bf16[384,384]{1,0:T(8,128)(2,1)S(1)} collective-permute-done((bf16[384,384]{1,0:T(8,128)(2,1)S(1)}, bf16[384,384]{1,0:T(8,128)(2,1)S(1)}, u32[]{:S(2)}, u32[]{:S(2)}) %collective-permute-start.26) | collective-permute-done | bytes 294944 | tf_op jit(solution)/shard_map/ppermute | solution.py:39
  112.5 2.9 %collective-permute-done.30.refs_14_ = bf16[192,384]{1,0:T(8,128)(2,1)S(1)} collective-permute-done((bf16[192,384]{1,0:T(8,128)(2,1)S(1)}, bf16[192,384]{1,0:T(8,128)(2,1)S(1)}, u32[]{:S(2)}, u32[]{:S(2)}) %collective-permute-start.30) | collective-permute-done | bytes 147488 | tf_op jit(solution)/shard_map/ppermute | solution.py:39
  115.6 2.4 %collective-permute-start.31 = (bf16[1536,384]{1,0:T(8,128)(2,1)S(1)}, bf16[1536,384]{1,0:T(8,128)(2,1)S(1)}, u32[]{:S(2)}, u32[]{:S(2)}) collective-permute-start(bf16[1536,384]{1,0:T(8,128)(2,1)S(1)} %pad_maximum_fusion), channel_id=1, source_target_pairs={{1,0},{0,1},{3,2},{2,3},{5,4},{4,5},{7,6},{6,7},{9,8},{8,9},{11,10... | collective-permute-start | bytes 3538952 | tf_op jit(solution)/shard_map/ppermute | solution.py:39
  118.2 3.1 %collective-permute-done.32.refs_11_ = bf16[768,384]{1,0:T(8,128)(2,1)S(1)} collective-permute-done((bf16[768,384]{1,0:T(8,128)(2,1)S(1)}, bf16[768,384]{1,0:T(8,128)(2,1)S(1)}, u32[]{:S(2)}, u32[]{:S(2)}) %collective-permute-start.32) | collective-permute-done | bytes 589856 | tf_op jit(solution)/shard_map/ppermute | solution.py:39
  121.3 8.8 %series.1 = (bf16[192,1536]{1,0:T(8,128)(2,1)S(1)}, bf16[192,384]{1,0:T(8,128)(2,1)S(1)}) custom-call(bf16[192,384]{1,0:T(8,128)(2,1)S(1)} %generator.1.refs_0_, bf16[768,384]{1,0:T(8,128)(2,1)S(1)} %collective-permute-done.21.refs_1_, bf16[192,384]{1,0:T(8,128)(2,1)S(1)} %collective-permute-done.18.refs_2_, ...), custom_call_target="tpu_custom_call" | custom-call | flops 1000 | bytes 1000 | tf_op jit(solution)/shard_map/series/pallas_call | solution.py:473
  132.9 2.4 %collective-permute-done.33.refs_1_ = bf16[192,384]{1,0:T(8,128)(2,1)S(1)} collective-permute-done((bf16[192,384]{1,0:T(8,128)(2,1)S(1)}, bf16[192,384]{1,0:T(8,128)(2,1)S(1)}, u32[]{:S(2)}, u32[]{:S(2)}) %collective-permute-start.33) | collective-permute-done | bytes 147488 | tf_op jit(solution)/shard_map/ppermute | solution.py:39
  136.1 3.2 %collective-permute-done.35.refs_3_ = bf16[192,384]{1,0:T(8,128)(2,1)S(1)} collective-permute-done((bf16[192,384]{1,0:T(8,128)(2,1)S(1)}, bf16[192,384]{1,0:T(8,128)(2,1)S(1)}, u32[]{:S(2)}, u32[]{:S(2)}) %collective-permute-start.35) | collective-permute-done | bytes 147488 | tf_op jit(solution)/shard_map/ppermute | solution.py:39
  143.3 2.5 %collective-permute-start.42 = (bf16[192,384]{1,0:T(8,128)(2,1)S(1)}, bf16[192,384]{1,0:T(8,128)(2,1)S(1)}, u32[]{:S(2)}, u32[]{:S(2)}) collective-permute-start(bf16[192,384]{1,0:T(8,128)(2,1)S(1)} %square.1.refs_0_), channel_id=1, source_target_pairs={{16,0},{17,1},{18,2},{19,3},{20,4},{21,5},{22,6},{23,7},{24,8},{25... | collective-permute-start | bytes 442376 | tf_op jit(solution)/shard_map/ppermute | solution.py:39
  148.9 3.8 %collective-permute-done.42.refs_6_ = bf16[192,384]{1,0:T(8,128)(2,1)S(1)} collective-permute-done((bf16[192,384]{1,0:T(8,128)(2,1)S(1)}, bf16[192,384]{1,0:T(8,128)(2,1)S(1)}, u32[]{:S(2)}, u32[]{:S(2)}) %collective-permute-start.42) | collective-permute-done | bytes 147488 | tf_op jit(solution)/shard_map/ppermute | solution.py:39
  162.8 3.3 %collective-permute-start.45 = (bf16[192,384]{1,0:T(8,128)(2,1)S(1)}, bf16[192,384]{1,0:T(8,128)(2,1)S(1)}, u32[]{:S(2)}, u32[]{:S(2)}) collective-permute-start(bf16[192,384]{1,0:T(8,128)(2,1)S(1)} %evolve.1), channel_id=1, source_target_pairs={{0,0},{4,1},{2,2},{6,3},{1,4},{5,5},{3,6},{7,7},{8,8},{12,9},{10,1... | collective-permute-start | bytes 442376 | tf_op jit(solution)/shard_map/ppermute | solution.py:39
  166.1 3.1 %collective-permute-done.45 = bf16[192,384]{1,0:T(8,128)(2,1)S(1)} collective-permute-done((bf16[192,384]{1,0:T(8,128)(2,1)S(1)}, bf16[192,384]{1,0:T(8,128)(2,1)S(1)}, u32[]{:S(2)}, u32[]{:S(2)}) %collective-permute-start.45) | collective-permute-done | bytes 147488 | tf_op jit(solution)/shard_map/ppermute | solution.py:39
  (103 shorter events, 60.2 us)
Async XLA Ops:
  7.4 11.3 %collective-permute-start.4 = (bf16[208,384]{1,0:T(8,128)(2,1)S(1)}, bf16[208,384]{1,0:T(8,128)(2,1)S(1)}, u32[]{:S(2)}, u32[]{:S(2)}) collective-permute-start(bf16[208,384]{1,0:T(8,128)(2,1)S(1)} %get-tuple-element.24), channel_id=1, source_target_pairs={{0,0},{4,1},{2,2},{6,3},{1,4},{5,5},{3,6},{7,7},{8,8},{12,9},{10,1... | collective-permute-start | bytes 479240 | tf_op jit(solution)/shard_map/ppermute | solution.py:39
  11.9 9.5 %collective-permute-start.5 = (bf16[208,384]{1,0:T(8,128)(2,1)S(1)}, bf16[208,384]{1,0:T(8,128)(2,1)S(1)}, u32[]{:S(2)}, u32[]{:S(2)}) collective-permute-start(bf16[208,384]{1,0:T(8,128)(2,1)S(1)} %get-tuple-element.24), channel_id=1, source_target_pairs={{8,0},{12,1},{10,2},{14,3},{9,4},{13,5},{11,6},{15,7},{0,8},{4,9},... | collective-permute-start | bytes 479240 | tf_op jit(solution)/shard_map/ppermute | solution.py:39
  13.0 9.5 %collective-permute-start.6 = (bf16[208,384]{1,0:T(8,128)(2,1)S(1)}, bf16[208,384]{1,0:T(8,128)(2,1)S(1)}, u32[]{:S(2)}, u32[]{:S(2)}) collective-permute-start(bf16[208,384]{1,0:T(8,128)(2,1)S(1)} %get-tuple-element.24), channel_id=1, source_target_pairs={{16,0},{20,1},{18,2},{22,3},{17,4},{21,5},{19,6},{23,7},{24,8},{28... | collective-permute-start | bytes 479240 | tf_op jit(solution)/shard_map/ppermute | solution.py:39
  16.8 16.4 %collective-permute-start = (bf16[384,384]{1,0:T(8,128)(2,1)S(1)}, bf16[384,384]{1,0:T(8,128)(2,1)S(1)}, u32[]{:S(2)}, u32[]{:S(2)}) collective-permute-start(bf16[384,384]{1,0:T(8,128)(2,1)S(1)} %get-tuple-element.23), channel_id=1, source_target_pairs={{0,0},{4,1},{2,2},{6,3},{1,4},{5,5},{3,6},{7,7},{8,8},{12,9},{10,1... | collective-permute-start | bytes 884744 | tf_op jit(solution)/shard_map/ppermute | solution.py:39
  18.7 14.5 %collective-permute-start.1 = (bf16[384,384]{1,0:T(8,128)(2,1)S(1)}, bf16[384,384]{1,0:T(8,128)(2,1)S(1)}, u32[]{:S(2)}, u32[]{:S(2)}) collective-permute-start(bf16[384,384]{1,0:T(8,128)(2,1)S(1)} %get-tuple-element.23), channel_id=1, source_target_pairs={{1,0},{5,1},{3,2},{7,3},{0,4},{4,5},{2,6},{6,7},{9,8},{13,9},{11,1... | collective-permute-start | bytes 884744 | tf_op jit(solution)/shard_map/ppermute | solution.py:39
  18.7 14.5 %collective-permute-start.2 = (bf16[384,384]{1,0:T(8,128)(2,1)S(1)}, bf16[384,384]{1,0:T(8,128)(2,1)S(1)}, u32[]{:S(2)}, u32[]{:S(2)}) collective-permute-start(bf16[384,384]{1,0:T(8,128)(2,1)S(1)} %get-tuple-element.23), channel_id=1, source_target_pairs={{2,0},{6,1},{0,2},{4,3},{3,4},{7,5},{1,6},{5,7},{10,8},{14,9},{8,1... | collective-permute-start | bytes 884744 | tf_op jit(solution)/shard_map/ppermute | solution.py:39
  21.4 13.2 %collective-permute-start.3 = (bf16[384,384]{1,0:T(8,128)(2,1)S(1)}, bf16[384,384]{1,0:T(8,128)(2,1)S(1)}, u32[]{:S(2)}, u32[]{:S(2)}) collective-permute-start(bf16[384,384]{1,0:T(8,128)(2,1)S(1)} %get-tuple-element.23), channel_id=1, source_target_pairs={{3,0},{7,1},{1,2},{5,3},{2,4},{6,5},{0,6},{4,7},{11,8},{15,9},{9,1... | collective-permute-start | bytes 884744 | tf_op jit(solution)/shard_map/ppermute | solution.py:39
  22.5 12.2 %collective-permute-start.7 = (bf16[208,384]{1,0:T(8,128)(2,1)S(1)}, bf16[208,384]{1,0:T(8,128)(2,1)S(1)}, u32[]{:S(2)}, u32[]{:S(2)}) collective-permute-start(bf16[208,384]{1,0:T(8,128)(2,1)S(1)} %collective-permute-done.6.refs_6_.refs_11_), channel_id=1, source_target_pairs={{8,0},{9,1},{10,2},{11,3},{12,4},{13,5},{14,6},{15,7},{0,8},{1,9},... | collective-permute-start | bytes 479240 | tf_op jit(solution)/shard_map/ppermute | solution.py:39
  34.7 16.6 %collective-permute-start.8 = (bf16[832,384]{1,0:T(8,128)(2,1)S(1)}, bf16[832,384]{1,0:T(8,128)(2,1)S(1)}, u32[]{:S(2)}, u32[]{:S(2)}) collective-permute-start(bf16[832,384]{1,0:T(8,128)(2,1)S(1)} %pad_maximum_fusion.1), channel_id=1, source_target_pairs={{1,0},{0,1},{3,2},{2,3},{5,4},{4,5},{7,6},{6,7},{9,8},{8,9},{11,10... | collective-permute-start | bytes 1916936 | tf_op jit(solution)/shard_map/ppermute | solution.py:39
  35.2 16.1 %collective-permute-start.13 = (bf16[384,384]{1,0:T(8,128)(2,1)S(1)}, bf16[384,384]{1,0:T(8,128)(2,1)S(1)}, u32[]{:S(2)}, u32[]{:S(2)}) collective-permute-start(bf16[384,384]{1,0:T(8,128)(2,1)S(1)} %collective-permute-done.refs_0_.refs_8_), channel_id=1, source_target_pairs={{16,0},{17,1},{18,2},{19,3},{20,4},{21,5},{22,6},{23,7},{24,8},{25... | collective-permute-start | bytes 884744 | tf_op jit(solution)/shard_map/ppermute | solution.py:39
  35.2 20.8 %collective-permute-start.12 = (bf16[384,384]{1,0:T(8,128)(2,1)S(1)}, bf16[384,384]{1,0:T(8,128)(2,1)S(1)}, u32[]{:S(2)}, u32[]{:S(2)}) collective-permute-start(bf16[384,384]{1,0:T(8,128)(2,1)S(1)} %collective-permute-done.refs_0_.refs_8_), channel_id=1, source_target_pairs={{8,0},{9,1},{10,2},{11,3},{12,4},{13,5},{14,6},{15,7},{0,8},{1,9},... | collective-permute-start | bytes 884744 | tf_op jit(solution)/shard_map/ppermute | solution.py:39
  51.3 8.1 %collective-permute-start.14 = (bf16[384,384]{1,0:T(8,128)(2,1)S(1)}, bf16[384,384]{1,0:T(8,128)(2,1)S(1)}, u32[]{:S(2)}, u32[]{:S(2)}) collective-permute-start(bf16[384,384]{1,0:T(8,128)(2,1)S(1)} %collective-permute-done.13.refs_10_), channel_id=1, source_target_pairs={{8,0},{9,1},{10,2},{11,3},{12,4},{13,5},{14,6},{15,7},{0,8},{1,9},... | collective-permute-start | bytes 884744 | tf_op jit(solution)/shard_map/ppermute | solution.py:39
  52.5 9.3 %collective-permute-start.9 = (bf16[384,384]{1,0:T(8,128)(2,1)S(1)}, bf16[384,384]{1,0:T(8,128)(2,1)S(1)}, u32[]{:S(2)}, u32[]{:S(2)}) collective-permute-start(bf16[384,384]{1,0:T(8,128)(2,1)S(1)} %first.1.refs_0_), channel_id=1, source_target_pairs={{4,0},{5,1},{6,2},{7,3},{0,4},{1,5},{2,6},{3,7},{12,8},{13,9},{14,... | collective-permute-start | bytes 884744 | tf_op jit(solution)/shard_map/ppermute | solution.py:39
  55.9 13.1 %collective-permute-start.11 = (bf16[384,384]{1,0:T(8,128)(2,1)S(1)}, bf16[384,384]{1,0:T(8,128)(2,1)S(1)}, u32[]{:S(2)}, u32[]{:S(2)}) collective-permute-start(bf16[384,384]{1,0:T(8,128)(2,1)S(1)} %first.1.refs_0_), channel_id=1, source_target_pairs={{6,0},{7,1},{4,2},{5,3},{2,4},{3,5},{0,6},{1,7},{14,8},{15,9},{12,... | collective-permute-start | bytes 884744 | tf_op jit(solution)/shard_map/ppermute | solution.py:39
  83.7 16.2 %collective-permute-start.21 = (bf16[768,384]{1,0:T(8,128)(2,1)S(1)}, bf16[768,384]{1,0:T(8,128)(2,1)S(1)}, u32[]{:S(2)}, u32[]{:S(2)}) collective-permute-start(bf16[768,384]{1,0:T(8,128)(2,1)S(1)} %pad_maximum_fusion.3), channel_id=1, source_target_pairs={{1,0},{0,1},{3,2},{2,3},{5,4},{4,5},{7,6},{6,7},{9,8},{8,9},{11,10... | collective-permute-start | bytes 1769480 | tf_op jit(solution)/shard_map/ppermute | solution.py:39
  84.8 9.5 %collective-permute-start.23 = (bf16[192,384]{1,0:T(8,128)(2,1)S(1)}, bf16[192,384]{1,0:T(8,128)(2,1)S(1)}, u32[]{:S(2)}, u32[]{:S(2)}) collective-permute-start(bf16[192,384]{1,0:T(8,128)(2,1)S(1)} %generator.1.refs_0_), channel_id=1, source_target_pairs={{16,0},{17,1},{18,2},{19,3},{20,4},{21,5},{22,6},{23,7},{24,8},{25... | collective-permute-start | bytes 442376 | tf_op jit(solution)/shard_map/ppermute | solution.py:39
  85.1 9.3 %collective-permute-start.22 = (bf16[192,384]{1,0:T(8,128)(2,1)S(1)}, bf16[192,384]{1,0:T(8,128)(2,1)S(1)}, u32[]{:S(2)}, u32[]{:S(2)}) collective-permute-start(bf16[192,384]{1,0:T(8,128)(2,1)S(1)} %generator.1.refs_0_), channel_id=1, source_target_pairs={{8,0},{9,1},{10,2},{11,3},{12,4},{13,5},{14,6},{15,7},{0,8},{1,9},... | collective-permute-start | bytes 442376 | tf_op jit(solution)/shard_map/ppermute | solution.py:39
  95.6 8.6 %collective-permute-start.25 = (bf16[384,384]{1,0:T(8,128)(2,1)S(1)}, bf16[384,384]{1,0:T(8,128)(2,1)S(1)}, u32[]{:S(2)}, u32[]{:S(2)}) collective-permute-start(bf16[384,384]{1,0:T(8,128)(2,1)S(1)} %pad_maximum_fusion.8.refs_5_), channel_id=1, source_target_pairs={{2,0},{3,1},{0,2},{1,3},{6,4},{7,5},{4,6},{5,7},{10,8},{11,9},{8,1... | collective-permute-start | bytes 884744 | tf_op jit(solution)/shard_map/ppermute | solution.py:39
  96.8 12.6 %collective-permute-start.26 = (bf16[384,384]{1,0:T(8,128)(2,1)S(1)}, bf16[384,384]{1,0:T(8,128)(2,1)S(1)}, u32[]{:S(2)}, u32[]{:S(2)}) collective-permute-start(bf16[384,384]{1,0:T(8,128)(2,1)S(1)} %pad_maximum_fusion.8.refs_5_), channel_id=1, source_target_pairs={{6,0},{7,1},{4,2},{5,3},{2,4},{3,5},{0,6},{1,7},{14,8},{15,9},{12,... | collective-permute-start | bytes 884744 | tf_op jit(solution)/shard_map/ppermute | solution.py:39
  99.9 11.7 %collective-permute-start.28 = (bf16[192,384]{1,0:T(8,128)(2,1)S(1)}, bf16[192,384]{1,0:T(8,128)(2,1)S(1)}, u32[]{:S(2)}, u32[]{:S(2)}) collective-permute-start(bf16[192,384]{1,0:T(8,128)(2,1)S(1)} %collective-permute-done.27.refs_10_), channel_id=1, source_target_pairs={{4,0},{5,1},{6,2},{7,3},{0,4},{1,5},{2,6},{3,7},{12,8},{13,9},{14,... | collective-permute-start | bytes 442376 | tf_op jit(solution)/shard_map/ppermute | solution.py:39
  100.2 12.3 %collective-permute-start.29 = (bf16[192,384]{1,0:T(8,128)(2,1)S(1)}, bf16[192,384]{1,0:T(8,128)(2,1)S(1)}, u32[]{:S(2)}, u32[]{:S(2)}) collective-permute-start(bf16[192,384]{1,0:T(8,128)(2,1)S(1)} %collective-permute-done.27.refs_10_), channel_id=1, source_target_pairs={{2,0},{3,1},{0,2},{1,3},{6,4},{7,5},{4,6},{5,7},{10,8},{11,9},{8,1... | collective-permute-start | bytes 442376 | tf_op jit(solution)/shard_map/ppermute | solution.py:39
  102.2 13.3 %collective-permute-start.30 = (bf16[192,384]{1,0:T(8,128)(2,1)S(1)}, bf16[192,384]{1,0:T(8,128)(2,1)S(1)}, u32[]{:S(2)}, u32[]{:S(2)}) collective-permute-start(bf16[192,384]{1,0:T(8,128)(2,1)S(1)} %collective-permute-done.27.refs_10_), channel_id=1, source_target_pairs={{6,0},{7,1},{4,2},{5,3},{2,4},{3,5},{0,6},{1,7},{14,8},{15,9},{12,... | collective-permute-start | bytes 442376 | tf_op jit(solution)/shard_map/ppermute | solution.py:39
  143.3 9.4 %collective-permute-start.42 = (bf16[192,384]{1,0:T(8,128)(2,1)S(1)}, bf16[192,384]{1,0:T(8,128)(2,1)S(1)}, u32[]{:S(2)}, u32[]{:S(2)}) collective-permute-start(bf16[192,384]{1,0:T(8,128)(2,1)S(1)} %square.1.refs_0_), channel_id=1, source_target_pairs={{16,0},{17,1},{18,2},{19,3},{20,4},{21,5},{22,6},{23,7},{24,8},{25... | collective-permute-start | bytes 442376 | tf_op jit(solution)/shard_map/ppermute | solution.py:39
  148.5 8.1 %collective-permute-start.41 = (bf16[192,384]{1,0:T(8,128)(2,1)S(1)}, bf16[192,384]{1,0:T(8,128)(2,1)S(1)}, u32[]{:S(2)}, u32[]{:S(2)}) collective-permute-start(bf16[192,384]{1,0:T(8,128)(2,1)S(1)} %square.1.refs_0_), channel_id=1, source_target_pairs={{8,0},{9,1},{10,2},{11,3},{12,4},{13,5},{14,6},{15,7},{0,8},{1,9},... | collective-permute-start | bytes 442376 | tf_op jit(solution)/shard_map/ppermute | solution.py:39
  (29 other events, 127.1 us)

commit v10 on v9

--- a/solution.py
+++ b/solution.py
@@ -147,8 +147,8 @@
 
 
 def mask_kernel(inputs, *refs):
-    sources, (tailed, duo) = refs[:inputs], refs[inputs : inputs + 2]
-    held, sems = refs[inputs + 2 : -1], refs[-1]
+    sources, (masked_density, duo, trio) = refs[:inputs], refs[inputs : inputs + 3]
+    held, sems = refs[inputs + 3 : -1], refs[-1]
     copies = [
         pltpu.make_async_copy(source, target, sems.at[n])
         for n, (source, target) in enumerate(zip(sources, held))
@@ -164,11 +164,14 @@
         mask = dot(dot(tall, fills[number].astype(BF16)).astype(BF16), wide)
         return (ref[...].astype(F32) * mask).astype(BF16)
 
-    wait_all(copies[:2])
-    tailed[TAIL:, :] = masked(density, 1)
-    wait_all(copies[2:])
-    duo[:rows, :] = masked(fock, 0)
-    duo[rows:, :] = masked(margin, 2)
+    wait_all(copies)
+    value = masked(density, 1)
+    masked_density[...] = value
+    trio[TAIL + 2 * rows :, :] = value
+    for half, (ref, number) in enumerate(((fock, 0), (margin, 2))):
+        value = masked(ref, number)
+        duo[half * rows : (half + 1) * rows, :] = value
+        trio[TAIL + half * rows : TAIL + (half + 1) * rows, :] = value
     top = (iota((TAIL, row_blocks), 0) == iota((TAIL, row_blocks), 1)).astype(BF16)
     tail = jnp.zeros((TAIL, columns), F32)
     for number in range(FIRST + seconds.shape[1]):
@@ -176,7 +179,7 @@
         column = iota((column_blocks, columns), 1) - number * column_blocks
         spread = (iota((column_blocks, columns), 0) == column).astype(BF16)
         tail += dot(dot(top, block.astype(BF16)).astype(BF16), spread)
-    tailed[:TAIL, :] = tail.astype(BF16)
+    trio[:TAIL, :] = tail.astype(BF16)
 
 
 def chunk(index, length):
@@ -391,35 +394,41 @@
         first_filters,
         second_filters.transpose(1, 0, 2),
     )
-    tailed, duo = call(
+    masked_density, duo, trio = call(
         functools.partial(mask_kernel, len(inputs)),
         [
-            jax.ShapeDtypeStruct((TAIL + rows, columns), BF16),
+            block,
             jax.ShapeDtypeStruct((2 * rows, columns), BF16),
+            jax.ShapeDtypeStruct((TAIL + 3 * rows, columns), BF16),
         ],
-        [pl.BlockSpec(memory_space=pltpu.HBM)] * len(inputs),
+        [ANY] * len(inputs),
         [pltpu.VMEM(value.shape, value.dtype) for value in inputs]
         + [pltpu.SemaphoreType.DMA((len(inputs),))],
         "mask",
+        room=60,
     )(*inputs)
 
-    pair = moves.relabel(duo)
+    trio = moves.relabel(trio)
     fock_rows = moves.plane(duo, True)
-    density_line = [moves.relabel(tailed)] + moves.line(tailed, True)
+    density_line = moves.line(masked_density, True, gate=(trio, *fock_rows))
+    density_near = [(trio, TAIL + 2 * rows)] + whole(density_line)
+    pair = trio[: TAIL + 2 * rows]
     pair_second, *_ = barrier((pair, *density_line))
     pair_line = moves.line(pair, second=pair_second)
-    ready = list(barrier((*density_line, *fock_rows, pair))[:count])
-    density_far = moves.cores(ready)
-    density_near = whole(density_line)
-    other = moves.core(pair)
+    density_line = list(barrier((*density_line, *fock_rows))[: count - 1])
+    trio_far = moves.core(trio)
+    density_far = [(trio_far, TAIL + 2 * rows)] + moves.cores(density_line)
+    early_far = moves.cores(pair_line[half - 1 : half])
+    trio, early, _ = barrier((trio, early_far[0][0], pair_line[half - 1]))
+    early_far = [(early, 0)]
 
     products = views_call(
         functools.partial(first_kernel, count),
         {
-            "plane": whole([pair] + fock_rows),
-            "tail": density_near,
-            "near": [(value, first + TAIL) for value, first in density_near],
-            "far": [(value, first + TAIL) for value, first in density_far],
+            "plane": [(trio, TAIL)] + whole(fock_rows),
+            "tail": [(trio, 0)],
+            "near": density_near,
+            "far": density_far,
         },
         jax.ShapeDtypeStruct((2 * rows, columns), BF16),
         [pltpu.VMEM((count, 2 * rows, columns), BF16)],
@@ -428,16 +437,18 @@
     )
     product_rows = [products] + moves.plane(products)
     pair_line = list(barrier((*pair_line, *product_rows[1:]))[: count - 1])
-    pair_far = [(other, 0)] + moves.cores(pair_line[:half]) + moves.cores(pair_line[half:])
-    pair_near = whole([pair] + pair_line)
+    rest = pair_line[: half - 1] + pair_line[half:]
+    rest_far = moves.cores(rest)
+    pair_far = [(trio_far, 0)] + rest_far[: half - 1] + early_far + rest_far[half - 1 :]
+    pair_near = [(trio, 0)] + whole(pair_line)
 
     generator = views_call(
         functools.partial(generator_kernel, count),
         {
             "plane": whole(product_rows),
-            "tail": density_near,
-            "near": pair_near,
-            "far": pair_far,
+            "tail": [(trio, 0)],
+            "near": [(value, first + TAIL) for value, first in pair_near],
+            "far": [(value, first + TAIL) for value, first in pair_far],
         },
         block,
         [pltpu.VMEM((2, count, rows, columns), BF16)],
@@ -445,22 +456,18 @@
     )
 
     lines = [generator] + moves.line(generator)
-    arrays, layout, done, own_far = [], [], [], []
+    arrays, layout, planes, done = [], [], [], []
     for held in (range(1), range(1, half + 1), range(half + 1, count)):
         group = lines[held[0]]
         if len(held) > 1:
             group = jnp.concatenate([lines[k] for k in held], axis=0)
         if held[0] == 1:
-            group, *_ = barrier((group, *done[0][1]))
-        if held[0] > 1:
-            group, _ = barrier((group, own_far[0][0]))
+            group, *planes = barrier((group, *planes))
         planes = [group] + moves.plane(group)
-        if held[0] == 0:
-            own_far = moves.cores(planes)
         done.append((held, planes))
     done[1] = (done[1][0], list(barrier((*done[1][1], *done[2][1][1:]))[:count]))
     for held, planes in done:
-        far = own_far if held[0] == 0 else moves.cores(planes)
+        far = moves.cores(planes)
         for s, value in enumerate(planes):
             for lane, (array, start) in enumerate(((value, 0), far[s])):
                 if not any(other is array for other in arrays):
@@ -468,7 +475,7 @@
                 index = [n for n, other in enumerate(arrays) if other is array][0]
                 for n, k in enumerate(held):
                     layout.append((index, start + n * rows, k, s, lane))
-    tails = [value[first : first + TAIL] for value, first in density_near + density_far]
+    tails = [value[first : first + TAIL] for value, first in pair_near + pair_far]
 
     panel, mine = call(
         functools.partial(series_kernel, layout, count, len(arrays)),
@@ -488,7 +495,7 @@
     near = [mine] + moves.plane(mine)
     square = views_call(
         functools.partial(square_kernel, count),
-        {"near": whole(near), "far": moves.cores(near), "tail": [density_near[0], density_far[0]]},
+        {"near": whole(near), "far": moves.cores(near), "tail": [(trio, 0), (trio_far, 0)]},
         block,
         [],
         "square",
@@ -505,7 +512,7 @@
             "plane_far": plane_far,
             "line_near": whole([square] + line),
             "line_far": plane_far[:1] + moves.cores(line),
-            "tail": density_near,
+            "tail": [(trio, 0)],
         },
         block,
         [pltpu.VMEM((count, columns, columns), BF16)],

time: 170 us -> 156 us (0.918)
  starting transfers between devices: 52.5 us -> 43.2 us
  local copies, waits for them, and re-layouts: 5.56 us -> 0.72 us
    ppermute x46 -> x45, starting transfers between devices: 52.5 us -> 43.2 us  [move(): return lax.ppermute(value, AXES, permutation(self.rows, self.cols, source))]
    unnamed x15 -> x3, local copies, waits for them, and re-layouts: 5.55 us -> 0.67 us
    ppermute x46 -> x45, waiting for transfers between devices: 95.3 us -> 93.7 us  [move(): return lax.ppermute(value, AXES, permutation(self.rows, self.cols, source))]
  transfers between devices with their start and end apart: 46 -> 45, of which waited for: 29 -> 31; matrix products, arithmetic and copies ran while one was open for 0% -> 0% of each run, Pallas kernels for 1% -> 1%
where the time goes in v10:
time: 156 us; the launch traced here: 155 us
  waiting for transfers between devices  93.7 us (60%)
  starting transfers between devices  43.2 us (28%)
  Pallas kernels  17 us (11%)
    ppermute x45, waiting for transfers between devices, move(): return lax.ppermute(value, AXES, permutation(self.rows, self.cols, source))  93.7 us
    ppermute x45, starting transfers between devices, move(): return lax.ppermute(value, AXES, permutation(self.rows, self.cols, source))  43.2 us
    pallas_call x1, Pallas kernels, on_device(): call(functools.partial(series_kernel, layout, count, len(arrays)), [jax.S...  8.85 us
    pallas_call x4, Pallas kernels, views_call(): call(body, outs, [INVMEM] * len(operands), scratch, name, flops)(*operands)  4.52 us
    pallas_call x1, Pallas kernels, on_device(): call(functools.partial(mask_kernel, len(inputs)), [block, jax.ShapeDtypeS...  3.59 us
  transfers between devices with their start and end apart: 45, of which 31 were waited for; matrix products, arithmetic and copies ran while one was open for 0% of the time, Pallas kernels for 1%

profile of v10, /device:TPU:1, one launch (start us, length us, event | category | flops | bytes accessed | tf_op | source)
XLA Modules:
  0.0 155.3 jit_solution(17683905591353706322)
XLA Ops:
  0.0 3.6 %mask.1 = (bf16[192,384]{1,0:T(8,128)(2,1)}, bf16[384,384]{1,0:T(8,128)(2,1)}, bf16[592,384]{1,0:T(8,128)(2,1)}) custom-call(s32[3,6,12]{2,1,0:T(8,128)} %refs_0_.1, bf16[192,384]{1,0:T(8,128)(2,1)} %refs_1_.1, bf16[192,384]{1,0:T(8,128)(2,1)} %refs_2_.1, bf16[192,384]{1,0:T(8,128)(2,1)} %refs_3_.1, s32[3,6,12]{2,1,0:T(8,128)} %refs_4_.1, s32[6,7,12]{2,1,0:T(8,128)} %bitcast.1), custom_call_target="tpu_custom_call" | custom-call | flops 1000 | bytes 1000 | tf_op jit(solution)/shard_map/mask/pallas_call | solution.py:397
  3.6 4.5 %collective-permute-start = (bf16[592,384]{1,0:T(8,128)(2,1)}, bf16[592,384]{1,0:T(8,128)(2,1)S(1)}, u32[]{:S(2)}, u32[]{:S(2)}) collective-permute-start(bf16[592,384]{1,0:T(8,128)(2,1)} %get-tuple-element.25), channel_id=1, source_target_pairs={{0,0},{4,1},{2,2},{6,3},{1,4},{5,5},{3,6},{7,7},{8,8},{12,9},{10,1... | collective-permute-start | bytes 1363976 | tf_op jit(solution)/shard_map/ppermute | solution.py:39
  10.1 3.2 %collective-permute-start.7 = (bf16[192,384]{1,0:T(8,128)(2,1)}, bf16[192,384]{1,0:T(8,128)(2,1)S(1)}, u32[]{:S(2)}, u32[]{:S(2)}) collective-permute-start(bf16[192,384]{1,0:T(8,128)(2,1)} %get-tuple-element.28), channel_id=1, source_target_pairs={{16,0},{20,1},{18,2},{22,3},{17,4},{21,5},{19,6},{23,7},{24,8},{28... | collective-permute-start | bytes 442376 | tf_op jit(solution)/shard_map/ppermute | solution.py:39
  13.3 7.7 %collective-permute-done.7.refs_6_ = bf16[192,384]{1,0:T(8,128)(2,1)S(1)} collective-permute-done((bf16[192,384]{1,0:T(8,128)(2,1)}, bf16[192,384]{1,0:T(8,128)(2,1)S(1)}, u32[]{:S(2)}, u32[]{:S(2)}) %collective-permute-start.7) | collective-permute-done | bytes 147488 | tf_op jit(solution)/shard_map/ppermute | solution.py:39
  22.1 5.3 %collective-permute-done.3.refs_1_ = bf16[384,384]{1,0:T(8,128)(2,1)S(1)} collective-permute-done((bf16[384,384]{1,0:T(8,128)(2,1)}, bf16[384,384]{1,0:T(8,128)(2,1)S(1)}, u32[]{:S(2)}, u32[]{:S(2)}) %collective-permute-start.3) | collective-permute-done | bytes 294944 | tf_op jit(solution)/shard_map/ppermute | solution.py:39
  28.4 2.7 %collective-permute-start.1 = (bf16[400,384]{1,0:T(8,128)(2,1)S(1)}, bf16[400,384]{1,0:T(8,128)(2,1)S(1)}, u32[]{:S(2)}, u32[]{:S(2)}) collective-permute-start(bf16[400,384]{1,0:T(8,128)(2,1)S(1)} %slice.36), channel_id=1, source_target_pairs={{16,0},{17,1},{18,2},{19,3},{20,4},{21,5},{22,6},{23,7},{24,8},{25... | collective-permute-start | bytes 921608 | tf_op jit(solution)/shard_map/ppermute | solution.py:39
  31.1 4.9 %collective-permute-done.8.refs_7_ = bf16[192,384]{1,0:T(8,128)(2,1)S(1)} collective-permute-done((bf16[192,384]{1,0:T(8,128)(2,1)S(1)}, bf16[192,384]{1,0:T(8,128)(2,1)S(1)}, u32[]{:S(2)}, u32[]{:S(2)}) %collective-permute-start.8) | collective-permute-done | bytes 147488 | tf_op jit(solution)/shard_map/ppermute | solution.py:39
  36.4 8.9 %collective-permute-done.1.refs_6_ = bf16[400,384]{1,0:T(8,128)(2,1)S(1)} collective-permute-done((bf16[400,384]{1,0:T(8,128)(2,1)S(1)}, bf16[400,384]{1,0:T(8,128)(2,1)S(1)}, u32[]{:S(2)}, u32[]{:S(2)}) %collective-permute-start.1) | collective-permute-done | bytes 307232 | tf_op jit(solution)/shard_map/ppermute | solution.py:39
  51.4 3.5 %collective-permute-done.14.refs_5_ = bf16[400,384]{1,0:T(8,128)(2,1)S(1)} collective-permute-done((bf16[400,384]{1,0:T(8,128)(2,1)S(1)}, bf16[400,384]{1,0:T(8,128)(2,1)S(1)}, u32[]{:S(2)}, u32[]{:S(2)}) %collective-permute-start.14) | collective-permute-done | bytes 307232 | tf_op jit(solution)/shard_map/ppermute | solution.py:39
  54.9 6.6 %collective-permute-done.15.refs_7_ = bf16[400,384]{1,0:T(8,128)(2,1)S(1)} collective-permute-done((bf16[400,384]{1,0:T(8,128)(2,1)S(1)}, bf16[400,384]{1,0:T(8,128)(2,1)S(1)}, u32[]{:S(2)}, u32[]{:S(2)}) %collective-permute-start.15) | collective-permute-done | bytes 307232 | tf_op jit(solution)/shard_map/ppermute | solution.py:39
  73.5 4.6 %collective-permute-done.22 = bf16[192,384]{1,0:T(8,128)(2,1)S(1)} collective-permute-done((bf16[192,384]{1,0:T(8,128)(2,1)S(1)}, bf16[192,384]{1,0:T(8,128)(2,1)S(1)}, u32[]{:S(2)}, u32[]{:S(2)}) %collective-permute-start.22) | collective-permute-done | bytes 147488 | tf_op jit(solution)/shard_map/ppermute | solution.py:39
  82.9 2.8 %collective-permute-done.26.refs_10_ = bf16[192,384]{1,0:T(8,128)(2,1)S(1)} collective-permute-done((bf16[192,384]{1,0:T(8,128)(2,1)S(1)}, bf16[192,384]{1,0:T(8,128)(2,1)S(1)}, u32[]{:S(2)}, u32[]{:S(2)}) %collective-permute-start.26) | collective-permute-done | bytes 147488 | tf_op jit(solution)/shard_map/ppermute | solution.py:39
  85.8 2.4 %collective-permute-start.29 = (bf16[192,384]{1,0:T(8,128)(2,1)S(1)}, bf16[192,384]{1,0:T(8,128)(2,1)S(1)}, u32[]{:S(2)}, u32[]{:S(2)}) collective-permute-start(bf16[192,384]{1,0:T(8,128)(2,1)S(1)} %collective-permute-done.26.refs_10_), channel_id=1, source_target_pairs={{6,0},{7,1},{4,2},{5,3},{2,4},{3,5},{0,6},{1,7},{14,8},{15,9},{12,... | collective-permute-start | bytes 442376 | tf_op jit(solution)/shard_map/ppermute | solution.py:39
  88.8 4.8 %collective-permute-done.24.refs_8_ = bf16[384,384]{1,0:T(8,128)(2,1)S(1)} collective-permute-done((bf16[384,384]{1,0:T(8,128)(2,1)S(1)}, bf16[384,384]{1,0:T(8,128)(2,1)S(1)}, u32[]{:S(2)}, u32[]{:S(2)}) %collective-permute-start.24) | collective-permute-done | bytes 294944 | tf_op jit(solution)/shard_map/ppermute | solution.py:39
  93.7 4.0 %collective-permute-done.23.refs_7_ = bf16[384,384]{1,0:T(8,128)(2,1)S(1)} collective-permute-done((bf16[384,384]{1,0:T(8,128)(2,1)S(1)}, bf16[384,384]{1,0:T(8,128)(2,1)S(1)}, u32[]{:S(2)}, u32[]{:S(2)}) %collective-permute-start.23) | collective-permute-done | bytes 294944 | tf_op jit(solution)/shard_map/ppermute | solution.py:39
  100.0 2.7 %collective-permute-done.27.refs_12_ = bf16[192,384]{1,0:T(8,128)(2,1)S(1)} collective-permute-done((bf16[192,384]{1,0:T(8,128)(2,1)S(1)}, bf16[192,384]{1,0:T(8,128)(2,1)S(1)}, u32[]{:S(2)}, u32[]{:S(2)}) %collective-permute-start.27) | collective-permute-done | bytes 147488 | tf_op jit(solution)/shard_map/ppermute | solution.py:39
  104.2 2.5 %collective-permute-done.20.refs_1_ = bf16[768,384]{1,0:T(8,128)(2,1)S(1)} collective-permute-done((bf16[768,384]{1,0:T(8,128)(2,1)S(1)}, bf16[768,384]{1,0:T(8,128)(2,1)S(1)}, u32[]{:S(2)}, u32[]{:S(2)}) %collective-permute-start.20) | collective-permute-done | bytes 589856 | tf_op jit(solution)/shard_map/ppermute | solution.py:39
  107.6 8.8 %series.1 = (bf16[192,1536]{1,0:T(8,128)(2,1)S(1)}, bf16[192,384]{1,0:T(8,128)(2,1)S(1)}) custom-call(bf16[192,384]{1,0:T(8,128)(2,1)S(1)} %generator.1.refs_0_, bf16[768,384]{1,0:T(8,128)(2,1)S(1)} %collective-permute-done.20.refs_1_, bf16[192,384]{1,0:T(8,128)(2,1)S(1)} %collective-permute-done.17.refs_2_, ...), custom_call_target="tpu_custom_call" | custom-call | flops 1000 | bytes 1000 | tf_op jit(solution)/shard_map/series/pallas_call | solution.py:480
  119.2 3.3 %collective-permute-done.34.refs_3_ = bf16[192,384]{1,0:T(8,128)(2,1)S(1)} collective-permute-done((bf16[192,384]{1,0:T(8,128)(2,1)S(1)}, bf16[192,384]{1,0:T(8,128)(2,1)S(1)}, u32[]{:S(2)}, u32[]{:S(2)}) %collective-permute-start.34) | collective-permute-done | bytes 147488 | tf_op jit(solution)/shard_map/ppermute | solution.py:39
  122.5 2.3 %collective-permute-done.33.refs_2_ = bf16[192,384]{1,0:T(8,128)(2,1)S(1)} collective-permute-done((bf16[192,384]{1,0:T(8,128)(2,1)S(1)}, bf16[192,384]{1,0:T(8,128)(2,1)S(1)}, u32[]{:S(2)}, u32[]{:S(2)}) %collective-permute-start.33) | collective-permute-done | bytes 147488 | tf_op jit(solution)/shard_map/ppermute | solution.py:39
  133.5 5.5 %collective-permute-done.41.refs_6_ = bf16[192,384]{1,0:T(8,128)(2,1)S(1)} collective-permute-done((bf16[192,384]{1,0:T(8,128)(2,1)S(1)}, bf16[192,384]{1,0:T(8,128)(2,1)S(1)}, u32[]{:S(2)}, u32[]{:S(2)}) %collective-permute-start.41) | collective-permute-done | bytes 147488 | tf_op jit(solution)/shard_map/ppermute | solution.py:39
  140.0 3.9 %collective-permute-done.42.refs_7_ = bf16[192,384]{1,0:T(8,128)(2,1)S(1)} collective-permute-done((bf16[192,384]{1,0:T(8,128)(2,1)S(1)}, bf16[192,384]{1,0:T(8,128)(2,1)S(1)}, u32[]{:S(2)}, u32[]{:S(2)}) %collective-permute-start.42) | collective-permute-done | bytes 147488 | tf_op jit(solution)/shard_map/ppermute | solution.py:39
  148.2 2.5 %collective-permute-start.44 = (bf16[192,384]{1,0:T(8,128)(2,1)S(1)}, bf16[192,384]{1,0:T(8,128)(2,1)S(1)}, u32[]{:S(2)}, u32[]{:S(2)}) collective-permute-start(bf16[192,384]{1,0:T(8,128)(2,1)S(1)} %evolve.1), channel_id=1, source_target_pairs={{0,0},{4,1},{2,2},{6,3},{1,4},{5,5},{3,6},{7,7},{8,8},{12,9},{10,1... | collective-permute-start | bytes 442376 | tf_op jit(solution)/shard_map/ppermute | solution.py:39
  150.7 4.0 %collective-permute-done.44 = bf16[192,384]{1,0:T(8,128)(2,1)S(1)} collective-permute-done((bf16[192,384]{1,0:T(8,128)(2,1)S(1)}, bf16[192,384]{1,0:T(8,128)(2,1)S(1)}, u32[]{:S(2)}, u32[]{:S(2)}) %collective-permute-start.44) | collective-permute-done | bytes 147488 | tf_op jit(solution)/shard_map/ppermute | solution.py:39
  (92 shorter events, 50.1 us)
Async XLA Ops:
  3.6 23.8 %collective-permute-start = (bf16[592,384]{1,0:T(8,128)(2,1)}, bf16[592,384]{1,0:T(8,128)(2,1)S(1)}, u32[]{:S(2)}, u32[]{:S(2)}) collective-permute-start(bf16[592,384]{1,0:T(8,128)(2,1)} %get-tuple-element.25), channel_id=1, source_target_pairs={{0,0},{4,1},{2,2},{6,3},{1,4},{5,5},{3,6},{7,7},{8,8},{12,9},{10,1... | collective-permute-start | bytes 1363976 | tf_op jit(solution)/shard_map/ppermute | solution.py:39
  8.1 13.4 %collective-permute-start.5 = (bf16[384,384]{1,0:T(8,128)(2,1)}, bf16[384,384]{1,0:T(8,128)(2,1)S(1)}, u32[]{:S(2)}, u32[]{:S(2)}) collective-permute-start(bf16[384,384]{1,0:T(8,128)(2,1)} %get-tuple-element.27), channel_id=1, source_target_pairs={{3,0},{7,1},{1,2},{5,3},{2,4},{6,5},{0,6},{4,7},{11,8},{15,9},{9,1... | collective-permute-start | bytes 884744 | tf_op jit(solution)/shard_map/ppermute | solution.py:39
  8.2 13.9 %collective-permute-start.4 = (bf16[384,384]{1,0:T(8,128)(2,1)}, bf16[384,384]{1,0:T(8,128)(2,1)S(1)}, u32[]{:S(2)}, u32[]{:S(2)}) collective-permute-start(bf16[384,384]{1,0:T(8,128)(2,1)} %get-tuple-element.27), channel_id=1, source_target_pairs={{2,0},{6,1},{0,2},{4,3},{3,4},{7,5},{1,6},{5,7},{10,8},{14,9},{8,1... | collective-permute-start | bytes 884744 | tf_op jit(solution)/shard_map/ppermute | solution.py:39
  9.2 18.2 %collective-permute-start.3 = (bf16[384,384]{1,0:T(8,128)(2,1)}, bf16[384,384]{1,0:T(8,128)(2,1)S(1)}, u32[]{:S(2)}, u32[]{:S(2)}) collective-permute-start(bf16[384,384]{1,0:T(8,128)(2,1)} %get-tuple-element.27), channel_id=1, source_target_pairs={{1,0},{5,1},{3,2},{7,3},{0,4},{4,5},{2,6},{6,7},{9,8},{13,9},{11,1... | collective-permute-start | bytes 884744 | tf_op jit(solution)/shard_map/ppermute | solution.py:39
  10.1 10.9 %collective-permute-start.7 = (bf16[192,384]{1,0:T(8,128)(2,1)}, bf16[192,384]{1,0:T(8,128)(2,1)S(1)}, u32[]{:S(2)}, u32[]{:S(2)}) collective-permute-start(bf16[192,384]{1,0:T(8,128)(2,1)} %get-tuple-element.28), channel_id=1, source_target_pairs={{16,0},{20,1},{18,2},{22,3},{17,4},{21,5},{19,6},{23,7},{24,8},{28... | collective-permute-start | bytes 442376 | tf_op jit(solution)/shard_map/ppermute | solution.py:39
  21.0 10.2 %collective-permute-start.6 = (bf16[192,384]{1,0:T(8,128)(2,1)}, bf16[192,384]{1,0:T(8,128)(2,1)S(1)}, u32[]{:S(2)}, u32[]{:S(2)}) collective-permute-start(bf16[192,384]{1,0:T(8,128)(2,1)} %get-tuple-element.28), channel_id=1, source_target_pairs={{8,0},{12,1},{10,2},{14,3},{9,4},{13,5},{11,6},{15,7},{0,8},{4,9},... | collective-permute-start | bytes 442376 | tf_op jit(solution)/shard_map/ppermute | solution.py:39
  27.4 8.6 %collective-permute-start.8 = (bf16[192,384]{1,0:T(8,128)(2,1)S(1)}, bf16[192,384]{1,0:T(8,128)(2,1)S(1)}, u32[]{:S(2)}, u32[]{:S(2)}) collective-permute-start(bf16[192,384]{1,0:T(8,128)(2,1)S(1)} %collective-permute-done.7.refs_6_), channel_id=1, source_target_pairs={{8,0},{9,1},{10,2},{11,3},{12,4},{13,5},{14,6},{15,7},{0,8},{1,9},... | collective-permute-start | bytes 442376 | tf_op jit(solution)/shard_map/ppermute | solution.py:39
  28.4 16.9 %collective-permute-start.1 = (bf16[400,384]{1,0:T(8,128)(2,1)S(1)}, bf16[400,384]{1,0:T(8,128)(2,1)S(1)}, u32[]{:S(2)}, u32[]{:S(2)}) collective-permute-start(bf16[400,384]{1,0:T(8,128)(2,1)S(1)} %slice.36), channel_id=1, source_target_pairs={{16,0},{17,1},{18,2},{19,3},{20,4},{21,5},{22,6},{23,7},{24,8},{25... | collective-permute-start | bytes 921608 | tf_op jit(solution)/shard_map/ppermute | solution.py:39
  31.1 16.3 %collective-permute-start.9 = (bf16[592,384]{1,0:T(8,128)(2,1)S(1)}, bf16[592,384]{1,0:T(8,128)(2,1)S(1)}, u32[]{:S(2)}, u32[]{:S(2)}) collective-permute-start(bf16[592,384]{1,0:T(8,128)(2,1)S(1)} %collective-permute-done.refs_0_.refs_4_.refs_5_.refs_9_), channel_id=1, source_target_pairs={{1,0},{0,1},{3,2},{2,3},{5,4},{4,5},{7,6},{6,7},{9,8},{8,9},{11,10... | collective-permute-start | bytes 1363976 | tf_op jit(solution)/shard_map/ppermute | solution.py:39
  36.1 11.4 %collective-permute-start.10 = (bf16[576,384]{1,0:T(8,128)(2,1)S(1)}, bf16[576,384]{1,0:T(8,128)(2,1)S(1)}, u32[]{:S(2)}, u32[]{:S(2)}) collective-permute-start(bf16[576,384]{1,0:T(8,128)(2,1)S(1)} %pad_maximum_fusion.6), channel_id=1, source_target_pairs={{1,0},{0,1},{3,2},{2,3},{5,4},{4,5},{7,6},{6,7},{9,8},{8,9},{11,10... | collective-permute-start | bytes 1327112 | tf_op jit(solution)/shard_map/ppermute | solution.py:39
  46.0 8.9 %collective-permute-start.14 = (bf16[400,384]{1,0:T(8,128)(2,1)S(1)}, bf16[400,384]{1,0:T(8,128)(2,1)S(1)}, u32[]{:S(2)}, u32[]{:S(2)}) collective-permute-start(bf16[400,384]{1,0:T(8,128)(2,1)S(1)} %slice.36), channel_id=1, source_target_pairs={{8,0},{9,1},{10,2},{11,3},{12,4},{13,5},{14,6},{15,7},{0,8},{1,9},... | collective-permute-start | bytes 921608 | tf_op jit(solution)/shard_map/ppermute | solution.py:39
  46.0 15.5 %collective-permute-start.15 = (bf16[400,384]{1,0:T(8,128)(2,1)S(1)}, bf16[400,384]{1,0:T(8,128)(2,1)S(1)}, u32[]{:S(2)}, u32[]{:S(2)}) collective-permute-start(bf16[400,384]{1,0:T(8,128)(2,1)S(1)} %collective-permute-done.1.refs_6_), channel_id=1, source_target_pairs={{8,0},{9,1},{10,2},{11,3},{12,4},{13,5},{14,6},{15,7},{0,8},{1,9},... | collective-permute-start | bytes 921608 | tf_op jit(solution)/shard_map/ppermute | solution.py:39
  48.7 12.8 %collective-permute-start.13 = (bf16[384,384]{1,0:T(8,128)(2,1)S(1)}, bf16[384,384]{1,0:T(8,128)(2,1)S(1)}, u32[]{:S(2)}, u32[]{:S(2)}) collective-permute-start(bf16[384,384]{1,0:T(8,128)(2,1)S(1)} %first.1.refs_0_), channel_id=1, source_target_pairs={{6,0},{7,1},{4,2},{5,3},{2,4},{3,5},{0,6},{1,7},{14,8},{15,9},{12,... | collective-permute-start | bytes 884744 | tf_op jit(solution)/shard_map/ppermute | solution.py:39
  49.1 14.1 %collective-permute-start.12 = (bf16[384,384]{1,0:T(8,128)(2,1)S(1)}, bf16[384,384]{1,0:T(8,128)(2,1)S(1)}, u32[]{:S(2)}, u32[]{:S(2)}) collective-permute-start(bf16[384,384]{1,0:T(8,128)(2,1)S(1)} %first.1.refs_0_), channel_id=1, source_target_pairs={{2,0},{3,1},{0,2},{1,3},{6,4},{7,5},{4,6},{5,7},{10,8},{11,9},{8,1... | collective-permute-start | bytes 884744 | tf_op jit(solution)/shard_map/ppermute | solution.py:39
  50.0 14.8 %collective-permute-start.11 = (bf16[384,384]{1,0:T(8,128)(2,1)S(1)}, bf16[384,384]{1,0:T(8,128)(2,1)S(1)}, u32[]{:S(2)}, u32[]{:S(2)}) collective-permute-start(bf16[384,384]{1,0:T(8,128)(2,1)S(1)} %first.1.refs_0_), channel_id=1, source_target_pairs={{4,0},{5,1},{6,2},{7,3},{0,4},{1,5},{2,6},{3,7},{12,8},{13,9},{14,... | collective-permute-start | bytes 884744 | tf_op jit(solution)/shard_map/ppermute | solution.py:39
  68.4 9.7 %collective-permute-start.22 = (bf16[192,384]{1,0:T(8,128)(2,1)S(1)}, bf16[192,384]{1,0:T(8,128)(2,1)S(1)}, u32[]{:S(2)}, u32[]{:S(2)}) collective-permute-start(bf16[192,384]{1,0:T(8,128)(2,1)S(1)} %generator.1.refs_0_), channel_id=1, source_target_pairs={{16,0},{17,1},{18,2},{19,3},{20,4},{21,5},{22,6},{23,7},{24,8},{25... | collective-permute-start | bytes 442376 | tf_op jit(solution)/shard_map/ppermute | solution.py:39
  69.4 8.7 %collective-permute-start.21 = (bf16[192,384]{1,0:T(8,128)(2,1)S(1)}, bf16[192,384]{1,0:T(8,128)(2,1)S(1)}, u32[]{:S(2)}, u32[]{:S(2)}) collective-permute-start(bf16[192,384]{1,0:T(8,128)(2,1)S(1)} %generator.1.refs_0_), channel_id=1, source_target_pairs={{8,0},{9,1},{10,2},{11,3},{12,4},{13,5},{14,6},{15,7},{0,8},{1,9},... | collective-permute-start | bytes 442376 | tf_op jit(solution)/shard_map/ppermute | solution.py:39
  81.1 12.5 %collective-permute-start.24 = (bf16[384,384]{1,0:T(8,128)(2,1)S(1)}, bf16[384,384]{1,0:T(8,128)(2,1)S(1)}, u32[]{:S(2)}, u32[]{:S(2)}) collective-permute-start(bf16[384,384]{1,0:T(8,128)(2,1)S(1)} %pad_maximum_fusion.8.refs_5_), channel_id=1, source_target_pairs={{2,0},{3,1},{0,2},{1,3},{6,4},{7,5},{4,6},{5,7},{10,8},{11,9},{8,1... | collective-permute-start | bytes 884744 | tf_op jit(solution)/shard_map/ppermute | solution.py:39
  81.5 16.1 %collective-permute-start.23 = (bf16[384,384]{1,0:T(8,128)(2,1)S(1)}, bf16[384,384]{1,0:T(8,128)(2,1)S(1)}, u32[]{:S(2)}, u32[]{:S(2)}) collective-permute-start(bf16[384,384]{1,0:T(8,128)(2,1)S(1)} %pad_maximum_fusion.8.refs_5_), channel_id=1, source_target_pairs={{4,0},{5,1},{6,2},{7,3},{0,4},{1,5},{2,6},{3,7},{12,8},{13,9},{14,... | collective-permute-start | bytes 884744 | tf_op jit(solution)/shard_map/ppermute | solution.py:39
  85.8 12.6 %collective-permute-start.29 = (bf16[192,384]{1,0:T(8,128)(2,1)S(1)}, bf16[192,384]{1,0:T(8,128)(2,1)S(1)}, u32[]{:S(2)}, u32[]{:S(2)}) collective-permute-start(bf16[192,384]{1,0:T(8,128)(2,1)S(1)} %collective-permute-done.26.refs_10_), channel_id=1, source_target_pairs={{6,0},{7,1},{4,2},{5,3},{2,4},{3,5},{0,6},{1,7},{14,8},{15,9},{12,... | collective-permute-start | bytes 442376 | tf_op jit(solution)/shard_map/ppermute | solution.py:39
  88.1 11.9 %collective-permute-start.28 = (bf16[192,384]{1,0:T(8,128)(2,1)S(1)}, bf16[192,384]{1,0:T(8,128)(2,1)S(1)}, u32[]{:S(2)}, u32[]{:S(2)}) collective-permute-start(bf16[192,384]{1,0:T(8,128)(2,1)S(1)} %collective-permute-done.26.refs_10_), channel_id=1, source_target_pairs={{2,0},{3,1},{0,2},{1,3},{6,4},{7,5},{4,6},{5,7},{10,8},{11,9},{8,1... | collective-permute-start | bytes 442376 | tf_op jit(solution)/shard_map/ppermute | solution.py:39
  88.8 13.9 %collective-permute-start.27 = (bf16[192,384]{1,0:T(8,128)(2,1)S(1)}, bf16[192,384]{1,0:T(8,128)(2,1)S(1)}, u32[]{:S(2)}, u32[]{:S(2)}) collective-permute-start(bf16[192,384]{1,0:T(8,128)(2,1)S(1)} %collective-permute-done.26.refs_10_), channel_id=1, source_target_pairs={{4,0},{5,1},{6,2},{7,3},{0,4},{1,5},{2,6},{3,7},{12,8},{13,9},{14,... | collective-permute-start | bytes 442376 | tf_op jit(solution)/shard_map/ppermute | solution.py:39
  129.3 9.7 %collective-permute-start.41 = (bf16[192,384]{1,0:T(8,128)(2,1)S(1)}, bf16[192,384]{1,0:T(8,128)(2,1)S(1)}, u32[]{:S(2)}, u32[]{:S(2)}) collective-permute-start(bf16[192,384]{1,0:T(8,128)(2,1)S(1)} %square.1.refs_0_), channel_id=1, source_target_pairs={{16,0},{17,1},{18,2},{19,3},{20,4},{21,5},{22,6},{23,7},{24,8},{25... | collective-permute-start | bytes 442376 | tf_op jit(solution)/shard_map/ppermute | solution.py:39
  129.5 9.5 %collective-permute-start.38 = (bf16[192,384]{1,0:T(8,128)(2,1)S(1)}, bf16[192,384]{1,0:T(8,128)(2,1)S(1)}, u32[]{:S(2)}, u32[]{:S(2)}) collective-permute-start(bf16[192,384]{1,0:T(8,128)(2,1)S(1)} %square.1.refs_0_), channel_id=1, source_target_pairs={{6,0},{7,1},{4,2},{5,3},{2,4},{3,5},{0,6},{1,7},{14,8},{15,9},{12,... | collective-permute-start | bytes 442376 | tf_op jit(solution)/shard_map/ppermute | solution.py:39
  (22 other events, 125.1 us)

commit v11 on v10

--- a/solution.py
+++ b/solution.py
@@ -49,7 +49,7 @@
         held = {0: value}
         for bit in reversed(bits):
             for k, part in list(held.items()):
-                if k == 0 and relabel:
+                if k == 0 and relabel and (second is None or bit == bits[-1]):
                     held[bit] = self.relabel(value, bit)
                 else:
                     if k and gate is not None:
@@ -408,19 +408,18 @@
         room=60,
     )(*inputs)
 
-    trio = moves.relabel(trio)
+    home = trio
+    trio = moves.relabel(home)
     fock_rows = moves.plane(duo, True)
-    density_line = moves.line(masked_density, True, gate=(trio, *fock_rows))
+    density_line = moves.line(masked_density, True)
     density_near = [(trio, TAIL + 2 * rows)] + whole(density_line)
-    pair = trio[: TAIL + 2 * rows]
-    pair_second, *_ = barrier((pair, *density_line))
-    pair_line = moves.line(pair, second=pair_second)
-    density_line = list(barrier((*density_line, *fock_rows))[: count - 1])
+    span = TAIL + 2 * rows
+    pair_second, *_ = barrier((trio[:span], *density_line))
+    pair_line = moves.line(home[:span], True, second=pair_second)
+    early = barrier((*density_line, trio, pair_line[half - 1], *fock_rows))
+    density_line, trio, pair_line[half - 1] = list(early[: count - 1]), early[count - 1], early[count]
     trio_far = moves.core(trio)
     density_far = [(trio_far, TAIL + 2 * rows)] + moves.cores(density_line)
-    early_far = moves.cores(pair_line[half - 1 : half])
-    trio, early, _ = barrier((trio, early_far[0][0], pair_line[half - 1]))
-    early_far = [(early, 0)]
 
     products = views_call(
         functools.partial(first_kernel, count),
@@ -437,9 +436,7 @@
     )
     product_rows = [products] + moves.plane(products)
     pair_line = list(barrier((*pair_line, *product_rows[1:]))[: count - 1])
-    rest = pair_line[: half - 1] + pair_line[half:]
-    rest_far = moves.cores(rest)
-    pair_far = [(trio_far, 0)] + rest_far[: half - 1] + early_far + rest_far[half - 1 :]
+    pair_far = [(trio_far, 0)] + moves.cores(pair_line[:half]) + moves.cores(pair_line[half:])
     pair_near = [(trio, 0)] + whole(pair_line)
 
     generator = views_call(

time: 156 us -> 148 us (0.949)
  waiting for transfers between devices: 93.7 us -> 81.6 us
  starting transfers between devices: 43.2 us -> 47.1 us
    ppermute x45, waiting for transfers between devices: 93.7 us -> 81.6 us  [move(): return lax.ppermute(value, AXES, permutation(self.rows, self.cols, source))]
    ppermute x45, starting transfers between devices: 43.2 us -> 47.1 us  [move(): return lax.ppermute(value, AXES, permutation(self.rows, self.cols, source))]
  transfers between devices with their start and end apart: 45 -> 45, of which waited for: 31 -> 31; matrix products, arithmetic and copies ran while one was open for 0% -> 1% of each run, Pallas kernels for 1% -> 1%
where the time goes in v11:
time: 148 us
  waiting for transfers between devices  81.6 us (55%)
  starting transfers between devices  47.1 us (32%)
  Pallas kernels  17 us (11%)
  local copies, waits for them, and re-layouts  1.71 us (1%)
    ppermute x45, waiting for transfers between devices, move(): return lax.ppermute(value, AXES, permutation(self.rows, self.cols, source))  81.6 us
    ppermute x45, starting transfers between devices, move(): return lax.ppermute(value, AXES, permutation(self.rows, self.cols, source))  47.1 us
    pallas_call x1, Pallas kernels, on_device(): call(functools.partial(series_kernel, layout, count, len(arrays)), [jax.S...  8.84 us
    pallas_call x4, Pallas kernels, views_call(): call(body, outs, [INVMEM] * len(operands), scratch, name, flops)(*operands)  4.53 us
    pallas_call x1, Pallas kernels, on_device(): call(functools.partial(mask_kernel, len(inputs)), [block, jax.ShapeDtypeS...  3.59 us
  transfers between devices with their start and end apart: 45, of which 31 were waited for; matrix products, arithmetic and copies ran while one was open for 1% of the time, Pallas kernels for 1%

profile of v11, /device:TPU:1, one launch (start us, length us, event | category | flops | bytes accessed | tf_op | source)
XLA Modules:
  0.0 148.2 jit_solution(8525092013665095734)
XLA Ops:
  0.0 3.6 %mask.1 = (bf16[192,384]{1,0:T(8,128)(2,1)}, bf16[384,384]{1,0:T(8,128)(2,1)}, bf16[592,384]{1,0:T(8,128)(2,1)}) custom-call(s32[3,6,12]{2,1,0:T(8,128)} %refs_0_.1, bf16[192,384]{1,0:T(8,128)(2,1)} %refs_1_.1, bf16[192,384]{1,0:T(8,128)(2,1)} %refs_2_.1, bf16[192,384]{1,0:T(8,128)(2,1)} %refs_3_.1, s32[3,6,12]{2,1,0:T(8,128)} %refs_4_.1, s32[6,7,12]{2,1,0:T(8,128)} %bitcast.1), custom_call_target="tpu_custom_call" | custom-call | flops 1000 | bytes 1000 | tf_op jit(solution)/shard_map/mask/pallas_call | solution.py:397
  3.6 4.7 %collective-permute-start.1 = (bf16[192,384]{1,0:T(8,128)(2,1)}, bf16[192,384]{1,0:T(8,128)(2,1)S(1)}, u32[]{:S(2)}, u32[]{:S(2)}) collective-permute-start(bf16[192,384]{1,0:T(8,128)(2,1)} %get-tuple-element.24), channel_id=1, source_target_pairs={{16,0},{20,1},{18,2},{22,3},{17,4},{21,5},{19,6},{23,7},{24,8},{28... | collective-permute-start | bytes 442376 | tf_op jit(solution)/shard_map/ppermute | solution.py:39
  10.2 2.8 %collective-permute-start = (bf16[192,384]{1,0:T(8,128)(2,1)}, bf16[192,384]{1,0:T(8,128)(2,1)S(1)}, u32[]{:S(2)}, u32[]{:S(2)}) collective-permute-start(bf16[192,384]{1,0:T(8,128)(2,1)} %get-tuple-element.24), channel_id=1, source_target_pairs={{8,0},{12,1},{10,2},{14,3},{9,4},{13,5},{11,6},{15,7},{0,8},{4,9},... | collective-permute-start | bytes 442376 | tf_op jit(solution)/shard_map/ppermute | solution.py:39
  13.1 2.5 %collective-permute-done.1.refs_6_ = bf16[192,384]{1,0:T(8,128)(2,1)S(1)} collective-permute-done((bf16[192,384]{1,0:T(8,128)(2,1)}, bf16[192,384]{1,0:T(8,128)(2,1)S(1)}, u32[]{:S(2)}, u32[]{:S(2)}) %collective-permute-start.1) | collective-permute-done | bytes 147488 | tf_op jit(solution)/shard_map/ppermute | solution.py:39
  17.3 4.5 %collective-permute-start.4 = (bf16[400,384]{1,0:T(8,128)(2,1)S(1)}, bf16[400,384]{1,0:T(8,128)(2,1)S(1)}, u32[]{:S(2)}, u32[]{:S(2)}) collective-permute-start(bf16[400,384]{1,0:T(8,128)(2,1)S(1)} %slice.30), channel_id=1, source_target_pairs={{16,0},{20,1},{18,2},{22,3},{17,4},{21,5},{19,6},{23,7},{24,8},{28... | collective-permute-start | bytes 921608 | tf_op jit(solution)/shard_map/ppermute | solution.py:39
  23.3 10.2 %collective-permute-done.7.refs_3_ = bf16[384,384]{1,0:T(8,128)(2,1)S(1)} collective-permute-done((bf16[384,384]{1,0:T(8,128)(2,1)}, bf16[384,384]{1,0:T(8,128)(2,1)S(1)}, u32[]{:S(2)}, u32[]{:S(2)}) %collective-permute-start.7) | collective-permute-done | bytes 294944 | tf_op jit(solution)/shard_map/ppermute | solution.py:39
  33.5 2.8 %collective-permute-done.6.refs_2_ = bf16[384,384]{1,0:T(8,128)(2,1)S(1)} collective-permute-done((bf16[384,384]{1,0:T(8,128)(2,1)}, bf16[384,384]{1,0:T(8,128)(2,1)S(1)}, u32[]{:S(2)}, u32[]{:S(2)}) %collective-permute-start.6) | collective-permute-done | bytes 294944 | tf_op jit(solution)/shard_map/ppermute | solution.py:39
  44.4 3.1 %collective-permute-done.14.refs_7_ = bf16[400,384]{1,0:T(8,128)(2,1)S(1)} collective-permute-done((bf16[400,384]{1,0:T(8,128)(2,1)S(1)}, bf16[400,384]{1,0:T(8,128)(2,1)S(1)}, u32[]{:S(2)}, u32[]{:S(2)}) %collective-permute-start.14) | collective-permute-done | bytes 307232 | tf_op jit(solution)/shard_map/ppermute | solution.py:39
  47.5 6.6 %collective-permute-done.13.refs_5_ = bf16[400,384]{1,0:T(8,128)(2,1)S(1)} collective-permute-done((bf16[400,384]{1,0:T(8,128)(2,1)S(1)}, bf16[400,384]{1,0:T(8,128)(2,1)S(1)}, u32[]{:S(2)}, u32[]{:S(2)}) %collective-permute-start.13) | collective-permute-done | bytes 307232 | tf_op jit(solution)/shard_map/ppermute | solution.py:39
  66.1 5.3 %collective-permute-done.22 = bf16[192,384]{1,0:T(8,128)(2,1)S(1)} collective-permute-done((bf16[192,384]{1,0:T(8,128)(2,1)S(1)}, bf16[192,384]{1,0:T(8,128)(2,1)S(1)}, u32[]{:S(2)}, u32[]{:S(2)}) %collective-permute-start.22) | collective-permute-done | bytes 147488 | tf_op jit(solution)/shard_map/ppermute | solution.py:39
  72.5 2.5 %collective-permute-start.25 = (bf16[384,384]{1,0:T(8,128)(2,1)S(1)}, bf16[384,384]{1,0:T(8,128)(2,1)S(1)}, u32[]{:S(2)}, u32[]{:S(2)}) collective-permute-start(bf16[384,384]{1,0:T(8,128)(2,1)S(1)} %pad_maximum_fusion.8.refs_5_), channel_id=1, source_target_pairs={{6,0},{7,1},{4,2},{5,3},{2,4},{3,5},{0,6},{1,7},{14,8},{15,9},{12,... | collective-permute-start | bytes 884744 | tf_op jit(solution)/shard_map/ppermute | solution.py:39
  75.6 3.9 %collective-permute-done.26.refs_10_ = bf16[192,384]{1,0:T(8,128)(2,1)S(1)} collective-permute-done((bf16[192,384]{1,0:T(8,128)(2,1)S(1)}, bf16[192,384]{1,0:T(8,128)(2,1)S(1)}, u32[]{:S(2)}, u32[]{:S(2)}) %collective-permute-start.26) | collective-permute-done | bytes 147488 | tf_op jit(solution)/shard_map/ppermute | solution.py:39
  82.6 5.1 %collective-permute-done.24.refs_8_ = bf16[384,384]{1,0:T(8,128)(2,1)S(1)} collective-permute-done((bf16[384,384]{1,0:T(8,128)(2,1)S(1)}, bf16[384,384]{1,0:T(8,128)(2,1)S(1)}, u32[]{:S(2)}, u32[]{:S(2)}) %collective-permute-start.24) | collective-permute-done | bytes 294944 | tf_op jit(solution)/shard_map/ppermute | solution.py:39
  87.7 2.6 %collective-permute-done.23.refs_7_ = bf16[384,384]{1,0:T(8,128)(2,1)S(1)} collective-permute-done((bf16[384,384]{1,0:T(8,128)(2,1)S(1)}, bf16[384,384]{1,0:T(8,128)(2,1)S(1)}, u32[]{:S(2)}, u32[]{:S(2)}) %collective-permute-start.23) | collective-permute-done | bytes 294944 | tf_op jit(solution)/shard_map/ppermute | solution.py:39
  90.3 3.7 %collective-permute-done.28.refs_13_ = bf16[192,384]{1,0:T(8,128)(2,1)S(1)} collective-permute-done((bf16[192,384]{1,0:T(8,128)(2,1)S(1)}, bf16[192,384]{1,0:T(8,128)(2,1)S(1)}, u32[]{:S(2)}, u32[]{:S(2)}) %collective-permute-start.28) | collective-permute-done | bytes 147488 | tf_op jit(solution)/shard_map/ppermute | solution.py:39
  96.9 2.5 %collective-permute-done.20.refs_1_ = bf16[768,384]{1,0:T(8,128)(2,1)S(1)} collective-permute-done((bf16[768,384]{1,0:T(8,128)(2,1)S(1)}, bf16[768,384]{1,0:T(8,128)(2,1)S(1)}, u32[]{:S(2)}, u32[]{:S(2)}) %collective-permute-start.20) | collective-permute-done | bytes 589856 | tf_op jit(solution)/shard_map/ppermute | solution.py:39
  100.2 8.8 %series.1 = (bf16[192,1536]{1,0:T(8,128)(2,1)S(1)}, bf16[192,384]{1,0:T(8,128)(2,1)S(1)}) custom-call(bf16[192,384]{1,0:T(8,128)(2,1)S(1)} %generator.1.refs_0_, bf16[768,384]{1,0:T(8,128)(2,1)S(1)} %collective-permute-done.20.refs_1_, bf16[192,384]{1,0:T(8,128)(2,1)S(1)} %collective-permute-done.17.refs_2_, ...), custom_call_target="tpu_custom_call" | custom-call | flops 1000 | bytes 1000 | tf_op jit(solution)/shard_map/series/pallas_call | solution.py:477
  109.1 2.1 %collective-permute-start.34 = (bf16[192,384]{1,0:T(8,128)(2,1)S(1)}, bf16[192,384]{1,0:T(8,128)(2,1)S(1)}, u32[]{:S(2)}, u32[]{:S(2)}) collective-permute-start(bf16[192,384]{1,0:T(8,128)(2,1)S(1)} %get-tuple-element.41.refs_0_), channel_id=1, source_target_pairs={{6,0},{7,1},{4,2},{5,3},{2,4},{3,5},{0,6},{1,7},{14,8},{15,9},{12,... | collective-permute-start | bytes 442376 | tf_op jit(solution)/shard_map/ppermute | solution.py:39
  111.8 3.3 %collective-permute-done.34.refs_3_ = bf16[192,384]{1,0:T(8,128)(2,1)S(1)} collective-permute-done((bf16[192,384]{1,0:T(8,128)(2,1)S(1)}, bf16[192,384]{1,0:T(8,128)(2,1)S(1)}, u32[]{:S(2)}, u32[]{:S(2)}) %collective-permute-start.34) | collective-permute-done | bytes 147488 | tf_op jit(solution)/shard_map/ppermute | solution.py:39
  115.1 3.1 %collective-permute-done.33.refs_2_ = bf16[192,384]{1,0:T(8,128)(2,1)S(1)} collective-permute-done((bf16[192,384]{1,0:T(8,128)(2,1)S(1)}, bf16[192,384]{1,0:T(8,128)(2,1)S(1)}, u32[]{:S(2)}, u32[]{:S(2)}) %collective-permute-start.33) | collective-permute-done | bytes 147488 | tf_op jit(solution)/shard_map/ppermute | solution.py:39
  126.9 4.9 %collective-permute-done.41.refs_6_ = bf16[192,384]{1,0:T(8,128)(2,1)S(1)} collective-permute-done((bf16[192,384]{1,0:T(8,128)(2,1)S(1)}, bf16[192,384]{1,0:T(8,128)(2,1)S(1)}, u32[]{:S(2)}, u32[]{:S(2)}) %collective-permute-start.41) | collective-permute-done | bytes 147488 | tf_op jit(solution)/shard_map/ppermute | solution.py:39
  134.0 2.8 %collective-permute-done.42.refs_7_ = bf16[192,384]{1,0:T(8,128)(2,1)S(1)} collective-permute-done((bf16[192,384]{1,0:T(8,128)(2,1)S(1)}, bf16[192,384]{1,0:T(8,128)(2,1)S(1)}, u32[]{:S(2)}, u32[]{:S(2)}) %collective-permute-start.42) | collective-permute-done | bytes 147488 | tf_op jit(solution)/shard_map/ppermute | solution.py:39
  141.1 3.2 %collective-permute-start.44 = (bf16[192,384]{1,0:T(8,128)(2,1)S(1)}, bf16[192,384]{1,0:T(8,128)(2,1)S(1)}, u32[]{:S(2)}, u32[]{:S(2)}) collective-permute-start(bf16[192,384]{1,0:T(8,128)(2,1)S(1)} %evolve.1), channel_id=1, source_target_pairs={{0,0},{4,1},{2,2},{6,3},{1,4},{5,5},{3,6},{7,7},{8,8},{12,9},{10,1... | collective-permute-start | bytes 442376 | tf_op jit(solution)/shard_map/ppermute | solution.py:39
  144.3 3.2 %collective-permute-done.44 = bf16[192,384]{1,0:T(8,128)(2,1)S(1)} collective-permute-done((bf16[192,384]{1,0:T(8,128)(2,1)S(1)}, bf16[192,384]{1,0:T(8,128)(2,1)S(1)}, u32[]{:S(2)}, u32[]{:S(2)}) %collective-permute-start.44) | collective-permute-done | bytes 147488 | tf_op jit(solution)/shard_map/ppermute | solution.py:39
  (93 shorter events, 50.0 us)
Async XLA Ops:
  3.6 11.9 %collective-permute-start.1 = (bf16[192,384]{1,0:T(8,128)(2,1)}, bf16[192,384]{1,0:T(8,128)(2,1)S(1)}, u32[]{:S(2)}, u32[]{:S(2)}) collective-permute-start(bf16[192,384]{1,0:T(8,128)(2,1)} %get-tuple-element.24), channel_id=1, source_target_pairs={{16,0},{20,1},{18,2},{22,3},{17,4},{21,5},{19,6},{23,7},{24,8},{28... | collective-permute-start | bytes 442376 | tf_op jit(solution)/shard_map/ppermute | solution.py:39
  8.3 29.7 %collective-permute-start.3 = (bf16[592,384]{1,0:T(8,128)(2,1)}, bf16[592,384]{1,0:T(8,128)(2,1)S(1)}, u32[]{:S(2)}, u32[]{:S(2)}) collective-permute-start(bf16[592,384]{1,0:T(8,128)(2,1)} %get-tuple-element.25), channel_id=1, source_target_pairs={{0,0},{4,1},{2,2},{6,3},{1,4},{5,5},{3,6},{7,7},{8,8},{12,9},{10,1... | collective-permute-start | bytes 1363976 | tf_op jit(solution)/shard_map/ppermute | solution.py:39
  10.2 12.2 %collective-permute-start = (bf16[192,384]{1,0:T(8,128)(2,1)}, bf16[192,384]{1,0:T(8,128)(2,1)S(1)}, u32[]{:S(2)}, u32[]{:S(2)}) collective-permute-start(bf16[192,384]{1,0:T(8,128)(2,1)} %get-tuple-element.24), channel_id=1, source_target_pairs={{8,0},{12,1},{10,2},{14,3},{9,4},{13,5},{11,6},{15,7},{0,8},{4,9},... | collective-permute-start | bytes 442376 | tf_op jit(solution)/shard_map/ppermute | solution.py:39
  17.3 20.7 %collective-permute-start.4 = (bf16[400,384]{1,0:T(8,128)(2,1)S(1)}, bf16[400,384]{1,0:T(8,128)(2,1)S(1)}, u32[]{:S(2)}, u32[]{:S(2)}) collective-permute-start(bf16[400,384]{1,0:T(8,128)(2,1)S(1)} %slice.30), channel_id=1, source_target_pairs={{16,0},{20,1},{18,2},{22,3},{17,4},{21,5},{19,6},{23,7},{24,8},{28... | collective-permute-start | bytes 921608 | tf_op jit(solution)/shard_map/ppermute | solution.py:39
  21.9 11.6 %collective-permute-start.7 = (bf16[384,384]{1,0:T(8,128)(2,1)}, bf16[384,384]{1,0:T(8,128)(2,1)S(1)}, u32[]{:S(2)}, u32[]{:S(2)}) collective-permute-start(bf16[384,384]{1,0:T(8,128)(2,1)} %get-tuple-element.26), channel_id=1, source_target_pairs={{3,0},{7,1},{1,2},{5,3},{2,4},{6,5},{0,6},{4,7},{11,8},{15,9},{9,1... | collective-permute-start | bytes 884744 | tf_op jit(solution)/shard_map/ppermute | solution.py:39
  22.5 13.9 %collective-permute-start.6 = (bf16[384,384]{1,0:T(8,128)(2,1)}, bf16[384,384]{1,0:T(8,128)(2,1)S(1)}, u32[]{:S(2)}, u32[]{:S(2)}) collective-permute-start(bf16[384,384]{1,0:T(8,128)(2,1)} %get-tuple-element.26), channel_id=1, source_target_pairs={{2,0},{6,1},{0,2},{4,3},{3,4},{7,5},{1,6},{5,7},{10,8},{14,9},{8,1... | collective-permute-start | bytes 884744 | tf_op jit(solution)/shard_map/ppermute | solution.py:39
  22.5 15.5 %collective-permute-start.5 = (bf16[384,384]{1,0:T(8,128)(2,1)}, bf16[384,384]{1,0:T(8,128)(2,1)S(1)}, u32[]{:S(2)}, u32[]{:S(2)}) collective-permute-start(bf16[384,384]{1,0:T(8,128)(2,1)} %get-tuple-element.26), channel_id=1, source_target_pairs={{1,0},{5,1},{3,2},{7,3},{0,4},{4,5},{2,6},{6,7},{9,8},{13,9},{11,1... | collective-permute-start | bytes 884744 | tf_op jit(solution)/shard_map/ppermute | solution.py:39
  38.6 8.9 %collective-permute-start.14 = (bf16[400,384]{1,0:T(8,128)(2,1)S(1)}, bf16[400,384]{1,0:T(8,128)(2,1)S(1)}, u32[]{:S(2)}, u32[]{:S(2)}) collective-permute-start(bf16[400,384]{1,0:T(8,128)(2,1)S(1)} %collective-permute-done.4.refs_6_), channel_id=1, source_target_pairs={{8,0},{9,1},{10,2},{11,3},{12,4},{13,5},{14,6},{15,7},{0,8},{1,9},... | collective-permute-start | bytes 921608 | tf_op jit(solution)/shard_map/ppermute | solution.py:39
  38.7 15.4 %collective-permute-start.13 = (bf16[400,384]{1,0:T(8,128)(2,1)S(1)}, bf16[400,384]{1,0:T(8,128)(2,1)S(1)}, u32[]{:S(2)}, u32[]{:S(2)}) collective-permute-start(bf16[400,384]{1,0:T(8,128)(2,1)S(1)} %slice.40), channel_id=1, source_target_pairs={{8,0},{9,1},{10,2},{11,3},{12,4},{13,5},{14,6},{15,7},{0,8},{1,9},... | collective-permute-start | bytes 921608 | tf_op jit(solution)/shard_map/ppermute | solution.py:39
  41.7 12.4 %collective-permute-start.12 = (bf16[384,384]{1,0:T(8,128)(2,1)S(1)}, bf16[384,384]{1,0:T(8,128)(2,1)S(1)}, u32[]{:S(2)}, u32[]{:S(2)}) collective-permute-start(bf16[384,384]{1,0:T(8,128)(2,1)S(1)} %first.1.refs_0_), channel_id=1, source_target_pairs={{6,0},{7,1},{4,2},{5,3},{2,4},{3,5},{0,6},{1,7},{14,8},{15,9},{12,... | collective-permute-start | bytes 884744 | tf_op jit(solution)/shard_map/ppermute | solution.py:39
  43.2 12.9 %collective-permute-start.11 = (bf16[384,384]{1,0:T(8,128)(2,1)S(1)}, bf16[384,384]{1,0:T(8,128)(2,1)S(1)}, u32[]{:S(2)}, u32[]{:S(2)}) collective-permute-start(bf16[384,384]{1,0:T(8,128)(2,1)S(1)} %first.1.refs_0_), channel_id=1, source_target_pairs={{2,0},{3,1},{0,2},{1,3},{6,4},{7,5},{4,6},{5,7},{10,8},{11,9},{8,1... | collective-permute-start | bytes 884744 | tf_op jit(solution)/shard_map/ppermute | solution.py:39
  43.4 14.5 %collective-permute-start.10 = (bf16[384,384]{1,0:T(8,128)(2,1)S(1)}, bf16[384,384]{1,0:T(8,128)(2,1)S(1)}, u32[]{:S(2)}, u32[]{:S(2)}) collective-permute-start(bf16[384,384]{1,0:T(8,128)(2,1)S(1)} %first.1.refs_0_), channel_id=1, source_target_pairs={{4,0},{5,1},{6,2},{7,3},{0,4},{1,5},{2,6},{3,7},{12,8},{13,9},{14,... | collective-permute-start | bytes 884744 | tf_op jit(solution)/shard_map/ppermute | solution.py:39
  61.9 9.5 %collective-permute-start.22 = (bf16[192,384]{1,0:T(8,128)(2,1)S(1)}, bf16[192,384]{1,0:T(8,128)(2,1)S(1)}, u32[]{:S(2)}, u32[]{:S(2)}) collective-permute-start(bf16[192,384]{1,0:T(8,128)(2,1)S(1)} %generator.1.refs_0_), channel_id=1, source_target_pairs={{16,0},{17,1},{18,2},{19,3},{20,4},{21,5},{22,6},{23,7},{24,8},{25... | collective-permute-start | bytes 442376 | tf_op jit(solution)/shard_map/ppermute | solution.py:39
  62.4 9.0 %collective-permute-start.21 = (bf16[192,384]{1,0:T(8,128)(2,1)S(1)}, bf16[192,384]{1,0:T(8,128)(2,1)S(1)}, u32[]{:S(2)}, u32[]{:S(2)}) collective-permute-start(bf16[192,384]{1,0:T(8,128)(2,1)S(1)} %generator.1.refs_0_), channel_id=1, source_target_pairs={{8,0},{9,1},{10,2},{11,3},{12,4},{13,5},{14,6},{15,7},{0,8},{1,9},... | collective-permute-start | bytes 442376 | tf_op jit(solution)/shard_map/ppermute | solution.py:39
  72.5 8.3 %collective-permute-start.25 = (bf16[384,384]{1,0:T(8,128)(2,1)S(1)}, bf16[384,384]{1,0:T(8,128)(2,1)S(1)}, u32[]{:S(2)}, u32[]{:S(2)}) collective-permute-start(bf16[384,384]{1,0:T(8,128)(2,1)S(1)} %pad_maximum_fusion.8.refs_5_), channel_id=1, source_target_pairs={{6,0},{7,1},{4,2},{5,3},{2,4},{3,5},{0,6},{1,7},{14,8},{15,9},{12,... | collective-permute-start | bytes 884744 | tf_op jit(solution)/shard_map/ppermute | solution.py:39
  74.9 12.8 %collective-permute-start.24 = (bf16[384,384]{1,0:T(8,128)(2,1)S(1)}, bf16[384,384]{1,0:T(8,128)(2,1)S(1)}, u32[]{:S(2)}, u32[]{:S(2)}) collective-permute-start(bf16[384,384]{1,0:T(8,128)(2,1)S(1)} %pad_maximum_fusion.8.refs_5_), channel_id=1, source_target_pairs={{2,0},{3,1},{0,2},{1,3},{6,4},{7,5},{4,6},{5,7},{10,8},{11,9},{8,1... | collective-permute-start | bytes 884744 | tf_op jit(solution)/shard_map/ppermute | solution.py:39
  75.5 14.8 %collective-permute-start.23 = (bf16[384,384]{1,0:T(8,128)(2,1)S(1)}, bf16[384,384]{1,0:T(8,128)(2,1)S(1)}, u32[]{:S(2)}, u32[]{:S(2)}) collective-permute-start(bf16[384,384]{1,0:T(8,128)(2,1)S(1)} %pad_maximum_fusion.8.refs_5_), channel_id=1, source_target_pairs={{4,0},{5,1},{6,2},{7,3},{0,4},{1,5},{2,6},{3,7},{12,8},{13,9},{14,... | collective-permute-start | bytes 884744 | tf_op jit(solution)/shard_map/ppermute | solution.py:39
  79.5 10.8 %collective-permute-start.29 = (bf16[192,384]{1,0:T(8,128)(2,1)S(1)}, bf16[192,384]{1,0:T(8,128)(2,1)S(1)}, u32[]{:S(2)}, u32[]{:S(2)}) collective-permute-start(bf16[192,384]{1,0:T(8,128)(2,1)S(1)} %collective-permute-done.26.refs_10_), channel_id=1, source_target_pairs={{6,0},{7,1},{4,2},{5,3},{2,4},{3,5},{0,6},{1,7},{14,8},{15,9},{12,... | collective-permute-start | bytes 442376 | tf_op jit(solution)/shard_map/ppermute | solution.py:39
  80.4 13.7 %collective-permute-start.28 = (bf16[192,384]{1,0:T(8,128)(2,1)S(1)}, bf16[192,384]{1,0:T(8,128)(2,1)S(1)}, u32[]{:S(2)}, u32[]{:S(2)}) collective-permute-start(bf16[192,384]{1,0:T(8,128)(2,1)S(1)} %collective-permute-done.26.refs_10_), channel_id=1, source_target_pairs={{2,0},{3,1},{0,2},{1,3},{6,4},{7,5},{4,6},{5,7},{10,8},{11,9},{8,1... | collective-permute-start | bytes 442376 | tf_op jit(solution)/shard_map/ppermute | solution.py:39
  80.8 14.2 %collective-permute-start.27 = (bf16[192,384]{1,0:T(8,128)(2,1)S(1)}, bf16[192,384]{1,0:T(8,128)(2,1)S(1)}, u32[]{:S(2)}, u32[]{:S(2)}) collective-permute-start(bf16[192,384]{1,0:T(8,128)(2,1)S(1)} %collective-permute-done.26.refs_10_), channel_id=1, source_target_pairs={{4,0},{5,1},{6,2},{7,3},{0,4},{1,5},{2,6},{3,7},{12,8},{13,9},{14,... | collective-permute-start | bytes 442376 | tf_op jit(solution)/shard_map/ppermute | solution.py:39
  122.0 9.9 %collective-permute-start.41 = (bf16[192,384]{1,0:T(8,128)(2,1)S(1)}, bf16[192,384]{1,0:T(8,128)(2,1)S(1)}, u32[]{:S(2)}, u32[]{:S(2)}) collective-permute-start(bf16[192,384]{1,0:T(8,128)(2,1)S(1)} %square.1.refs_0_), channel_id=1, source_target_pairs={{16,0},{17,1},{18,2},{19,3},{20,4},{21,5},{22,6},{23,7},{24,8},{25... | collective-permute-start | bytes 442376 | tf_op jit(solution)/shard_map/ppermute | solution.py:39
  123.1 8.8 %collective-permute-start.38 = (bf16[192,384]{1,0:T(8,128)(2,1)S(1)}, bf16[192,384]{1,0:T(8,128)(2,1)S(1)}, u32[]{:S(2)}, u32[]{:S(2)}) collective-permute-start(bf16[192,384]{1,0:T(8,128)(2,1)S(1)} %square.1.refs_0_), channel_id=1, source_target_pairs={{6,0},{7,1},{4,2},{5,3},{2,4},{3,5},{0,6},{1,7},{14,8},{15,9},{12,... | collective-permute-start | bytes 442376 | tf_op jit(solution)/shard_map/ppermute | solution.py:39
  124.6 8.3 %collective-permute-start.36 = (bf16[192,384]{1,0:T(8,128)(2,1)S(1)}, bf16[192,384]{1,0:T(8,128)(2,1)S(1)}, u32[]{:S(2)}, u32[]{:S(2)}) collective-permute-start(bf16[192,384]{1,0:T(8,128)(2,1)S(1)} %square.1.refs_0_), channel_id=1, source_target_pairs={{4,0},{5,1},{6,2},{7,3},{0,4},{1,5},{2,6},{3,7},{12,8},{13,9},{14,... | collective-permute-start | bytes 442376 | tf_op jit(solution)/shard_map/ppermute | solution.py:39
  125.7 8.2 %collective-permute-start.40 = (bf16[192,384]{1,0:T(8,128)(2,1)S(1)}, bf16[192,384]{1,0:T(8,128)(2,1)S(1)}, u32[]{:S(2)}, u32[]{:S(2)}) collective-permute-start(bf16[192,384]{1,0:T(8,128)(2,1)S(1)} %square.1.refs_0_), channel_id=1, source_target_pairs={{8,0},{9,1},{10,2},{11,3},{12,4},{13,5},{14,6},{15,7},{0,8},{1,9},... | collective-permute-start | bytes 442376 | tf_op jit(solution)/shard_map/ppermute | solution.py:39
  (22 other events, 110.5 us)

commit v12 on v11

--- a/solution.py
+++ b/solution.py
@@ -411,7 +411,7 @@
     home = trio
     trio = moves.relabel(home)
     fock_rows = moves.plane(duo, True)
-    density_line = moves.line(masked_density, True)
+    density_line = moves.line(masked_density, True, gate=tuple(fock_rows))
     density_near = [(trio, TAIL + 2 * rows)] + whole(density_line)
     span = TAIL + 2 * rows
     pair_second, *_ = barrier((trio[:span], *density_line))

time: 148 us -> 148 us (level)
  starting transfers between devices: 47.1 us -> 50.8 us
  waiting for transfers between devices: 81.6 us -> 78 us
    ppermute x45, starting transfers between devices: 47.1 us -> 50.8 us  [move(): return lax.ppermute(value, AXES, permutation(self.rows, self.cols, source))]
    ppermute x45, waiting for transfers between devices: 81.6 us -> 78 us  [move(): return lax.ppermute(value, AXES, permutation(self.rows, self.cols, source))]
  transfers between devices with their start and end apart: 45 -> 45, of which waited for: 31 -> 32; matrix products, arithmetic and copies ran while one was open for 1% -> 1% of each run, Pallas kernels for 1% -> 1%
where the time goes in v12:
time: 148 us
  waiting for transfers between devices  78 us (53%)
  starting transfers between devices  50.8 us (34%)
  Pallas kernels  17 us (11%)
  local copies, waits for them, and re-layouts  1.71 us (1%)
    ppermute x45, waiting for transfers between devices, move(): return lax.ppermute(value, AXES, permutation(self.rows, self.cols, source))  78 us
    ppermute x45, starting transfers between devices, move(): return lax.ppermute(value, AXES, permutation(self.rows, self.cols, source))  50.8 us
    pallas_call x1, Pallas kernels, on_device(): call(functools.partial(series_kernel, layout, count, len(arrays)), [jax.S...  8.84 us
    pallas_call x4, Pallas kernels, views_call(): call(body, outs, [INVMEM] * len(operands), scratch, name, flops)(*operands)  4.53 us
    pallas_call x1, Pallas kernels, on_device(): call(functools.partial(mask_kernel, len(inputs)), [block, jax.ShapeDtypeS...  3.59 us
  transfers between devices with their start and end apart: 45, of which 32 were waited for; matrix products, arithmetic and copies ran while one was open for 1% of the time, Pallas kernels for 1%

profile of v12, /device:TPU:1, one launch (start us, length us, event | category | flops | bytes accessed | tf_op | source)
XLA Modules:
  0.0 148.3 jit_solution(12732167186308852640)
XLA Ops:
  0.0 3.6 %mask.1 = (bf16[192,384]{1,0:T(8,128)(2,1)}, bf16[384,384]{1,0:T(8,128)(2,1)}, bf16[592,384]{1,0:T(8,128)(2,1)}) custom-call(s32[3,6,12]{2,1,0:T(8,128)} %refs_0_.1, bf16[192,384]{1,0:T(8,128)(2,1)} %refs_1_.1, bf16[192,384]{1,0:T(8,128)(2,1)} %refs_2_.1, bf16[192,384]{1,0:T(8,128)(2,1)} %refs_3_.1, s32[3,6,12]{2,1,0:T(8,128)} %refs_4_.1, s32[6,7,12]{2,1,0:T(8,128)} %bitcast.1), custom_call_target="tpu_custom_call" | custom-call | flops 1000 | bytes 1000 | tf_op jit(solution)/shard_map/mask/pallas_call | solution.py:397
  3.6 4.7 %collective-permute-start.1 = (bf16[192,384]{1,0:T(8,128)(2,1)}, bf16[192,384]{1,0:T(8,128)(2,1)S(1)}, u32[]{:S(2)}, u32[]{:S(2)}) collective-permute-start(bf16[192,384]{1,0:T(8,128)(2,1)} %get-tuple-element.25), channel_id=1, source_target_pairs={{16,0},{20,1},{18,2},{22,3},{17,4},{21,5},{19,6},{23,7},{24,8},{28... | collective-permute-start | bytes 442376 | tf_op jit(solution)/shard_map/ppermute | solution.py:39
  10.5 2.5 %collective-permute-start.3 = (bf16[384,384]{1,0:T(8,128)(2,1)}, bf16[384,384]{1,0:T(8,128)(2,1)S(1)}, u32[]{:S(2)}, u32[]{:S(2)}) collective-permute-start(bf16[384,384]{1,0:T(8,128)(2,1)} %get-tuple-element.26), channel_id=1, source_target_pairs={{2,0},{6,1},{0,2},{4,3},{3,4},{7,5},{1,6},{5,7},{10,8},{14,9},{8,1... | collective-permute-start | bytes 884744 | tf_op jit(solution)/shard_map/ppermute | solution.py:39
  16.2 3.7 %collective-permute-done.4.refs_3_ = bf16[384,384]{1,0:T(8,128)(2,1)S(1)} collective-permute-done((bf16[384,384]{1,0:T(8,128)(2,1)}, bf16[384,384]{1,0:T(8,128)(2,1)S(1)}, u32[]{:S(2)}, u32[]{:S(2)}) %collective-permute-start.4) | collective-permute-done | bytes 294944 | tf_op jit(solution)/shard_map/ppermute | solution.py:39
  19.9 7.0 %collective-permute-start = (bf16[192,384]{1,0:T(8,128)(2,1)}, bf16[192,384]{1,0:T(8,128)(2,1)S(1)}, u32[]{:S(2)}, u32[]{:S(2)}) collective-permute-start(bf16[192,384]{1,0:T(8,128)(2,1)} %get-tuple-element.25), channel_id=1, source_target_pairs={{8,0},{12,1},{10,2},{14,3},{9,4},{13,5},{11,6},{15,7},{0,8},{4,9},... | collective-permute-start | bytes 442376 | tf_op jit(solution)/shard_map/ppermute | solution.py:39
  26.9 2.3 %collective-permute-done.2.refs_1_ = bf16[384,384]{1,0:T(8,128)(2,1)S(1)} collective-permute-done((bf16[384,384]{1,0:T(8,128)(2,1)}, bf16[384,384]{1,0:T(8,128)(2,1)S(1)}, u32[]{:S(2)}, u32[]{:S(2)}) %collective-permute-start.2) | collective-permute-done | bytes 294944 | tf_op jit(solution)/shard_map/ppermute | solution.py:39
  29.3 4.1 %collective-permute-start.5 = (bf16[192,384]{1,0:T(8,128)(2,1)S(1)}, bf16[192,384]{1,0:T(8,128)(2,1)S(1)}, u32[]{:S(2)}, u32[]{:S(2)}) collective-permute-start(bf16[192,384]{1,0:T(8,128)(2,1)S(1)} %collective-permute-done.1.refs_6_), channel_id=1, source_target_pairs={{8,0},{9,1},{10,2},{11,3},{12,4},{13,5},{14,6},{15,7},{0,8},{1,9},... | collective-permute-start | bytes 442376 | tf_op jit(solution)/shard_map/ppermute | solution.py:39
  33.4 4.4 %collective-permute-done.5.refs_7_ = bf16[192,384]{1,0:T(8,128)(2,1)S(1)} collective-permute-done((bf16[192,384]{1,0:T(8,128)(2,1)S(1)}, bf16[192,384]{1,0:T(8,128)(2,1)S(1)}, u32[]{:S(2)}, u32[]{:S(2)}) %collective-permute-start.5) | collective-permute-done | bytes 147488 | tf_op jit(solution)/shard_map/ppermute | solution.py:39
  44.4 2.6 %collective-permute-done.14.refs_7_ = bf16[400,384]{1,0:T(8,128)(2,1)S(1)} collective-permute-done((bf16[400,384]{1,0:T(8,128)(2,1)S(1)}, bf16[400,384]{1,0:T(8,128)(2,1)S(1)}, u32[]{:S(2)}, u32[]{:S(2)}) %collective-permute-start.14) | collective-permute-done | bytes 307232 | tf_op jit(solution)/shard_map/ppermute | solution.py:39
  47.0 6.6 %collective-permute-done.13.refs_5_ = bf16[400,384]{1,0:T(8,128)(2,1)S(1)} collective-permute-done((bf16[400,384]{1,0:T(8,128)(2,1)S(1)}, bf16[400,384]{1,0:T(8,128)(2,1)S(1)}, u32[]{:S(2)}, u32[]{:S(2)}) %collective-permute-start.13) | collective-permute-done | bytes 307232 | tf_op jit(solution)/shard_map/ppermute | solution.py:39
  55.3 2.6 %collective-permute-done.10.refs_1_ = bf16[384,384]{1,0:T(8,128)(2,1)S(1)} collective-permute-done((bf16[384,384]{1,0:T(8,128)(2,1)S(1)}, bf16[384,384]{1,0:T(8,128)(2,1)S(1)}, u32[]{:S(2)}, u32[]{:S(2)}) %collective-permute-start.10) | collective-permute-done | bytes 294944 | tf_op jit(solution)/shard_map/ppermute | solution.py:39
  66.0 5.5 %collective-permute-done.22 = bf16[192,384]{1,0:T(8,128)(2,1)S(1)} collective-permute-done((bf16[192,384]{1,0:T(8,128)(2,1)S(1)}, bf16[192,384]{1,0:T(8,128)(2,1)S(1)}, u32[]{:S(2)}, u32[]{:S(2)}) %collective-permute-start.22) | collective-permute-done | bytes 147488 | tf_op jit(solution)/shard_map/ppermute | solution.py:39
  75.7 2.9 %collective-permute-done.26.refs_10_ = bf16[192,384]{1,0:T(8,128)(2,1)S(1)} collective-permute-done((bf16[192,384]{1,0:T(8,128)(2,1)S(1)}, bf16[192,384]{1,0:T(8,128)(2,1)S(1)}, u32[]{:S(2)}, u32[]{:S(2)}) %collective-permute-start.26) | collective-permute-done | bytes 147488 | tf_op jit(solution)/shard_map/ppermute | solution.py:39
  81.4 4.8 %collective-permute-done.24.refs_8_ = bf16[384,384]{1,0:T(8,128)(2,1)S(1)} collective-permute-done((bf16[384,384]{1,0:T(8,128)(2,1)S(1)}, bf16[384,384]{1,0:T(8,128)(2,1)S(1)}, u32[]{:S(2)}, u32[]{:S(2)}) %collective-permute-start.24) | collective-permute-done | bytes 294944 | tf_op jit(solution)/shard_map/ppermute | solution.py:39
  86.2 4.0 %collective-permute-done.23.refs_7_ = bf16[384,384]{1,0:T(8,128)(2,1)S(1)} collective-permute-done((bf16[384,384]{1,0:T(8,128)(2,1)S(1)}, bf16[384,384]{1,0:T(8,128)(2,1)S(1)}, u32[]{:S(2)}, u32[]{:S(2)}) %collective-permute-start.23) | collective-permute-done | bytes 294944 | tf_op jit(solution)/shard_map/ppermute | solution.py:39
  92.5 2.8 %collective-permute-done.27.refs_12_ = bf16[192,384]{1,0:T(8,128)(2,1)S(1)} collective-permute-done((bf16[192,384]{1,0:T(8,128)(2,1)S(1)}, bf16[192,384]{1,0:T(8,128)(2,1)S(1)}, u32[]{:S(2)}, u32[]{:S(2)}) %collective-permute-start.27) | collective-permute-done | bytes 147488 | tf_op jit(solution)/shard_map/ppermute | solution.py:39
  96.8 2.5 %collective-permute-done.20.refs_1_ = bf16[768,384]{1,0:T(8,128)(2,1)S(1)} collective-permute-done((bf16[768,384]{1,0:T(8,128)(2,1)S(1)}, bf16[768,384]{1,0:T(8,128)(2,1)S(1)}, u32[]{:S(2)}, u32[]{:S(2)}) %collective-permute-start.20) | collective-permute-done | bytes 589856 | tf_op jit(solution)/shard_map/ppermute | solution.py:39
  100.1 8.8 %series.1 = (bf16[192,1536]{1,0:T(8,128)(2,1)S(1)}, bf16[192,384]{1,0:T(8,128)(2,1)S(1)}) custom-call(bf16[192,384]{1,0:T(8,128)(2,1)S(1)} %generator.1.refs_0_, bf16[768,384]{1,0:T(8,128)(2,1)S(1)} %collective-permute-done.20.refs_1_, bf16[192,384]{1,0:T(8,128)(2,1)S(1)} %collective-permute-done.17.refs_2_, ...), custom_call_target="tpu_custom_call" | custom-call | flops 1000 | bytes 1000 | tf_op jit(solution)/shard_map/series/pallas_call | solution.py:477
  111.7 3.3 %collective-permute-done.34.refs_3_ = bf16[192,384]{1,0:T(8,128)(2,1)S(1)} collective-permute-done((bf16[192,384]{1,0:T(8,128)(2,1)S(1)}, bf16[192,384]{1,0:T(8,128)(2,1)S(1)}, u32[]{:S(2)}, u32[]{:S(2)}) %collective-permute-start.34) | collective-permute-done | bytes 147488 | tf_op jit(solution)/shard_map/ppermute | solution.py:39
  115.1 2.3 %collective-permute-done.33.refs_2_ = bf16[192,384]{1,0:T(8,128)(2,1)S(1)} collective-permute-done((bf16[192,384]{1,0:T(8,128)(2,1)S(1)}, bf16[192,384]{1,0:T(8,128)(2,1)S(1)}, u32[]{:S(2)}, u32[]{:S(2)}) %collective-permute-start.33) | collective-permute-done | bytes 147488 | tf_op jit(solution)/shard_map/ppermute | solution.py:39
  127.0 4.9 %collective-permute-done.41.refs_6_ = bf16[192,384]{1,0:T(8,128)(2,1)S(1)} collective-permute-done((bf16[192,384]{1,0:T(8,128)(2,1)S(1)}, bf16[192,384]{1,0:T(8,128)(2,1)S(1)}, u32[]{:S(2)}, u32[]{:S(2)}) %collective-permute-start.41) | collective-permute-done | bytes 147488 | tf_op jit(solution)/shard_map/ppermute | solution.py:39
  134.2 2.8 %collective-permute-done.42.refs_7_ = bf16[192,384]{1,0:T(8,128)(2,1)S(1)} collective-permute-done((bf16[192,384]{1,0:T(8,128)(2,1)S(1)}, bf16[192,384]{1,0:T(8,128)(2,1)S(1)}, u32[]{:S(2)}, u32[]{:S(2)}) %collective-permute-start.42) | collective-permute-done | bytes 147488 | tf_op jit(solution)/shard_map/ppermute | solution.py:39
  141.1 2.5 %collective-permute-start.44 = (bf16[192,384]{1,0:T(8,128)(2,1)S(1)}, bf16[192,384]{1,0:T(8,128)(2,1)S(1)}, u32[]{:S(2)}, u32[]{:S(2)}) collective-permute-start(bf16[192,384]{1,0:T(8,128)(2,1)S(1)} %evolve.1), channel_id=1, source_target_pairs={{0,0},{4,1},{2,2},{6,3},{1,4},{5,5},{3,6},{7,7},{8,8},{12,9},{10,1... | collective-permute-start | bytes 442376 | tf_op jit(solution)/shard_map/ppermute | solution.py:39
  143.7 3.9 %collective-permute-done.44 = bf16[192,384]{1,0:T(8,128)(2,1)S(1)} collective-permute-done((bf16[192,384]{1,0:T(8,128)(2,1)S(1)}, bf16[192,384]{1,0:T(8,128)(2,1)S(1)}, u32[]{:S(2)}, u32[]{:S(2)}) %collective-permute-start.44) | collective-permute-done | bytes 147488 | tf_op jit(solution)/shard_map/ppermute | solution.py:39
  (93 shorter events, 52.8 us)
Async XLA Ops:
  3.6 12.5 %collective-permute-start.1 = (bf16[192,384]{1,0:T(8,128)(2,1)}, bf16[192,384]{1,0:T(8,128)(2,1)S(1)}, u32[]{:S(2)}, u32[]{:S(2)}) collective-permute-start(bf16[192,384]{1,0:T(8,128)(2,1)} %get-tuple-element.25), channel_id=1, source_target_pairs={{16,0},{20,1},{18,2},{22,3},{17,4},{21,5},{19,6},{23,7},{24,8},{28... | collective-permute-start | bytes 442376 | tf_op jit(solution)/shard_map/ppermute | solution.py:39
  8.3 29.5 %collective-permute-start.6 = (bf16[592,384]{1,0:T(8,128)(2,1)}, bf16[592,384]{1,0:T(8,128)(2,1)S(1)}, u32[]{:S(2)}, u32[]{:S(2)}) collective-permute-start(bf16[592,384]{1,0:T(8,128)(2,1)} %get-tuple-element.28), channel_id=1, source_target_pairs={{0,0},{4,1},{2,2},{6,3},{1,4},{5,5},{3,6},{7,7},{8,8},{12,9},{10,1... | collective-permute-start | bytes 1363976 | tf_op jit(solution)/shard_map/ppermute | solution.py:39
  10.2 9.7 %collective-permute-start.4 = (bf16[384,384]{1,0:T(8,128)(2,1)}, bf16[384,384]{1,0:T(8,128)(2,1)S(1)}, u32[]{:S(2)}, u32[]{:S(2)}) collective-permute-start(bf16[384,384]{1,0:T(8,128)(2,1)} %get-tuple-element.26), channel_id=1, source_target_pairs={{3,0},{7,1},{1,2},{5,3},{2,4},{6,5},{0,6},{4,7},{11,8},{15,9},{9,1... | collective-permute-start | bytes 884744 | tf_op jit(solution)/shard_map/ppermute | solution.py:39
  10.5 16.4 %collective-permute-start.3 = (bf16[384,384]{1,0:T(8,128)(2,1)}, bf16[384,384]{1,0:T(8,128)(2,1)S(1)}, u32[]{:S(2)}, u32[]{:S(2)}) collective-permute-start(bf16[384,384]{1,0:T(8,128)(2,1)} %get-tuple-element.26), channel_id=1, source_target_pairs={{2,0},{6,1},{0,2},{4,3},{3,4},{7,5},{1,6},{5,7},{10,8},{14,9},{8,1... | collective-permute-start | bytes 884744 | tf_op jit(solution)/shard_map/ppermute | solution.py:39
  13.0 16.2 %collective-permute-start.2 = (bf16[384,384]{1,0:T(8,128)(2,1)}, bf16[384,384]{1,0:T(8,128)(2,1)S(1)}, u32[]{:S(2)}, u32[]{:S(2)}) collective-permute-start(bf16[384,384]{1,0:T(8,128)(2,1)} %get-tuple-element.26), channel_id=1, source_target_pairs={{1,0},{5,1},{3,2},{7,3},{0,4},{4,5},{2,6},{6,7},{9,8},{13,9},{11,1... | collective-permute-start | bytes 884744 | tf_op jit(solution)/shard_map/ppermute | solution.py:39
  16.1 17.4 %collective-permute-start.7 = (bf16[400,384]{1,0:T(8,128)(2,1)S(1)}, bf16[400,384]{1,0:T(8,128)(2,1)S(1)}, u32[]{:S(2)}, u32[]{:S(2)}) collective-permute-start(bf16[400,384]{1,0:T(8,128)(2,1)S(1)} %slice.30), channel_id=1, source_target_pairs={{16,0},{20,1},{18,2},{22,3},{17,4},{21,5},{19,6},{23,7},{24,8},{28... | collective-permute-start | bytes 921608 | tf_op jit(solution)/shard_map/ppermute | solution.py:39
  19.9 13.5 %collective-permute-start = (bf16[192,384]{1,0:T(8,128)(2,1)}, bf16[192,384]{1,0:T(8,128)(2,1)S(1)}, u32[]{:S(2)}, u32[]{:S(2)}) collective-permute-start(bf16[192,384]{1,0:T(8,128)(2,1)} %get-tuple-element.25), channel_id=1, source_target_pairs={{8,0},{12,1},{10,2},{14,3},{9,4},{13,5},{11,6},{15,7},{0,8},{4,9},... | collective-permute-start | bytes 442376 | tf_op jit(solution)/shard_map/ppermute | solution.py:39
  29.3 8.5 %collective-permute-start.5 = (bf16[192,384]{1,0:T(8,128)(2,1)S(1)}, bf16[192,384]{1,0:T(8,128)(2,1)S(1)}, u32[]{:S(2)}, u32[]{:S(2)}) collective-permute-start(bf16[192,384]{1,0:T(8,128)(2,1)S(1)} %collective-permute-done.1.refs_6_), channel_id=1, source_target_pairs={{8,0},{9,1},{10,2},{11,3},{12,4},{13,5},{14,6},{15,7},{0,8},{1,9},... | collective-permute-start | bytes 442376 | tf_op jit(solution)/shard_map/ppermute | solution.py:39
  38.5 8.5 %collective-permute-start.14 = (bf16[400,384]{1,0:T(8,128)(2,1)S(1)}, bf16[400,384]{1,0:T(8,128)(2,1)S(1)}, u32[]{:S(2)}, u32[]{:S(2)}) collective-permute-start(bf16[400,384]{1,0:T(8,128)(2,1)S(1)} %collective-permute-done.7.refs_6_), channel_id=1, source_target_pairs={{8,0},{9,1},{10,2},{11,3},{12,4},{13,5},{14,6},{15,7},{0,8},{1,9},... | collective-permute-start | bytes 921608 | tf_op jit(solution)/shard_map/ppermute | solution.py:39
  39.2 14.4 %collective-permute-start.13 = (bf16[400,384]{1,0:T(8,128)(2,1)S(1)}, bf16[400,384]{1,0:T(8,128)(2,1)S(1)}, u32[]{:S(2)}, u32[]{:S(2)}) collective-permute-start(bf16[400,384]{1,0:T(8,128)(2,1)S(1)} %slice.40), channel_id=1, source_target_pairs={{8,0},{9,1},{10,2},{11,3},{12,4},{13,5},{14,6},{15,7},{0,8},{1,9},... | collective-permute-start | bytes 921608 | tf_op jit(solution)/shard_map/ppermute | solution.py:39
  41.7 11.9 %collective-permute-start.12 = (bf16[384,384]{1,0:T(8,128)(2,1)S(1)}, bf16[384,384]{1,0:T(8,128)(2,1)S(1)}, u32[]{:S(2)}, u32[]{:S(2)}) collective-permute-start(bf16[384,384]{1,0:T(8,128)(2,1)S(1)} %first.1.refs_0_), channel_id=1, source_target_pairs={{6,0},{7,1},{4,2},{5,3},{2,4},{3,5},{0,6},{1,7},{14,8},{15,9},{12,... | collective-permute-start | bytes 884744 | tf_op jit(solution)/shard_map/ppermute | solution.py:39
  42.3 13.0 %collective-permute-start.11 = (bf16[384,384]{1,0:T(8,128)(2,1)S(1)}, bf16[384,384]{1,0:T(8,128)(2,1)S(1)}, u32[]{:S(2)}, u32[]{:S(2)}) collective-permute-start(bf16[384,384]{1,0:T(8,128)(2,1)S(1)} %first.1.refs_0_), channel_id=1, source_target_pairs={{2,0},{3,1},{0,2},{1,3},{6,4},{7,5},{4,6},{5,7},{10,8},{11,9},{8,1... | collective-permute-start | bytes 884744 | tf_op jit(solution)/shard_map/ppermute | solution.py:39
  42.5 15.4 %collective-permute-start.10 = (bf16[384,384]{1,0:T(8,128)(2,1)S(1)}, bf16[384,384]{1,0:T(8,128)(2,1)S(1)}, u32[]{:S(2)}, u32[]{:S(2)}) collective-permute-start(bf16[384,384]{1,0:T(8,128)(2,1)S(1)} %first.1.refs_0_), channel_id=1, source_target_pairs={{4,0},{5,1},{6,2},{7,3},{0,4},{1,5},{2,6},{3,7},{12,8},{13,9},{14,... | collective-permute-start | bytes 884744 | tf_op jit(solution)/shard_map/ppermute | solution.py:39
  61.9 9.7 %collective-permute-start.22 = (bf16[192,384]{1,0:T(8,128)(2,1)S(1)}, bf16[192,384]{1,0:T(8,128)(2,1)S(1)}, u32[]{:S(2)}, u32[]{:S(2)}) collective-permute-start(bf16[192,384]{1,0:T(8,128)(2,1)S(1)} %generator.1.refs_0_), channel_id=1, source_target_pairs={{16,0},{17,1},{18,2},{19,3},{20,4},{21,5},{22,6},{23,7},{24,8},{25... | collective-permute-start | bytes 442376 | tf_op jit(solution)/shard_map/ppermute | solution.py:39
  62.4 9.1 %collective-permute-start.21 = (bf16[192,384]{1,0:T(8,128)(2,1)S(1)}, bf16[192,384]{1,0:T(8,128)(2,1)S(1)}, u32[]{:S(2)}, u32[]{:S(2)}) collective-permute-start(bf16[192,384]{1,0:T(8,128)(2,1)S(1)} %generator.1.refs_0_), channel_id=1, source_target_pairs={{8,0},{9,1},{10,2},{11,3},{12,4},{13,5},{14,6},{15,7},{0,8},{1,9},... | collective-permute-start | bytes 442376 | tf_op jit(solution)/shard_map/ppermute | solution.py:39
  72.8 8.6 %collective-permute-start.25 = (bf16[384,384]{1,0:T(8,128)(2,1)S(1)}, bf16[384,384]{1,0:T(8,128)(2,1)S(1)}, u32[]{:S(2)}, u32[]{:S(2)}) collective-permute-start(bf16[384,384]{1,0:T(8,128)(2,1)S(1)} %pad_maximum_fusion.8.refs_5_), channel_id=1, source_target_pairs={{6,0},{7,1},{4,2},{5,3},{2,4},{3,5},{0,6},{1,7},{14,8},{15,9},{12,... | collective-permute-start | bytes 884744 | tf_op jit(solution)/shard_map/ppermute | solution.py:39
  74.4 11.8 %collective-permute-start.24 = (bf16[384,384]{1,0:T(8,128)(2,1)S(1)}, bf16[384,384]{1,0:T(8,128)(2,1)S(1)}, u32[]{:S(2)}, u32[]{:S(2)}) collective-permute-start(bf16[384,384]{1,0:T(8,128)(2,1)S(1)} %pad_maximum_fusion.8.refs_5_), channel_id=1, source_target_pairs={{2,0},{3,1},{0,2},{1,3},{6,4},{7,5},{4,6},{5,7},{10,8},{11,9},{8,1... | collective-permute-start | bytes 884744 | tf_op jit(solution)/shard_map/ppermute | solution.py:39
  75.2 15.0 %collective-permute-start.23 = (bf16[384,384]{1,0:T(8,128)(2,1)S(1)}, bf16[384,384]{1,0:T(8,128)(2,1)S(1)}, u32[]{:S(2)}, u32[]{:S(2)}) collective-permute-start(bf16[384,384]{1,0:T(8,128)(2,1)S(1)} %pad_maximum_fusion.8.refs_5_), channel_id=1, source_target_pairs={{4,0},{5,1},{6,2},{7,3},{0,4},{1,5},{2,6},{3,7},{12,8},{13,9},{14,... | collective-permute-start | bytes 884744 | tf_op jit(solution)/shard_map/ppermute | solution.py:39
  78.7 12.2 %collective-permute-start.29 = (bf16[192,384]{1,0:T(8,128)(2,1)S(1)}, bf16[192,384]{1,0:T(8,128)(2,1)S(1)}, u32[]{:S(2)}, u32[]{:S(2)}) collective-permute-start(bf16[192,384]{1,0:T(8,128)(2,1)S(1)} %collective-permute-done.26.refs_10_), channel_id=1, source_target_pairs={{6,0},{7,1},{4,2},{5,3},{2,4},{3,5},{0,6},{1,7},{14,8},{15,9},{12,... | collective-permute-start | bytes 442376 | tf_op jit(solution)/shard_map/ppermute | solution.py:39
  79.8 12.7 %collective-permute-start.28 = (bf16[192,384]{1,0:T(8,128)(2,1)S(1)}, bf16[192,384]{1,0:T(8,128)(2,1)S(1)}, u32[]{:S(2)}, u32[]{:S(2)}) collective-permute-start(bf16[192,384]{1,0:T(8,128)(2,1)S(1)} %collective-permute-done.26.refs_10_), channel_id=1, source_target_pairs={{2,0},{3,1},{0,2},{1,3},{6,4},{7,5},{4,6},{5,7},{10,8},{11,9},{8,1... | collective-permute-start | bytes 442376 | tf_op jit(solution)/shard_map/ppermute | solution.py:39
  81.4 13.9 %collective-permute-start.27 = (bf16[192,384]{1,0:T(8,128)(2,1)S(1)}, bf16[192,384]{1,0:T(8,128)(2,1)S(1)}, u32[]{:S(2)}, u32[]{:S(2)}) collective-permute-start(bf16[192,384]{1,0:T(8,128)(2,1)S(1)} %collective-permute-done.26.refs_10_), channel_id=1, source_target_pairs={{4,0},{5,1},{6,2},{7,3},{0,4},{1,5},{2,6},{3,7},{12,8},{13,9},{14,... | collective-permute-start | bytes 442376 | tf_op jit(solution)/shard_map/ppermute | solution.py:39
  121.9 9.9 %collective-permute-start.41 = (bf16[192,384]{1,0:T(8,128)(2,1)S(1)}, bf16[192,384]{1,0:T(8,128)(2,1)S(1)}, u32[]{:S(2)}, u32[]{:S(2)}) collective-permute-start(bf16[192,384]{1,0:T(8,128)(2,1)S(1)} %square.1.refs_0_), channel_id=1, source_target_pairs={{16,0},{17,1},{18,2},{19,3},{20,4},{21,5},{22,6},{23,7},{24,8},{25... | collective-permute-start | bytes 442376 | tf_op jit(solution)/shard_map/ppermute | solution.py:39
  123.1 8.7 %collective-permute-start.38 = (bf16[192,384]{1,0:T(8,128)(2,1)S(1)}, bf16[192,384]{1,0:T(8,128)(2,1)S(1)}, u32[]{:S(2)}, u32[]{:S(2)}) collective-permute-start(bf16[192,384]{1,0:T(8,128)(2,1)S(1)} %square.1.refs_0_), channel_id=1, source_target_pairs={{6,0},{7,1},{4,2},{5,3},{2,4},{3,5},{0,6},{1,7},{14,8},{15,9},{12,... | collective-permute-start | bytes 442376 | tf_op jit(solution)/shard_map/ppermute | solution.py:39
  125.8 8.4 %collective-permute-start.40 = (bf16[192,384]{1,0:T(8,128)(2,1)S(1)}, bf16[192,384]{1,0:T(8,128)(2,1)S(1)}, u32[]{:S(2)}, u32[]{:S(2)}) collective-permute-start(bf16[192,384]{1,0:T(8,128)(2,1)S(1)} %square.1.refs_0_), channel_id=1, source_target_pairs={{8,0},{9,1},{10,2},{11,3},{12,4},{13,5},{14,6},{15,7},{0,8},{1,9},... | collective-permute-start | bytes 442376 | tf_op jit(solution)/shard_map/ppermute | solution.py:39
  (22 other events, 112.1 us)

commit v13 on v12

--- a/solution.py
+++ b/solution.py
@@ -53,7 +53,7 @@
                     held[bit] = self.relabel(value, bit)
                 else:
                     if k and gate is not None:
-                        part, _ = lax.optimization_barrier((part, gate))
+                        part, _ = lax.optimization_barrier((part, (gate, held[bit])))
                     held[k | bit] = self.along_z(part, bit)
             if second is not None:
                 held[0] = second
@@ -411,11 +411,12 @@
     home = trio
     trio = moves.relabel(home)
     fock_rows = moves.plane(duo, True)
-    density_line = moves.line(masked_density, True, gate=tuple(fock_rows))
+    density_line = moves.line(masked_density, True, gate=tuple(fock_rows[-2:]))
     density_near = [(trio, TAIL + 2 * rows)] + whole(density_line)
     span = TAIL + 2 * rows
     pair_second, *_ = barrier((trio[:span], *density_line))
-    pair_line = moves.line(home[:span], True, second=pair_second)
+    gated, _ = barrier((home[:span], density_line[half - 1]))
+    pair_line = moves.line(gated, True, second=pair_second)
     early = barrier((*density_line, trio, pair_line[half - 1], *fock_rows))
     density_line, trio, pair_line[half - 1] = list(early[: count - 1]), early[count - 1], early[count]
     trio_far = moves.core(trio)

time: 148 us -> 148 us (level)
  starting transfers between devices: 50.8 us -> 42.5 us
  waiting for transfers between devices: 78 us -> 85.5 us
    ppermute x45, starting transfers between devices: 50.8 us -> 42.5 us  [move(): return lax.ppermute(value, AXES, permutation(self.rows, self.cols, source))]
    ppermute x45, waiting for transfers between devices: 78 us -> 85.5 us  [move(): return lax.ppermute(value, AXES, permutation(self.rows, self.cols, source))]
  transfers between devices with their start and end apart: 45 -> 45, of which waited for: 32 -> 31; matrix products, arithmetic and copies ran while one was open for 1% -> 1% of each run, Pallas kernels for 1% -> 1%
where the time goes in v13:
time: 148 us; the launch traced here: 147 us
  waiting for transfers between devices  85.5 us (58%)
  starting transfers between devices  42.5 us (29%)
  Pallas kernels  16.9 us (11%)
  local copies, waits for them, and re-layouts  1.71 us (1%)
    ppermute x45, waiting for transfers between devices, move(): return lax.ppermute(value, AXES, permutation(self.rows, self.cols, source))  85.5 us
    ppermute x45, starting transfers between devices, move(): return lax.ppermute(value, AXES, permutation(self.rows, self.cols, source))  42.5 us
    pallas_call x1, Pallas kernels, on_device(): call(functools.partial(series_kernel, layout, count, len(arrays)), [jax.S...  8.84 us
    pallas_call x4, Pallas kernels, views_call(): call(body, outs, [INVMEM] * len(operands), scratch, name, flops)(*operands)  4.52 us
    pallas_call x1, Pallas kernels, on_device(): call(functools.partial(mask_kernel, len(inputs)), [block, jax.ShapeDtypeS...  3.59 us
  transfers between devices with their start and end apart: 45, of which 31 were waited for; matrix products, arithmetic and copies ran while one was open for 1% of the time, Pallas kernels for 1%

profile of v13, /device:TPU:1, one launch (start us, length us, event | category | flops | bytes accessed | tf_op | source)
XLA Modules:
  0.0 147.4 jit_solution(11640643894707177085)
XLA Ops:
  0.0 3.6 %mask.1 = (bf16[192,384]{1,0:T(8,128)(2,1)}, bf16[384,384]{1,0:T(8,128)(2,1)}, bf16[592,384]{1,0:T(8,128)(2,1)}) custom-call(s32[3,6,12]{2,1,0:T(8,128)} %refs_0_.1, bf16[192,384]{1,0:T(8,128)(2,1)} %refs_1_.1, bf16[192,384]{1,0:T(8,128)(2,1)} %refs_2_.1, bf16[192,384]{1,0:T(8,128)(2,1)} %refs_3_.1, s32[3,6,12]{2,1,0:T(8,128)} %refs_4_.1, s32[6,7,12]{2,1,0:T(8,128)} %bitcast.1), custom_call_target="tpu_custom_call" | custom-call | flops 1000 | bytes 1000 | tf_op jit(solution)/shard_map/mask/pallas_call | solution.py:397
  3.6 4.7 %collective-permute-start.1 = (bf16[192,384]{1,0:T(8,128)(2,1)}, bf16[192,384]{1,0:T(8,128)(2,1)S(1)}, u32[]{:S(2)}, u32[]{:S(2)}) collective-permute-start(bf16[192,384]{1,0:T(8,128)(2,1)} %get-tuple-element.26), channel_id=1, source_target_pairs={{16,0},{20,1},{18,2},{22,3},{17,4},{21,5},{19,6},{23,7},{24,8},{28... | collective-permute-start | bytes 442376 | tf_op jit(solution)/shard_map/ppermute | solution.py:39
  10.5 2.5 %collective-permute-start.2 = (bf16[384,384]{1,0:T(8,128)(2,1)}, bf16[384,384]{1,0:T(8,128)(2,1)S(1)}, u32[]{:S(2)}, u32[]{:S(2)}) collective-permute-start(bf16[384,384]{1,0:T(8,128)(2,1)} %get-tuple-element.27), channel_id=1, source_target_pairs={{2,0},{6,1},{0,2},{4,3},{3,4},{7,5},{1,6},{5,7},{10,8},{14,9},{8,1... | collective-permute-start | bytes 884744 | tf_op jit(solution)/shard_map/ppermute | solution.py:39
  16.6 3.6 %collective-permute-done.refs_5_ = bf16[192,384]{1,0:T(8,128)(2,1)S(1)} collective-permute-done((bf16[192,384]{1,0:T(8,128)(2,1)}, bf16[192,384]{1,0:T(8,128)(2,1)S(1)}, u32[]{:S(2)}, u32[]{:S(2)}) %collective-permute-start) | collective-permute-done | bytes 147488 | tf_op jit(solution)/shard_map/ppermute | solution.py:39
  20.2 6.5 %collective-permute-done.2.refs_2_ = bf16[384,384]{1,0:T(8,128)(2,1)S(1)} collective-permute-done((bf16[384,384]{1,0:T(8,128)(2,1)}, bf16[384,384]{1,0:T(8,128)(2,1)S(1)}, u32[]{:S(2)}, u32[]{:S(2)}) %collective-permute-start.2) | collective-permute-done | bytes 294944 | tf_op jit(solution)/shard_map/ppermute | solution.py:39
  28.7 5.6 %collective-permute-done.7.refs_1_ = bf16[384,384]{1,0:T(8,128)(2,1)S(1)} collective-permute-done((bf16[384,384]{1,0:T(8,128)(2,1)}, bf16[384,384]{1,0:T(8,128)(2,1)S(1)}, u32[]{:S(2)}, u32[]{:S(2)}) %collective-permute-start.7) | collective-permute-done | bytes 294944 | tf_op jit(solution)/shard_map/ppermute | solution.py:39
  34.3 2.0 %collective-permute-done.4.refs_7_ = bf16[192,384]{1,0:T(8,128)(2,1)S(1)} collective-permute-done((bf16[192,384]{1,0:T(8,128)(2,1)S(1)}, bf16[192,384]{1,0:T(8,128)(2,1)S(1)}, u32[]{:S(2)}, u32[]{:S(2)}) %collective-permute-start.4) | collective-permute-done | bytes 147488 | tf_op jit(solution)/shard_map/ppermute | solution.py:39
  42.8 9.1 %collective-permute-done.14.refs_7_ = bf16[400,384]{1,0:T(8,128)(2,1)S(1)} collective-permute-done((bf16[400,384]{1,0:T(8,128)(2,1)S(1)}, bf16[400,384]{1,0:T(8,128)(2,1)S(1)}, u32[]{:S(2)}, u32[]{:S(2)}) %collective-permute-start.14) | collective-permute-done | bytes 307232 | tf_op jit(solution)/shard_map/ppermute | solution.py:39
  52.0 2.3 %collective-permute-done.11.refs_2_ = bf16[384,384]{1,0:T(8,128)(2,1)S(1)} collective-permute-done((bf16[384,384]{1,0:T(8,128)(2,1)S(1)}, bf16[384,384]{1,0:T(8,128)(2,1)S(1)}, u32[]{:S(2)}, u32[]{:S(2)}) %collective-permute-start.11) | collective-permute-done | bytes 294944 | tf_op jit(solution)/shard_map/ppermute | solution.py:39
  57.0 2.0 %collective-permute-done.16.refs_10_ = bf16[400,384]{1,0:T(8,128)(2,1)S(1)} collective-permute-done((bf16[400,384]{1,0:T(8,128)(2,1)S(1)}, bf16[400,384]{1,0:T(8,128)(2,1)S(1)}, u32[]{:S(2)}, u32[]{:S(2)}) %collective-permute-start.16) | collective-permute-done | bytes 307232 | tf_op jit(solution)/shard_map/ppermute | solution.py:39
  65.4 4.6 %collective-permute-done.22 = bf16[192,384]{1,0:T(8,128)(2,1)S(1)} collective-permute-done((bf16[192,384]{1,0:T(8,128)(2,1)S(1)}, bf16[192,384]{1,0:T(8,128)(2,1)S(1)}, u32[]{:S(2)}, u32[]{:S(2)}) %collective-permute-start.22) | collective-permute-done | bytes 147488 | tf_op jit(solution)/shard_map/ppermute | solution.py:39
  75.2 2.4 %collective-permute-done.26.refs_10_ = bf16[192,384]{1,0:T(8,128)(2,1)S(1)} collective-permute-done((bf16[192,384]{1,0:T(8,128)(2,1)S(1)}, bf16[192,384]{1,0:T(8,128)(2,1)S(1)}, u32[]{:S(2)}, u32[]{:S(2)}) %collective-permute-start.26) | collective-permute-done | bytes 147488 | tf_op jit(solution)/shard_map/ppermute | solution.py:39
  77.6 2.2 %collective-permute-start.29 = (bf16[192,384]{1,0:T(8,128)(2,1)S(1)}, bf16[192,384]{1,0:T(8,128)(2,1)S(1)}, u32[]{:S(2)}, u32[]{:S(2)}) collective-permute-start(bf16[192,384]{1,0:T(8,128)(2,1)S(1)} %collective-permute-done.26.refs_10_), channel_id=1, source_target_pairs={{6,0},{7,1},{4,2},{5,3},{2,4},{3,5},{0,6},{1,7},{14,8},{15,9},{12,... | collective-permute-start | bytes 442376 | tf_op jit(solution)/shard_map/ppermute | solution.py:39
  80.8 4.7 %collective-permute-done.24.refs_8_ = bf16[384,384]{1,0:T(8,128)(2,1)S(1)} collective-permute-done((bf16[384,384]{1,0:T(8,128)(2,1)S(1)}, bf16[384,384]{1,0:T(8,128)(2,1)S(1)}, u32[]{:S(2)}, u32[]{:S(2)}) %collective-permute-start.24) | collective-permute-done | bytes 294944 | tf_op jit(solution)/shard_map/ppermute | solution.py:39
  85.4 4.2 %collective-permute-done.23.refs_7_ = bf16[384,384]{1,0:T(8,128)(2,1)S(1)} collective-permute-done((bf16[384,384]{1,0:T(8,128)(2,1)S(1)}, bf16[384,384]{1,0:T(8,128)(2,1)S(1)}, u32[]{:S(2)}, u32[]{:S(2)}) %collective-permute-start.23) | collective-permute-done | bytes 294944 | tf_op jit(solution)/shard_map/ppermute | solution.py:39
  91.8 2.9 %collective-permute-done.27.refs_12_ = bf16[192,384]{1,0:T(8,128)(2,1)S(1)} collective-permute-done((bf16[192,384]{1,0:T(8,128)(2,1)S(1)}, bf16[192,384]{1,0:T(8,128)(2,1)S(1)}, u32[]{:S(2)}, u32[]{:S(2)}) %collective-permute-start.27) | collective-permute-done | bytes 147488 | tf_op jit(solution)/shard_map/ppermute | solution.py:39
  96.2 2.5 %collective-permute-done.20.refs_1_ = bf16[768,384]{1,0:T(8,128)(2,1)S(1)} collective-permute-done((bf16[768,384]{1,0:T(8,128)(2,1)S(1)}, bf16[768,384]{1,0:T(8,128)(2,1)S(1)}, u32[]{:S(2)}, u32[]{:S(2)}) %collective-permute-start.20) | collective-permute-done | bytes 589856 | tf_op jit(solution)/shard_map/ppermute | solution.py:39
  99.5 8.8 %series.1 = (bf16[192,1536]{1,0:T(8,128)(2,1)S(1)}, bf16[192,384]{1,0:T(8,128)(2,1)S(1)}) custom-call(bf16[192,384]{1,0:T(8,128)(2,1)S(1)} %generator.1.refs_0_, bf16[768,384]{1,0:T(8,128)(2,1)S(1)} %collective-permute-done.20.refs_1_, bf16[192,384]{1,0:T(8,128)(2,1)S(1)} %collective-permute-done.17.refs_2_, ...), custom_call_target="tpu_custom_call" | custom-call | flops 1000 | bytes 1000 | tf_op jit(solution)/shard_map/series/pallas_call | solution.py:478
  111.1 3.3 %collective-permute-done.34.refs_3_ = bf16[192,384]{1,0:T(8,128)(2,1)S(1)} collective-permute-done((bf16[192,384]{1,0:T(8,128)(2,1)S(1)}, bf16[192,384]{1,0:T(8,128)(2,1)S(1)}, u32[]{:S(2)}, u32[]{:S(2)}) %collective-permute-start.34) | collective-permute-done | bytes 147488 | tf_op jit(solution)/shard_map/ppermute | solution.py:39
  114.4 2.3 %collective-permute-done.33.refs_2_ = bf16[192,384]{1,0:T(8,128)(2,1)S(1)} collective-permute-done((bf16[192,384]{1,0:T(8,128)(2,1)S(1)}, bf16[192,384]{1,0:T(8,128)(2,1)S(1)}, u32[]{:S(2)}, u32[]{:S(2)}) %collective-permute-start.33) | collective-permute-done | bytes 147488 | tf_op jit(solution)/shard_map/ppermute | solution.py:39
  125.4 5.7 %collective-permute-done.41.refs_6_ = bf16[192,384]{1,0:T(8,128)(2,1)S(1)} collective-permute-done((bf16[192,384]{1,0:T(8,128)(2,1)S(1)}, bf16[192,384]{1,0:T(8,128)(2,1)S(1)}, u32[]{:S(2)}, u32[]{:S(2)}) %collective-permute-start.41) | collective-permute-done | bytes 147488 | tf_op jit(solution)/shard_map/ppermute | solution.py:39
  132.3 3.6 %collective-permute-done.42.refs_7_ = bf16[192,384]{1,0:T(8,128)(2,1)S(1)} collective-permute-done((bf16[192,384]{1,0:T(8,128)(2,1)S(1)}, bf16[192,384]{1,0:T(8,128)(2,1)S(1)}, u32[]{:S(2)}, u32[]{:S(2)}) %collective-permute-start.42) | collective-permute-done | bytes 147488 | tf_op jit(solution)/shard_map/ppermute | solution.py:39
  140.3 2.5 %collective-permute-start.44 = (bf16[192,384]{1,0:T(8,128)(2,1)S(1)}, bf16[192,384]{1,0:T(8,128)(2,1)S(1)}, u32[]{:S(2)}, u32[]{:S(2)}) collective-permute-start(bf16[192,384]{1,0:T(8,128)(2,1)S(1)} %evolve.1), channel_id=1, source_target_pairs={{0,0},{4,1},{2,2},{6,3},{1,4},{5,5},{3,6},{7,7},{8,8},{12,9},{10,1... | collective-permute-start | bytes 442376 | tf_op jit(solution)/shard_map/ppermute | solution.py:39
  142.7 4.0 %collective-permute-done.44 = bf16[192,384]{1,0:T(8,128)(2,1)S(1)} collective-permute-done((bf16[192,384]{1,0:T(8,128)(2,1)S(1)}, bf16[192,384]{1,0:T(8,128)(2,1)S(1)}, u32[]{:S(2)}, u32[]{:S(2)}) %collective-permute-start.44) | collective-permute-done | bytes 147488 | tf_op jit(solution)/shard_map/ppermute | solution.py:39
  (93 shorter events, 51.4 us)
Async XLA Ops:
  3.6 12.5 %collective-permute-start.1 = (bf16[192,384]{1,0:T(8,128)(2,1)}, bf16[192,384]{1,0:T(8,128)(2,1)S(1)}, u32[]{:S(2)}, u32[]{:S(2)}) collective-permute-start(bf16[192,384]{1,0:T(8,128)(2,1)} %get-tuple-element.26), channel_id=1, source_target_pairs={{16,0},{20,1},{18,2},{22,3},{17,4},{21,5},{19,6},{23,7},{24,8},{28... | collective-permute-start | bytes 442376 | tf_op jit(solution)/shard_map/ppermute | solution.py:39
  8.3 28.0 %collective-permute-start.5 = (bf16[592,384]{1,0:T(8,128)(2,1)}, bf16[592,384]{1,0:T(8,128)(2,1)S(1)}, u32[]{:S(2)}, u32[]{:S(2)}) collective-permute-start(bf16[592,384]{1,0:T(8,128)(2,1)} %get-tuple-element.29), channel_id=1, source_target_pairs={{0,0},{4,1},{2,2},{6,3},{1,4},{5,5},{3,6},{7,7},{8,8},{12,9},{10,1... | collective-permute-start | bytes 1363976 | tf_op jit(solution)/shard_map/ppermute | solution.py:39
  10.2 10.0 %collective-permute-start.3 = (bf16[384,384]{1,0:T(8,128)(2,1)}, bf16[384,384]{1,0:T(8,128)(2,1)S(1)}, u32[]{:S(2)}, u32[]{:S(2)}) collective-permute-start(bf16[384,384]{1,0:T(8,128)(2,1)} %get-tuple-element.27), channel_id=1, source_target_pairs={{3,0},{7,1},{1,2},{5,3},{2,4},{6,5},{0,6},{4,7},{11,8},{15,9},{9,1... | collective-permute-start | bytes 884744 | tf_op jit(solution)/shard_map/ppermute | solution.py:39
  10.5 16.2 %collective-permute-start.2 = (bf16[384,384]{1,0:T(8,128)(2,1)}, bf16[384,384]{1,0:T(8,128)(2,1)S(1)}, u32[]{:S(2)}, u32[]{:S(2)}) collective-permute-start(bf16[384,384]{1,0:T(8,128)(2,1)} %get-tuple-element.27), channel_id=1, source_target_pairs={{2,0},{6,1},{0,2},{4,3},{3,4},{7,5},{1,6},{5,7},{10,8},{14,9},{8,1... | collective-permute-start | bytes 884744 | tf_op jit(solution)/shard_map/ppermute | solution.py:39
  16.1 20.2 %collective-permute-start.6 = (bf16[400,384]{1,0:T(8,128)(2,1)S(1)}, bf16[400,384]{1,0:T(8,128)(2,1)S(1)}, u32[]{:S(2)}, u32[]{:S(2)}) collective-permute-start(bf16[400,384]{1,0:T(8,128)(2,1)S(1)} %slice.30), channel_id=1, source_target_pairs={{16,0},{20,1},{18,2},{22,3},{17,4},{21,5},{19,6},{23,7},{24,8},{28... | collective-permute-start | bytes 921608 | tf_op jit(solution)/shard_map/ppermute | solution.py:39
  20.2 14.0 %collective-permute-start.7 = (bf16[384,384]{1,0:T(8,128)(2,1)}, bf16[384,384]{1,0:T(8,128)(2,1)S(1)}, u32[]{:S(2)}, u32[]{:S(2)}) collective-permute-start(bf16[384,384]{1,0:T(8,128)(2,1)} %get-tuple-element.27), channel_id=1, source_target_pairs={{1,0},{5,1},{3,2},{7,3},{0,4},{4,5},{2,6},{6,7},{9,8},{13,9},{11,1... | collective-permute-start | bytes 884744 | tf_op jit(solution)/shard_map/ppermute | solution.py:39
  26.8 9.5 %collective-permute-start.4 = (bf16[192,384]{1,0:T(8,128)(2,1)S(1)}, bf16[192,384]{1,0:T(8,128)(2,1)S(1)}, u32[]{:S(2)}, u32[]{:S(2)}) collective-permute-start(bf16[192,384]{1,0:T(8,128)(2,1)S(1)} %collective-permute-done.1.refs_6_), channel_id=1, source_target_pairs={{8,0},{9,1},{10,2},{11,3},{12,4},{13,5},{14,6},{15,7},{0,8},{1,9},... | collective-permute-start | bytes 442376 | tf_op jit(solution)/shard_map/ppermute | solution.py:39
  37.0 15.0 %collective-permute-start.13 = (bf16[400,384]{1,0:T(8,128)(2,1)S(1)}, bf16[400,384]{1,0:T(8,128)(2,1)S(1)}, u32[]{:S(2)}, u32[]{:S(2)}) collective-permute-start(bf16[400,384]{1,0:T(8,128)(2,1)S(1)} %slice.40), channel_id=1, source_target_pairs={{8,0},{9,1},{10,2},{11,3},{12,4},{13,5},{14,6},{15,7},{0,8},{1,9},... | collective-permute-start | bytes 921608 | tf_op jit(solution)/shard_map/ppermute | solution.py:39
  37.1 14.9 %collective-permute-start.14 = (bf16[400,384]{1,0:T(8,128)(2,1)S(1)}, bf16[400,384]{1,0:T(8,128)(2,1)S(1)}, u32[]{:S(2)}, u32[]{:S(2)}) collective-permute-start(bf16[400,384]{1,0:T(8,128)(2,1)S(1)} %collective-permute-done.6.refs_6_), channel_id=1, source_target_pairs={{8,0},{9,1},{10,2},{11,3},{12,4},{13,5},{14,6},{15,7},{0,8},{1,9},... | collective-permute-start | bytes 921608 | tf_op jit(solution)/shard_map/ppermute | solution.py:39
  40.1 11.9 %collective-permute-start.12 = (bf16[384,384]{1,0:T(8,128)(2,1)S(1)}, bf16[384,384]{1,0:T(8,128)(2,1)S(1)}, u32[]{:S(2)}, u32[]{:S(2)}) collective-permute-start(bf16[384,384]{1,0:T(8,128)(2,1)S(1)} %first.1.refs_0_), channel_id=1, source_target_pairs={{6,0},{7,1},{4,2},{5,3},{2,4},{3,5},{0,6},{1,7},{14,8},{15,9},{12,... | collective-permute-start | bytes 884744 | tf_op jit(solution)/shard_map/ppermute | solution.py:39
  40.2 14.1 %collective-permute-start.11 = (bf16[384,384]{1,0:T(8,128)(2,1)S(1)}, bf16[384,384]{1,0:T(8,128)(2,1)S(1)}, u32[]{:S(2)}, u32[]{:S(2)}) collective-permute-start(bf16[384,384]{1,0:T(8,128)(2,1)S(1)} %first.1.refs_0_), channel_id=1, source_target_pairs={{2,0},{3,1},{0,2},{1,3},{6,4},{7,5},{4,6},{5,7},{10,8},{11,9},{8,1... | collective-permute-start | bytes 884744 | tf_op jit(solution)/shard_map/ppermute | solution.py:39
  41.3 15.0 %collective-permute-start.10 = (bf16[384,384]{1,0:T(8,128)(2,1)S(1)}, bf16[384,384]{1,0:T(8,128)(2,1)S(1)}, u32[]{:S(2)}, u32[]{:S(2)}) collective-permute-start(bf16[384,384]{1,0:T(8,128)(2,1)S(1)} %first.1.refs_0_), channel_id=1, source_target_pairs={{4,0},{5,1},{6,2},{7,3},{0,4},{1,5},{2,6},{3,7},{12,8},{13,9},{14,... | collective-permute-start | bytes 884744 | tf_op jit(solution)/shard_map/ppermute | solution.py:39
  60.3 9.7 %collective-permute-start.22 = (bf16[192,384]{1,0:T(8,128)(2,1)S(1)}, bf16[192,384]{1,0:T(8,128)(2,1)S(1)}, u32[]{:S(2)}, u32[]{:S(2)}) collective-permute-start(bf16[192,384]{1,0:T(8,128)(2,1)S(1)} %generator.1.refs_0_), channel_id=1, source_target_pairs={{16,0},{17,1},{18,2},{19,3},{20,4},{21,5},{22,6},{23,7},{24,8},{25... | collective-permute-start | bytes 442376 | tf_op jit(solution)/shard_map/ppermute | solution.py:39
  61.0 9.0 %collective-permute-start.21 = (bf16[192,384]{1,0:T(8,128)(2,1)S(1)}, bf16[192,384]{1,0:T(8,128)(2,1)S(1)}, u32[]{:S(2)}, u32[]{:S(2)}) collective-permute-start(bf16[192,384]{1,0:T(8,128)(2,1)S(1)} %generator.1.refs_0_), channel_id=1, source_target_pairs={{8,0},{9,1},{10,2},{11,3},{12,4},{13,5},{14,6},{15,7},{0,8},{1,9},... | collective-permute-start | bytes 442376 | tf_op jit(solution)/shard_map/ppermute | solution.py:39
  72.2 8.6 %collective-permute-start.25 = (bf16[384,384]{1,0:T(8,128)(2,1)S(1)}, bf16[384,384]{1,0:T(8,128)(2,1)S(1)}, u32[]{:S(2)}, u32[]{:S(2)}) collective-permute-start(bf16[384,384]{1,0:T(8,128)(2,1)S(1)} %pad_maximum_fusion.8.refs_5_), channel_id=1, source_target_pairs={{6,0},{7,1},{4,2},{5,3},{2,4},{3,5},{0,6},{1,7},{14,8},{15,9},{12,... | collective-permute-start | bytes 884744 | tf_op jit(solution)/shard_map/ppermute | solution.py:39
  72.8 12.6 %collective-permute-start.24 = (bf16[384,384]{1,0:T(8,128)(2,1)S(1)}, bf16[384,384]{1,0:T(8,128)(2,1)S(1)}, u32[]{:S(2)}, u32[]{:S(2)}) collective-permute-start(bf16[384,384]{1,0:T(8,128)(2,1)S(1)} %pad_maximum_fusion.8.refs_5_), channel_id=1, source_target_pairs={{2,0},{3,1},{0,2},{1,3},{6,4},{7,5},{4,6},{5,7},{10,8},{11,9},{8,1... | collective-permute-start | bytes 884744 | tf_op jit(solution)/shard_map/ppermute | solution.py:39
  73.6 16.0 %collective-permute-start.23 = (bf16[384,384]{1,0:T(8,128)(2,1)S(1)}, bf16[384,384]{1,0:T(8,128)(2,1)S(1)}, u32[]{:S(2)}, u32[]{:S(2)}) collective-permute-start(bf16[384,384]{1,0:T(8,128)(2,1)S(1)} %pad_maximum_fusion.8.refs_5_), channel_id=1, source_target_pairs={{4,0},{5,1},{6,2},{7,3},{0,4},{1,5},{2,6},{3,7},{12,8},{13,9},{14,... | collective-permute-start | bytes 884744 | tf_op jit(solution)/shard_map/ppermute | solution.py:39
  77.6 12.6 %collective-permute-start.29 = (bf16[192,384]{1,0:T(8,128)(2,1)S(1)}, bf16[192,384]{1,0:T(8,128)(2,1)S(1)}, u32[]{:S(2)}, u32[]{:S(2)}) collective-permute-start(bf16[192,384]{1,0:T(8,128)(2,1)S(1)} %collective-permute-done.26.refs_10_), channel_id=1, source_target_pairs={{6,0},{7,1},{4,2},{5,3},{2,4},{3,5},{0,6},{1,7},{14,8},{15,9},{12,... | collective-permute-start | bytes 442376 | tf_op jit(solution)/shard_map/ppermute | solution.py:39
  79.8 11.9 %collective-permute-start.28 = (bf16[192,384]{1,0:T(8,128)(2,1)S(1)}, bf16[192,384]{1,0:T(8,128)(2,1)S(1)}, u32[]{:S(2)}, u32[]{:S(2)}) collective-permute-start(bf16[192,384]{1,0:T(8,128)(2,1)S(1)} %collective-permute-done.26.refs_10_), channel_id=1, source_target_pairs={{2,0},{3,1},{0,2},{1,3},{6,4},{7,5},{4,6},{5,7},{10,8},{11,9},{8,1... | collective-permute-start | bytes 442376 | tf_op jit(solution)/shard_map/ppermute | solution.py:39
  80.8 13.9 %collective-permute-start.27 = (bf16[192,384]{1,0:T(8,128)(2,1)S(1)}, bf16[192,384]{1,0:T(8,128)(2,1)S(1)}, u32[]{:S(2)}, u32[]{:S(2)}) collective-permute-start(bf16[192,384]{1,0:T(8,128)(2,1)S(1)} %collective-permute-done.26.refs_10_), channel_id=1, source_target_pairs={{4,0},{5,1},{6,2},{7,3},{0,4},{1,5},{2,6},{3,7},{12,8},{13,9},{14,... | collective-permute-start | bytes 442376 | tf_op jit(solution)/shard_map/ppermute | solution.py:39
  110.0 8.3 %collective-permute-start.32 = (bf16[192,384]{1,0:T(8,128)(2,1)S(1)}, bf16[192,384]{1,0:T(8,128)(2,1)S(1)}, u32[]{:S(2)}, u32[]{:S(2)}) collective-permute-start(bf16[192,384]{1,0:T(8,128)(2,1)S(1)} %get-tuple-element.45.refs_0_), channel_id=1, source_target_pairs={{4,0},{5,1},{6,2},{7,3},{0,4},{1,5},{2,6},{3,7},{12,8},{13,9},{14,... | collective-permute-start | bytes 442376 | tf_op jit(solution)/shard_map/ppermute | solution.py:39
  121.3 9.8 %collective-permute-start.41 = (bf16[192,384]{1,0:T(8,128)(2,1)S(1)}, bf16[192,384]{1,0:T(8,128)(2,1)S(1)}, u32[]{:S(2)}, u32[]{:S(2)}) collective-permute-start(bf16[192,384]{1,0:T(8,128)(2,1)S(1)} %square.1.refs_0_), channel_id=1, source_target_pairs={{16,0},{17,1},{18,2},{19,3},{20,4},{21,5},{22,6},{23,7},{24,8},{25... | collective-permute-start | bytes 442376 | tf_op jit(solution)/shard_map/ppermute | solution.py:39
  121.8 9.3 %collective-permute-start.38 = (bf16[192,384]{1,0:T(8,128)(2,1)S(1)}, bf16[192,384]{1,0:T(8,128)(2,1)S(1)}, u32[]{:S(2)}, u32[]{:S(2)}) collective-permute-start(bf16[192,384]{1,0:T(8,128)(2,1)S(1)} %square.1.refs_0_), channel_id=1, source_target_pairs={{6,0},{7,1},{4,2},{5,3},{2,4},{3,5},{0,6},{1,7},{14,8},{15,9},{12,... | collective-permute-start | bytes 442376 | tf_op jit(solution)/shard_map/ppermute | solution.py:39
  122.8 8.3 %collective-permute-start.37 = (bf16[192,384]{1,0:T(8,128)(2,1)S(1)}, bf16[192,384]{1,0:T(8,128)(2,1)S(1)}, u32[]{:S(2)}, u32[]{:S(2)}) collective-permute-start(bf16[192,384]{1,0:T(8,128)(2,1)S(1)} %square.1.refs_0_), channel_id=1, source_target_pairs={{2,0},{3,1},{0,2},{1,3},{6,4},{7,5},{4,6},{5,7},{10,8},{11,9},{8,1... | collective-permute-start | bytes 442376 | tf_op jit(solution)/shard_map/ppermute | solution.py:39
  (22 other events, 112.4 us)

commit v14 on v13

--- a/solution.py
+++ b/solution.py
@@ -147,8 +147,8 @@
 
 
 def mask_kernel(inputs, *refs):
-    sources, (masked_density, duo, trio) = refs[:inputs], refs[inputs : inputs + 3]
-    held, sems = refs[inputs + 3 : -1], refs[-1]
+    sources, (masked_density, duo, sent, trio) = refs[:inputs], refs[inputs : inputs + 4]
+    held, sems = refs[inputs + 4 : -1], refs[-1]
     copies = [
         pltpu.make_async_copy(source, target, sems.at[n])
         for n, (source, target) in enumerate(zip(sources, held))
@@ -171,6 +171,7 @@
     for half, (ref, number) in enumerate(((fock, 0), (margin, 2))):
         value = masked(ref, number)
         duo[half * rows : (half + 1) * rows, :] = value
+        sent[TAIL + half * rows : TAIL + (half + 1) * rows, :] = value
         trio[TAIL + half * rows : TAIL + (half + 1) * rows, :] = value
     top = (iota((TAIL, row_blocks), 0) == iota((TAIL, row_blocks), 1)).astype(BF16)
     tail = jnp.zeros((TAIL, columns), F32)
@@ -179,6 +180,7 @@
         column = iota((column_blocks, columns), 1) - number * column_blocks
         spread = (iota((column_blocks, columns), 0) == column).astype(BF16)
         tail += dot(dot(top, block.astype(BF16)).astype(BF16), spread)
+    sent[:TAIL, :] = tail.astype(BF16)
     trio[:TAIL, :] = tail.astype(BF16)
 
 
@@ -394,11 +396,12 @@
         first_filters,
         second_filters.transpose(1, 0, 2),
     )
-    masked_density, duo, trio = call(
+    masked_density, duo, sent, trio = call(
         functools.partial(mask_kernel, len(inputs)),
         [
             block,
             jax.ShapeDtypeStruct((2 * rows, columns), BF16),
+            jax.ShapeDtypeStruct((TAIL + 2 * rows, columns), BF16),
             jax.ShapeDtypeStruct((TAIL + 3 * rows, columns), BF16),
         ],
         [ANY] * len(inputs),
@@ -408,14 +411,13 @@
         room=60,
     )(*inputs)
 
-    home = trio
-    trio = moves.relabel(home)
+    trio = moves.relabel(trio)
     fock_rows = moves.plane(duo, True)
-    density_line = moves.line(masked_density, True, gate=tuple(fock_rows[-2:]))
+    density_line = moves.line(masked_density, True, gate=tuple(fock_rows[-1:]))
     density_near = [(trio, TAIL + 2 * rows)] + whole(density_line)
     span = TAIL + 2 * rows
     pair_second, *_ = barrier((trio[:span], *density_line))
-    gated, _ = barrier((home[:span], density_line[half - 1]))
+    gated, _ = barrier((sent, density_line[half - 1]))
     pair_line = moves.line(gated, True, second=pair_second)
     early = barrier((*density_line, trio, pair_line[half - 1], *fock_rows))
     density_line, trio, pair_line[half - 1] = list(early[: count - 1]), early[count - 1], early[count]
@@ -464,8 +466,10 @@
         planes = [group] + moves.plane(group)
         done.append((held, planes))
     done[1] = (done[1][0], list(barrier((*done[1][1], *done[2][1][1:]))[:count]))
+    own_far = moves.cores(done[0][1])
+    done[2] = (done[2][0], list(barrier((*done[2][1], own_far[0][0]))[:count]))
     for held, planes in done:
-        far = moves.cores(planes)
+        far = own_far if held[0] == 0 else moves.cores(planes)
         for s, value in enumerate(planes):
             for lane, (array, start) in enumerate(((value, 0), far[s])):
                 if not any(other is array for other in arrays):

time: 148 us -> 144 us (0.973)
  waiting for transfers between devices: 85.5 us -> 79.4 us
  starting transfers between devices: 42.5 us -> 45.6 us
    ppermute x45, waiting for transfers between devices: 85.5 us -> 79.4 us  [move(): return lax.ppermute(value, AXES, permutation(self.rows, self.cols, source))]
    ppermute x45, starting transfers between devices: 42.5 us -> 45.6 us  [move(): return lax.ppermute(value, AXES, permutation(self.rows, self.cols, source))]
  transfers between devices with their start and end apart: 45 -> 45, of which waited for: 31 -> 29; matrix products, arithmetic and copies ran while one was open for 1% -> 0% of each run, Pallas kernels for 1% -> 1%
where the time goes in v14:
time: 144 us
  waiting for transfers between devices  79.4 us (55%)
  starting transfers between devices  45.6 us (32%)
  Pallas kernels  17.1 us (12%)
    ppermute x45, waiting for transfers between devices, move(): return lax.ppermute(value, AXES, permutation(self.rows, self.cols, source))  79.4 us
    ppermute x45, starting transfers between devices, move(): return lax.ppermute(value, AXES, permutation(self.rows, self.cols, source))  45.6 us
    pallas_call x1, Pallas kernels, on_device(): call(functools.partial(series_kernel, layout, count, len(arrays)), [jax.S...  8.84 us
    pallas_call x4, Pallas kernels, views_call(): call(body, outs, [INVMEM] * len(operands), scratch, name, flops)(*operands)  4.53 us
    pallas_call x1, Pallas kernels, on_device(): call(functools.partial(mask_kernel, len(inputs)), [block, jax.ShapeDtypeS...  3.68 us
  transfers between devices with their start and end apart: 45, of which 29 were waited for; matrix products, arithmetic and copies ran while one was open for 0% of the time, Pallas kernels for 1%

profile of v14, /device:TPU:1, one launch (start us, length us, event | category | flops | bytes accessed | tf_op | source)
XLA Modules:
  0.0 143.5 jit_solution(18332118211440354448)
XLA Ops:
  0.0 3.7 %mask.1 = (bf16[192,384]{1,0:T(8,128)(2,1)}, bf16[384,384]{1,0:T(8,128)(2,1)}, bf16[400,384]{1,0:T(8,128)(2,1)}, bf16[592,384]{1,0:T(8,128)(2,1)}) custom-call(s32[3,6,12]{2,1,0:T(8,128)} %refs_0_.1, bf16[192,384]{1,0:T(8,128)(2,1)} %refs_1_.1, bf16[192,384]{1,0:T(8,128)(2,1)} %refs_2_.1, bf16[192,384]{1,0:T(8,128)(2,1)} %refs_3_.1, s32[3,6,12]{2,1,0:T(8,128)} %refs_4_.1, ...), custom_call_target="tpu_custom_call" | custom-call | flops 1000 | bytes 1000 | tf_op jit(solution)/shard_map/mask/pallas_call | solution.py:399
  3.7 4.7 %collective-permute-start.1 = (bf16[192,384]{1,0:T(8,128)(2,1)}, bf16[192,384]{1,0:T(8,128)(2,1)S(1)}, u32[]{:S(2)}, u32[]{:S(2)}) collective-permute-start(bf16[192,384]{1,0:T(8,128)(2,1)} %get-tuple-element.31), channel_id=1, source_target_pairs={{16,0},{20,1},{18,2},{22,3},{17,4},{21,5},{19,6},{23,7},{24,8},{28... | collective-permute-start | bytes 442376 | tf_op jit(solution)/shard_map/ppermute | solution.py:39
  10.6 2.6 %collective-permute-start = (bf16[192,384]{1,0:T(8,128)(2,1)}, bf16[192,384]{1,0:T(8,128)(2,1)S(1)}, u32[]{:S(2)}, u32[]{:S(2)}) collective-permute-start(bf16[192,384]{1,0:T(8,128)(2,1)} %get-tuple-element.31), channel_id=1, source_target_pairs={{8,0},{12,1},{10,2},{14,3},{9,4},{13,5},{11,6},{15,7},{0,8},{4,9},... | collective-permute-start | bytes 442376 | tf_op jit(solution)/shard_map/ppermute | solution.py:39
  13.2 3.0 %collective-permute-done.1.refs_6_ = bf16[192,384]{1,0:T(8,128)(2,1)S(1)} collective-permute-done((bf16[192,384]{1,0:T(8,128)(2,1)}, bf16[192,384]{1,0:T(8,128)(2,1)S(1)}, u32[]{:S(2)}, u32[]{:S(2)}) %collective-permute-start.1) | collective-permute-done | bytes 147488 | tf_op jit(solution)/shard_map/ppermute | solution.py:39
  16.5 2.2 %collective-permute-start.7 = (bf16[384,384]{1,0:T(8,128)(2,1)}, bf16[384,384]{1,0:T(8,128)(2,1)S(1)}, u32[]{:S(2)}, u32[]{:S(2)}) collective-permute-start(bf16[384,384]{1,0:T(8,128)(2,1)} %get-tuple-element.32), channel_id=1, source_target_pairs={{2,0},{6,1},{0,2},{4,3},{3,4},{7,5},{1,6},{5,7},{10,8},{14,9},{8,1... | collective-permute-start | bytes 884744 | tf_op jit(solution)/shard_map/ppermute | solution.py:39
  21.6 5.3 %collective-permute-done.7.refs_2_ = bf16[384,384]{1,0:T(8,128)(2,1)S(1)} collective-permute-done((bf16[384,384]{1,0:T(8,128)(2,1)}, bf16[384,384]{1,0:T(8,128)(2,1)S(1)}, u32[]{:S(2)}, u32[]{:S(2)}) %collective-permute-start.7) | collective-permute-done | bytes 294944 | tf_op jit(solution)/shard_map/ppermute | solution.py:39
  26.9 7.2 %collective-permute-done.6.refs_1_ = bf16[384,384]{1,0:T(8,128)(2,1)S(1)} collective-permute-done((bf16[384,384]{1,0:T(8,128)(2,1)}, bf16[384,384]{1,0:T(8,128)(2,1)S(1)}, u32[]{:S(2)}, u32[]{:S(2)}) %collective-permute-start.6) | collective-permute-done | bytes 294944 | tf_op jit(solution)/shard_map/ppermute | solution.py:39
  40.5 9.8 %collective-permute-done.14.refs_7_ = bf16[400,384]{1,0:T(8,128)(2,1)S(1)} collective-permute-done((bf16[400,384]{1,0:T(8,128)(2,1)S(1)}, bf16[400,384]{1,0:T(8,128)(2,1)S(1)}, u32[]{:S(2)}, u32[]{:S(2)}) %collective-permute-start.14) | collective-permute-done | bytes 307232 | tf_op jit(solution)/shard_map/ppermute | solution.py:39
  52.0 2.1 %collective-permute-done.10.refs_1_ = bf16[384,384]{1,0:T(8,128)(2,1)S(1)} collective-permute-done((bf16[384,384]{1,0:T(8,128)(2,1)S(1)}, bf16[384,384]{1,0:T(8,128)(2,1)S(1)}, u32[]{:S(2)}, u32[]{:S(2)}) %collective-permute-start.10) | collective-permute-done | bytes 294944 | tf_op jit(solution)/shard_map/ppermute | solution.py:39
  54.7 2.0 %collective-permute-done.16.refs_10_ = bf16[400,384]{1,0:T(8,128)(2,1)S(1)} collective-permute-done((bf16[400,384]{1,0:T(8,128)(2,1)S(1)}, bf16[400,384]{1,0:T(8,128)(2,1)S(1)}, u32[]{:S(2)}, u32[]{:S(2)}) %collective-permute-start.16) | collective-permute-done | bytes 307232 | tf_op jit(solution)/shard_map/ppermute | solution.py:39
  62.5 5.1 %collective-permute-done.22 = bf16[192,384]{1,0:T(8,128)(2,1)S(1)} collective-permute-done((bf16[192,384]{1,0:T(8,128)(2,1)S(1)}, bf16[192,384]{1,0:T(8,128)(2,1)S(1)}, u32[]{:S(2)}, u32[]{:S(2)}) %collective-permute-start.22) | collective-permute-done | bytes 147488 | tf_op jit(solution)/shard_map/ppermute | solution.py:39
  72.1 2.9 %collective-permute-done.26.refs_10_ = bf16[192,384]{1,0:T(8,128)(2,1)S(1)} collective-permute-done((bf16[192,384]{1,0:T(8,128)(2,1)S(1)}, bf16[192,384]{1,0:T(8,128)(2,1)S(1)}, u32[]{:S(2)}, u32[]{:S(2)}) %collective-permute-start.26) | collective-permute-done | bytes 147488 | tf_op jit(solution)/shard_map/ppermute | solution.py:39
  77.9 5.1 %collective-permute-done.24.refs_8_ = bf16[384,384]{1,0:T(8,128)(2,1)S(1)} collective-permute-done((bf16[384,384]{1,0:T(8,128)(2,1)S(1)}, bf16[384,384]{1,0:T(8,128)(2,1)S(1)}, u32[]{:S(2)}, u32[]{:S(2)}) %collective-permute-start.24) | collective-permute-done | bytes 294944 | tf_op jit(solution)/shard_map/ppermute | solution.py:39
  82.9 3.8 %collective-permute-start.20 = (bf16[768,384]{1,0:T(8,128)(2,1)S(1)}, bf16[768,384]{1,0:T(8,128)(2,1)S(1)}, u32[]{:S(2)}, u32[]{:S(2)}) collective-permute-start(bf16[768,384]{1,0:T(8,128)(2,1)S(1)} %pad_maximum_fusion.2), channel_id=1, source_target_pairs={{1,0},{0,1},{3,2},{2,3},{5,4},{4,5},{7,6},{6,7},{9,8},{8,9},{11,10... | collective-permute-start | bytes 1769480 | tf_op jit(solution)/shard_map/ppermute | solution.py:39
  87.0 2.2 %collective-permute-done.28.refs_13_ = bf16[192,384]{1,0:T(8,128)(2,1)S(1)} collective-permute-done((bf16[192,384]{1,0:T(8,128)(2,1)S(1)}, bf16[192,384]{1,0:T(8,128)(2,1)S(1)}, u32[]{:S(2)}, u32[]{:S(2)}) %collective-permute-start.28) | collective-permute-done | bytes 147488 | tf_op jit(solution)/shard_map/ppermute | solution.py:39
  89.3 2.3 %collective-permute-done.27.refs_12_ = bf16[192,384]{1,0:T(8,128)(2,1)S(1)} collective-permute-done((bf16[192,384]{1,0:T(8,128)(2,1)S(1)}, bf16[192,384]{1,0:T(8,128)(2,1)S(1)}, u32[]{:S(2)}, u32[]{:S(2)}) %collective-permute-start.27) | collective-permute-done | bytes 147488 | tf_op jit(solution)/shard_map/ppermute | solution.py:39
  92.5 3.1 %collective-permute-done.31.refs_11_ = bf16[768,384]{1,0:T(8,128)(2,1)S(1)} collective-permute-done((bf16[768,384]{1,0:T(8,128)(2,1)S(1)}, bf16[768,384]{1,0:T(8,128)(2,1)S(1)}, u32[]{:S(2)}, u32[]{:S(2)}) %collective-permute-start.31) | collective-permute-done | bytes 589856 | tf_op jit(solution)/shard_map/ppermute | solution.py:39
  95.6 8.8 %series.1 = (bf16[192,1536]{1,0:T(8,128)(2,1)S(1)}, bf16[192,384]{1,0:T(8,128)(2,1)S(1)}) custom-call(bf16[192,384]{1,0:T(8,128)(2,1)S(1)} %generator.1.refs_0_, bf16[768,384]{1,0:T(8,128)(2,1)S(1)} %collective-permute-done.20.refs_1_, bf16[192,384]{1,0:T(8,128)(2,1)S(1)} %collective-permute-done.17.refs_2_, ...), custom_call_target="tpu_custom_call" | custom-call | flops 1000 | bytes 1000 | tf_op jit(solution)/shard_map/series/pallas_call | solution.py:482
  107.2 3.3 %collective-permute-done.34.refs_3_ = bf16[192,384]{1,0:T(8,128)(2,1)S(1)} collective-permute-done((bf16[192,384]{1,0:T(8,128)(2,1)S(1)}, bf16[192,384]{1,0:T(8,128)(2,1)S(1)}, u32[]{:S(2)}, u32[]{:S(2)}) %collective-permute-start.34) | collective-permute-done | bytes 147488 | tf_op jit(solution)/shard_map/ppermute | solution.py:39
  110.5 2.4 %collective-permute-done.33.refs_2_ = bf16[192,384]{1,0:T(8,128)(2,1)S(1)} collective-permute-done((bf16[192,384]{1,0:T(8,128)(2,1)S(1)}, bf16[192,384]{1,0:T(8,128)(2,1)S(1)}, u32[]{:S(2)}, u32[]{:S(2)}) %collective-permute-start.33) | collective-permute-done | bytes 147488 | tf_op jit(solution)/shard_map/ppermute | solution.py:39
  122.3 5.0 %collective-permute-done.41.refs_6_ = bf16[192,384]{1,0:T(8,128)(2,1)S(1)} collective-permute-done((bf16[192,384]{1,0:T(8,128)(2,1)S(1)}, bf16[192,384]{1,0:T(8,128)(2,1)S(1)}, u32[]{:S(2)}, u32[]{:S(2)}) %collective-permute-start.41) | collective-permute-done | bytes 147488 | tf_op jit(solution)/shard_map/ppermute | solution.py:39
  128.8 3.2 %collective-permute-done.42.refs_7_ = bf16[192,384]{1,0:T(8,128)(2,1)S(1)} collective-permute-done((bf16[192,384]{1,0:T(8,128)(2,1)S(1)}, bf16[192,384]{1,0:T(8,128)(2,1)S(1)}, u32[]{:S(2)}, u32[]{:S(2)}) %collective-permute-start.42) | collective-permute-done | bytes 147488 | tf_op jit(solution)/shard_map/ppermute | solution.py:39
  136.4 2.6 %collective-permute-start.44 = (bf16[192,384]{1,0:T(8,128)(2,1)S(1)}, bf16[192,384]{1,0:T(8,128)(2,1)S(1)}, u32[]{:S(2)}, u32[]{:S(2)}) collective-permute-start(bf16[192,384]{1,0:T(8,128)(2,1)S(1)} %evolve.1), channel_id=1, source_target_pairs={{0,0},{4,1},{2,2},{6,3},{1,4},{5,5},{3,6},{7,7},{8,8},{12,9},{10,1... | collective-permute-start | bytes 442376 | tf_op jit(solution)/shard_map/ppermute | solution.py:39
  139.0 3.9 %collective-permute-done.44 = bf16[192,384]{1,0:T(8,128)(2,1)S(1)} collective-permute-done((bf16[192,384]{1,0:T(8,128)(2,1)S(1)}, bf16[192,384]{1,0:T(8,128)(2,1)S(1)}, u32[]{:S(2)}, u32[]{:S(2)}) %collective-permute-start.44) | collective-permute-done | bytes 147488 | tf_op jit(solution)/shard_map/ppermute | solution.py:39
  (92 shorter events, 46.9 us)
Async XLA Ops:
  3.7 12.6 %collective-permute-start.1 = (bf16[192,384]{1,0:T(8,128)(2,1)}, bf16[192,384]{1,0:T(8,128)(2,1)S(1)}, u32[]{:S(2)}, u32[]{:S(2)}) collective-permute-start(bf16[192,384]{1,0:T(8,128)(2,1)} %get-tuple-element.31), channel_id=1, source_target_pairs={{16,0},{20,1},{18,2},{22,3},{17,4},{21,5},{19,6},{23,7},{24,8},{28... | collective-permute-start | bytes 442376 | tf_op jit(solution)/shard_map/ppermute | solution.py:39
  8.4 25.6 %collective-permute-start.4 = (bf16[592,384]{1,0:T(8,128)(2,1)}, bf16[592,384]{1,0:T(8,128)(2,1)S(1)}, u32[]{:S(2)}, u32[]{:S(2)}) collective-permute-start(bf16[592,384]{1,0:T(8,128)(2,1)} %get-tuple-element.34), channel_id=1, source_target_pairs={{0,0},{4,1},{2,2},{6,3},{1,4},{5,5},{3,6},{7,7},{8,8},{12,9},{10,1... | collective-permute-start | bytes 1363976 | tf_op jit(solution)/shard_map/ppermute | solution.py:39
  10.3 10.3 %collective-permute-start.2 = (bf16[384,384]{1,0:T(8,128)(2,1)}, bf16[384,384]{1,0:T(8,128)(2,1)S(1)}, u32[]{:S(2)}, u32[]{:S(2)}) collective-permute-start(bf16[384,384]{1,0:T(8,128)(2,1)} %get-tuple-element.32), channel_id=1, source_target_pairs={{3,0},{7,1},{1,2},{5,3},{2,4},{6,5},{0,6},{4,7},{11,8},{15,9},{9,1... | collective-permute-start | bytes 884744 | tf_op jit(solution)/shard_map/ppermute | solution.py:39
  10.6 10.1 %collective-permute-start = (bf16[192,384]{1,0:T(8,128)(2,1)}, bf16[192,384]{1,0:T(8,128)(2,1)S(1)}, u32[]{:S(2)}, u32[]{:S(2)}) collective-permute-start(bf16[192,384]{1,0:T(8,128)(2,1)} %get-tuple-element.31), channel_id=1, source_target_pairs={{8,0},{12,1},{10,2},{14,3},{9,4},{13,5},{11,6},{15,7},{0,8},{4,9},... | collective-permute-start | bytes 442376 | tf_op jit(solution)/shard_map/ppermute | solution.py:39
  16.3 17.8 %collective-permute-start.5 = (bf16[400,384]{1,0:T(8,128)(2,1)}, bf16[400,384]{1,0:T(8,128)(2,1)S(1)}, u32[]{:S(2)}, u32[]{:S(2)}) collective-permute-start(bf16[400,384]{1,0:T(8,128)(2,1)} %get-tuple-element.36), channel_id=1, source_target_pairs={{16,0},{20,1},{18,2},{22,3},{17,4},{21,5},{19,6},{23,7},{24,8},{28... | collective-permute-start | bytes 921608 | tf_op jit(solution)/shard_map/ppermute | solution.py:39
  16.5 10.4 %collective-permute-start.7 = (bf16[384,384]{1,0:T(8,128)(2,1)}, bf16[384,384]{1,0:T(8,128)(2,1)S(1)}, u32[]{:S(2)}, u32[]{:S(2)}) collective-permute-start(bf16[384,384]{1,0:T(8,128)(2,1)} %get-tuple-element.32), channel_id=1, source_target_pairs={{2,0},{6,1},{0,2},{4,3},{3,4},{7,5},{1,6},{5,7},{10,8},{14,9},{8,1... | collective-permute-start | bytes 884744 | tf_op jit(solution)/shard_map/ppermute | solution.py:39
  20.7 13.4 %collective-permute-start.6 = (bf16[384,384]{1,0:T(8,128)(2,1)}, bf16[384,384]{1,0:T(8,128)(2,1)S(1)}, u32[]{:S(2)}, u32[]{:S(2)}) collective-permute-start(bf16[384,384]{1,0:T(8,128)(2,1)} %get-tuple-element.32), channel_id=1, source_target_pairs={{1,0},{5,1},{3,2},{7,3},{0,4},{4,5},{2,6},{6,7},{9,8},{13,9},{11,1... | collective-permute-start | bytes 884744 | tf_op jit(solution)/shard_map/ppermute | solution.py:39
  20.7 13.4 %collective-permute-start.3 = (bf16[192,384]{1,0:T(8,128)(2,1)S(1)}, bf16[192,384]{1,0:T(8,128)(2,1)S(1)}, u32[]{:S(2)}, u32[]{:S(2)}) collective-permute-start(bf16[192,384]{1,0:T(8,128)(2,1)S(1)} %collective-permute-done.1.refs_6_), channel_id=1, source_target_pairs={{8,0},{9,1},{10,2},{11,3},{12,4},{13,5},{14,6},{15,7},{0,8},{1,9},... | collective-permute-start | bytes 442376 | tf_op jit(solution)/shard_map/ppermute | solution.py:39
  34.8 15.5 %collective-permute-start.13 = (bf16[400,384]{1,0:T(8,128)(2,1)S(1)}, bf16[400,384]{1,0:T(8,128)(2,1)S(1)}, u32[]{:S(2)}, u32[]{:S(2)}) collective-permute-start(bf16[400,384]{1,0:T(8,128)(2,1)S(1)} %slice.36), channel_id=1, source_target_pairs={{8,0},{9,1},{10,2},{11,3},{12,4},{13,5},{14,6},{15,7},{0,8},{1,9},... | collective-permute-start | bytes 921608 | tf_op jit(solution)/shard_map/ppermute | solution.py:39
  34.9 15.5 %collective-permute-start.14 = (bf16[400,384]{1,0:T(8,128)(2,1)S(1)}, bf16[400,384]{1,0:T(8,128)(2,1)S(1)}, u32[]{:S(2)}, u32[]{:S(2)}) collective-permute-start(bf16[400,384]{1,0:T(8,128)(2,1)S(1)} %collective-permute-done.5.refs_6_), channel_id=1, source_target_pairs={{8,0},{9,1},{10,2},{11,3},{12,4},{13,5},{14,6},{15,7},{0,8},{1,9},... | collective-permute-start | bytes 921608 | tf_op jit(solution)/shard_map/ppermute | solution.py:39
  37.8 12.5 %collective-permute-start.12 = (bf16[384,384]{1,0:T(8,128)(2,1)S(1)}, bf16[384,384]{1,0:T(8,128)(2,1)S(1)}, u32[]{:S(2)}, u32[]{:S(2)}) collective-permute-start(bf16[384,384]{1,0:T(8,128)(2,1)S(1)} %first.1.refs_0_), channel_id=1, source_target_pairs={{6,0},{7,1},{4,2},{5,3},{2,4},{3,5},{0,6},{1,7},{14,8},{15,9},{12,... | collective-permute-start | bytes 884744 | tf_op jit(solution)/shard_map/ppermute | solution.py:39
  39.3 12.7 %collective-permute-start.11 = (bf16[384,384]{1,0:T(8,128)(2,1)S(1)}, bf16[384,384]{1,0:T(8,128)(2,1)S(1)}, u32[]{:S(2)}, u32[]{:S(2)}) collective-permute-start(bf16[384,384]{1,0:T(8,128)(2,1)S(1)} %first.1.refs_0_), channel_id=1, source_target_pairs={{2,0},{3,1},{0,2},{1,3},{6,4},{7,5},{4,6},{5,7},{10,8},{11,9},{8,1... | collective-permute-start | bytes 884744 | tf_op jit(solution)/shard_map/ppermute | solution.py:39
  39.3 14.8 %collective-permute-start.10 = (bf16[384,384]{1,0:T(8,128)(2,1)S(1)}, bf16[384,384]{1,0:T(8,128)(2,1)S(1)}, u32[]{:S(2)}, u32[]{:S(2)}) collective-permute-start(bf16[384,384]{1,0:T(8,128)(2,1)S(1)} %first.1.refs_0_), channel_id=1, source_target_pairs={{4,0},{5,1},{6,2},{7,3},{0,4},{1,5},{2,6},{3,7},{12,8},{13,9},{14,... | collective-permute-start | bytes 884744 | tf_op jit(solution)/shard_map/ppermute | solution.py:39
  58.0 9.6 %collective-permute-start.22 = (bf16[192,384]{1,0:T(8,128)(2,1)S(1)}, bf16[192,384]{1,0:T(8,128)(2,1)S(1)}, u32[]{:S(2)}, u32[]{:S(2)}) collective-permute-start(bf16[192,384]{1,0:T(8,128)(2,1)S(1)} %generator.1.refs_0_), channel_id=1, source_target_pairs={{16,0},{17,1},{18,2},{19,3},{20,4},{21,5},{22,6},{23,7},{24,8},{25... | collective-permute-start | bytes 442376 | tf_op jit(solution)/shard_map/ppermute | solution.py:39
  58.2 9.4 %collective-permute-start.21 = (bf16[192,384]{1,0:T(8,128)(2,1)S(1)}, bf16[192,384]{1,0:T(8,128)(2,1)S(1)}, u32[]{:S(2)}, u32[]{:S(2)}) collective-permute-start(bf16[192,384]{1,0:T(8,128)(2,1)S(1)} %generator.1.refs_0_), channel_id=1, source_target_pairs={{8,0},{9,1},{10,2},{11,3},{12,4},{13,5},{14,6},{15,7},{0,8},{1,9},... | collective-permute-start | bytes 442376 | tf_op jit(solution)/shard_map/ppermute | solution.py:39
  69.1 8.4 %collective-permute-start.25 = (bf16[384,384]{1,0:T(8,128)(2,1)S(1)}, bf16[384,384]{1,0:T(8,128)(2,1)S(1)}, u32[]{:S(2)}, u32[]{:S(2)}) collective-permute-start(bf16[384,384]{1,0:T(8,128)(2,1)S(1)} %pad_maximum_fusion.8.refs_5_), channel_id=1, source_target_pairs={{6,0},{7,1},{4,2},{5,3},{2,4},{3,5},{0,6},{1,7},{14,8},{15,9},{12,... | collective-permute-start | bytes 884744 | tf_op jit(solution)/shard_map/ppermute | solution.py:39
  70.2 12.7 %collective-permute-start.24 = (bf16[384,384]{1,0:T(8,128)(2,1)S(1)}, bf16[384,384]{1,0:T(8,128)(2,1)S(1)}, u32[]{:S(2)}, u32[]{:S(2)}) collective-permute-start(bf16[384,384]{1,0:T(8,128)(2,1)S(1)} %pad_maximum_fusion.8.refs_5_), channel_id=1, source_target_pairs={{2,0},{3,1},{0,2},{1,3},{6,4},{7,5},{4,6},{5,7},{10,8},{11,9},{8,1... | collective-permute-start | bytes 884744 | tf_op jit(solution)/shard_map/ppermute | solution.py:39
  71.0 15.8 %collective-permute-start.23 = (bf16[384,384]{1,0:T(8,128)(2,1)S(1)}, bf16[384,384]{1,0:T(8,128)(2,1)S(1)}, u32[]{:S(2)}, u32[]{:S(2)}) collective-permute-start(bf16[384,384]{1,0:T(8,128)(2,1)S(1)} %pad_maximum_fusion.8.refs_5_), channel_id=1, source_target_pairs={{4,0},{5,1},{6,2},{7,3},{0,4},{1,5},{2,6},{3,7},{12,8},{13,9},{14,... | collective-permute-start | bytes 884744 | tf_op jit(solution)/shard_map/ppermute | solution.py:39
  75.0 12.0 %collective-permute-start.29 = (bf16[192,384]{1,0:T(8,128)(2,1)S(1)}, bf16[192,384]{1,0:T(8,128)(2,1)S(1)}, u32[]{:S(2)}, u32[]{:S(2)}) collective-permute-start(bf16[192,384]{1,0:T(8,128)(2,1)S(1)} %collective-permute-done.26.refs_10_), channel_id=1, source_target_pairs={{6,0},{7,1},{4,2},{5,3},{2,4},{3,5},{0,6},{1,7},{14,8},{15,9},{12,... | collective-permute-start | bytes 442376 | tf_op jit(solution)/shard_map/ppermute | solution.py:39
  77.0 12.3 %collective-permute-start.28 = (bf16[192,384]{1,0:T(8,128)(2,1)S(1)}, bf16[192,384]{1,0:T(8,128)(2,1)S(1)}, u32[]{:S(2)}, u32[]{:S(2)}) collective-permute-start(bf16[192,384]{1,0:T(8,128)(2,1)S(1)} %collective-permute-done.26.refs_10_), channel_id=1, source_target_pairs={{2,0},{3,1},{0,2},{1,3},{6,4},{7,5},{4,6},{5,7},{10,8},{11,9},{8,1... | collective-permute-start | bytes 442376 | tf_op jit(solution)/shard_map/ppermute | solution.py:39
  77.6 14.0 %collective-permute-start.27 = (bf16[192,384]{1,0:T(8,128)(2,1)S(1)}, bf16[192,384]{1,0:T(8,128)(2,1)S(1)}, u32[]{:S(2)}, u32[]{:S(2)}) collective-permute-start(bf16[192,384]{1,0:T(8,128)(2,1)S(1)} %collective-permute-done.26.refs_10_), channel_id=1, source_target_pairs={{4,0},{5,1},{6,2},{7,3},{0,4},{1,5},{2,6},{3,7},{12,8},{13,9},{14,... | collective-permute-start | bytes 442376 | tf_op jit(solution)/shard_map/ppermute | solution.py:39
  82.9 9.3 %collective-permute-start.20 = (bf16[768,384]{1,0:T(8,128)(2,1)S(1)}, bf16[768,384]{1,0:T(8,128)(2,1)S(1)}, u32[]{:S(2)}, u32[]{:S(2)}) collective-permute-start(bf16[768,384]{1,0:T(8,128)(2,1)S(1)} %pad_maximum_fusion.2), channel_id=1, source_target_pairs={{1,0},{0,1},{3,2},{2,3},{5,4},{4,5},{7,6},{6,7},{9,8},{8,9},{11,10... | collective-permute-start | bytes 1769480 | tf_op jit(solution)/shard_map/ppermute | solution.py:39
  117.4 9.9 %collective-permute-start.41 = (bf16[192,384]{1,0:T(8,128)(2,1)S(1)}, bf16[192,384]{1,0:T(8,128)(2,1)S(1)}, u32[]{:S(2)}, u32[]{:S(2)}) collective-permute-start(bf16[192,384]{1,0:T(8,128)(2,1)S(1)} %square.1.refs_0_), channel_id=1, source_target_pairs={{16,0},{17,1},{18,2},{19,3},{20,4},{21,5},{22,6},{23,7},{24,8},{25... | collective-permute-start | bytes 442376 | tf_op jit(solution)/shard_map/ppermute | solution.py:39
  118.2 9.1 %collective-permute-start.38 = (bf16[192,384]{1,0:T(8,128)(2,1)S(1)}, bf16[192,384]{1,0:T(8,128)(2,1)S(1)}, u32[]{:S(2)}, u32[]{:S(2)}) collective-permute-start(bf16[192,384]{1,0:T(8,128)(2,1)S(1)} %square.1.refs_0_), channel_id=1, source_target_pairs={{6,0},{7,1},{4,2},{5,3},{2,4},{3,5},{0,6},{1,7},{14,8},{15,9},{12,... | collective-permute-start | bytes 442376 | tf_op jit(solution)/shard_map/ppermute | solution.py:39
  (22 other events, 115.8 us)

commit v15 on v14

--- a/solution.py
+++ b/solution.py
@@ -174,12 +174,13 @@
         sent[TAIL + half * rows : TAIL + (half + 1) * rows, :] = value
         trio[TAIL + half * rows : TAIL + (half + 1) * rows, :] = value
     top = (iota((TAIL, row_blocks), 0) == iota((TAIL, row_blocks), 1)).astype(BF16)
-    tail = jnp.zeros((TAIL, columns), F32)
+    packed = jnp.zeros((row_blocks, columns), F32)
     for number in range(FIRST + seconds.shape[1]):
         block = firsts[number] if number < FIRST else seconds[:, number - FIRST, :]
         column = iota((column_blocks, columns), 1) - number * column_blocks
         spread = (iota((column_blocks, columns), 0) == column).astype(BF16)
-        tail += dot(dot(top, block.astype(BF16)).astype(BF16), spread)
+        packed += dot(block.astype(BF16), spread)
+    tail = dot(top, packed.astype(BF16))
     sent[:TAIL, :] = tail.astype(BF16)
     trio[:TAIL, :] = tail.astype(BF16)
 

time: 144 us -> 143 us (level)
  no operation moved by 1% of the time
where the time goes in v15:
time: 143 us
  waiting for transfers between devices  79.4 us (56%)
  starting transfers between devices  45.6 us (32%)
  Pallas kernels  16.1 us (11%)
    ppermute x45, waiting for transfers between devices, move(): return lax.ppermute(value, AXES, permutation(self.rows, self.cols, source))  79.4 us
    ppermute x45, starting transfers between devices, move(): return lax.ppermute(value, AXES, permutation(self.rows, self.cols, source))  45.6 us
    pallas_call x1, Pallas kernels, on_device(): call(functools.partial(series_kernel, layout, count, len(arrays)), [jax.S...  8.84 us
    pallas_call x4, Pallas kernels, views_call(): call(body, outs, [INVMEM] * len(operands), scratch, name, flops)(*operands)  4.52 us
  transfers between devices with their start and end apart: 45, of which 29 were waited for; matrix products, arithmetic and copies ran while one was open for 0% of the time, Pallas kernels for 1%

profile of v15, /device:TPU:1, one launch (start us, length us, event | category | flops | bytes accessed | tf_op | source)
XLA Modules:
  0.0 142.7 jit_solution(14926516839159807763)
XLA Ops:
  0.0 2.8 %mask.1 = (bf16[192,384]{1,0:T(8,128)(2,1)}, bf16[384,384]{1,0:T(8,128)(2,1)}, bf16[400,384]{1,0:T(8,128)(2,1)}, bf16[592,384]{1,0:T(8,128)(2,1)}) custom-call(s32[3,6,12]{2,1,0:T(8,128)} %refs_0_.1, bf16[192,384]{1,0:T(8,128)(2,1)} %refs_1_.1, bf16[192,384]{1,0:T(8,128)(2,1)} %refs_2_.1, bf16[192,384]{1,0:T(8,128)(2,1)} %refs_3_.1, s32[3,6,12]{2,1,0:T(8,128)} %refs_4_.1, ...), custom_call_target="tpu_custom_call" | custom-call | flops 1000 | bytes 1000 | tf_op jit(solution)/shard_map/mask/pallas_call | solution.py:400
  2.8 4.7 %collective-permute-start.1 = (bf16[192,384]{1,0:T(8,128)(2,1)}, bf16[192,384]{1,0:T(8,128)(2,1)S(1)}, u32[]{:S(2)}, u32[]{:S(2)}) collective-permute-start(bf16[192,384]{1,0:T(8,128)(2,1)} %get-tuple-element.31), channel_id=1, source_target_pairs={{16,0},{20,1},{18,2},{22,3},{17,4},{21,5},{19,6},{23,7},{24,8},{28... | collective-permute-start | bytes 442376 | tf_op jit(solution)/shard_map/ppermute | solution.py:39
  9.7 2.6 %collective-permute-start = (bf16[192,384]{1,0:T(8,128)(2,1)}, bf16[192,384]{1,0:T(8,128)(2,1)S(1)}, u32[]{:S(2)}, u32[]{:S(2)}) collective-permute-start(bf16[192,384]{1,0:T(8,128)(2,1)} %get-tuple-element.31), channel_id=1, source_target_pairs={{8,0},{12,1},{10,2},{14,3},{9,4},{13,5},{11,6},{15,7},{0,8},{4,9},... | collective-permute-start | bytes 442376 | tf_op jit(solution)/shard_map/ppermute | solution.py:39
  12.3 3.0 %collective-permute-done.1.refs_6_ = bf16[192,384]{1,0:T(8,128)(2,1)S(1)} collective-permute-done((bf16[192,384]{1,0:T(8,128)(2,1)}, bf16[192,384]{1,0:T(8,128)(2,1)S(1)}, u32[]{:S(2)}, u32[]{:S(2)}) %collective-permute-start.1) | collective-permute-done | bytes 147488 | tf_op jit(solution)/shard_map/ppermute | solution.py:39
  15.6 2.2 %collective-permute-start.7 = (bf16[384,384]{1,0:T(8,128)(2,1)}, bf16[384,384]{1,0:T(8,128)(2,1)S(1)}, u32[]{:S(2)}, u32[]{:S(2)}) collective-permute-start(bf16[384,384]{1,0:T(8,128)(2,1)} %get-tuple-element.32), channel_id=1, source_target_pairs={{2,0},{6,1},{0,2},{4,3},{3,4},{7,5},{1,6},{5,7},{10,8},{14,9},{8,1... | collective-permute-start | bytes 884744 | tf_op jit(solution)/shard_map/ppermute | solution.py:39
  20.7 5.3 %collective-permute-done.7.refs_2_ = bf16[384,384]{1,0:T(8,128)(2,1)S(1)} collective-permute-done((bf16[384,384]{1,0:T(8,128)(2,1)}, bf16[384,384]{1,0:T(8,128)(2,1)S(1)}, u32[]{:S(2)}, u32[]{:S(2)}) %collective-permute-start.7) | collective-permute-done | bytes 294944 | tf_op jit(solution)/shard_map/ppermute | solution.py:39
  26.0 7.2 %collective-permute-done.6.refs_1_ = bf16[384,384]{1,0:T(8,128)(2,1)S(1)} collective-permute-done((bf16[384,384]{1,0:T(8,128)(2,1)}, bf16[384,384]{1,0:T(8,128)(2,1)S(1)}, u32[]{:S(2)}, u32[]{:S(2)}) %collective-permute-start.6) | collective-permute-done | bytes 294944 | tf_op jit(solution)/shard_map/ppermute | solution.py:39
  39.6 9.8 %collective-permute-done.14.refs_7_ = bf16[400,384]{1,0:T(8,128)(2,1)S(1)} collective-permute-done((bf16[400,384]{1,0:T(8,128)(2,1)S(1)}, bf16[400,384]{1,0:T(8,128)(2,1)S(1)}, u32[]{:S(2)}, u32[]{:S(2)}) %collective-permute-start.14) | collective-permute-done | bytes 307232 | tf_op jit(solution)/shard_map/ppermute | solution.py:39
  51.1 2.1 %collective-permute-done.10.refs_1_ = bf16[384,384]{1,0:T(8,128)(2,1)S(1)} collective-permute-done((bf16[384,384]{1,0:T(8,128)(2,1)S(1)}, bf16[384,384]{1,0:T(8,128)(2,1)S(1)}, u32[]{:S(2)}, u32[]{:S(2)}) %collective-permute-start.10) | collective-permute-done | bytes 294944 | tf_op jit(solution)/shard_map/ppermute | solution.py:39
  53.8 2.0 %collective-permute-done.16.refs_10_ = bf16[400,384]{1,0:T(8,128)(2,1)S(1)} collective-permute-done((bf16[400,384]{1,0:T(8,128)(2,1)S(1)}, bf16[400,384]{1,0:T(8,128)(2,1)S(1)}, u32[]{:S(2)}, u32[]{:S(2)}) %collective-permute-start.16) | collective-permute-done | bytes 307232 | tf_op jit(solution)/shard_map/ppermute | solution.py:39
  61.6 5.1 %collective-permute-done.22 = bf16[192,384]{1,0:T(8,128)(2,1)S(1)} collective-permute-done((bf16[192,384]{1,0:T(8,128)(2,1)S(1)}, bf16[192,384]{1,0:T(8,128)(2,1)S(1)}, u32[]{:S(2)}, u32[]{:S(2)}) %collective-permute-start.22) | collective-permute-done | bytes 147488 | tf_op jit(solution)/shard_map/ppermute | solution.py:39
  71.2 2.9 %collective-permute-done.26.refs_10_ = bf16[192,384]{1,0:T(8,128)(2,1)S(1)} collective-permute-done((bf16[192,384]{1,0:T(8,128)(2,1)S(1)}, bf16[192,384]{1,0:T(8,128)(2,1)S(1)}, u32[]{:S(2)}, u32[]{:S(2)}) %collective-permute-start.26) | collective-permute-done | bytes 147488 | tf_op jit(solution)/shard_map/ppermute | solution.py:39
  77.0 5.1 %collective-permute-done.24.refs_8_ = bf16[384,384]{1,0:T(8,128)(2,1)S(1)} collective-permute-done((bf16[384,384]{1,0:T(8,128)(2,1)S(1)}, bf16[384,384]{1,0:T(8,128)(2,1)S(1)}, u32[]{:S(2)}, u32[]{:S(2)}) %collective-permute-start.24) | collective-permute-done | bytes 294944 | tf_op jit(solution)/shard_map/ppermute | solution.py:39
  82.1 3.8 %collective-permute-start.20 = (bf16[768,384]{1,0:T(8,128)(2,1)S(1)}, bf16[768,384]{1,0:T(8,128)(2,1)S(1)}, u32[]{:S(2)}, u32[]{:S(2)}) collective-permute-start(bf16[768,384]{1,0:T(8,128)(2,1)S(1)} %pad_maximum_fusion.2), channel_id=1, source_target_pairs={{1,0},{0,1},{3,2},{2,3},{5,4},{4,5},{7,6},{6,7},{9,8},{8,9},{11,10... | collective-permute-start | bytes 1769480 | tf_op jit(solution)/shard_map/ppermute | solution.py:39
  86.1 2.2 %collective-permute-done.28.refs_13_ = bf16[192,384]{1,0:T(8,128)(2,1)S(1)} collective-permute-done((bf16[192,384]{1,0:T(8,128)(2,1)S(1)}, bf16[192,384]{1,0:T(8,128)(2,1)S(1)}, u32[]{:S(2)}, u32[]{:S(2)}) %collective-permute-start.28) | collective-permute-done | bytes 147488 | tf_op jit(solution)/shard_map/ppermute | solution.py:39
  88.4 2.3 %collective-permute-done.27.refs_12_ = bf16[192,384]{1,0:T(8,128)(2,1)S(1)} collective-permute-done((bf16[192,384]{1,0:T(8,128)(2,1)S(1)}, bf16[192,384]{1,0:T(8,128)(2,1)S(1)}, u32[]{:S(2)}, u32[]{:S(2)}) %collective-permute-start.27) | collective-permute-done | bytes 147488 | tf_op jit(solution)/shard_map/ppermute | solution.py:39
  91.6 3.1 %collective-permute-done.31.refs_11_ = bf16[768,384]{1,0:T(8,128)(2,1)S(1)} collective-permute-done((bf16[768,384]{1,0:T(8,128)(2,1)S(1)}, bf16[768,384]{1,0:T(8,128)(2,1)S(1)}, u32[]{:S(2)}, u32[]{:S(2)}) %collective-permute-start.31) | collective-permute-done | bytes 589856 | tf_op jit(solution)/shard_map/ppermute | solution.py:39
  94.7 8.8 %series.1 = (bf16[192,1536]{1,0:T(8,128)(2,1)S(1)}, bf16[192,384]{1,0:T(8,128)(2,1)S(1)}) custom-call(bf16[192,384]{1,0:T(8,128)(2,1)S(1)} %generator.1.refs_0_, bf16[768,384]{1,0:T(8,128)(2,1)S(1)} %collective-permute-done.20.refs_1_, bf16[192,384]{1,0:T(8,128)(2,1)S(1)} %collective-permute-done.17.refs_2_, ...), custom_call_target="tpu_custom_call" | custom-call | flops 1000 | bytes 1000 | tf_op jit(solution)/shard_map/series/pallas_call | solution.py:483
  106.3 3.3 %collective-permute-done.34.refs_3_ = bf16[192,384]{1,0:T(8,128)(2,1)S(1)} collective-permute-done((bf16[192,384]{1,0:T(8,128)(2,1)S(1)}, bf16[192,384]{1,0:T(8,128)(2,1)S(1)}, u32[]{:S(2)}, u32[]{:S(2)}) %collective-permute-start.34) | collective-permute-done | bytes 147488 | tf_op jit(solution)/shard_map/ppermute | solution.py:39
  109.6 2.4 %collective-permute-done.33.refs_2_ = bf16[192,384]{1,0:T(8,128)(2,1)S(1)} collective-permute-done((bf16[192,384]{1,0:T(8,128)(2,1)S(1)}, bf16[192,384]{1,0:T(8,128)(2,1)S(1)}, u32[]{:S(2)}, u32[]{:S(2)}) %collective-permute-start.33) | collective-permute-done | bytes 147488 | tf_op jit(solution)/shard_map/ppermute | solution.py:39
  121.4 5.0 %collective-permute-done.41.refs_6_ = bf16[192,384]{1,0:T(8,128)(2,1)S(1)} collective-permute-done((bf16[192,384]{1,0:T(8,128)(2,1)S(1)}, bf16[192,384]{1,0:T(8,128)(2,1)S(1)}, u32[]{:S(2)}, u32[]{:S(2)}) %collective-permute-start.41) | collective-permute-done | bytes 147488 | tf_op jit(solution)/shard_map/ppermute | solution.py:39
  127.9 3.3 %collective-permute-done.42.refs_7_ = bf16[192,384]{1,0:T(8,128)(2,1)S(1)} collective-permute-done((bf16[192,384]{1,0:T(8,128)(2,1)S(1)}, bf16[192,384]{1,0:T(8,128)(2,1)S(1)}, u32[]{:S(2)}, u32[]{:S(2)}) %collective-permute-start.42) | collective-permute-done | bytes 147488 | tf_op jit(solution)/shard_map/ppermute | solution.py:39
  135.5 2.6 %collective-permute-start.44 = (bf16[192,384]{1,0:T(8,128)(2,1)S(1)}, bf16[192,384]{1,0:T(8,128)(2,1)S(1)}, u32[]{:S(2)}, u32[]{:S(2)}) collective-permute-start(bf16[192,384]{1,0:T(8,128)(2,1)S(1)} %evolve.1), channel_id=1, source_target_pairs={{0,0},{4,1},{2,2},{6,3},{1,4},{5,5},{3,6},{7,7},{8,8},{12,9},{10,1... | collective-permute-start | bytes 442376 | tf_op jit(solution)/shard_map/ppermute | solution.py:39
  138.1 3.9 %collective-permute-done.44 = bf16[192,384]{1,0:T(8,128)(2,1)S(1)} collective-permute-done((bf16[192,384]{1,0:T(8,128)(2,1)S(1)}, bf16[192,384]{1,0:T(8,128)(2,1)S(1)}, u32[]{:S(2)}, u32[]{:S(2)}) %collective-permute-start.44) | collective-permute-done | bytes 147488 | tf_op jit(solution)/shard_map/ppermute | solution.py:39
  (92 shorter events, 46.9 us)
Async XLA Ops:
  2.8 12.6 %collective-permute-start.1 = (bf16[192,384]{1,0:T(8,128)(2,1)}, bf16[192,384]{1,0:T(8,128)(2,1)S(1)}, u32[]{:S(2)}, u32[]{:S(2)}) collective-permute-start(bf16[192,384]{1,0:T(8,128)(2,1)} %get-tuple-element.31), channel_id=1, source_target_pairs={{16,0},{20,1},{18,2},{22,3},{17,4},{21,5},{19,6},{23,7},{24,8},{28... | collective-permute-start | bytes 442376 | tf_op jit(solution)/shard_map/ppermute | solution.py:39
  7.5 25.6 %collective-permute-start.4 = (bf16[592,384]{1,0:T(8,128)(2,1)}, bf16[592,384]{1,0:T(8,128)(2,1)S(1)}, u32[]{:S(2)}, u32[]{:S(2)}) collective-permute-start(bf16[592,384]{1,0:T(8,128)(2,1)} %get-tuple-element.34), channel_id=1, source_target_pairs={{0,0},{4,1},{2,2},{6,3},{1,4},{5,5},{3,6},{7,7},{8,8},{12,9},{10,1... | collective-permute-start | bytes 1363976 | tf_op jit(solution)/shard_map/ppermute | solution.py:39
  9.4 10.3 %collective-permute-start.2 = (bf16[384,384]{1,0:T(8,128)(2,1)}, bf16[384,384]{1,0:T(8,128)(2,1)S(1)}, u32[]{:S(2)}, u32[]{:S(2)}) collective-permute-start(bf16[384,384]{1,0:T(8,128)(2,1)} %get-tuple-element.32), channel_id=1, source_target_pairs={{3,0},{7,1},{1,2},{5,3},{2,4},{6,5},{0,6},{4,7},{11,8},{15,9},{9,1... | collective-permute-start | bytes 884744 | tf_op jit(solution)/shard_map/ppermute | solution.py:39
  9.7 10.1 %collective-permute-start = (bf16[192,384]{1,0:T(8,128)(2,1)}, bf16[192,384]{1,0:T(8,128)(2,1)S(1)}, u32[]{:S(2)}, u32[]{:S(2)}) collective-permute-start(bf16[192,384]{1,0:T(8,128)(2,1)} %get-tuple-element.31), channel_id=1, source_target_pairs={{8,0},{12,1},{10,2},{14,3},{9,4},{13,5},{11,6},{15,7},{0,8},{4,9},... | collective-permute-start | bytes 442376 | tf_op jit(solution)/shard_map/ppermute | solution.py:39
  15.4 17.8 %collective-permute-start.5 = (bf16[400,384]{1,0:T(8,128)(2,1)}, bf16[400,384]{1,0:T(8,128)(2,1)S(1)}, u32[]{:S(2)}, u32[]{:S(2)}) collective-permute-start(bf16[400,384]{1,0:T(8,128)(2,1)} %get-tuple-element.36), channel_id=1, source_target_pairs={{16,0},{20,1},{18,2},{22,3},{17,4},{21,5},{19,6},{23,7},{24,8},{28... | collective-permute-start | bytes 921608 | tf_op jit(solution)/shard_map/ppermute | solution.py:39
  15.6 10.4 %collective-permute-start.7 = (bf16[384,384]{1,0:T(8,128)(2,1)}, bf16[384,384]{1,0:T(8,128)(2,1)S(1)}, u32[]{:S(2)}, u32[]{:S(2)}) collective-permute-start(bf16[384,384]{1,0:T(8,128)(2,1)} %get-tuple-element.32), channel_id=1, source_target_pairs={{2,0},{6,1},{0,2},{4,3},{3,4},{7,5},{1,6},{5,7},{10,8},{14,9},{8,1... | collective-permute-start | bytes 884744 | tf_op jit(solution)/shard_map/ppermute | solution.py:39
  19.8 13.4 %collective-permute-start.6 = (bf16[384,384]{1,0:T(8,128)(2,1)}, bf16[384,384]{1,0:T(8,128)(2,1)S(1)}, u32[]{:S(2)}, u32[]{:S(2)}) collective-permute-start(bf16[384,384]{1,0:T(8,128)(2,1)} %get-tuple-element.32), channel_id=1, source_target_pairs={{1,0},{5,1},{3,2},{7,3},{0,4},{4,5},{2,6},{6,7},{9,8},{13,9},{11,1... | collective-permute-start | bytes 884744 | tf_op jit(solution)/shard_map/ppermute | solution.py:39
  19.8 13.4 %collective-permute-start.3 = (bf16[192,384]{1,0:T(8,128)(2,1)S(1)}, bf16[192,384]{1,0:T(8,128)(2,1)S(1)}, u32[]{:S(2)}, u32[]{:S(2)}) collective-permute-start(bf16[192,384]{1,0:T(8,128)(2,1)S(1)} %collective-permute-done.1.refs_6_), channel_id=1, source_target_pairs={{8,0},{9,1},{10,2},{11,3},{12,4},{13,5},{14,6},{15,7},{0,8},{1,9},... | collective-permute-start | bytes 442376 | tf_op jit(solution)/shard_map/ppermute | solution.py:39
  33.9 15.5 %collective-permute-start.13 = (bf16[400,384]{1,0:T(8,128)(2,1)S(1)}, bf16[400,384]{1,0:T(8,128)(2,1)S(1)}, u32[]{:S(2)}, u32[]{:S(2)}) collective-permute-start(bf16[400,384]{1,0:T(8,128)(2,1)S(1)} %slice.36), channel_id=1, source_target_pairs={{8,0},{9,1},{10,2},{11,3},{12,4},{13,5},{14,6},{15,7},{0,8},{1,9},... | collective-permute-start | bytes 921608 | tf_op jit(solution)/shard_map/ppermute | solution.py:39
  34.0 15.5 %collective-permute-start.14 = (bf16[400,384]{1,0:T(8,128)(2,1)S(1)}, bf16[400,384]{1,0:T(8,128)(2,1)S(1)}, u32[]{:S(2)}, u32[]{:S(2)}) collective-permute-start(bf16[400,384]{1,0:T(8,128)(2,1)S(1)} %collective-permute-done.5.refs_6_), channel_id=1, source_target_pairs={{8,0},{9,1},{10,2},{11,3},{12,4},{13,5},{14,6},{15,7},{0,8},{1,9},... | collective-permute-start | bytes 921608 | tf_op jit(solution)/shard_map/ppermute | solution.py:39
  36.9 12.5 %collective-permute-start.12 = (bf16[384,384]{1,0:T(8,128)(2,1)S(1)}, bf16[384,384]{1,0:T(8,128)(2,1)S(1)}, u32[]{:S(2)}, u32[]{:S(2)}) collective-permute-start(bf16[384,384]{1,0:T(8,128)(2,1)S(1)} %first.1.refs_0_), channel_id=1, source_target_pairs={{6,0},{7,1},{4,2},{5,3},{2,4},{3,5},{0,6},{1,7},{14,8},{15,9},{12,... | collective-permute-start | bytes 884744 | tf_op jit(solution)/shard_map/ppermute | solution.py:39
  38.4 12.7 %collective-permute-start.11 = (bf16[384,384]{1,0:T(8,128)(2,1)S(1)}, bf16[384,384]{1,0:T(8,128)(2,1)S(1)}, u32[]{:S(2)}, u32[]{:S(2)}) collective-permute-start(bf16[384,384]{1,0:T(8,128)(2,1)S(1)} %first.1.refs_0_), channel_id=1, source_target_pairs={{2,0},{3,1},{0,2},{1,3},{6,4},{7,5},{4,6},{5,7},{10,8},{11,9},{8,1... | collective-permute-start | bytes 884744 | tf_op jit(solution)/shard_map/ppermute | solution.py:39
  38.4 14.8 %collective-permute-start.10 = (bf16[384,384]{1,0:T(8,128)(2,1)S(1)}, bf16[384,384]{1,0:T(8,128)(2,1)S(1)}, u32[]{:S(2)}, u32[]{:S(2)}) collective-permute-start(bf16[384,384]{1,0:T(8,128)(2,1)S(1)} %first.1.refs_0_), channel_id=1, source_target_pairs={{4,0},{5,1},{6,2},{7,3},{0,4},{1,5},{2,6},{3,7},{12,8},{13,9},{14,... | collective-permute-start | bytes 884744 | tf_op jit(solution)/shard_map/ppermute | solution.py:39
  57.1 9.6 %collective-permute-start.22 = (bf16[192,384]{1,0:T(8,128)(2,1)S(1)}, bf16[192,384]{1,0:T(8,128)(2,1)S(1)}, u32[]{:S(2)}, u32[]{:S(2)}) collective-permute-start(bf16[192,384]{1,0:T(8,128)(2,1)S(1)} %generator.1.refs_0_), channel_id=1, source_target_pairs={{16,0},{17,1},{18,2},{19,3},{20,4},{21,5},{22,6},{23,7},{24,8},{25... | collective-permute-start | bytes 442376 | tf_op jit(solution)/shard_map/ppermute | solution.py:39
  57.3 9.4 %collective-permute-start.21 = (bf16[192,384]{1,0:T(8,128)(2,1)S(1)}, bf16[192,384]{1,0:T(8,128)(2,1)S(1)}, u32[]{:S(2)}, u32[]{:S(2)}) collective-permute-start(bf16[192,384]{1,0:T(8,128)(2,1)S(1)} %generator.1.refs_0_), channel_id=1, source_target_pairs={{8,0},{9,1},{10,2},{11,3},{12,4},{13,5},{14,6},{15,7},{0,8},{1,9},... | collective-permute-start | bytes 442376 | tf_op jit(solution)/shard_map/ppermute | solution.py:39
  68.2 8.4 %collective-permute-start.25 = (bf16[384,384]{1,0:T(8,128)(2,1)S(1)}, bf16[384,384]{1,0:T(8,128)(2,1)S(1)}, u32[]{:S(2)}, u32[]{:S(2)}) collective-permute-start(bf16[384,384]{1,0:T(8,128)(2,1)S(1)} %pad_maximum_fusion.8.refs_5_), channel_id=1, source_target_pairs={{6,0},{7,1},{4,2},{5,3},{2,4},{3,5},{0,6},{1,7},{14,8},{15,9},{12,... | collective-permute-start | bytes 884744 | tf_op jit(solution)/shard_map/ppermute | solution.py:39
  69.3 12.7 %collective-permute-start.24 = (bf16[384,384]{1,0:T(8,128)(2,1)S(1)}, bf16[384,384]{1,0:T(8,128)(2,1)S(1)}, u32[]{:S(2)}, u32[]{:S(2)}) collective-permute-start(bf16[384,384]{1,0:T(8,128)(2,1)S(1)} %pad_maximum_fusion.8.refs_5_), channel_id=1, source_target_pairs={{2,0},{3,1},{0,2},{1,3},{6,4},{7,5},{4,6},{5,7},{10,8},{11,9},{8,1... | collective-permute-start | bytes 884744 | tf_op jit(solution)/shard_map/ppermute | solution.py:39
  70.1 15.8 %collective-permute-start.23 = (bf16[384,384]{1,0:T(8,128)(2,1)S(1)}, bf16[384,384]{1,0:T(8,128)(2,1)S(1)}, u32[]{:S(2)}, u32[]{:S(2)}) collective-permute-start(bf16[384,384]{1,0:T(8,128)(2,1)S(1)} %pad_maximum_fusion.8.refs_5_), channel_id=1, source_target_pairs={{4,0},{5,1},{6,2},{7,3},{0,4},{1,5},{2,6},{3,7},{12,8},{13,9},{14,... | collective-permute-start | bytes 884744 | tf_op jit(solution)/shard_map/ppermute | solution.py:39
  74.1 12.0 %collective-permute-start.29 = (bf16[192,384]{1,0:T(8,128)(2,1)S(1)}, bf16[192,384]{1,0:T(8,128)(2,1)S(1)}, u32[]{:S(2)}, u32[]{:S(2)}) collective-permute-start(bf16[192,384]{1,0:T(8,128)(2,1)S(1)} %collective-permute-done.26.refs_10_), channel_id=1, source_target_pairs={{6,0},{7,1},{4,2},{5,3},{2,4},{3,5},{0,6},{1,7},{14,8},{15,9},{12,... | collective-permute-start | bytes 442376 | tf_op jit(solution)/shard_map/ppermute | solution.py:39
  76.1 12.2 %collective-permute-start.28 = (bf16[192,384]{1,0:T(8,128)(2,1)S(1)}, bf16[192,384]{1,0:T(8,128)(2,1)S(1)}, u32[]{:S(2)}, u32[]{:S(2)}) collective-permute-start(bf16[192,384]{1,0:T(8,128)(2,1)S(1)} %collective-permute-done.26.refs_10_), channel_id=1, source_target_pairs={{2,0},{3,1},{0,2},{1,3},{6,4},{7,5},{4,6},{5,7},{10,8},{11,9},{8,1... | collective-permute-start | bytes 442376 | tf_op jit(solution)/shard_map/ppermute | solution.py:39
  76.7 14.0 %collective-permute-start.27 = (bf16[192,384]{1,0:T(8,128)(2,1)S(1)}, bf16[192,384]{1,0:T(8,128)(2,1)S(1)}, u32[]{:S(2)}, u32[]{:S(2)}) collective-permute-start(bf16[192,384]{1,0:T(8,128)(2,1)S(1)} %collective-permute-done.26.refs_10_), channel_id=1, source_target_pairs={{4,0},{5,1},{6,2},{7,3},{0,4},{1,5},{2,6},{3,7},{12,8},{13,9},{14,... | collective-permute-start | bytes 442376 | tf_op jit(solution)/shard_map/ppermute | solution.py:39
  82.1 9.3 %collective-permute-start.20 = (bf16[768,384]{1,0:T(8,128)(2,1)S(1)}, bf16[768,384]{1,0:T(8,128)(2,1)S(1)}, u32[]{:S(2)}, u32[]{:S(2)}) collective-permute-start(bf16[768,384]{1,0:T(8,128)(2,1)S(1)} %pad_maximum_fusion.2), channel_id=1, source_target_pairs={{1,0},{0,1},{3,2},{2,3},{5,4},{4,5},{7,6},{6,7},{9,8},{8,9},{11,10... | collective-permute-start | bytes 1769480 | tf_op jit(solution)/shard_map/ppermute | solution.py:39
  116.5 9.9 %collective-permute-start.41 = (bf16[192,384]{1,0:T(8,128)(2,1)S(1)}, bf16[192,384]{1,0:T(8,128)(2,1)S(1)}, u32[]{:S(2)}, u32[]{:S(2)}) collective-permute-start(bf16[192,384]{1,0:T(8,128)(2,1)S(1)} %square.1.refs_0_), channel_id=1, source_target_pairs={{16,0},{17,1},{18,2},{19,3},{20,4},{21,5},{22,6},{23,7},{24,8},{25... | collective-permute-start | bytes 442376 | tf_op jit(solution)/shard_map/ppermute | solution.py:39
  117.3 9.1 %collective-permute-start.38 = (bf16[192,384]{1,0:T(8,128)(2,1)S(1)}, bf16[192,384]{1,0:T(8,128)(2,1)S(1)}, u32[]{:S(2)}, u32[]{:S(2)}) collective-permute-start(bf16[192,384]{1,0:T(8,128)(2,1)S(1)} %square.1.refs_0_), channel_id=1, source_target_pairs={{6,0},{7,1},{4,2},{5,3},{2,4},{3,5},{0,6},{1,7},{14,8},{15,9},{12,... | collective-permute-start | bytes 442376 | tf_op jit(solution)/shard_map/ppermute | solution.py:39
  (22 other events, 115.7 us)
